TPU v7x, 32 devices: a whole 2x2x4 slice. The times are simulated.
32 devices in a mesh: section: 4 (over y, x), expert: 8 (over z, core).
Axes of the slice: x: 2, y: 2, z: 4, core: 2. Of those that a mesh axis runs over, the one named last changes fastest.
Arguments:
- forward_sent: bfloat16 [4, 512, 2048], P('section', 'expert'), may hold values from -6 to 6
- embedded: bfloat16 [512, 2048], P('expert'), may hold values from -6 to 6
- forward_routes: int32 [4, 512, 2], P('section', 'expert'), may hold values from 0 to 63, all different within a row; in each aligned block of 64 rows (0 to 63, 64 to 127, ..., all dimensions but the last counted through in order) at most 3 rows name the same one
- backward_sent: bfloat16 [4, 512, 2048], P('section', 'expert'), may hold values from -6 to 6
- loss_gradient: bfloat16 [512, 2048], P('expert'), may hold values from -6 to 6
- saved_inputs: bfloat16 [4, 512, 2048], P('section', 'expert'), may hold values from -6 to 6
- backward_routes: int32 [4, 512, 2], P('section', 'expert'), may hold values from 0 to 63, all different within a row; in each aligned block of 64 rows (0 to 63, 64 to 127, ..., all dimensions but the last counted through in order) at most 3 rows name the same one
- pre_activation: bfloat16 [4, 8, 64, 3, 1024], P('section', None, 'expert'), may hold values from -6 to 6
- norm_gain: bfloat16 [4, 2048], P('section'), may hold values from 0.099609375 to 1.8984375
- router: bfloat16 [4, 2048, 64], P('section'), may hold values from -0.125 to 0.125
- up_weight: bfloat16 [64, 2048, 1024], P('expert'), may hold values from -0.125 to 0.125
- down_weight: bfloat16 [64, 1024, 2048], P('expert'), may hold values from -0.1875 to 0.1875
Outputs:
- forward_output: bfloat16 [4, 512, 2048], P('section', 'expert')
- input_gradient: bfloat16 [4, 512, 2048], P('section', 'expert')
Inputs may be any that keep to these rules, and one draw needn't show every extreme that they name: `forward_routes`: in each aligned block of 64 rows (one device's tokens at one section) no expert is named by more than 3 rows, a bound that some block reaches; the 2 entries of a row differ. `backward_routes`: in each aligned block of 64 rows (one device's tokens at one section) no expert is named by more than 3 rows, a bound that some block reaches; the 2 entries of a row differ.
All inputs are finite; a program needn't handle non-finite values.
Results may differ from a plain program's by a relative error of at most 0.0053.
Values may be sent and summed in bfloat16 or wider, within the bound.
No kernel may reach another device: no remote copies, remote signals or barrier semaphores. Data moves between devices by JAX's collectives and lax.ppermute only.
A program may use at most 128 MiB of HBM per device.

v0:
```python
import jax
import jax.numpy as jnp
from jax import lax
from jax.sharding import PartitionSpec as P

EPS = 1e-06
HIGH = lax.Precision.HIGHEST


def from_behind(block, axis, distance):
    devices = range(lax.axis_size(axis))
    route = [(i - distance, i) for i in devices if i - distance in devices]
    return lax.ppermute(block, axis, route)


def slot_targets(routes, experts, capacity):
    flattened = routes.reshape(-1)
    onehot = (flattened[:, None] == jnp.arange(experts, dtype=jnp.int32)[None, :]).astype(jnp.int32)
    before = jnp.cumsum(onehot, axis=0) - onehot
    ranked = jnp.sum(before * onehot, axis=1)
    return (flattened * capacity + ranked).reshape(routes.shape)


def prepare_routes(tokens, gain_row, router_mat, routes, experts, capacity):
    widened = tokens.astype(jnp.float32)
    inv_rms = lax.rsqrt(jnp.mean(widened * widened, axis=-1) + EPS)
    normed = (widened * inv_rms[:, None] * gain_row.astype(jnp.float32)).astype(jnp.bfloat16)
    logits = jnp.dot(normed, router_mat, preferred_element_type=jnp.float32)
    chosen = jnp.take_along_axis(logits, routes, axis=1)
    exponent = jnp.exp(chosen)
    shares = exponent / jnp.sum(exponent, axis=1, keepdims=True)
    rounded = lax.optimization_barrier(shares.astype(jnp.bfloat16)).astype(jnp.float32)
    targets = slot_targets(routes, experts, capacity)
    slot_table = (targets[..., None] == jnp.arange(experts * capacity, dtype=jnp.int32)).astype(
        jnp.float32
    )
    placing = jnp.sum(slot_table, axis=1).astype(jnp.bfloat16)
    mixing = jnp.sum(slot_table * rounded[..., None], axis=1).astype(jnp.bfloat16)
    return (widened, inv_rms, normed, shares, slot_table, placing, mixing)


def on_device(
    forward_sent,
    embedded,
    forward_routes,
    backward_sent,
    loss_gradient,
    saved_inputs,
    backward_routes,
    pre_activation,
    norm_gain,
    router,
    up_weight,
    down_weight,
):
    section_index = lax.axis_index("section")
    final_section = lax.axis_size("section") - 1
    sources = lax.axis_size("expert")
    experts = router.shape[2]
    capacity = pre_activation.shape[3]
    local_count = up_weight.shape[0]
    width = up_weight.shape[1]
    slots = experts * capacity
    gain_row = norm_gain[0]
    router_mat = router[0]
    arrived = from_behind(forward_sent[0], "section", 1)
    tokens = jnp.where(section_index == 0, embedded, arrived)
    returned_grad = from_behind(backward_sent[0], "section", -1)
    upstream = jnp.where(section_index == final_section, loss_gradient, returned_grad)
    widened, inv_rms, normed, shares, slot_table, placing, mixing = prepare_routes(
        tokens, gain_row, router_mat, forward_routes[0], experts, capacity
    )
    saved_wide, saved_rms, saved_normed, saved_shares, saved_table, saved_placing, saved_mixing = (
        prepare_routes(saved_inputs[0], gain_row, router_mat, backward_routes[0], experts, capacity)
    )
    send_forward = jnp.einsum(
        "ts,td->sd", placing, normed, preferred_element_type=jnp.float32
    ).astype(jnp.bfloat16)
    send_forward = send_forward.reshape(sources, local_count * capacity, width)
    send_backward = jnp.einsum(
        "ts,td->sd", saved_placing, upstream, preferred_element_type=jnp.float32
    ).astype(jnp.bfloat16)
    send_backward = send_backward.reshape(sources, local_count * capacity, width)
    saved_pre = pre_activation[0].astype(jnp.float32)
    got_forward = lax.all_to_all(send_forward, "expert", split_axis=0, concat_axis=0, tiled=True)
    blocked = got_forward.reshape(sources, local_count, capacity, width)
    pre_act = jnp.einsum("jecd,edf->jecf", blocked, up_weight, preferred_element_type=jnp.float32)
    hidden = jax.nn.silu(pre_act).astype(jnp.bfloat16)
    result = jnp.einsum(
        "jecf,efd->jecd", hidden, down_weight, preferred_element_type=jnp.float32
    ).astype(jnp.bfloat16)
    back_forward = lax.all_to_all(
        result.reshape(sources, local_count * capacity, width),
        "expert",
        split_axis=0,
        concat_axis=0,
        tiled=True,
    )
    got_backward = lax.all_to_all(send_backward, "expert", split_axis=0, concat_axis=0, tiled=True)
    blocked = got_backward.reshape(sources, local_count, capacity, width)
    hidden_grad = jnp.einsum(
        "jecd,efd->jecf", blocked, down_weight, preferred_element_type=jnp.float32
    )
    hidden_rounded = lax.optimization_barrier(jax.nn.silu(saved_pre).astype(jnp.bfloat16)).astype(
        jnp.float32
    )
    inner_sums = jnp.sum(hidden_grad * hidden_rounded, axis=-1).astype(jnp.bfloat16)
    sigmoid_pre = jax.nn.sigmoid(saved_pre)
    pre_grad = (hidden_grad * sigmoid_pre * (1.0 + saved_pre * (1.0 - sigmoid_pre))).astype(
        jnp.bfloat16
    )
    input_rows = jnp.einsum(
        "jecf,edf->jecd", pre_grad, up_weight, preferred_element_type=jnp.float32
    ).astype(jnp.bfloat16)
    backward_rows, inner_sums = (
        input_rows.reshape(sources, local_count * capacity, width),
        inner_sums.reshape(sources, local_count * capacity),
    )
    back_rows, back_sums = (
        lax.all_to_all(backward_rows, "expert", split_axis=0, concat_axis=0, tiled=True),
        lax.all_to_all(inner_sums, "expert", split_axis=0, concat_axis=0, tiled=True),
    )
    expert_sum = jnp.dot(
        mixing, back_forward.reshape(slots, width), preferred_element_type=jnp.float32
    )
    forward_output = (widened + expert_sum).astype(jnp.bfloat16)
    normed_grad = jnp.dot(
        saved_mixing, back_rows.reshape(slots, width), preferred_element_type=jnp.float32
    )
    route_sums = jnp.einsum(
        "tks,s->tk", saved_table, back_sums.reshape(slots).astype(jnp.float32), precision=HIGH
    )
    chosen_grad = saved_shares * (
        route_sums - jnp.sum(saved_shares * route_sums, axis=1, keepdims=True)
    )
    route_hits = (backward_routes[0][..., None] == jnp.arange(experts, dtype=jnp.int32)).astype(
        jnp.float32
    )
    logit_grad = jnp.einsum("tk,tke->te", chosen_grad, route_hits, precision=HIGH)
    normed_grad = normed_grad + jnp.dot(
        logit_grad, router_mat.astype(jnp.float32).T, precision=HIGH
    )
    gained_grad = normed_grad * gain_row.astype(jnp.float32)
    input_grad = saved_rms[:, None] * gained_grad - saved_wide * (saved_rms**3)[
        :, None
    ] * jnp.mean(saved_wide * gained_grad, axis=-1, keepdims=True)
    input_gradient = (upstream.astype(jnp.float32) + input_grad).astype(jnp.bfloat16)
    return (forward_output[None], input_gradient[None])


def solution(mesh):
    return jax.shard_map(
        on_device,
        mesh=mesh,
        in_specs=(
            P("section", "expert", None),
            P("expert", None),
            P("section", "expert", None),
            P("section", "expert", None),
            P("expert", None),
            P("section", "expert", None),
            P("section", "expert", None),
            P("section", None, "expert", None, None),
            P("section", None),
            P("section", None, None),
            P("expert", None, None),
            P("expert", None, None),
        ),
        out_specs=(P("section", "expert", None), P("section", "expert", None)),
        check_vma=False,
    )
```

profile of v0, /device:TPU:0, one launch (start us, length us, event | category | flops | bytes accessed | tf_op | source)
XLA Modules:
  0.0 152.7 jit_solution(623828121843521382)
XLA Ops:
  0.7 5.0 %collective-permute-start = (bf16[64,2048]{1,0:T(8,128)(2,1)}, bf16[64,2048]{1,0:T(8,128)(2,1)S(1)}, u32[]{:S(2)}, u32[]{:S(2)}) collective-permute-start(bf16[64,2048]{1,0:T(8,128)(2,1)} %bitcast.150), channel_id=1, source_target_pairs={{0,8},{8,16},{16,24},{1,9},{9,17},{17,25},{2,10},{10,18},{18,26},{... | collective-permute-start | bytes 786440 | tf_op jit(solution)/shard_map/ppermute | solution.py:13
  5.7 1.3 collective-permute-start.1
  7.0 0.7 bitcast_or_fusion
  7.7 0.8 copy.92
  8.4 0.7 mul.175
  9.1 1.1 fusion.35
  10.2 0.6 multiply_multiply_fusion
  10.8 0.7 bitcast_or_fusion.1
  11.5 0.1 eq.84
  11.7 0.1 fusion.67
  11.8 0.2 reduce_window_sum.18
  11.9 1.2 fusion.51
  13.2 0.2 select_reduce_fusion.2
  13.4 0.8 copy.86
  14.1 0.1 copy.94
  14.2 0.1 reshape.160
  14.4 1.3 gather_fusion.1
  15.7 0.1 reshape.163
  15.8 0.1 copy.95
  15.9 0.1 copy.88
  16.0 0.2 reshape.155
  16.1 0.1 eq.76
  16.3 0.1 reduce_sum.129
  16.4 0.1 copy.93
  16.5 0.2 fusion.43
  16.7 0.3 fusion.56
  17.0 1.3 gather_fusion
  18.3 0.1 reshape.158
  18.6 0.7 select_reduce_fusion
  19.3 1.3 convolution_convert_fusion
  20.6 4.9 %all-to-all-start.2 = ((bf16[8,24,2048]{2,1,0:T(8,128)(2,1)}), bf16[8,24,2048]{2,1,0:T(8,128)(2,1)S(1)}, u32[]{:S(2)}, u32[]{:S(2)}) async-start(bf16[8,24,2048]{2,1,0:T(8,128)(2,1)} %bitcast.21), calls=%async_computation.2 | async-start | bytes 1572864 | tf_op jit(solution)/shard_map/all_to_all | solution.py:99
  25.5 0.1 fusion.68
  25.6 0.2 reduce_window_sum.17
  25.7 0.2 select_reduce_fusion.3
  25.9 0.1 reduce_sum.122
  26.1 0.1 copy.87
  26.1 1.1 fusion.29
  27.2 0.7 copy.100
  27.9 0.7 select_reduce_fusion.1
  28.6 1.3 convolution_convert_fusion.1
  29.9 16.5 %all-to-all-done.2 = bf16[8,24,2048]{2,1,0:T(8,128)(2,1)S(1)} async-done(((bf16[8,24,2048]{2,1,0:T(8,128)(2,1)}), bf16[8,24,2048]{2,1,0:T(8,128)(2,1)S(1)}, u32[]{:S(2)}, u32[]{:S(2)}) %all-to-all-start.2) | async-done | bytes 786464 | tf_op jit(solution)/shard_map/all_to_all | solution.py:99
  46.5 3.5 %all-to-all-start = ((bf16[8,24,2048]{2,1,0:T(8,128)(2,1)}), bf16[8,24,2048]{2,1,0:T(8,128)(2,1)S(1)}, u32[]{:S(2)}, u32[]{:S(2)}) async-start(bf16[8,24,2048]{2,1,0:T(8,128)(2,1)} %bitcast.5), calls=%async_computation | async-start | bytes 1572864 | tf_op jit(solution)/shard_map/all_to_all | solution.py:85
  50.0 0.4 copy.96
  50.5 14.2 %multiply_reduce_fusion = (bf16[8,8,3]{0,2,1:T(4,128)(2,1)S(1)}, f32[8,8,3,1024]{3,0,2,1:T(8,128)S(1)}) fusion(bf16[8,8,3,1024]{3,0,2,1:T(8,128)(2,1)} %fusion.29, bf16[8,8,3,2048]{3,0,2,1:T(8,128)(2,1)S(1)} %bitcast.139, bf16[8,1024,2048]{2,1,0:T(8,128)(2,1)} %param.25), kind=kOutput, calls=%fused_computation.31 | convolution fusion | flops 805896000 | bytes 35520896 | tf_op jit(solution)/shard_map/jecd,efd->jecf/dot_general | solution.py:101
  64.7 0.7 copy.99
  65.4 14.1 %fusion.11 = bf16[8,8,3,2048]{3,1,2,0:T(8,128)(2,1)S(1)} fusion(bf16[8,2048,1024]{2,1,0:T(8,128)(2,1)} %param.24, f32[8,8,3,1024]{3,0,2,1:T(8,128)S(1)} %get-tuple-element.18, bf16[1,8,8,3,1024]{4,2,3,1,0:T(8,128)(2,1)S(1)} %copy-done.4), kind=kOutput, calls=%fused_computation.11 | convolution fusion | flops 807665664 | bytes 35520512 | tf_op jit(solution)/shard_map/jecf,edf->jecd/dot_general | solution.py:112
  79.5 5.0 %all-to-all-start.4 = ((bf16[8,1,24]{2,1,0:T(2,128)(2,1)}), bf16[8,1,24]{2,1,0:T(2,128)(2,1)S(1)}, u32[]{:S(2)}, u32[]{:S(2)}) async-start(bf16[8,1,24]{2,1,0:T(2,128)(2,1)} %copy.99), calls=%async_computation.4 | async-start | bytes 8192 | tf_op jit(solution)/shard_map/all_to_all | solution.py:121
  84.6 0.4 copy.90
  85.1 13.2 %multiply_convert_fusion = bf16[8,8,3,1024]{3,0,2,1:T(8,128)(2,1)S(1)} fusion(bf16[8,8,3,2048]{3,0,2,1:T(8,128)(2,1)S(1)} %bitcast.140, bf16[8,2048,1024]{2,1,0:T(8,128)(2,1)} %param.24), kind=kOutput, calls=%fused_computation.32 | convolution fusion | flops 806289408 | bytes 34734080 | tf_op jit(solution)/shard_map/jecd,edf->jecf/dot_general | solution.py:87
  98.2 1.3 copy.98
  99.6 5.1 %all-to-all-start.3 = ((bf16[8,24,2048]{2,1,0:T(8,128)(2,1)}), bf16[8,24,2048]{2,1,0:T(8,128)(2,1)S(1)}, u32[]{:S(2)}, u32[]{:S(2)}) async-start(bf16[8,24,2048]{2,1,0:T(8,128)(2,1)} %copy.98), calls=%async_computation.3 | async-start | bytes 1572864 | tf_op jit(solution)/shard_map/all_to_all | solution.py:120
  104.7 12.9 %fusion.8 = bf16[8,8,3,2048]{3,1,2,0:T(8,128)(2,1)S(1)} fusion(bf16[8,8,3,1024]{3,0,2,1:T(8,128)(2,1)S(1)} %multiply_convert_fusion, bf16[8,1024,2048]{2,1,0:T(8,128)(2,1)} %param.25), kind=kOutput, calls=%fused_computation.10 | convolution fusion | flops 805699584 | bytes 34734080 | tf_op jit(solution)/shard_map/jecf,efd->jecd/dot_general | solution.py:89
  117.6 1.3 copy.91
  118.9 0.1 reshape.166
  119.0 6.6 %all-to-all-done.3 = bf16[8,24,2048]{2,1,0:T(8,128)(2,1)S(1)} async-done(((bf16[8,24,2048]{2,1,0:T(8,128)(2,1)}), bf16[8,24,2048]{2,1,0:T(8,128)(2,1)S(1)}, u32[]{:S(2)}, u32[]{:S(2)}) %all-to-all-start.3) | async-done | bytes 786464 | tf_op jit(solution)/shard_map/all_to_all | solution.py:120
  125.6 3.5 %all-to-all-start.1 = ((bf16[8,24,2048]{2,1,0:T(8,128)(2,1)}), bf16[8,24,2048]{2,1,0:T(8,128)(2,1)S(1)}, u32[]{:S(2)}, u32[]{:S(2)}) async-start(bf16[8,24,2048]{2,1,0:T(8,128)(2,1)} %copy.91), calls=%async_computation.1 | async-start | bytes 1572864 | tf_op jit(solution)/shard_map/all_to_all | solution.py:92
  129.2 0.2 fusion.60
  129.5 0.1 copy.104
  129.6 0.4 fusion.61
  130.0 0.3 fusion.84
  130.3 0.5 fusion.40
  130.8 19.3 %all-to-all-done.1 = bf16[8,24,2048]{2,1,0:T(8,128)(2,1)S(1)} async-done(((bf16[8,24,2048]{2,1,0:T(8,128)(2,1)}), bf16[8,24,2048]{2,1,0:T(8,128)(2,1)S(1)}, u32[]{:S(2)}, u32[]{:S(2)}) %all-to-all-start.1) | async-done | bytes 786464 | tf_op jit(solution)/shard_map/all_to_all | solution.py:92
  150.1 1.0 fusion.16
  151.1 1.6 %fusion.53 = bf16[1,64,2048]{2,1,0:T(8,128)(2,1)} fusion(bf16[1,64,2048]{2,1,0:T(8,128)(2,1)S(1)} %copy-done.1, f32[64,2048]{1,0:T(8,128)S(1)} %get-tuple-element.20, f32[64]{0:T(128)S(1)} %broadcast_multiply_fusion, f32[64]{0:T(128)} %get-tuple-element.15, f32[64]{0:T(128)} %copy-done.14, bf16[64,2048]{1,0:T(8,128)(2,1)S(1)} %copy-done.5, ...), kind=kLoop, calls=%fused_computation.56 | loop fusion | flops 1179648 | bytes 1573633 | tf_op jit(solution)/shard_map/broadcast_in_dim | solution.py:148
  (48 shorter events, 0.3 us)
Async XLA Ops:
  0.6 11.3 %copy-start = (bf16[1,2048,64]{1,2,0:T(8,128)(2,1)S(1)}, bf16[1,2048,64]{1,2,0:T(8,128)(2,1)}, u32[]{:S(2)}) copy-start(bf16[1,2048,64]{1,2,0:T(8,128)(2,1)} %param.23) | copy-start | bytes 786436
  0.6 15.9 %copy-start.12 = (s32[1,64,2]{1,2,0:T(2,128)S(1)}, s32[1,64,2]{1,2,0:T(2,128)}, u32[]{:S(2)}) copy-start(s32[1,64,2]{1,2,0:T(2,128)} %param.20) | copy-start | bytes 1540
  0.7 15.9 %copy-start.8 = (bf16[64,2048]{1,0:T(8,128)(2,1)S(1)}, bf16[64,2048]{1,0:T(8,128)(2,1)}, u32[]{:S(2)}) copy-start(bf16[64,2048]{1,0:T(8,128)(2,1)} %param.15) | copy-start | bytes 786436
  0.7 15.8 %collective-permute-start = (bf16[64,2048]{1,0:T(8,128)(2,1)}, bf16[64,2048]{1,0:T(8,128)(2,1)S(1)}, u32[]{:S(2)}, u32[]{:S(2)}) collective-permute-start(bf16[64,2048]{1,0:T(8,128)(2,1)} %bitcast.150), channel_id=1, source_target_pairs={{0,8},{8,16},{16,24},{1,9},{9,17},{17,25},{2,10},{10,18},{18,26},{... | collective-permute-start | bytes 786440 | tf_op jit(solution)/shard_map/ppermute | solution.py:13
  5.7 13.6 %collective-permute-start.1 = (bf16[64,2048]{1,0:T(8,128)(2,1)}, bf16[64,2048]{1,0:T(8,128)(2,1)S(1)}, u32[]{:S(2)}, u32[]{:S(2)}) collective-permute-start(bf16[64,2048]{1,0:T(8,128)(2,1)} %bitcast.151), channel_id=1, source_target_pairs={{8,0},{16,8},{24,16},{9,1},{17,9},{25,17},{10,2},{18,10},{26,18},{... | collective-permute-start | bytes 786440 | tf_op jit(solution)/shard_map/ppermute | solution.py:13
  10.8 1.1 copy-start.14
  14.4 4.2 %copy-start.13 = (s32[1,64,2]{1,2,0:T(2,128)S(1)}, s32[1,64,2]{1,2,0:T(2,128)}, u32[]{:S(2)}) copy-start(s32[1,64,2]{1,2,0:T(2,128)} %param.16) | copy-start | bytes 1540
  14.4 4.9 %copy-start.5 = (bf16[64,2048]{1,0:T(8,128)(2,1)S(1)}, bf16[64,2048]{1,0:T(8,128)(2,1)}, u32[]{:S(2)}) copy-start(bf16[64,2048]{1,0:T(8,128)(2,1)} %param.18) | copy-start | bytes 786436
  14.4 11.7 %copy-start.4 = (bf16[1,8,8,3,1024]{4,2,3,1,0:T(8,128)(2,1)S(1)}, bf16[1,8,8,3,1024]{4,2,3,1,0:T(8,128)(2,1)}, u32[]{:S(2)}) copy-start(bf16[1,8,8,3,1024]{4,2,3,1,0:T(8,128)(2,1)} %param.21) | copy-start | bytes 1179652
  16.7 29.7 %copy-start.2 = (bf16[64,2048]{1,0:T(8,128)(2,1)}, bf16[64,2048]{1,0:T(8,128)(2,1)S(1)}, u32[]{:S(2)}) copy-start(bf16[64,2048]{1,0:T(8,128)(2,1)S(1)} %get-tuple-element.14) | copy-start | bytes 786436
  19.3 1.3 copy-start.6
  20.6 25.9 %all-to-all-start.2 = ((bf16[8,24,2048]{2,1,0:T(8,128)(2,1)}), bf16[8,24,2048]{2,1,0:T(8,128)(2,1)S(1)}, u32[]{:S(2)}, u32[]{:S(2)}) async-start(bf16[8,24,2048]{2,1,0:T(8,128)(2,1)} %bitcast.21), calls=%async_computation.2 | async-start | bytes 1572864 | tf_op jit(solution)/shard_map/all_to_all | solution.py:99
  46.5 33.0 %all-to-all-start = ((bf16[8,24,2048]{2,1,0:T(8,128)(2,1)}), bf16[8,24,2048]{2,1,0:T(8,128)(2,1)S(1)}, u32[]{:S(2)}, u32[]{:S(2)}) async-start(bf16[8,24,2048]{2,1,0:T(8,128)(2,1)} %bitcast.5), calls=%async_computation | async-start | bytes 1572864 | tf_op jit(solution)/shard_map/all_to_all | solution.py:85
  79.5 20.0 %all-to-all-start.4 = ((bf16[8,1,24]{2,1,0:T(2,128)(2,1)}), bf16[8,1,24]{2,1,0:T(2,128)(2,1)S(1)}, u32[]{:S(2)}, u32[]{:S(2)}) async-start(bf16[8,1,24]{2,1,0:T(2,128)(2,1)} %copy.99), calls=%async_computation.4 | async-start | bytes 8192 | tf_op jit(solution)/shard_map/all_to_all | solution.py:121
  85.0 44.6 %copy-start.11 = (s32[64,2]{1,0:T(8,128)S(1)}, s32[64,2]{1,0:T(8,128)}, u32[]{:S(2)}) copy-start(s32[64,2]{1,0:T(8,128)} %copy.100) | copy-start | bytes 1540
  85.0 45.0 %copy-start.9 = (bf16[64,192]{1,0:T(8,128)(2,1)S(1)}, bf16[64,192]{1,0:T(8,128)(2,1)}, u32[]{:S(2)}) copy-start(bf16[64,192]{1,0:T(8,128)(2,1)} %get-tuple-element.3) | copy-start | bytes 73732
  85.0 45.2 %copy-start.1 = (bf16[1,64,2048]{2,1,0:T(8,128)(2,1)S(1)}, bf16[1,64,2048]{2,1,0:T(8,128)(2,1)}, u32[]{:S(2)}) copy-start(bf16[1,64,2048]{2,1,0:T(8,128)(2,1)} %param.19) | copy-start | bytes 786436
  85.0 65.1 %copy-start.3 = (bf16[64,2048]{1,0:T(8,128)(2,1)S(1)}, bf16[64,2048]{1,0:T(8,128)(2,1)}, u32[]{:S(2)}) copy-start(bf16[64,2048]{1,0:T(8,128)(2,1)} %copy-done.2) | copy-start | bytes 786436
  85.0 65.1 %copy-start.10 = (bf16[64,192]{1,0:T(8,128)(2,1)S(1)}, bf16[64,192]{1,0:T(8,128)(2,1)}, u32[]{:S(2)}) copy-start(bf16[64,192]{1,0:T(8,128)(2,1)} %get-tuple-element.5) | copy-start | bytes 73732
  85.0 66.0 %copy-start.7 = (bf16[64,2048]{1,0:T(8,128)(2,1)S(1)}, bf16[64,2048]{1,0:T(8,128)(2,1)}, u32[]{:S(2)}) copy-start(bf16[64,2048]{1,0:T(8,128)(2,1)} %copy-done.6) | copy-start | bytes 786436
  99.6 26.1 %all-to-all-start.3 = ((bf16[8,24,2048]{2,1,0:T(8,128)(2,1)}), bf16[8,24,2048]{2,1,0:T(8,128)(2,1)S(1)}, u32[]{:S(2)}, u32[]{:S(2)}) async-start(bf16[8,24,2048]{2,1,0:T(8,128)(2,1)} %copy.98), calls=%async_computation.3 | async-start | bytes 1572864 | tf_op jit(solution)/shard_map/all_to_all | solution.py:120
  125.6 24.5 %all-to-all-start.1 = ((bf16[8,24,2048]{2,1,0:T(8,128)(2,1)}), bf16[8,24,2048]{2,1,0:T(8,128)(2,1)S(1)}, u32[]{:S(2)}, u32[]{:S(2)}) async-start(bf16[8,24,2048]{2,1,0:T(8,128)(2,1)} %copy.91), calls=%async_computation.1 | async-start | bytes 1572864 | tf_op jit(solution)/shard_map/all_to_all | solution.py:92
where the time goes:
time: 154 us; the launch traced here: 153 us
  matrix products  60.9 us (40%)
  waiting for transfers between devices  42.5 us (28%)
  starting transfers between devices  28.4 us (18%)
  local copies, waits for them, and re-layouts  10.8 us (7%)
  other arithmetic  9.08 us (6%)
    all_to_all x1, waiting for transfers between devices, on_device(): lax.all_to_all(result.reshape(sources, local_count * capacity, width), 'e...  19.3 us
    all_to_all x1, waiting for transfers between devices, on_device(): lax.all_to_all(send_backward, 'expert', split_axis=0, concat_axis=0, tile...  16.5 us
    dot_general x1, matrix products, on_device(): jnp.einsum('jecd,efd->jecf', blocked, down_weight, preferred_element_type...  14.2 us
    dot_general x1, matrix products, on_device(): jnp.einsum('jecf,edf->jecd', pre_grad, up_weight, preferred_element_type=...  14.1 us
    dot_general x1, matrix products, on_device(): jnp.einsum('jecd,edf->jecf', blocked, up_weight, preferred_element_type=j...  13.2 us
    dot_general x1, matrix products, on_device(): jnp.einsum('jecf,efd->jecd', hidden, down_weight, preferred_element_type=...  12.9 us
    all_to_all x1, waiting for transfers between devices, on_device(): lax.all_to_all(backward_rows, 'expert', split_axis=0, concat_axis=0, tile...  6.63 us
    ppermute x2, starting transfers between devices, from_behind(): return lax.ppermute(block, axis, route)  6.28 us
  transfers between devices with their start and end apart: 7, of which 3 were waited for; matrix products, arithmetic and copies ran while one was open for 50% of the time, Pallas kernels for 0%

commit v1 on v0

v1 whole, which is shorter than its diff:
```python
import functools

import jax
import jax.numpy as jnp
import numpy as np
from jax import lax
from jax.experimental import pallas as pl
from jax.experimental.pallas import tpu as pltpu
from jax.sharding import PartitionSpec as P

EPS = 1e-06
BF16 = jnp.bfloat16
F32 = jnp.float32
LANES = 128
ROWS = 16
VMEM_LIMIT = 48 * 1024 * 1024
NT = (((1,), (1,)), ((), ()))
TN = (((0,), (0,)), ((), ()))


def dot(a, b, dims=(((1,), (0,)), ((), ()))):
    return lax.dot_general(a, b, dims, preferred_element_type=F32)


def call(kernel, out_shape, cost, **kwargs):
    flops, moved = cost
    return pl.pallas_call(
        kernel,
        out_shape=out_shape,
        compiler_params=pltpu.CompilerParams(vmem_limit_bytes=VMEM_LIMIT),
        cost_estimate=pl.CostEstimate(flops=flops, bytes_accessed=moved, transcendentals=0),
        **kwargs,
    )


def full_spec(shape):
    return pl.BlockSpec(shape, lambda *_: (0,) * len(shape))


SMEM = pl.BlockSpec(memory_space=pltpu.SMEM)
VMEM = pl.BlockSpec(memory_space=pltpu.VMEM)


def rotate(block, axis, distance):
    size = lax.axis_size(axis)
    return lax.ppermute(block, axis, [(i, (i + distance) % size) for i in range(size)])


def expert_hits(routes, experts):
    count, top = routes.shape
    lane = lax.broadcasted_iota(jnp.int32, (count, experts), 1)
    return [(routes[:, k : k + 1] == lane).astype(F32) for k in range(top)]


def slot_tables(routes, experts, capacity):
    count, top = routes.shape
    hits = expert_hits(routes, experts)
    earlier = lax.broadcasted_iota(jnp.int32, (count, count), 1) < lax.broadcasted_iota(
        jnp.int32, (count, count), 0
    )
    before = dot(earlier.astype(F32).astype(BF16), sum(hits).astype(BF16))
    lane = lax.broadcasted_iota(jnp.int32, (count, experts * capacity), 1)
    tables = []
    for k in range(top):
        ranked = jnp.sum((before + sum(hits[:k], jnp.zeros_like(before))) * hits[k], 1, keepdims=True)
        target = routes[:, k : k + 1] * capacity + ranked.astype(jnp.int32)
        tables.append((lane == target).astype(F32))
    return tables, hits


def normalise(tokens, gain):
    widened = tokens.astype(F32)
    inv_rms = lax.rsqrt(jnp.mean(widened * widened, axis=-1, keepdims=True) + EPS)
    return widened, inv_rms, (widened * inv_rms * gain.astype(F32)).astype(BF16)


def route_shares(normed, router, hits):
    logits = dot(normed, router)
    exponents = [jnp.exp(jnp.sum(logits * hit, axis=1, keepdims=True)) for hit in hits]
    total = sum(exponents)
    return [exponent / total for exponent in exponents]


def forward_send_kernel(capacity, experts, pick, sent, first, gain, routes, tokens, normed, send):
    chosen = jnp.where(pick[0] == 1, first[...], sent[...])
    tokens[...] = chosen
    _, _, rows = normalise(chosen, gain[...])
    normed[...] = rows
    tables, _ = slot_tables(routes[...], experts, capacity)
    send[...] = dot(sum(tables).astype(BF16), rows, TN).astype(BF16)


def backward_send_kernel(capacity, experts, pick, arrived, last, routes, upstream, send):
    chosen = jnp.where(pick[0] == 1, last[...], arrived[...])
    upstream[...] = chosen
    tables, _ = slot_tables(routes[...], experts, capacity)
    send[...] = dot(sum(tables).astype(BF16), chosen, TN).astype(BF16)


def mixing_kernel(
    capacity, experts, normed, router_f, routes_f, saved, gain, router_b, routes_b,
    mixing_f, mixing_b, tables_b, shares_b,
):
    tables, hits = slot_tables(routes_f[...], experts, capacity)
    shares = route_shares(normed[...], router_f[...], hits)
    mixing_f[...] = sum(t * s.astype(BF16).astype(F32) for t, s in zip(tables, shares)).astype(BF16)
    tables, hits = slot_tables(routes_b[...], experts, capacity)
    _, _, rows = normalise(saved[...], gain[...])
    shares = route_shares(rows, router_b[...], hits)
    mixing_b[...] = sum(t * s.astype(BF16).astype(F32) for t, s in zip(tables, shares)).astype(BF16)
    for k in range(len(tables)):
        tables_b[k] = tables[k].astype(BF16)
        shares_b[k] = jnp.broadcast_to(shares[k], shares_b.shape[1:])


def forward_expert_kernel(padded, steps, recv, order, back_order, up, down, out, rows, total, results):
    expert, step = pl.program_id(0), pl.program_id(1)

    @pl.when((expert == 0) & (step == 0))
    def _():
        rows[...] = dot(order[...], recv[...]).astype(BF16)

    own = pl.ds(pl.multiple_of(expert * padded, ROWS), padded)
    pre_act = dot(rows[own, :], up[0])
    hidden = (pre_act / (1.0 + jnp.exp(-pre_act))).astype(BF16)
    part = dot(hidden, down[0])

    @pl.when(step == 0)
    def _():
        total[...] = part

    @pl.when(step > 0)
    def _():
        total[...] += part

    @pl.when(step == steps - 1)
    def _():
        results[own, :] = total[...].astype(BF16)

    @pl.when((expert == pl.num_programs(0) - 1) & (step == steps - 1))
    def _():
        out[...] = dot(back_order[...], results[...]).astype(BF16)


def backward_expert_kernel(
    padded, steps, recv, order, back_order, saved_pre, up, down, out, rows, total, inner, results
):
    expert, step = pl.program_id(0), pl.program_id(1)
    width = rows.shape[1]

    @pl.when((expert == 0) & (step == 0))
    def _():
        rows[...] = dot(order[...], recv[...]).astype(BF16)

    own = pl.ds(pl.multiple_of(expert * padded, ROWS), padded)
    hidden_grad = dot(rows[own, :], down[0], NT)
    pre = saved_pre[0].astype(F32)
    gate = 1.0 / (1.0 + jnp.exp(-pre))
    hidden = (pre * gate).astype(BF16).astype(F32)
    inner_part = jnp.sum(hidden_grad * hidden, axis=1, keepdims=True)
    pre_grad = (hidden_grad * gate * (1.0 + pre * (1.0 - gate))).astype(BF16)
    part = dot(pre_grad, up[0], NT)

    @pl.when(step == 0)
    def _():
        total[...] = part
        inner[...] = jnp.broadcast_to(inner_part, inner.shape)

    @pl.when(step > 0)
    def _():
        total[...] += part
        inner[...] += jnp.broadcast_to(inner_part, inner.shape)

    @pl.when(step == steps - 1)
    def _():
        results[own, :width] = total[...].astype(BF16)
        results[own, width:] = inner[...].astype(BF16)

    @pl.when((expert == pl.num_programs(0) - 1) & (step == steps - 1))
    def _():
        out[...] = dot(back_order[...], results[...]).astype(BF16)


def forward_combine_kernel(tokens, mixing, back, out):
    out[...] = (tokens[...].astype(F32) + dot(mixing[...], back[...])).astype(BF16)


def backward_combine_kernel(
    experts, saved, upstream, gain, router, routes, mixing, tables, shares, back, out
):
    width = saved.shape[1]
    widened = saved[...].astype(F32)
    inv_rms = lax.rsqrt(jnp.mean(widened * widened, axis=-1, keepdims=True) + EPS)
    hits = expert_hits(routes[...], experts)
    top = len(hits)
    share = [shares[k][:, :1] for k in range(top)]
    inner = [dot(tables[k], back[:, width:])[:, :1] for k in range(top)]
    mean = sum(share[k] * inner[k] for k in range(top))
    logit_grad = sum(share[k] * (inner[k] - mean) * hits[k] for k in range(top))
    high = logit_grad.astype(BF16)
    rest = logit_grad - high.astype(F32)
    middle = rest.astype(BF16)
    low = (rest - middle.astype(F32)).astype(BF16)
    normed_grad = dot(mixing[...], back[:, :width])
    for piece in (high, middle, low):
        normed_grad += dot(piece, router[...], NT)
    gained = normed_grad * gain[...].astype(F32)
    projected = jnp.mean(widened * gained, axis=-1, keepdims=True)
    grad = inv_rms * gained - widened * (inv_rms * inv_rms * inv_rms * projected)
    out[...] = (upstream[...].astype(F32) + grad).astype(BF16)


def row_order(sources, local, capacity, padded):
    table = np.zeros((local * padded, sources * local * capacity), np.float32)
    for expert in range(local):
        for source in range(sources):
            for slot in range(capacity):
                table[
                    expert * padded + source * capacity + slot,
                    (source * local + expert) * capacity + slot,
                ] = 1.0
    return table


def on_device(
    forward_sent,
    embedded,
    forward_routes,
    backward_sent,
    loss_gradient,
    saved_inputs,
    backward_routes,
    pre_activation,
    norm_gain,
    router,
    up_weight,
    down_weight,
):
    section = lax.axis_index("section")
    last = lax.axis_size("section") - 1
    sources = lax.axis_size("expert")
    experts = router.shape[2]
    capacity = pre_activation.shape[3]
    local, width, hidden = up_weight.shape
    count = embedded.shape[0]
    top = forward_routes.shape[2]
    slots = experts * capacity
    rows = sources * capacity
    padded = -(-rows // ROWS) * ROWS
    steps = 2
    chunk = hidden // steps
    at_last = (section == last).astype(jnp.int32).reshape(1)
    shape = jax.ShapeDtypeStruct

    routes_f = rotate(forward_routes[0], "section", -1)
    gain_f = rotate(norm_gain, "section", -1)
    arrived = rotate(backward_sent[0], "section", -1)
    router_f = rotate(router[0], "section", -1)

    tokens, normed, send_f = call(
        functools.partial(forward_send_kernel, capacity, experts),
        (shape((count, width), BF16), shape((count, width), BF16), shape((slots, width), BF16)),
        (2 * slots * count * width, 2 * (4 * count + slots) * width),
        in_specs=[SMEM, VMEM, VMEM, VMEM, VMEM],
    )(at_last, forward_sent[0], embedded, gain_f, routes_f)
    got_f = lax.all_to_all(send_f, "expert", split_axis=0, concat_axis=0, tiled=True)

    upstream, send_b = call(
        functools.partial(backward_send_kernel, capacity, experts),
        (shape((count, width), BF16), shape((slots, width), BF16)),
        (2 * slots * count * width, 2 * (3 * count + slots) * width),
        in_specs=[SMEM, VMEM, VMEM, VMEM],
    )(at_last, arrived, loss_gradient, backward_routes[0])
    got_b = lax.all_to_all(send_b, "expert", split_axis=0, concat_axis=0, tiled=True)

    mixing_f, mixing_b, tables_b, shares_b = call(
        functools.partial(mixing_kernel, capacity, experts),
        (
            shape((count, slots), BF16),
            shape((count, slots), BF16),
            shape((top, count, slots), BF16),
            shape((top, count, LANES), F32),
        ),
        (4 * count * width * experts, 4 * (count + LANES) * width),
    )(
        normed, router_f, routes_f, saved_inputs[0], norm_gain, router[0], backward_routes[0]
    )
    saved_pre = jnp.transpose(pre_activation[0], (1, 0, 2, 3)).reshape(local, rows, hidden)
    saved_pre = jnp.pad(saved_pre, ((0, 0), (0, padded - rows), (0, 0)))

    order = row_order(sources, local, capacity, padded)
    order, back_order = jnp.asarray(order, BF16), jnp.asarray(order.T, BF16)
    weight_specs = [
        pl.BlockSpec((1, width, chunk), lambda e, f: (e, 0, f)),
        pl.BlockSpec((1, chunk, width), lambda e, f: (e, f, 0)),
    ]
    expert_cost = (
        4 * local * padded * width * hidden,
        4 * local * width * hidden,
    )
    result_f = call(
        functools.partial(forward_expert_kernel, padded, steps),
        shape((slots, width), BF16),
        expert_cost,
        grid=(local, steps),
        in_specs=[
            full_spec((slots, width)),
            full_spec(order.shape),
            full_spec(back_order.shape),
            *weight_specs,
        ],
        out_specs=full_spec((slots, width)),
        scratch_shapes=[
            pltpu.VMEM((local * padded, width), BF16),
            pltpu.VMEM((padded, width), F32),
            pltpu.VMEM((local * padded, width), BF16),
        ],
    )(got_f, order, back_order, up_weight, down_weight)
    back_f = lax.all_to_all(result_f, "expert", split_axis=0, concat_axis=0, tiled=True)

    result_b = call(
        functools.partial(backward_expert_kernel, padded, steps),
        shape((slots, width + LANES), BF16),
        expert_cost,
        grid=(local, steps),
        in_specs=[
            full_spec((slots, width)),
            full_spec(order.shape),
            full_spec(back_order.shape),
            pl.BlockSpec((1, padded, chunk), lambda e, f: (e, 0, f)),
            *weight_specs,
        ],
        out_specs=full_spec((slots, width + LANES)),
        scratch_shapes=[
            pltpu.VMEM((local * padded, width), BF16),
            pltpu.VMEM((padded, width), F32),
            pltpu.VMEM((padded, LANES), F32),
            pltpu.VMEM((local * padded, width + LANES), BF16),
        ],
    )(got_b, order, back_order, saved_pre, up_weight, down_weight)
    back_b = lax.all_to_all(result_b, "expert", split_axis=0, concat_axis=0, tiled=True)

    output = call(
        forward_combine_kernel,
        shape((count, width), BF16),
        (2 * slots * count * width, 2 * (2 * count + slots) * width),
    )(tokens, mixing_f, back_f)
    forward_output = rotate(output, "section", 1)

    input_gradient = call(
        functools.partial(backward_combine_kernel, experts),
        shape((count, width), BF16),
        (2 * slots * count * width, 2 * (3 * count + slots) * width),
    )(
        saved_inputs[0], upstream, norm_gain, router[0], backward_routes[0],
        mixing_b, tables_b, shares_b, back_b,
    )
    return (forward_output[None], input_gradient[None])


def solution(mesh):
    return jax.shard_map(
        on_device,
        mesh=mesh,
        in_specs=(
            P("section", "expert", None),
            P("expert", None),
            P("section", "expert", None),
            P("section", "expert", None),
            P("expert", None),
            P("section", "expert", None),
            P("section", "expert", None),
            P("section", None, "expert", None, None),
            P("section", None),
            P("section", None, None),
            P("expert", None, None),
            P("expert", None, None),
        ),
        out_specs=(P("section", "expert", None), P("section", "expert", None)),
        check_vma=False,
    )
```

time: 154 us -> 148 us (0.961)
  Pallas kernels: 0 us -> 68.9 us
  matrix products: 60.9 us -> 0 us
  other arithmetic: 9.08 us -> 0 us
  waiting for transfers between devices: 42.5 us -> 39.9 us
    pallas_call x0 -> x7, Pallas kernels: none -> 68.9 us  [the longest x1 33.4 us: on_device(): call(functools.partial(backward_expert_kernel, padded, steps), shape((slo...]
    dot_general x13 -> x0, matrix products: 60.9 us -> none  [the longest x1 14.2 us: on_device(): jnp.einsum('jecd,efd->jecf', blocked, down_weight, preferred_element_type...]
    all_to_all x5 -> x4, waiting for transfers between devices: 42.4 us -> 9.46 us  [the longest x1 9.45 us: on_device(): lax.all_to_all(send_f, 'expert', split_axis=0, concat_axis=0, tiled=True)]
    ppermute x2 -> x5, waiting for transfers between devices: 0.02 us -> 30.5 us  [rotate(): lax.ppermute(block, axis, [(i, (i + distance) % size) for i in range(size)])]
    unnamed x32 -> x26, local copies, waits for them, and re-layouts: 1.62 us -> 7.29 us
    all_to_all x5 -> x4, starting transfers between devices: 22.1 us -> 18.6 us  [the longest x1 5.11 us: on_device(): lax.all_to_all(result_b, 'expert', split_axis=0, concat_axis=0, tiled=True)]
    gather x10 -> x0, local copies, waits for them, and re-layouts: 3.42 us -> none  [prepare_routes(): chosen = jnp.take_along_axis(logits, routes, axis=1)]
    reduce_sum x8 -> x0, other arithmetic: 3.15 us -> none  [the longest x2 1.43 us: prepare_routes(): jnp.sum(slot_table * rounded[..., None], axis=1).astype(jnp.bfloat16)]
  transfers between devices with their start and end apart: 7 -> 9, of which waited for: 3 -> 5; matrix products, arithmetic and copies ran while one was open for 50% -> 2% of each run, Pallas kernels for 0% -> 44%
where the time goes in v1:
time: 148 us; the launch traced here: 147 us
  Pallas kernels  68.9 us (47%)
  waiting for transfers between devices  39.9 us (27%)
  starting transfers between devices  27.4 us (19%)
  local copies, waits for them, and re-layouts  10.1 us (7%)
    pallas_call x1, Pallas kernels, on_device(): call(functools.partial(backward_expert_kernel, padded, steps), shape((slo...  33.4 us
    ppermute x5, waiting for transfers between devices, rotate(): lax.ppermute(block, axis, [(i, (i + distance) % size) for i in range(size)])  30.5 us
    pallas_call x1, Pallas kernels, on_device(): call(functools.partial(forward_expert_kernel, padded, steps), shape((slot...  29.6 us
    all_to_all x1, waiting for transfers between devices, on_device(): lax.all_to_all(send_f, 'expert', split_axis=0, concat_axis=0, tiled=True)  9.45 us
    ppermute x5, starting transfers between devices, rotate(): lax.ppermute(block, axis, [(i, (i + distance) % size) for i in range(size)])  8.85 us
    unnamed x26, local copies, waits for them, and re-layouts  7.29 us
    all_to_all x1, starting transfers between devices, on_device(): lax.all_to_all(result_b, 'expert', split_axis=0, concat_axis=0, tiled=True)  5.11 us
    all_to_all x1, starting transfers between devices, on_device(): lax.all_to_all(result_f, 'expert', split_axis=0, concat_axis=0, tiled=True)  5.03 us
  transfers between devices with their start and end apart: 9, of which 5 were waited for; matrix products, arithmetic and copies ran while one was open for 2% of the time, Pallas kernels for 44%

profile of v1, /device:TPU:0, one launch (start us, length us, event | category | flops | bytes accessed | tf_op | source)
XLA Modules:
  0.0 147.1 jit_solution(7839014364678254194)
XLA Ops:
  0.6 3.9 %collective-permute-start = (bf16[1,2048]{1,0:T(2,128)(2,1)}, bf16[1,2048]{1,0:T(2,128)(2,1)S(1)}, u32[]{:S(2)}, u32[]{:S(2)}) collective-permute-start(bf16[1,2048]{1,0:T(2,128)(2,1)} %gain.3), channel_id=1, source_target_pairs={{0,24},{8,0},{16,8},{24,16},{1,25},{9,1},{17,9},{25,17},{2,26},{10... | collective-permute-start | bytes 12296 | tf_op jit(solution)/shard_map/ppermute | solution.py:46
  4.6 0.8 copy.22
  5.3 0.6 collective-permute-start.1
  5.9 3.4 %collective-permute-done.1.routes.routes_f = s32[64,2]{1,0:T(8,128)S(1)} collective-permute-done((s32[64,2]{1,0:T(8,128)S(1)}, s32[64,2]{1,0:T(8,128)S(1)}, u32[]{:S(2)}, u32[]{:S(2)}) %collective-permute-start.1) | collective-permute-done | bytes 544 | tf_op jit(solution)/shard_map/ppermute | solution.py:46
  9.3 0.0 collective-permute-done.gain
  9.3 0.0 copy-start.5
  9.3 0.9 copy-done.5
  10.2 0.0 copy-start.6
  10.2 0.9 copy-done.6
  11.2 1.7 %shard_map.149 = (bf16[64,2048]{1,0:T(8,128)(2,1)S(1)}, bf16[64,2048]{1,0:T(8,128)(2,1)S(1)}, bf16[192,2048]{1,0:T(8,128)(2,1)}) custom-call(s32[1]{0:T(128)} %bitcast.pick, bf16[64,2048]{1,0:T(8,128)(2,1)S(1)} %bitcast.31, bf16[64,2048]{1,0:T(8,128)(2,1)S(1)} %copy-done.6, bf16[1,2048]{1,0:T(2,128)(2,1)S(1)} %collective-permute-done.gain, ...), custom_call_target="tpu_custom_call" | custom-call | flops 50331648 | bytes 1835008 | tf_op jit(solution)/shard_map/pallas_call | solution.py:260
  12.9 0.0 copy-start.8
  12.9 0.7 copy-done.8
  13.6 4.9 %all-to-all-start = ((bf16[8,24,2048]{2,1,0:T(8,128)(2,1)}), bf16[8,24,2048]{2,1,0:T(8,128)(2,1)S(1)}, u32[]{:S(2)}, u32[]{:S(2)}) async-start(bf16[8,24,2048]{2,1,0:T(8,128)(2,1)} %bitcast.6), calls=%async_computation | async-start | bytes 1572864 | tf_op jit(solution)/shard_map/all_to_all | solution.py:266
  18.5 1.4 collective-permute-start.4
  19.9 0.8 copy.24.routes_b.routes
  20.7 6.7 %collective-permute-done.4.arrived = bf16[64,2048]{1,0:T(8,128)(2,1)S(1)} collective-permute-done((bf16[64,2048]{1,0:T(8,128)(2,1)}, bf16[64,2048]{1,0:T(8,128)(2,1)S(1)}, u32[]{:S(2)}, u32[]{:S(2)}) %collective-permute-start.4) | collective-permute-done | bytes 262176 | tf_op jit(solution)/shard_map/ppermute | solution.py:46
  27.4 0.0 copy-start.7
  27.4 0.9 copy-done.7
  28.3 1.7 %shard_map.153 = (bf16[64,2048]{1,0:T(8,128)(2,1)S(1)}, bf16[192,2048]{1,0:T(8,128)(2,1)}) custom-call(s32[1]{0:T(128)} %bitcast.pick, bf16[64,2048]{1,0:T(8,128)(2,1)S(1)} %collective-permute-done.4.arrived, bf16[64,2048]{1,0:T(8,128)(2,1)S(1)} %copy-done.7, s32[64,2]{1,0:T(8,128)S(1)} %copy.24.routes_b.routes), custom_call_target="tpu_custom_call" | custom-call | flops 50331648 | bytes 1572864 | tf_op jit(solution)/shard_map/pallas_call | solution.py:268
  30.0 9.4 %all-to-all-done = bf16[8,24,2048]{2,1,0:T(8,128)(2,1)S(1)} async-done(((bf16[8,24,2048]{2,1,0:T(8,128)(2,1)}), bf16[8,24,2048]{2,1,0:T(8,128)(2,1)S(1)}, u32[]{:S(2)}, u32[]{:S(2)}) %all-to-all-start) | async-done | bytes 786464 | tf_op jit(solution)/shard_map/all_to_all | solution.py:266
  39.4 3.5 %all-to-all-start.2 = ((bf16[8,24,2048]{2,1,0:T(8,128)(2,1)}), bf16[8,24,2048]{2,1,0:T(8,128)(2,1)S(1)}, u32[]{:S(2)}, u32[]{:S(2)}) async-start(bf16[8,24,2048]{2,1,0:T(8,128)(2,1)} %bitcast.12), calls=%async_computation.2 | async-start | bytes 1572864 | tf_op jit(solution)/shard_map/all_to_all | solution.py:274
  43.0 0.0 copy-start.1
  43.0 0.9 copy-done.1
  43.9 0.0 copy-start.3
  43.9 0.9 copy-done.3
  44.8 0.0 copy-start.2
  44.8 0.0 copy-start.4
  44.8 29.6 %shard_map.151 = bf16[192,2048]{1,0:T(8,128)(2,1)} custom-call(bf16[192,2048]{1,0:T(8,128)(2,1)S(1)} %bitcast.26, bf16[256,192]{1,0:T(8,128)(2,1)S(1)} %copy-done.1, bf16[192,256]{1,0:T(8,128)(2,1)S(1)} %copy-done.3, bf16[8,2048,1024]{2,1,0:T(8,128)(2,1)} %up.3, bf16[8,1024,2048]{2,1,0:T(8,128)(2,1)} %down.3), custom_call_target="tpu_custom_call" | custom-call | flops 2147483648 | bytes 67108864 | tf_op jit(solution)/shard_map/pallas_call | solution.py:301
  74.4 0.0 all-to-all-done.2
  74.4 5.0 %all-to-all-start.1 = ((bf16[8,24,2048]{2,1,0:T(8,128)(2,1)}), bf16[8,24,2048]{2,1,0:T(8,128)(2,1)S(1)}, u32[]{:S(2)}, u32[]{:S(2)}) async-start(bf16[8,24,2048]{2,1,0:T(8,128)(2,1)} %bitcast.8), calls=%async_computation.1 | async-start | bytes 1572864 | tf_op jit(solution)/shard_map/all_to_all | solution.py:319
  79.4 1.2 copy.26
  80.7 0.0 copy-done.2
  80.7 0.0 copy-done.4
  80.7 0.0 copy-start.11
  80.7 0.0 copy-start
  80.7 0.0 copy-start.10
  80.7 33.4 %shard_map.154 = bf16[192,2176]{1,0:T(8,128)(2,1)} custom-call(bf16[192,2048]{1,0:T(8,128)(2,1)S(1)} %bitcast.27, bf16[256,192]{1,0:T(8,128)(2,1)S(1)} %copy-done.2, bf16[192,256]{1,0:T(8,128)(2,1)S(1)} %copy-done.4, bf16[8,32,1024]{2,1,0:T(8,128)(2,1)S(1)} %pad.4.saved_pre, bf16[8,2048,1024]{2,1,0:T(8,128)(2,1)} %up.3, bf16[8,1024,2048]{2,1,0:T(8,128)(2,1)} %down.3), custom_call_target="tpu_custom_call" | custom-call | flops 2147483648 | bytes 67108864 | tf_op jit(solution)/shard_map/pallas_call | solution.py:321
  114.1 0.0 all-to-all-done.1
  114.1 5.1 %all-to-all-start.3 = ((bf16[8,24,2176]{2,1,0:T(8,128)(2,1)}), bf16[8,24,2176]{2,1,0:T(8,128)(2,1)S(1)}, u32[]{:S(2)}, u32[]{:S(2)}) async-start(bf16[8,24,2176]{2,1,0:T(8,128)(2,1)} %bitcast.17), calls=%async_computation.3 | async-start | bytes 1671168 | tf_op jit(solution)/shard_map/all_to_all | solution.py:341
  119.2 0.0 copy-done.11
  119.2 0.3 copy.23
  119.5 1.5 %collective-permute-start.2 = (bf16[2048,64]{1,0:T(8,128)(2,1)S(1)}, bf16[2048,64]{1,0:T(8,128)(2,1)S(1)}, u32[]{:S(2)}, u32[]{:S(2)}) collective-permute-start(bf16[2048,64]{1,0:T(8,128)(2,1)S(1)} %bitcast.22), channel_id=1, source_target_pairs={{0,24},{8,0},{16,8},{24,16},{1,25},{9,1},{17,9},{25,17},{2,26},{10... | collective-permute-start | bytes 786440 | tf_op jit(solution)/shard_map/ppermute | solution.py:46
  121.0 12.9 %collective-permute-done.2.router_f = bf16[2048,64]{1,0:T(8,128)(2,1)S(1)} collective-permute-done((bf16[2048,64]{1,0:T(8,128)(2,1)S(1)}, bf16[2048,64]{1,0:T(8,128)(2,1)S(1)}, u32[]{:S(2)}, u32[]{:S(2)}) %collective-permute-start.2) | collective-permute-done | bytes 262176 | tf_op jit(solution)/shard_map/ppermute | solution.py:46
  133.9 0.0 copy-done
  133.9 0.0 copy-done.10
  133.9 0.5 shard_map.150
  134.4 0.0 copy-start.9
  134.4 0.9 copy-done.9
  135.4 0.3 shard_map.152
  135.7 1.4 collective-permute-start.3
  137.1 7.5 %collective-permute-done.3 = bf16[64,2048]{1,0:T(8,128)(2,1)S(1)} collective-permute-done((bf16[64,2048]{1,0:T(8,128)(2,1)S(1)}, bf16[64,2048]{1,0:T(8,128)(2,1)S(1)}, u32[]{:S(2)}, u32[]{:S(2)}) %collective-permute-start.3) | collective-permute-done | bytes 262176 | tf_op jit(solution)/shard_map/ppermute | solution.py:46
  144.5 0.0 all-to-all-done.3
  144.5 1.8 %shard_map.155 = bf16[64,2048]{1,0:T(8,128)(2,1)} custom-call(bf16[64,2048]{1,0:T(8,128)(2,1)S(1)} %bitcast.30, bf16[64,2048]{1,0:T(8,128)(2,1)S(1)} %get-tuple-element.15.upstream, bf16[1,2048]{1,0:T(2,128)(2,1)S(1)} %copy-done.10, bf16[2048,64]{1,0:T(8,128)(2,1)S(1)} %bitcast.24, s32[64,2]{1,0:T(8,128)S(1)} %copy.24.routes_b.routes, ...), custom_call_target="tpu_custom_call" | custom-call | flops 50331648 | bytes 1572864 | tf_op jit(solution)/shard_map/pallas_call | solution.py:350
  146.4 0.7 copy.29
  (1 shorter events, 0.0 us)
Async XLA Ops:
  0.6 8.7 %collective-permute-start = (bf16[1,2048]{1,0:T(2,128)(2,1)}, bf16[1,2048]{1,0:T(2,128)(2,1)S(1)}, u32[]{:S(2)}, u32[]{:S(2)}) collective-permute-start(bf16[1,2048]{1,0:T(2,128)(2,1)} %gain.3), channel_id=1, source_target_pairs={{0,24},{8,0},{16,8},{24,16},{1,25},{9,1},{17,9},{25,17},{2,26},{10... | collective-permute-start | bytes 12296 | tf_op jit(solution)/shard_map/ppermute | solution.py:46
  5.3 3.9 %collective-permute-start.1 = (s32[64,2]{1,0:T(8,128)S(1)}, s32[64,2]{1,0:T(8,128)S(1)}, u32[]{:S(2)}, u32[]{:S(2)}) collective-permute-start(s32[64,2]{1,0:T(8,128)S(1)} %copy.22), channel_id=1, source_target_pairs={{0,24},{8,0},{16,8},{24,16},{1,25},{9,1},{17,9},{25,17},{2,26},{10... | collective-permute-start | bytes 1544 | tf_op jit(solution)/shard_map/ppermute | solution.py:46
  9.3 1.0 copy-start.5
  10.2 0.9 copy-start.6
  12.9 0.7 copy-start.8
  13.6 25.9 %all-to-all-start = ((bf16[8,24,2048]{2,1,0:T(8,128)(2,1)}), bf16[8,24,2048]{2,1,0:T(8,128)(2,1)S(1)}, u32[]{:S(2)}, u32[]{:S(2)}) async-start(bf16[8,24,2048]{2,1,0:T(8,128)(2,1)} %bitcast.6), calls=%async_computation | async-start | bytes 1572864 | tf_op jit(solution)/shard_map/all_to_all | solution.py:266
  18.5 8.9 %collective-permute-start.4 = (bf16[64,2048]{1,0:T(8,128)(2,1)}, bf16[64,2048]{1,0:T(8,128)(2,1)S(1)}, u32[]{:S(2)}, u32[]{:S(2)}) collective-permute-start(bf16[64,2048]{1,0:T(8,128)(2,1)} %bitcast.37), channel_id=1, source_target_pairs={{0,24},{8,0},{16,8},{24,16},{1,25},{9,1},{17,9},{25,17},{2,26},{10... | collective-permute-start | bytes 786440 | tf_op jit(solution)/shard_map/ppermute | solution.py:46
  27.4 1.0 copy-start.7
  39.4 34.9 %all-to-all-start.2 = ((bf16[8,24,2048]{2,1,0:T(8,128)(2,1)}), bf16[8,24,2048]{2,1,0:T(8,128)(2,1)S(1)}, u32[]{:S(2)}, u32[]{:S(2)}) async-start(bf16[8,24,2048]{2,1,0:T(8,128)(2,1)} %bitcast.12), calls=%async_computation.2 | async-start | bytes 1572864 | tf_op jit(solution)/shard_map/all_to_all | solution.py:274
  43.0 0.9 copy-start.1
  43.9 0.9 copy-start.3
  44.8 35.9 %copy-start.2 = (bf16[256,192]{1,0:T(8,128)(2,1)S(1)}, bf16[256,192]{1,0:T(8,128)(2,1)}, u32[]{:S(2)}) copy-start(bf16[256,192]{1,0:T(8,128)(2,1)} %constant.14.clone.order) | copy-start | bytes 294916
  44.8 35.9 %copy-start.4 = (bf16[192,256]{1,0:T(8,128)(2,1)S(1)}, bf16[192,256]{1,0:T(8,128)(2,1)}, u32[]{:S(2)}) copy-start(bf16[192,256]{1,0:T(8,128)(2,1)} %constant.15.clone.back_order) | copy-start | bytes 294916
  74.4 39.7 %all-to-all-start.1 = ((bf16[8,24,2048]{2,1,0:T(8,128)(2,1)}), bf16[8,24,2048]{2,1,0:T(8,128)(2,1)S(1)}, u32[]{:S(2)}, u32[]{:S(2)}) async-start(bf16[8,24,2048]{2,1,0:T(8,128)(2,1)} %bitcast.8), calls=%async_computation.1 | async-start | bytes 1572864 | tf_op jit(solution)/shard_map/all_to_all | solution.py:319
  80.7 38.5 %copy-start.11 = (bf16[1,2048,64]{1,2,0:T(8,128)(2,1)S(1)}, bf16[1,2048,64]{1,2,0:T(8,128)(2,1)}, u32[]{:S(2)}) copy-start(bf16[1,2048,64]{1,2,0:T(8,128)(2,1)} %param.23) | copy-start | bytes 786436
  80.7 53.2 %copy-start = (bf16[1,64,2048]{2,1,0:T(8,128)(2,1)S(1)}, bf16[1,64,2048]{2,1,0:T(8,128)(2,1)}, u32[]{:S(2)}) copy-start(bf16[1,64,2048]{2,1,0:T(8,128)(2,1)} %param.19) | copy-start | bytes 786436
  80.7 53.2 %copy-start.10 = (bf16[1,2048]{1,0:T(2,128)(2,1)S(1)}, bf16[1,2048]{1,0:T(2,128)(2,1)}, u32[]{:S(2)}) copy-start(bf16[1,2048]{1,0:T(2,128)(2,1)} %gain.3) | copy-start | bytes 12292
  114.1 30.4 %all-to-all-start.3 = ((bf16[8,24,2176]{2,1,0:T(8,128)(2,1)}), bf16[8,24,2176]{2,1,0:T(8,128)(2,1)S(1)}, u32[]{:S(2)}, u32[]{:S(2)}) async-start(bf16[8,24,2176]{2,1,0:T(8,128)(2,1)} %bitcast.17), calls=%async_computation.3 | async-start | bytes 1671168 | tf_op jit(solution)/shard_map/all_to_all | solution.py:341
  119.5 14.4 %collective-permute-start.2 = (bf16[2048,64]{1,0:T(8,128)(2,1)S(1)}, bf16[2048,64]{1,0:T(8,128)(2,1)S(1)}, u32[]{:S(2)}, u32[]{:S(2)}) collective-permute-start(bf16[2048,64]{1,0:T(8,128)(2,1)S(1)} %bitcast.22), channel_id=1, source_target_pairs={{0,24},{8,0},{16,8},{24,16},{1,25},{9,1},{17,9},{25,17},{2,26},{10... | collective-permute-start | bytes 786440 | tf_op jit(solution)/shard_map/ppermute | solution.py:46
  134.4 1.0 copy-start.9
  135.7 8.9 %collective-permute-start.3 = (bf16[64,2048]{1,0:T(8,128)(2,1)S(1)}, bf16[64,2048]{1,0:T(8,128)(2,1)S(1)}, u32[]{:S(2)}, u32[]{:S(2)}) collective-permute-start(bf16[64,2048]{1,0:T(8,128)(2,1)S(1)} %shard_map.152), channel_id=1, source_target_pairs={{0,8},{8,16},{16,24},{24,0},{1,9},{9,17},{17,25},{25,1},{2,10},{10... | collective-permute-start | bytes 786440 | tf_op jit(solution)/shard_map/ppermute | solution.py:46

commit v2 on v1

--- a/solution.py
+++ b/solution.py
@@ -52,20 +52,24 @@
     return [(routes[:, k : k + 1] == lane).astype(F32) for k in range(top)]
 
 
-def slot_tables(routes, experts, capacity):
+def slot_targets(routes, experts, capacity):
     count, top = routes.shape
     hits = expert_hits(routes, experts)
     earlier = lax.broadcasted_iota(jnp.int32, (count, count), 1) < lax.broadcasted_iota(
         jnp.int32, (count, count), 0
     )
     before = dot(earlier.astype(F32).astype(BF16), sum(hits).astype(BF16))
-    lane = lax.broadcasted_iota(jnp.int32, (count, experts * capacity), 1)
-    tables = []
+    targets = []
     for k in range(top):
         ranked = jnp.sum((before + sum(hits[:k], jnp.zeros_like(before))) * hits[k], 1, keepdims=True)
-        target = routes[:, k : k + 1] * capacity + ranked.astype(jnp.int32)
-        tables.append((lane == target).astype(F32))
-    return tables, hits
+        targets.append(routes[:, k : k + 1] * capacity + ranked.astype(jnp.int32))
+    return targets, hits
+
+
+def slot_tables(routes, experts, capacity):
+    targets, hits = slot_targets(routes, experts, capacity)
+    lane = lax.broadcasted_iota(jnp.int32, (routes.shape[0], experts * capacity), 1)
+    return [(lane == target).astype(F32) for target in targets], hits
 
 
 def normalise(tokens, gain):
@@ -75,37 +79,32 @@
 
 
 def route_shares(normed, router, hits):
-    logits = dot(normed, router)
+    logits = dot(normed, router, NT)
     exponents = [jnp.exp(jnp.sum(logits * hit, axis=1, keepdims=True)) for hit in hits]
     total = sum(exponents)
     return [exponent / total for exponent in exponents]
 
 
-def forward_send_kernel(capacity, experts, pick, sent, first, gain, routes, tokens, normed, send):
-    chosen = jnp.where(pick[0] == 1, first[...], sent[...])
-    tokens[...] = chosen
-    _, _, rows = normalise(chosen, gain[...])
-    normed[...] = rows
-    tables, _ = slot_tables(routes[...], experts, capacity)
-    send[...] = dot(sum(tables).astype(BF16), rows, TN).astype(BF16)
-
-
-def backward_send_kernel(capacity, experts, pick, arrived, last, routes, upstream, send):
-    chosen = jnp.where(pick[0] == 1, last[...], arrived[...])
-    upstream[...] = chosen
-    tables, _ = slot_tables(routes[...], experts, capacity)
-    send[...] = dot(sum(tables).astype(BF16), chosen, TN).astype(BF16)
+def slot_keys_kernel(capacity, experts, block, routes_f, routes_b, keys_f, keys_b):
+    slots = experts * capacity
+    for routes, keys in ((routes_f, keys_f), (routes_b, keys_b)):
+        lane = lax.broadcasted_iota(jnp.int32, keys.shape, 1)
+        out = jnp.zeros(keys.shape, jnp.int32)
+        for k, target in enumerate(slot_targets(routes[...], experts, capacity)[0]):
+            out += jnp.where(lane == k, target + block[0] * slots, 0)
+        keys[...] = out
 
 
 def mixing_kernel(
-    capacity, experts, normed, router_f, routes_f, saved, gain, router_b, routes_b,
+    capacity, experts, tokens, gain_f, router_f, routes_f, saved, gain_b, router_b, routes_b,
     mixing_f, mixing_b, tables_b, shares_b,
 ):
     tables, hits = slot_tables(routes_f[...], experts, capacity)
-    shares = route_shares(normed[...], router_f[...], hits)
+    _, _, rows = normalise(tokens[...], gain_f[...])
+    shares = route_shares(rows, router_f[...], hits)
     mixing_f[...] = sum(t * s.astype(BF16).astype(F32) for t, s in zip(tables, shares)).astype(BF16)
     tables, hits = slot_tables(routes_b[...], experts, capacity)
-    _, _, rows = normalise(saved[...], gain[...])
+    _, _, rows = normalise(saved[...], gain_b[...])
     shares = route_shares(rows, router_b[...], hits)
     mixing_b[...] = sum(t * s.astype(BF16).astype(F32) for t, s in zip(tables, shares)).astype(BF16)
     for k in range(len(tables)):
@@ -113,12 +112,27 @@
         shares_b[k] = jnp.broadcast_to(shares[k], shares_b.shape[1:])
 
 
-def forward_expert_kernel(padded, steps, recv, order, back_order, up, down, out, rows, total, results):
+def send_rows_kernel(capacity, experts, routes, tokens, send):
+    tables, _ = slot_tables(routes[...], experts, capacity)
+    send[...] = dot(sum(tables).astype(BF16), tokens[...], TN).astype(BF16)
+
+
+def picked_rows(offset, row_keys, keys, tokens):
+    wanted = row_keys[...] + offset
+    held = sum((keys[:, k : k + 1] == wanted).astype(F32) for k in range(keys.shape[1]))
+    return dot(held.astype(BF16), tokens[...], TN)
+
+
+def forward_expert_kernel(
+    padded, steps, offset, row_keys, keys, tokens, gain, back_order, up, down,
+    out, rows, total, results,
+):
     expert, step = pl.program_id(0), pl.program_id(1)
 
     @pl.when((expert == 0) & (step == 0))
     def _():
-        rows[...] = dot(order[...], recv[...]).astype(BF16)
+        picked = picked_rows(offset[0], row_keys, keys, tokens)
+        rows[...] = normalise(picked, gain[...])[2]
 
     own = pl.ds(pl.multiple_of(expert * padded, ROWS), padded)
     pre_act = dot(rows[own, :], up[0])
@@ -143,23 +157,25 @@
 
 
 def backward_expert_kernel(
-    padded, steps, recv, order, back_order, saved_pre, up, down, out, rows, total, inner, results
+    padded, steps, offset, row_keys, keys, upstream, back_order, saved_pre, up, down,
+    out, rows, total, inner, results,
 ):
     expert, step = pl.program_id(0), pl.program_id(1)
     width = rows.shape[1]
 
     @pl.when((expert == 0) & (step == 0))
     def _():
-        rows[...] = dot(order[...], recv[...]).astype(BF16)
+        picked = picked_rows(offset[0], row_keys, keys, upstream)
+        rows[...] = picked.astype(BF16)
 
     own = pl.ds(pl.multiple_of(expert * padded, ROWS), padded)
-    hidden_grad = dot(rows[own, :], down[0], NT)
+    hidden_grad = jnp.transpose(dot(down[0], rows[own, :], NT))
     pre = saved_pre[0].astype(F32)
     gate = 1.0 / (1.0 + jnp.exp(-pre))
     hidden = (pre * gate).astype(BF16).astype(F32)
     inner_part = jnp.sum(hidden_grad * hidden, axis=1, keepdims=True)
     pre_grad = (hidden_grad * gate * (1.0 + pre * (1.0 - gate))).astype(BF16)
-    part = dot(pre_grad, up[0], NT)
+    part = dot(up[0], pre_grad, NT)
 
     @pl.when(step == 0)
     def _():
@@ -173,7 +189,7 @@
 
     @pl.when(step == steps - 1)
     def _():
-        results[own, :width] = total[...].astype(BF16)
+        results[own, :width] = jnp.transpose(total[...]).astype(BF16)
         results[own, width:] = inner[...].astype(BF16)
 
     @pl.when((expert == pl.num_programs(0) - 1) & (step == steps - 1))
@@ -203,23 +219,23 @@
     low = (rest - middle.astype(F32)).astype(BF16)
     normed_grad = dot(mixing[...], back[:, :width])
     for piece in (high, middle, low):
-        normed_grad += dot(piece, router[...], NT)
+        normed_grad += dot(piece, router[...])
     gained = normed_grad * gain[...].astype(F32)
     projected = jnp.mean(widened * gained, axis=-1, keepdims=True)
     grad = inv_rms * gained - widened * (inv_rms * inv_rms * inv_rms * projected)
     out[...] = (upstream[...].astype(F32) + grad).astype(BF16)
 
 
-def row_order(sources, local, capacity, padded):
-    table = np.zeros((local * padded, sources * local * capacity), np.float32)
+def row_order(sources, local, capacity, padded, slots):
+    keys = np.full((1, local * padded), -sources * slots, np.int32)
+    back = np.zeros((sources * local * capacity, local * padded), np.float32)
     for expert in range(local):
         for source in range(sources):
             for slot in range(capacity):
-                table[
-                    expert * padded + source * capacity + slot,
-                    (source * local + expert) * capacity + slot,
-                ] = 1.0
-    return table
+                row = expert * padded + source * capacity + slot
+                keys[0, row] = source * slots + expert * capacity + slot
+                back[(source * local + expert) * capacity + slot, row] = 1.0
+    return keys, back
 
 
 def on_device(
@@ -252,26 +268,43 @@
     at_last = (section == last).astype(jnp.int32).reshape(1)
     shape = jax.ShapeDtypeStruct
 
+    router_t = router[0].T
+    arrived = rotate(backward_sent[0], "section", -1)
+    tokens = jnp.where(section == last, embedded, forward_sent[0])
     routes_f = rotate(forward_routes[0], "section", -1)
     gain_f = rotate(norm_gain, "section", -1)
-    arrived = rotate(backward_sent[0], "section", -1)
-    router_f = rotate(router[0], "section", -1)
-
-    tokens, normed, send_f = call(
-        functools.partial(forward_send_kernel, capacity, experts),
-        (shape((count, width), BF16), shape((count, width), BF16), shape((slots, width), BF16)),
-        (2 * slots * count * width, 2 * (4 * count + slots) * width),
-        in_specs=[SMEM, VMEM, VMEM, VMEM, VMEM],
-    )(at_last, forward_sent[0], embedded, gain_f, routes_f)
-    got_f = lax.all_to_all(send_f, "expert", split_axis=0, concat_axis=0, tiled=True)
-
-    upstream, send_b = call(
-        functools.partial(backward_send_kernel, capacity, experts),
-        (shape((count, width), BF16), shape((slots, width), BF16)),
-        (2 * slots * count * width, 2 * (3 * count + slots) * width),
-        in_specs=[SMEM, VMEM, VMEM, VMEM],
-    )(at_last, arrived, loss_gradient, backward_routes[0])
-    got_b = lax.all_to_all(send_b, "expert", split_axis=0, concat_axis=0, tiled=True)
+    router_f = rotate(router_t, "section", -1)
+    upstream = jnp.where(section == last, loss_gradient, arrived)
+    here = lax.axis_index("expert")
+    if sources * count <= 4 * slots:
+        got_f = lax.all_gather(tokens, "expert", axis=0, tiled=True)
+        keys = call(
+            functools.partial(slot_keys_kernel, capacity, experts),
+            (shape((count, top), jnp.int32),) * 2,
+            (4 * count * count * experts, 4 * count * LANES),
+            in_specs=[SMEM, VMEM, VMEM],
+        )(here.reshape(1), forward_routes[0], backward_routes[0])
+        keys_f, keys_b = lax.all_gather(keys, "expert", axis=0, tiled=True)
+        keys_f = rotate(keys_f, "section", -1)
+        got_b = lax.all_gather(upstream, "expert", axis=0, tiled=True)
+    else:
+        got_f, got_b = [
+            lax.all_to_all(
+                call(
+                    functools.partial(send_rows_kernel, capacity, experts),
+                    shape((slots, width), BF16),
+                    (2 * slots * count * width, 2 * (count + slots) * width),
+                )(routes, data),
+                "expert",
+                split_axis=0,
+                concat_axis=0,
+                tiled=True,
+            )
+            for routes, data in ((routes_f, tokens), (backward_routes[0], upstream))
+        ]
+        place = jnp.arange(slots, dtype=jnp.int32)[:, None]
+        share = local * capacity
+        keys_f = keys_b = place // share * slots + here * share + place % share
 
     mixing_f, mixing_b, tables_b, shares_b = call(
         functools.partial(mixing_kernel, capacity, experts),
@@ -283,13 +316,14 @@
         ),
         (4 * count * width * experts, 4 * (count + LANES) * width),
     )(
-        normed, router_f, routes_f, saved_inputs[0], norm_gain, router[0], backward_routes[0]
+        tokens, gain_f, router_f, routes_f, saved_inputs[0], norm_gain, router_t, backward_routes[0]
     )
     saved_pre = jnp.transpose(pre_activation[0], (1, 0, 2, 3)).reshape(local, rows, hidden)
     saved_pre = jnp.pad(saved_pre, ((0, 0), (0, padded - rows), (0, 0)))
 
-    order = row_order(sources, local, capacity, padded)
-    order, back_order = jnp.asarray(order, BF16), jnp.asarray(order.T, BF16)
+    row_keys, back_order = row_order(sources, local, capacity, padded, slots)
+    back_order = jnp.asarray(back_order, BF16)
+    offset = (here * (local * capacity)).reshape(1)
     weight_specs = [
         pl.BlockSpec((1, width, chunk), lambda e, f: (e, 0, f)),
         pl.BlockSpec((1, chunk, width), lambda e, f: (e, f, 0)),
@@ -304,8 +338,11 @@
         expert_cost,
         grid=(local, steps),
         in_specs=[
-            full_spec((slots, width)),
-            full_spec(order.shape),
+            SMEM,
+            full_spec(row_keys.shape),
+            full_spec(keys_f.shape),
+            full_spec(got_f.shape),
+            full_spec(gain_f.shape),
             full_spec(back_order.shape),
             *weight_specs,
         ],
@@ -315,7 +352,7 @@
             pltpu.VMEM((padded, width), F32),
             pltpu.VMEM((local * padded, width), BF16),
         ],
-    )(got_f, order, back_order, up_weight, down_weight)
+    )(offset, row_keys, keys_f, got_f, gain_f, back_order, up_weight, down_weight)
     back_f = lax.all_to_all(result_f, "expert", split_axis=0, concat_axis=0, tiled=True)
 
     result_b = call(
@@ -324,8 +361,10 @@
         expert_cost,
         grid=(local, steps),
         in_specs=[
-            full_spec((slots, width)),
-            full_spec(order.shape),
+            SMEM,
+            full_spec(row_keys.shape),
+            full_spec(keys_b.shape),
+            full_spec(got_b.shape),
             full_spec(back_order.shape),
             pl.BlockSpec((1, padded, chunk), lambda e, f: (e, 0, f)),
             *weight_specs,
@@ -333,11 +372,11 @@
         out_specs=full_spec((slots, width + LANES)),
         scratch_shapes=[
             pltpu.VMEM((local * padded, width), BF16),
-            pltpu.VMEM((padded, width), F32),
+            pltpu.VMEM((width, padded), F32),
             pltpu.VMEM((padded, LANES), F32),
             pltpu.VMEM((local * padded, width + LANES), BF16),
         ],
-    )(got_b, order, back_order, saved_pre, up_weight, down_weight)
+    )(offset, row_keys, keys_b, got_b, back_order, saved_pre, up_weight, down_weight)
     back_b = lax.all_to_all(result_b, "expert", split_axis=0, concat_axis=0, tiled=True)
 
     output = call(
@@ -352,7 +391,7 @@
         shape((count, width), BF16),
         (2 * slots * count * width, 2 * (3 * count + slots) * width),
     )(
-        saved_inputs[0], upstream, norm_gain, router[0], backward_routes[0],
+        saved_inputs[0], upstream, norm_gain, router_t, backward_routes[0],
         mixing_b, tables_b, shares_b, back_b,
     )
     return (forward_output[None], input_gradient[None])

time: 148 us -> 191 us (1.29)
  blocking collectives: 0 us -> 32.5 us
  between operations: 0.75 us -> 14.2 us
  Pallas kernels: 68.9 us -> 79.9 us
  starting transfers between devices: 27.4 us -> 19.5 us
  waiting for transfers between devices: 39.9 us -> 34.2 us
  other arithmetic: 0 us -> 2.44 us
  local copies, waits for them, and re-layouts: 10.1 us -> 7.72 us
    all_gather x0 -> x2, blocking collectives: none -> 32.5 us  [on_device(): keys_f, keys_b = lax.all_gather(keys, 'expert', axis=0, tiled=True)]
    pallas_call x1, Pallas kernels: 33.4 us -> 46.2 us  [on_device(): call(functools.partial(backward_expert_kernel, padded, steps), shape((slo...]
    all_to_all x2 -> x0, waiting for transfers between devices: 9.45 us -> none  [the longest x1 9.45 us: on_device(): lax.all_to_all(send_f, 'expert', split_axis=0, concat_axis=0, tiled=True)]
    all_to_all x2 -> x0, starting transfers between devices: 8.42 us -> none  [the longest x1 4.87 us: on_device(): lax.all_to_all(send_f, 'expert', split_axis=0, concat_axis=0, tiled=True)]
    pallas_call x2 -> x1, Pallas kernels: 3.35 us -> 0.42 us  [on_device(): call(functools.partial(slot_keys_kernel, capacity, experts), (shape((coun...]
    all_to_all x1, waiting for transfers between devices: 0.01 us -> 2.88 us  [on_device(): lax.all_to_all(result_b, 'expert', split_axis=0, concat_axis=0, tiled=True)]
    select_n x0 -> x2, other arithmetic: none -> 2.44 us  [the longest x1 1.69 us: on_device(): tokens = jnp.where(section == last, embedded, forward_sent[0])]
    unnamed x26 -> x25, local copies, waits for them, and re-layouts: 7.29 us -> 5.48 us
  transfers between devices with their start and end apart: 9 -> 10, of which waited for: 5 -> 5; matrix products, arithmetic and copies ran while one was open for 2% -> 2% of each run, Pallas kernels for 44% -> 41%
where the time goes in v2:
time: 191 us; the launch traced here: 190 us
  Pallas kernels  79.9 us (42%)
  waiting for transfers between devices  34.2 us (18%)
  blocking collectives  32.5 us (17%)
  starting transfers between devices  19.5 us (10%)
  between operations  14.2 us (7%)
  local copies, waits for them, and re-layouts  7.72 us (4%)
  other arithmetic  2.44 us (1%)
    pallas_call x1, Pallas kernels, on_device(): call(functools.partial(backward_expert_kernel, padded, steps), shape((slo...  46.2 us
    all_gather x2, blocking collectives, on_device(): keys_f, keys_b = lax.all_gather(keys, 'expert', axis=0, tiled=True)  32.5 us
    ppermute x6, waiting for transfers between devices, rotate(): lax.ppermute(block, axis, [(i, (i + distance) % size) for i in range(size)])  31.3 us
    pallas_call x1, Pallas kernels, on_device(): call(functools.partial(forward_expert_kernel, padded, steps), shape((slot...  30.8 us
    ppermute x6, starting transfers between devices, rotate(): lax.ppermute(block, axis, [(i, (i + distance) % size) for i in range(size)])  9.74 us
    all_to_all x1, starting transfers between devices, on_device(): lax.all_to_all(result_b, 'expert', split_axis=0, concat_axis=0, tiled=True)  6.18 us
    unnamed x25, local copies, waits for them, and re-layouts  5.48 us
  transfers between devices with their start and end apart: 10, of which 5 were waited for; matrix products, arithmetic and copies ran while one was open for 2% of the time, Pallas kernels for 41%

profile of v2, /device:TPU:0, one launch (start us, length us, event | category | flops | bytes accessed | tf_op | source)
XLA Modules:
  0.0 190.4 jit_solution(14000117258661771073)
XLA Ops:
  7.2 0.0 all-gather.5.cloned.1.call-start
  7.2 1.7 bitcast_select_fusion.tokens
  8.9 0.0 all-gather.5.cloned.1.call-update
  8.9 0.0 all-gather.7.cloned.1.call-start
  9.0 4.0 %collective-permute-start.5 = (bf16[64,2048]{1,0:T(8,128)(2,1)}, bf16[64,2048]{1,0:T(8,128)(2,1)S(1)}, u32[]{:S(2)}, u32[]{:S(2)}) collective-permute-start(bf16[64,2048]{1,0:T(8,128)(2,1)} %bitcast.42), channel_id=1, source_target_pairs={{0,24},{8,0},{16,8},{24,16},{1,25},{9,1},{17,9},{25,17},{2,26},{10... | collective-permute-start | bytes 786440 | tf_op jit(solution)/shard_map/ppermute | solution.py:46
  13.0 5.9 %collective-permute-done.5 = bf16[64,2048]{1,0:T(8,128)(2,1)S(1)} collective-permute-done((bf16[64,2048]{1,0:T(8,128)(2,1)}, bf16[64,2048]{1,0:T(8,128)(2,1)S(1)}, u32[]{:S(2)}, u32[]{:S(2)}) %collective-permute-start.5) | collective-permute-done | bytes 262176 | tf_op jit(solution)/shard_map/ppermute | solution.py:46
  18.9 0.7 broadcast_select_fusion.upstream
  19.6 0.0 all-gather.7.cloned.1.call-update
  19.7 4.3 %collective-permute-start = (bf16[1,2048]{1,0:T(2,128)(2,1)}, bf16[1,2048]{1,0:T(2,128)(2,1)S(1)}, u32[]{:S(2)}, u32[]{:S(2)}) collective-permute-start(bf16[1,2048]{1,0:T(2,128)(2,1)} %gain.1), channel_id=1, source_target_pairs={{0,24},{8,0},{16,8},{24,16},{1,25},{9,1},{17,9},{25,17},{2,26},{10... | collective-permute-start | bytes 12296 | tf_op jit(solution)/shard_map/ppermute | solution.py:46
  23.9 0.8 copy.37.routes_b.routes
  24.7 0.8 copy.36.routes_f
  25.5 0.4 shard_map.150
  25.9 0.1 copy.40
  26.0 12.1 %all-gather = s32[8,64,2]{1,2,0:T(2,128)S(1)} all-gather(s32[1,64,2]{1,2,0:T(2,128)S(1)} %bitcast.38), channel_id=1, replica_groups=mesh['section'=4,'expert'=8] {'expert'}, dimensions={0}, use_global_device_ids=true | all-gather | bytes 4608 | tf_op jit(solution)/shard_map/all_gather | solution.py:287
  38.1 0.1 copy.41
  38.2 0.1 collective-permute-start.3
  38.3 0.0 collective-permute-done.gain_f.gain
  38.3 8.5 %collective-permute-done.3.keys = s32[512,2]{1,0:T(8,128)S(1)} collective-permute-done((s32[512,2]{1,0:T(8,128)S(1)}, s32[512,2]{1,0:T(8,128)S(1)}, u32[]{:S(2)}, u32[]{:S(2)}) %collective-permute-start.3) | collective-permute-done | bytes 4128 | tf_op jit(solution)/shard_map/ppermute | solution.py:46
  46.8 0.0 all-gather.5.cloned.1.call-done.tokens
  46.8 0.0 copy-start.3
  46.8 1.6 copy-done.3
  48.4 0.0 copy-start.6
  48.4 0.9 copy-done.6
  49.3 0.0 copy-start.9
  49.3 0.7 copy-done.9
  50.0 0.0 copy-start.11
  50.0 0.0 copy-start.7
  50.0 0.0 copy-start.10
  50.0 30.8 %shard_map.151 = bf16[192,2048]{1,0:T(8,128)(2,1)} custom-call(s32[1]{0:T(128)} %bitcast.6.offset, s32[1,256]{1,0:T(1,128)S(1)} %copy-done.9, s32[512,2]{1,0:T(8,128)S(1)} %collective-permute-done.3.keys, bf16[512,2048]{1,0:T(8,128)(2,1)S(1)} %copy-done.3, bf16[1,2048]{1,0:T(2,128)(2,1)S(1)} %collective-permute-done.gain_f.gain, ...), custom_call_target="tpu_custom_call" | custom-call | flops 2147483648 | bytes 67108864 | tf_op jit(solution)/shard_map/pallas_call | solution.py:335
  80.8 3.5 %all-to-all-start = ((bf16[8,24,2048]{2,1,0:T(8,128)(2,1)}), bf16[8,24,2048]{2,1,0:T(8,128)(2,1)S(1)}, u32[]{:S(2)}, u32[]{:S(2)}) async-start(bf16[8,24,2048]{2,1,0:T(8,128)(2,1)} %bitcast.10), calls=%async_computation | async-start | bytes 1572864 | tf_op jit(solution)/shard_map/all_to_all | solution.py:356
  84.3 0.1 copy.42
  84.4 20.4 %all-gather.1 = s32[8,64,2]{1,2,0:T(2,128)S(1)} all-gather(s32[1,64,2]{1,2,0:T(2,128)S(1)} %bitcast.39), channel_id=1, replica_groups=mesh['section'=4,'expert'=8] {'expert'}, dimensions={0}, use_global_device_ids=true | all-gather | bytes 4608 | tf_op jit(solution)/shard_map/all_gather | solution.py:287
  104.8 0.1 copy.43
  104.9 0.0 copy-done.11
  105.0 0.2 copy.44
  105.2 0.0 all-gather.7.cloned.1.call-done.upstream
  105.3 0.0 copy-done.7
  105.3 0.0 copy-done.10
  105.3 0.0 copy-start.2
  105.3 1.6 copy-done.2
  106.9 0.0 copy-start.4
  106.9 0.0 copy-start
  106.9 0.0 copy-start.5
  106.9 0.0 copy-start.8
  106.9 0.0 copy-start.1
  106.9 46.2 %shard_map.153 = bf16[192,2176]{1,0:T(8,128)(2,1)} custom-call(s32[1]{0:T(128)} %bitcast.6.offset, s32[1,256]{1,0:T(1,128)S(1)} %copy-done.10, s32[512,2]{1,0:T(8,128)S(1)} %bitcast.28, bf16[512,2048]{1,0:T(8,128)(2,1)S(1)} %copy-done.2, bf16[192,256]{1,0:T(8,128)(2,1)S(1)} %copy-done.7, bf16[8,32,1024]{2,1,0:T(8,128)(2,1)S(1)} %pad.4.saved_pre, ...), custom_call_target="tpu_custom_call" | custom-call | flops 2147483648 | bytes 67108864 | tf_op jit(solution)/shard_map/pallas_call | solution.py:358
  153.1 0.0 all-to-all-done
  153.1 6.2 %all-to-all-start.1 = ((bf16[8,24,2176]{2,1,0:T(8,128)(2,1)}), bf16[8,24,2176]{2,1,0:T(8,128)(2,1)S(1)}, u32[]{:S(2)}, u32[]{:S(2)}) async-start(bf16[8,24,2176]{2,1,0:T(8,128)(2,1)} %bitcast.20), calls=%async_computation.1 | async-start | bytes 1671168 | tf_op jit(solution)/shard_map/all_to_all | solution.py:380
  159.3 0.0 copy-done.4
  159.3 1.0 collective-permute-start.1
  160.3 0.1 collective-permute-start.2
  160.4 8.3 %collective-permute-done.2.routes_f = s32[64,2]{1,0:T(8,128)S(1)} collective-permute-done((s32[64,2]{1,0:T(8,128)S(1)}, s32[64,2]{1,0:T(8,128)S(1)}, u32[]{:S(2)}, u32[]{:S(2)}) %collective-permute-start.2) | collective-permute-done | bytes 544 | tf_op jit(solution)/shard_map/ppermute | solution.py:46
  168.7 0.0 collective-permute-done.1.router_f
  168.7 0.0 copy-done
  168.7 0.0 copy-done.5
  168.7 0.0 copy-done.8
  168.7 0.6 shard_map.149
  169.4 0.3 shard_map.152
  169.6 0.2 collective-permute-start.4
  169.9 8.6 %collective-permute-done.4 = bf16[64,2048]{1,0:T(8,128)(2,1)S(1)} collective-permute-done((bf16[64,2048]{1,0:T(8,128)(2,1)S(1)}, bf16[64,2048]{1,0:T(8,128)(2,1)S(1)}, u32[]{:S(2)}, u32[]{:S(2)}) %collective-permute-start.4) | collective-permute-done | bytes 262176 | tf_op jit(solution)/shard_map/ppermute | solution.py:46
  178.4 2.9 %all-to-all-done.1 = bf16[8,24,2176]{2,1,0:T(8,128)(2,1)S(1)} async-done(((bf16[8,24,2176]{2,1,0:T(8,128)(2,1)}), bf16[8,24,2176]{2,1,0:T(8,128)(2,1)S(1)}, u32[]{:S(2)}, u32[]{:S(2)}) %all-to-all-start.1) | async-done | bytes 835616 | tf_op jit(solution)/shard_map/all_to_all | solution.py:380
  181.3 0.0 copy-done.1
  181.3 1.6 shard_map.154
  182.9 0.7 copy.47
  (1 shorter events, 0.0 us)
Async XLA Ops:
  7.2 39.7 %all-gather.5.cloned.1.call-start = ((), (), s32[]{:S(2)}) async-start(), calls=%async_computation.2 | async-start | bytes 2359296 | tf_op jit(solution)/shard_map/all_gather | solution.py:280
  8.9 96.3 %all-gather.7.cloned.1.call-start = ((), (), s32[]{:S(2)}) async-start(), calls=%async_computation.3 | async-start | bytes 2359296 | tf_op jit(solution)/shard_map/all_gather | solution.py:289
  9.0 9.9 %collective-permute-start.5 = (bf16[64,2048]{1,0:T(8,128)(2,1)}, bf16[64,2048]{1,0:T(8,128)(2,1)S(1)}, u32[]{:S(2)}, u32[]{:S(2)}) collective-permute-start(bf16[64,2048]{1,0:T(8,128)(2,1)} %bitcast.42), channel_id=1, source_target_pairs={{0,24},{8,0},{16,8},{24,16},{1,25},{9,1},{17,9},{25,17},{2,26},{10... | collective-permute-start | bytes 786440 | tf_op jit(solution)/shard_map/ppermute | solution.py:46
  19.7 18.7 %collective-permute-start = (bf16[1,2048]{1,0:T(2,128)(2,1)}, bf16[1,2048]{1,0:T(2,128)(2,1)S(1)}, u32[]{:S(2)}, u32[]{:S(2)}) collective-permute-start(bf16[1,2048]{1,0:T(2,128)(2,1)} %gain.1), channel_id=1, source_target_pairs={{0,24},{8,0},{16,8},{24,16},{1,25},{9,1},{17,9},{25,17},{2,26},{10... | collective-permute-start | bytes 12296 | tf_op jit(solution)/shard_map/ppermute | solution.py:46
  38.2 8.6 %collective-permute-start.3 = (s32[512,2]{1,0:T(8,128)S(1)}, s32[512,2]{1,0:T(8,128)S(1)}, u32[]{:S(2)}, u32[]{:S(2)}) collective-permute-start(s32[512,2]{1,0:T(8,128)S(1)} %bitcast.36), channel_id=1, source_target_pairs={{0,24},{8,0},{16,8},{24,16},{1,25},{9,1},{17,9},{25,17},{2,26},{10... | collective-permute-start | bytes 12296 | tf_op jit(solution)/shard_map/ppermute | solution.py:46
  46.8 1.6 copy-start.3
  48.4 0.9 copy-start.6
  49.3 0.7 copy-start.9
  50.0 55.0 %copy-start.11 = (bf16[1,8,8,3,1024]{4,2,3,1,0:T(8,128)(2,1)S(1)}, bf16[1,8,8,3,1024]{4,2,3,1,0:T(8,128)(2,1)}, u32[]{:S(2)}) copy-start(bf16[1,8,8,3,1024]{4,2,3,1,0:T(8,128)(2,1)} %param.21) | copy-start | bytes 1179652
  50.0 55.3 %copy-start.7 = (bf16[192,256]{1,0:T(8,128)(2,1)S(1)}, bf16[192,256]{1,0:T(8,128)(2,1)}, u32[]{:S(2)}) copy-start(bf16[192,256]{1,0:T(8,128)(2,1)} %constant.19.clone.back_order) | copy-start | bytes 294916
  50.0 55.3 %copy-start.10 = (s32[1,256]{1,0:T(1,128)S(1)}, s32[1,256]{1,0:T(1,128)}, u32[]{:S(2)}) copy-start(s32[1,256]{1,0:T(1,128)} %constant.20.clone.row_keys) | copy-start | bytes 3076
  80.8 72.3 %all-to-all-start = ((bf16[8,24,2048]{2,1,0:T(8,128)(2,1)}), bf16[8,24,2048]{2,1,0:T(8,128)(2,1)S(1)}, u32[]{:S(2)}, u32[]{:S(2)}) async-start(bf16[8,24,2048]{2,1,0:T(8,128)(2,1)} %bitcast.10), calls=%async_computation | async-start | bytes 1572864 | tf_op jit(solution)/shard_map/all_to_all | solution.py:356
  105.3 1.6 copy-start.2
  106.9 52.4 %copy-start.4 = (bf16[1,2048,64]{1,2,0:T(8,128)(2,1)S(1)}, bf16[1,2048,64]{1,2,0:T(8,128)(2,1)}, u32[]{:S(2)}) copy-start(bf16[1,2048,64]{1,2,0:T(8,128)(2,1)} %param.23) | copy-start | bytes 786436
  106.9 61.8 %copy-start = (bf16[64,2048]{1,0:T(8,128)(2,1)S(1)}, bf16[64,2048]{1,0:T(8,128)(2,1)}, u32[]{:S(2)}) copy-start(bf16[64,2048]{1,0:T(8,128)(2,1)} %bitcast_select_fusion.tokens) | copy-start | bytes 786436
  106.9 61.8 %copy-start.5 = (bf16[1,64,2048]{2,1,0:T(8,128)(2,1)S(1)}, bf16[1,64,2048]{2,1,0:T(8,128)(2,1)}, u32[]{:S(2)}) copy-start(bf16[1,64,2048]{2,1,0:T(8,128)(2,1)} %param.19) | copy-start | bytes 786436
  106.9 61.8 %copy-start.8 = (bf16[1,2048]{1,0:T(2,128)(2,1)S(1)}, bf16[1,2048]{1,0:T(2,128)(2,1)}, u32[]{:S(2)}) copy-start(bf16[1,2048]{1,0:T(2,128)(2,1)} %gain.1) | copy-start | bytes 12292
  106.9 74.4 %copy-start.1 = (bf16[64,2048]{1,0:T(8,128)(2,1)S(1)}, bf16[64,2048]{1,0:T(8,128)(2,1)}, u32[]{:S(2)}) copy-start(bf16[64,2048]{1,0:T(8,128)(2,1)} %broadcast_select_fusion.upstream) | copy-start | bytes 786436
  153.1 28.2 %all-to-all-start.1 = ((bf16[8,24,2176]{2,1,0:T(8,128)(2,1)}), bf16[8,24,2176]{2,1,0:T(8,128)(2,1)S(1)}, u32[]{:S(2)}, u32[]{:S(2)}) async-start(bf16[8,24,2176]{2,1,0:T(8,128)(2,1)} %bitcast.20), calls=%async_computation.1 | async-start | bytes 1671168 | tf_op jit(solution)/shard_map/all_to_all | solution.py:380
  159.3 9.4 %collective-permute-start.1 = (bf16[64,2048]{1,0:T(8,128)(2,1)S(1)}, bf16[64,2048]{1,0:T(8,128)(2,1)S(1)}, u32[]{:S(2)}, u32[]{:S(2)}) collective-permute-start(bf16[64,2048]{1,0:T(8,128)(2,1)S(1)} %bitcast.29), channel_id=1, source_target_pairs={{0,24},{8,0},{16,8},{24,16},{1,25},{9,1},{17,9},{25,17},{2,26},{10... | collective-permute-start | bytes 786440 | tf_op jit(solution)/shard_map/ppermute | solution.py:46
  160.3 8.4 %collective-permute-start.2 = (s32[64,2]{1,0:T(8,128)S(1)}, s32[64,2]{1,0:T(8,128)S(1)}, u32[]{:S(2)}, u32[]{:S(2)}) collective-permute-start(s32[64,2]{1,0:T(8,128)S(1)} %copy.36.routes_f), channel_id=1, source_target_pairs={{0,24},{8,0},{16,8},{24,16},{1,25},{9,1},{17,9},{25,17},{2,26},{10... | collective-permute-start | bytes 1544 | tf_op jit(solution)/shard_map/ppermute | solution.py:46
  169.6 8.8 %collective-permute-start.4 = (bf16[64,2048]{1,0:T(8,128)(2,1)S(1)}, bf16[64,2048]{1,0:T(8,128)(2,1)S(1)}, u32[]{:S(2)}, u32[]{:S(2)}) collective-permute-start(bf16[64,2048]{1,0:T(8,128)(2,1)S(1)} %shard_map.152), channel_id=1, source_target_pairs={{0,8},{8,16},{16,24},{24,0},{1,9},{9,17},{17,25},{25,1},{2,10},{10... | collective-permute-start | bytes 786440 | tf_op jit(solution)/shard_map/ppermute | solution.py:46
Sparse Core Ops, SparseCore 0:
  10.2 31.8 all-gather.4
  44.2 28.5 all-gather.6

commit v3 on v1

v3 whole, which is shorter than its diff:
```python
import functools

import jax
import jax.numpy as jnp
import numpy as np
from jax import lax
from jax.experimental import pallas as pl
from jax.experimental.pallas import tpu as pltpu
from jax.sharding import PartitionSpec as P

EPS = 1e-06
BF16 = jnp.bfloat16
F32 = jnp.float32
LANES = 128
ROWS = 16
VMEM_LIMIT = 48 * 1024 * 1024
NT = (((1,), (1,)), ((), ()))
TN = (((0,), (0,)), ((), ()))


def dot(a, b, dims=(((1,), (0,)), ((), ()))):
    return lax.dot_general(a, b, dims, preferred_element_type=F32)


def call(kernel, out_shape, cost, **kwargs):
    flops, moved = cost
    return pl.pallas_call(
        kernel,
        out_shape=out_shape,
        compiler_params=pltpu.CompilerParams(vmem_limit_bytes=VMEM_LIMIT),
        cost_estimate=pl.CostEstimate(flops=flops, bytes_accessed=moved, transcendentals=0),
        **kwargs,
    )


def full_spec(shape):
    return pl.BlockSpec(shape, lambda *_: (0,) * len(shape))


SMEM = pl.BlockSpec(memory_space=pltpu.SMEM)
VMEM = pl.BlockSpec(memory_space=pltpu.VMEM)


def from_behind(block, axis, distance):
    devices = range(lax.axis_size(axis))
    route = [(i - distance, i) for i in devices if i - distance in devices]
    return lax.ppermute(block, axis, route)


def exchange(rows):
    return lax.all_to_all(rows, "expert", split_axis=0, concat_axis=0, tiled=True)


def expert_hits(routes, experts):
    count, top = routes.shape
    lane = lax.broadcasted_iota(jnp.int32, (count, experts), 1)
    return [(routes[:, k : k + 1] == lane).astype(F32) for k in range(top)]


def slot_targets(routes, experts, capacity):
    count, top = routes.shape
    hits = expert_hits(routes, experts)
    earlier = lax.broadcasted_iota(jnp.int32, (count, count), 1) < lax.broadcasted_iota(
        jnp.int32, (count, count), 0
    )
    before = dot(earlier.astype(F32).astype(BF16), sum(hits).astype(BF16))
    targets = []
    for k in range(top):
        ranked = jnp.sum((before + sum(hits[:k], jnp.zeros_like(before))) * hits[k], 1, keepdims=True)
        targets.append(routes[:, k : k + 1] * capacity + ranked.astype(jnp.int32))
    return targets, hits


def tables_of(targets, row_keys):
    return [(row_keys == target).astype(F32) for target in targets]


def normalise(tokens, gain):
    widened = tokens.astype(F32)
    inv_rms = lax.rsqrt(jnp.mean(widened * widened, axis=-1, keepdims=True) + EPS)
    return widened, inv_rms, (widened * inv_rms * gain.astype(F32)).astype(BF16)


def route_shares(normed, router, hits):
    logits = dot(normed, router, NT)
    exponents = [jnp.exp(jnp.sum(logits * hit, axis=1, keepdims=True)) for hit in hits]
    total = sum(exponents)
    return [exponent / total for exponent in exponents]


def first_send_kernel(
    capacity, experts, place, arrived_f, arrived_b, embedded, loss, gain, routes_f, routes_b,
    row_keys, tokens, upstream, data, send,
):
    count = embedded.shape[0]
    slots = experts * capacity
    chosen = jnp.where(place[0] == 0, embedded[...], arrived_f[...])
    tokens[...] = chosen
    data[:count, :] = normalise(chosen, gain[...])[2]
    chosen = jnp.where(place[0] == place[1], loss[...], arrived_b[...])
    upstream[...] = chosen
    data[count:, :] = chosen
    targets_f, _ = slot_targets(routes_f[...], experts, capacity)
    targets_b, _ = slot_targets(routes_b[...], experts, capacity)
    keys = row_keys[0:1, :]
    table_f = sum(tables_of(targets_f, keys))
    table_b = sum(tables_of([t + slots for t in targets_b], keys))
    table = jnp.concatenate([table_f, table_b], axis=0).astype(BF16)
    send[...] = dot(table, data[...], TN).astype(BF16)


def mixing_kernel(
    capacity, experts, data, saved, gain, router, routes_f, routes_b, row_keys,
    mixing_f, mixing_b, tables_b, shares_b, *sends,
):
    count = saved.shape[0]
    slots = experts * capacity
    targets_f, hits = slot_targets(routes_f[...], experts, capacity)
    shares_f = route_shares(data[:count, :], router[...], hits)
    targets_b, hits = slot_targets(routes_b[...], experts, capacity)
    targets_b = [t + slots for t in targets_b]
    _, _, rows = normalise(saved[...], gain[...])
    own_shares = route_shares(rows, router[...], hits)
    for k, share in enumerate(own_shares):
        shares_b[k] = jnp.broadcast_to(share, shares_b.shape[1:])
    for part in range(mixing_f.shape[0]):
        keys = row_keys[part : part + 1, :]
        found_f, found_b = tables_of(targets_f, keys), tables_of(targets_b, keys)
        mixing_f[part] = sum(
            t * s.astype(BF16).astype(F32) for t, s in zip(found_f, shares_f)
        ).astype(BF16)
        mixing_b[part] = sum(
            t * s.astype(BF16).astype(F32) for t, s in zip(found_b, own_shares)
        ).astype(BF16)
        for k, table in enumerate(found_b):
            tables_b[part, k] = table.astype(BF16)
        if part > 0:
            table = jnp.concatenate([sum(found_f), sum(found_b)], axis=0).astype(BF16)
            sends[part - 1][...] = dot(table, data[...], TN).astype(BF16)


def expert_kernel(
    padded, steps, recv, order, back_order, saved_pre, up, down,
    out, rows, total_f, total_b, inner, results,
):
    expert, step = pl.program_id(0), pl.program_id(1)
    held = pl.num_programs(0)
    width = rows.shape[1]

    @pl.when((expert == 0) & (step == 0))
    def _():
        rows[...] = dot(order[...], recv[...]).astype(BF16)
        results[:, width:] = jnp.zeros((results.shape[0], results.shape[1] - width), BF16)

    own_f = pl.ds(pl.multiple_of(expert * padded, ROWS), padded)
    own_b = pl.ds(pl.multiple_of((held + expert) * padded, ROWS), padded)
    pre_act = dot(rows[own_f, :], up[0])
    hidden_grad = dot(rows[own_b, :], down[0], NT)
    hidden = (pre_act / (1.0 + jnp.exp(-pre_act))).astype(BF16)
    pre = saved_pre[0].astype(F32)
    gate = 1.0 / (1.0 + jnp.exp(-pre))
    inner_part = jnp.sum(hidden_grad * (pre * gate).astype(BF16).astype(F32), axis=1, keepdims=True)
    pre_grad = (hidden_grad * gate * (1.0 + pre * (1.0 - gate))).astype(BF16)
    part_f = dot(hidden, down[0])
    part_b = dot(pre_grad, up[0], NT)

    @pl.when(step == 0)
    def _():
        total_f[...] = part_f
        total_b[...] = part_b
        inner[...] = jnp.broadcast_to(inner_part, inner.shape)

    @pl.when(step > 0)
    def _():
        total_f[...] += part_f
        total_b[...] += part_b
        inner[...] += jnp.broadcast_to(inner_part, inner.shape)

    @pl.when(step == steps - 1)
    def _():
        results[own_f, :width] = total_f[...].astype(BF16)
        results[own_b, :width] = total_b[...].astype(BF16)
        results[own_b, width:] = inner[...].astype(BF16)

    @pl.when((expert == held - 1) & (step == steps - 1))
    def _():
        out[...] = dot(back_order[...], results[...]).astype(BF16)


def combine_kernel(
    experts, tokens, saved, upstream, gain, router, routes, mixing_f, mixing_b, tables, shares, *refs
):
    *backs, output, gradient = refs
    width = tokens.shape[1]
    parts = range(len(backs))
    widened = saved[...].astype(F32)
    inv_rms = lax.rsqrt(jnp.mean(widened * widened, axis=-1, keepdims=True) + EPS)
    hits = expert_hits(routes[...], experts)
    top = len(hits)
    share = [shares[k][:, :1] for k in range(top)]
    inner = [sum(dot(tables[p, k], backs[p][:, width:]) for p in parts)[:, :1] for k in range(top)]
    mean = sum(share[k] * inner[k] for k in range(top))
    logit_grad = sum(share[k] * (inner[k] - mean) * hits[k] for k in range(top))
    high = logit_grad.astype(BF16)
    rest = logit_grad - high.astype(F32)
    middle = rest.astype(BF16)
    low = (rest - middle.astype(F32)).astype(BF16)
    output[0] = (
        tokens[...].astype(F32) + sum(dot(mixing_f[p], backs[p][:, :width]) for p in parts)
    ).astype(BF16)
    normed_grad = sum(dot(mixing_b[p], backs[p][:, :width]) for p in parts)
    for piece in (high, middle, low):
        normed_grad += dot(piece, router[...])
    gained = normed_grad * gain[...].astype(F32)
    projected = jnp.mean(widened * gained, axis=-1, keepdims=True)
    grad = inv_rms * gained - widened * (inv_rms * inv_rms * inv_rms * projected)
    gradient[0] = (upstream[...].astype(F32) + grad).astype(BF16)


def exchange_order(parts, sources, local, capacity, padded):
    held = local // parts
    slots = sources * local * capacity
    keys = np.zeros((parts, 2 * sources * held * capacity), np.int32)
    table = np.zeros((2 * held * padded, keys.shape[1]), np.float32)
    for source in range(sources):
        for batch in range(2):
            for expert in range(held):
                for slot in range(capacity):
                    row = ((source * 2 + batch) * held + expert) * capacity + slot
                    for part in range(parts):
                        full = (source * local + part * held + expert) * capacity + slot
                        keys[part, row] = batch * slots + full
                    table[(batch * held + expert) * padded + source * capacity + slot, row] = 1.0
    return keys, table


def on_device(
    forward_sent,
    embedded,
    forward_routes,
    backward_sent,
    loss_gradient,
    saved_inputs,
    backward_routes,
    pre_activation,
    norm_gain,
    router,
    up_weight,
    down_weight,
):
    section = lax.axis_index("section")
    last = lax.axis_size("section") - 1
    sources = lax.axis_size("expert")
    experts = router.shape[2]
    capacity = pre_activation.shape[3]
    local, width, hidden = up_weight.shape
    count = embedded.shape[0]
    top = forward_routes.shape[2]
    slots = experts * capacity
    rows = sources * capacity
    padded = -(-rows // ROWS) * ROWS
    steps = 2
    chunk = hidden // steps
    shape = jax.ShapeDtypeStruct
    parts = 2 if local % 2 == 0 else 1
    held = local // parts
    moved = 2 * slots // parts
    row_keys, order = exchange_order(parts, sources, local, capacity, padded)
    order, back_order = jnp.asarray(order, BF16), jnp.asarray(order.T, BF16)

    router_t = router[0].T
    arrived_f = from_behind(forward_sent[0], "section", 1)
    arrived_b = from_behind(backward_sent[0], "section", -1)
    tokens, upstream, data, send = call(
        functools.partial(first_send_kernel, capacity, experts),
        (
            shape((count, width), BF16),
            shape((count, width), BF16),
            shape((2 * count, width), BF16),
            shape((moved, width), BF16),
        ),
        (4 * moved * count * width, 2 * (8 * count + moved) * width),
        in_specs=[SMEM] + [VMEM] * 8,
    )(
        jnp.stack([section, jnp.full_like(section, last)]).astype(jnp.int32),
        arrived_f, arrived_b, embedded, loss_gradient, norm_gain,
        forward_routes[0], backward_routes[0], row_keys,
    )
    mixing_f, mixing_b, tables_b, shares_b, *sends = call(
        functools.partial(mixing_kernel, capacity, experts),
        (
            shape((parts, count, moved), BF16),
            shape((parts, count, moved), BF16),
            shape((parts, top, count, moved), BF16),
            shape((top, count, LANES), F32),
        )
        + (shape((moved, width), BF16),) * (parts - 1),
        (4 * moved * count * width, 2 * (4 * count + moved) * width),
    )(
        data, saved_inputs[0], norm_gain, router_t, forward_routes[0], backward_routes[0], row_keys
    )
    saved_pre = jnp.transpose(pre_activation[0], (1, 0, 2, 3)).reshape(local, rows, hidden)
    saved_pre = jnp.pad(saved_pre, ((0, 0), (0, padded - rows), (0, 0)))

    received = [exchange(data) for data in (send, *sends)]
    backs = []
    for part, got in enumerate(received):
        result = call(
            functools.partial(expert_kernel, padded, steps),
            shape((moved, width + LANES), BF16),
            (8 * held * padded * width * hidden, 4 * held * width * hidden),
            grid=(held, steps),
            in_specs=[
                full_spec((moved, width)),
                full_spec(order.shape),
                full_spec(back_order.shape),
                pl.BlockSpec((1, padded, chunk), lambda e, f, p=part: (p * held + e, 0, f)),
                pl.BlockSpec((1, width, chunk), lambda e, f, p=part: (p * held + e, 0, f)),
                pl.BlockSpec((1, chunk, width), lambda e, f, p=part: (p * held + e, f, 0)),
            ],
            out_specs=full_spec((moved, width + LANES)),
            scratch_shapes=[
                pltpu.VMEM((2 * held * padded, width), BF16),
                pltpu.VMEM((padded, width), F32),
                pltpu.VMEM((padded, width), F32),
                pltpu.VMEM((padded, LANES), F32),
                pltpu.VMEM((2 * held * padded, width + LANES), BF16),
            ],
        )(got, order, back_order, saved_pre, up_weight, down_weight)
        backs.append(exchange(result))
    return tuple(
        call(
            functools.partial(combine_kernel, experts),
            (shape((1, count, width), BF16),) * 2,
            (8 * moved * count * width, 2 * (5 * count + 2 * moved) * width),
        )(
            tokens, saved_inputs[0], upstream, norm_gain, router_t, backward_routes[0],
            mixing_f, mixing_b, tables_b, shares_b, *backs,
        )
    )


def solution(mesh):
    return jax.shard_map(
        on_device,
        mesh=mesh,
        in_specs=(
            P("section", "expert", None),
            P("expert", None),
            P("section", "expert", None),
            P("section", "expert", None),
            P("expert", None),
            P("section", "expert", None),
            P("section", "expert", None),
            P("section", None, "expert", None, None),
            P("section", None),
            P("section", None, None),
            P("expert", None, None),
            P("expert", None, None),
        ),
        out_specs=(P("section", "expert", None), P("section", "expert", None)),
        check_vma=False,
    )
```

time: 148 us -> 142 us (0.959)
  blocking collectives: 0 us -> 26.9 us
  Pallas kernels: 68.9 us -> 47.8 us
  waiting for transfers between devices: 39.9 us -> 23.8 us
  local copies, waits for them, and re-layouts: 10.1 us -> 22.2 us
  starting transfers between devices: 27.4 us -> 19.6 us
    all_to_all x0 -> x1, blocking collectives: none -> 26.9 us  [exchange(): lax.all_to_all(rows, 'expert', split_axis=0, concat_axis=0, tiled=True)]
    pallas_call x7 -> x5, Pallas kernels: 68.9 us -> 47.8 us  [the longest x2 42 us: on_device(): call(functools.partial(expert_kernel, padded, steps), shape((moved, width...]
    ppermute x5 -> x2, waiting for transfers between devices: 30.5 us -> 10.4 us  [from_behind(): return lax.ppermute(block, axis, route)]
    unnamed x26 -> x54, local copies, waits for them, and re-layouts: 7.29 us -> 19.4 us
    all_to_all x4 -> x3, starting transfers between devices: 18.6 us -> 13.5 us  [exchange(): lax.all_to_all(rows, 'expert', split_axis=0, concat_axis=0, tiled=True)]
    all_to_all x4 -> x3, waiting for transfers between devices: 9.46 us -> 13.5 us  [exchange(): lax.all_to_all(rows, 'expert', split_axis=0, concat_axis=0, tiled=True)]
    ppermute x5 -> x2, starting transfers between devices: 8.85 us -> 6.15 us  [from_behind(): return lax.ppermute(block, axis, route)]
  transfers between devices with their start and end apart: 9 -> 5, of which waited for: 5 -> 3; matrix products, arithmetic and copies ran while one was open for 2% -> 2% of each run, Pallas kernels for 44% -> 31%
where the time goes in v3:
time: 142 us; the launch traced here: 141 us
  Pallas kernels  47.8 us (34%)
  blocking collectives  26.9 us (19%)
  waiting for transfers between devices  23.8 us (17%)
  local copies, waits for them, and re-layouts  22.2 us (16%)
  starting transfers between devices  19.6 us (14%)
    pallas_call x2, Pallas kernels, on_device(): call(functools.partial(expert_kernel, padded, steps), shape((moved, width...  42 us
    all_to_all x1, blocking collectives, exchange(): lax.all_to_all(rows, 'expert', split_axis=0, concat_axis=0, tiled=True)  26.9 us
    unnamed x54, local copies, waits for them, and re-layouts  19.4 us
    all_to_all x3, starting transfers between devices, exchange(): lax.all_to_all(rows, 'expert', split_axis=0, concat_axis=0, tiled=True)  13.5 us
    all_to_all x3, waiting for transfers between devices, exchange(): lax.all_to_all(rows, 'expert', split_axis=0, concat_axis=0, tiled=True)  13.5 us
    ppermute x2, waiting for transfers between devices, from_behind(): return lax.ppermute(block, axis, route)  10.4 us
    ppermute x2, starting transfers between devices, from_behind(): return lax.ppermute(block, axis, route)  6.15 us
  transfers between devices with their start and end apart: 5, of which 3 were waited for; matrix products, arithmetic and copies ran while one was open for 2% of the time, Pallas kernels for 31%

profile of v3, /device:TPU:0, one launch (start us, length us, event | category | flops | bytes accessed | tf_op | source)
XLA Modules:
  0.0 141.1 jit_solution(1432043418765051359)
XLA Ops:
  0.6 4.9 %collective-permute-start = (bf16[64,2048]{1,0:T(8,128)(2,1)}, bf16[64,2048]{1,0:T(8,128)(2,1)S(1)}, u32[]{:S(2)}, u32[]{:S(2)}) collective-permute-start(bf16[64,2048]{1,0:T(8,128)(2,1)} %bitcast.34), channel_id=1, source_target_pairs={{0,8},{8,16},{16,24},{1,9},{9,17},{17,25},{2,10},{10,18},{18,26},{... | collective-permute-start | bytes 786440 | tf_op jit(solution)/shard_map/ppermute | solution.py:47
  5.5 1.3 collective-permute-start.1
  6.8 0.8 copy.24.routes_b.routes
  7.6 0.8 copy.23.routes_f
  8.3 0.1 pad_add_fusion.place
  8.4 2.9 %collective-permute-done.arrived_f = bf16[64,2048]{1,0:T(8,128)(2,1)S(1)} collective-permute-done((bf16[64,2048]{1,0:T(8,128)(2,1)}, bf16[64,2048]{1,0:T(8,128)(2,1)S(1)}, u32[]{:S(2)}, u32[]{:S(2)}) %collective-permute-start) | collective-permute-done | bytes 262176 | tf_op jit(solution)/shard_map/ppermute | solution.py:47
  11.3 7.5 %collective-permute-done.1.arrived_b = bf16[64,2048]{1,0:T(8,128)(2,1)S(1)} collective-permute-done((bf16[64,2048]{1,0:T(8,128)(2,1)}, bf16[64,2048]{1,0:T(8,128)(2,1)S(1)}, u32[]{:S(2)}, u32[]{:S(2)}) %collective-permute-start.1) | collective-permute-done | bytes 262176 | tf_op jit(solution)/shard_map/ppermute | solution.py:47
  18.8 0.0 copy-start.12
  18.8 0.9 copy-done.12
  19.8 0.0 copy-start.13
  19.8 0.9 copy-done.13
  20.7 0.0 copy-start.16
  20.7 0.7 copy-done.16
  21.4 0.0 copy-start.25
  21.4 0.7 copy-done.25
  22.1 2.2 %shard_map.158 = (bf16[64,2048]{1,0:T(8,128)(2,1)S(1)}, bf16[64,2048]{1,0:T(8,128)(2,1)S(1)}, bf16[128,2048]{1,0:T(8,128)(2,1)S(1)}, bf16[192,2048]{1,0:T(8,128)(2,1)}) custom-call(s32[2]{0:T(128)S(1)} %pad_add_fusion.place, bf16[64,2048]{1,0:T(8,128)(2,1)S(1)} %collective-permute-done.arrived_f, bf16[64,2048]{1,0:T(8,128)(2,1)S(1)} %collective-permute-done.1.arrived_b, ...), custom_call_target="tpu_custom_call" | custom-call | flops 100663296 | bytes 2883584 | tf_op jit(solution)/shard_map/pallas_call | solution.py:274
  24.3 0.0 copy-start.8
  24.3 0.7 copy-done.8
  25.0 0.0 copy-start.10
  25.0 0.7 copy-done.10
  25.7 4.9 %all-to-all-start = ((bf16[8,24,2048]{2,1,0:T(8,128)(2,1)}), bf16[8,24,2048]{2,1,0:T(8,128)(2,1)S(1)}, u32[]{:S(2)}, u32[]{:S(2)}) async-start(bf16[8,24,2048]{2,1,0:T(8,128)(2,1)} %bitcast.9), calls=%async_computation | async-start | bytes 1572864 | tf_op jit(solution)/shard_map/all_to_all | solution.py:51
  30.6 0.0 copy-start
  30.6 0.9 copy-done
  31.6 0.0 copy-start.2
  31.6 0.9 copy-done.2
  32.5 0.0 copy-start.17
  32.5 0.7 copy-done.17
  33.2 0.0 copy-start.26
  33.2 0.7 copy-done.26
  33.9 1.7 %shard_map.159 = (bf16[2,64,192]{2,1,0:T(8,128)(2,1)S(1)}, bf16[2,64,192]{2,1,0:T(8,128)(2,1)S(1)}, bf16[2,2,64,192]{3,2,1,0:T(8,128)(2,1)S(1)}, f32[2,64,128]{2,1,0:T(8,128)S(1)}, bf16[192,2048]{1,0:T(8,128)(2,1)}) custom-call(bf16[128,2048]{1,0:T(8,128)(2,1)S(1)} %get-tuple-element.13.data, bf16[64,2048]{1,0:T(8,128)(2,1)S(1)} %bitcast.27, ...), custom_call_target="tpu_custom_call" | custom-call | flops 100663296 | bytes 1835008 | tf_op jit(solution)/shard_map/pallas_call | solution.py:289
  35.6 0.0 copy-start.14
  35.6 0.6 copy-done.14
  36.3 0.0 copy-start.19
  36.3 0.6 copy-done.19
  36.9 0.0 copy-start.21
  36.9 0.6 copy-done.21
  37.5 0.0 copy-start.23
  37.5 0.6 copy-done.23
  38.1 13.5 %all-to-all-done = bf16[8,24,2048]{2,1,0:T(8,128)(2,1)S(1)} async-done(((bf16[8,24,2048]{2,1,0:T(8,128)(2,1)}), bf16[8,24,2048]{2,1,0:T(8,128)(2,1)S(1)}, u32[]{:S(2)}, u32[]{:S(2)}) %all-to-all-start) | async-done | bytes 786464 | tf_op jit(solution)/shard_map/all_to_all | solution.py:51
  51.6 3.5 %all-to-all-start.2 = ((bf16[8,24,2048]{2,1,0:T(8,128)(2,1)}), bf16[8,24,2048]{2,1,0:T(8,128)(2,1)S(1)}, u32[]{:S(2)}, u32[]{:S(2)}) async-start(bf16[8,24,2048]{2,1,0:T(8,128)(2,1)} %bitcast.16), calls=%async_computation.2 | async-start | bytes 1572864 | tf_op jit(solution)/shard_map/all_to_all | solution.py:51
  55.1 1.2 copy.27
  56.4 0.0 copy-start.4
  56.4 0.9 copy-done.4
  57.3 0.0 copy-start.6
  57.3 0.9 copy-done.6
  58.2 21.4 %shard_map.160 = bf16[192,2176]{1,0:T(8,128)(2,1)} custom-call(bf16[192,2048]{1,0:T(8,128)(2,1)S(1)} %bitcast.25, bf16[256,192]{1,0:T(8,128)(2,1)S(1)} %copy-done.4, bf16[192,256]{1,0:T(8,128)(2,1)S(1)} %copy-done.6, bf16[8,32,1024]{2,1,0:T(8,128)(2,1)S(1)} %pad.4.saved_pre, bf16[8,2048,1024]{2,1,0:T(8,128)(2,1)} %up.3, bf16[8,1024,2048]{2,1,0:T(8,128)(2,1)} %down.3), custom_call_target="tpu_custom_call" | custom-call | flops 2147483648 | bytes 33554432 | tf_op jit(solution)/shard_map/pallas_call | solution.py:308
  79.6 0.0 all-to-all-done.2
  79.6 5.0 %all-to-all-start.1 = ((bf16[8,24,2176]{2,1,0:T(8,128)(2,1)}), bf16[8,24,2176]{2,1,0:T(8,128)(2,1)S(1)}, u32[]{:S(2)}, u32[]{:S(2)}) async-start(bf16[8,24,2176]{2,1,0:T(8,128)(2,1)} %bitcast.14), calls=%async_computation.1 | async-start | bytes 1671168 | tf_op jit(solution)/shard_map/all_to_all | solution.py:51
  84.6 0.9 copy-done.5
  85.5 0.9 copy-done.7
  86.4 20.6 %shard_map.161 = bf16[192,2176]{1,0:T(8,128)(2,1)S(1)} custom-call(bf16[192,2048]{1,0:T(8,128)(2,1)S(1)} %bitcast.26, bf16[256,192]{1,0:T(8,128)(2,1)S(1)} %copy-done.5, bf16[192,256]{1,0:T(8,128)(2,1)S(1)} %copy-done.7, bf16[8,32,1024]{2,1,0:T(8,128)(2,1)S(1)} %pad.4.saved_pre, bf16[8,2048,1024]{2,1,0:T(8,128)(2,1)} %up.3, bf16[8,1024,2048]{2,1,0:T(8,128)(2,1)} %down.3), custom_call_target="tpu_custom_call" | custom-call | flops 2147483648 | bytes 33554432 | tf_op jit(solution)/shard_map/pallas_call | solution.py:308
  107.0 0.0 all-to-all-done.1
  107.0 26.9 %all_to_all.44 = bf16[8,24,2176]{2,1,0:T(8,128)(2,1)S(1)} all-to-all(bf16[8,24,2176]{2,1,0:T(8,128)(2,1)S(1)} %bitcast.22), channel_id=1, replica_groups=mesh['section'=4,'expert'=8] {'expert'}, dimensions={0} | all-to-all | bytes 1671168 | tf_op jit(solution)/shard_map/all_to_all | solution.py:51
  133.9 0.0 copy-done.1
  134.0 0.0 copy-done.3
  134.0 0.0 copy-done.18
  134.0 0.0 copy-start.9
  134.0 0.9 copy-done.9
  134.9 0.9 copy-done.11
  135.9 0.9 copy-done.15
  136.8 0.8 copy-done.20
  137.6 0.8 copy-done.22
  138.5 0.8 copy-done.24
  139.3 1.9 %shard_map.162 = (bf16[1,64,2048]{2,1,0:T(8,128)(2,1)}, bf16[1,64,2048]{2,1,0:T(8,128)(2,1)}) custom-call(bf16[64,2048]{1,0:T(8,128)(2,1)S(1)} %copy-done.9, bf16[64,2048]{1,0:T(8,128)(2,1)S(1)} %bitcast.28, bf16[64,2048]{1,0:T(8,128)(2,1)S(1)} %copy-done.11, bf16[1,2048]{1,0:T(2,128)(2,1)S(1)} %copy-done.18, bf16[64,2048]{1,0:T(8,128)(2,1)S(1)} %bitcast.30, ...), custom_call_target="tpu_custom_call" | custom-call | flops 201326592 | bytes 2883584 | tf_op jit(solution)/shard_map/pallas_call | solution.py:332
  (11 shorter events, 0.1 us)
Async XLA Ops:
  0.6 10.7 %collective-permute-start = (bf16[64,2048]{1,0:T(8,128)(2,1)}, bf16[64,2048]{1,0:T(8,128)(2,1)S(1)}, u32[]{:S(2)}, u32[]{:S(2)}) collective-permute-start(bf16[64,2048]{1,0:T(8,128)(2,1)} %bitcast.34), channel_id=1, source_target_pairs={{0,8},{8,16},{16,24},{1,9},{9,17},{17,25},{2,10},{10,18},{18,26},{... | collective-permute-start | bytes 786440 | tf_op jit(solution)/shard_map/ppermute | solution.py:47
  5.5 13.3 %collective-permute-start.1 = (bf16[64,2048]{1,0:T(8,128)(2,1)}, bf16[64,2048]{1,0:T(8,128)(2,1)S(1)}, u32[]{:S(2)}, u32[]{:S(2)}) collective-permute-start(bf16[64,2048]{1,0:T(8,128)(2,1)} %bitcast.35), channel_id=1, source_target_pairs={{8,0},{16,8},{24,16},{9,1},{17,9},{25,17},{10,2},{18,10},{26,18},{... | collective-permute-start | bytes 786440 | tf_op jit(solution)/shard_map/ppermute | solution.py:47
  18.8 1.0 copy-start.12
  19.8 0.9 copy-start.13
  20.7 0.7 copy-start.16
  21.4 0.7 copy-start.25
  24.3 0.7 copy-start.8
  25.0 0.7 copy-start.10
  25.7 25.9 %all-to-all-start = ((bf16[8,24,2048]{2,1,0:T(8,128)(2,1)}), bf16[8,24,2048]{2,1,0:T(8,128)(2,1)S(1)}, u32[]{:S(2)}, u32[]{:S(2)}) async-start(bf16[8,24,2048]{2,1,0:T(8,128)(2,1)} %bitcast.9), calls=%async_computation | async-start | bytes 1572864 | tf_op jit(solution)/shard_map/all_to_all | solution.py:51
  30.6 0.9 copy-start
  31.6 0.9 copy-start.2
  32.5 0.7 copy-start.17
  33.2 0.7 copy-start.26
  35.6 0.6 copy-start.14
  36.3 0.6 copy-start.19
  36.9 0.6 copy-start.21
  37.5 0.6 copy-start.23
  51.6 28.0 %all-to-all-start.2 = ((bf16[8,24,2048]{2,1,0:T(8,128)(2,1)}), bf16[8,24,2048]{2,1,0:T(8,128)(2,1)S(1)}, u32[]{:S(2)}, u32[]{:S(2)}) async-start(bf16[8,24,2048]{2,1,0:T(8,128)(2,1)} %bitcast.16), calls=%async_computation.2 | async-start | bytes 1572864 | tf_op jit(solution)/shard_map/all_to_all | solution.py:51
  56.4 0.9 copy-start.4
  57.3 0.9 copy-start.6
  79.6 27.4 %all-to-all-start.1 = ((bf16[8,24,2176]{2,1,0:T(8,128)(2,1)}), bf16[8,24,2176]{2,1,0:T(8,128)(2,1)S(1)}, u32[]{:S(2)}, u32[]{:S(2)}) async-start(bf16[8,24,2176]{2,1,0:T(8,128)(2,1)} %bitcast.14), calls=%async_computation.1 | async-start | bytes 1671168 | tf_op jit(solution)/shard_map/all_to_all | solution.py:51
  84.6 0.9 copy-start.5
  85.5 0.9 copy-start.7
  86.4 47.5 %copy-start.1 = (bf16[1,64,2048]{2,1,0:T(8,128)(2,1)S(1)}, bf16[1,64,2048]{2,1,0:T(8,128)(2,1)}, u32[]{:S(2)}) copy-start(bf16[1,64,2048]{2,1,0:T(8,128)(2,1)} %param.20) | copy-start | bytes 786436
  86.4 47.5 %copy-start.3 = (bf16[1,2048,64]{1,2,0:T(8,128)(2,1)S(1)}, bf16[1,2048,64]{1,2,0:T(8,128)(2,1)}, u32[]{:S(2)}) copy-start(bf16[1,2048,64]{1,2,0:T(8,128)(2,1)} %param.24) | copy-start | bytes 786436
  86.4 47.5 %copy-start.18 = (bf16[1,2048]{1,0:T(2,128)(2,1)S(1)}, bf16[1,2048]{1,0:T(2,128)(2,1)}, u32[]{:S(2)}) copy-start(bf16[1,2048]{1,0:T(2,128)(2,1)} %gain.5) | copy-start | bytes 12292
  134.0 1.0 copy-start.9
  134.9 0.9 copy-start.11
  135.9 0.9 copy-start.15
  136.8 0.8 copy-start.20
  137.6 0.8 copy-start.22
  138.4 0.8 copy-start.24

commit v4 on v3

v4 whole, which is shorter than its diff:
```python
import functools

import jax
import jax.numpy as jnp
import numpy as np
from jax import lax
from jax.experimental import pallas as pl
from jax.experimental.pallas import tpu as pltpu
from jax.sharding import PartitionSpec as P

EPS = 1e-06
BF16 = jnp.bfloat16
F32 = jnp.float32
LANES = 128
ROWS = 16
VMEM_LIMIT = 60 * 1024 * 1024
NT = (((1,), (1,)), ((), ()))
TN = (((0,), (0,)), ((), ()))


def dot(a, b, dims=(((1,), (0,)), ((), ()))):
    return lax.dot_general(a, b, dims, preferred_element_type=F32)


def call(kernel, out_shape, cost, **kwargs):
    flops, moved = cost
    return pl.pallas_call(
        kernel,
        out_shape=out_shape,
        compiler_params=pltpu.CompilerParams(vmem_limit_bytes=VMEM_LIMIT),
        cost_estimate=pl.CostEstimate(flops=flops, bytes_accessed=moved, transcendentals=0),
        **kwargs,
    )


def full_spec(shape):
    return pl.BlockSpec(shape, lambda *_: (0,) * len(shape))


SMEM = pl.BlockSpec(memory_space=pltpu.SMEM)
VMEM = pl.BlockSpec(memory_space=pltpu.VMEM)


def from_behind(block, axis, distance):
    devices = range(lax.axis_size(axis))
    route = [(i - distance, i) for i in devices if i - distance in devices]
    return lax.ppermute(block, axis, route)


def exchange(blocks, direction):
    size = lax.axis_size("expert")
    if len(blocks) == 1:
        return [lax.all_to_all(blocks[0], "expert", split_axis=0, concat_axis=0, tiled=True)]
    got = list(blocks)
    for d in sorted(range(1, size), key=lambda d: abs(2 * d - size)):
        route = [(i, (i + direction * d) % size) for i in range(size)]
        got[d] = lax.ppermute(blocks[d], "expert", route)
    return got


def joined(refs):
    if len(refs) == 1:
        return refs[0][...]
    return jnp.concatenate([ref[...].astype(F32) for ref in refs], axis=0).astype(BF16)


def parted(value, refs):
    share = value.shape[0] // len(refs)
    for d, ref in enumerate(refs):
        ref[...] = value[d * share : (d + 1) * share].astype(BF16)


def partners(me, distance, sources, direction, turned):
    if not turned:
        return distance
    device = me + direction * distance
    return jnp.where(device < 0, device + sources, jnp.where(device >= sources, device - sources, device))


def expert_hits(routes, experts):
    top, count = routes.shape
    lane = lax.broadcasted_iota(jnp.int32, (experts, count), 0)
    return [(routes[k : k + 1, :] == lane).astype(F32) for k in range(top)]


def slot_targets(routes, experts, capacity):
    top, count = routes.shape
    hits = expert_hits(routes, experts)
    earlier = lax.broadcasted_iota(jnp.int32, (count, count), 0) < lax.broadcasted_iota(
        jnp.int32, (count, count), 1
    )
    before = dot(sum(hits).astype(BF16), earlier.astype(F32).astype(BF16))
    targets = []
    for k in range(top):
        ranked = jnp.sum((before + sum(hits[:k], jnp.zeros_like(before))) * hits[k], 0, keepdims=True)
        targets.append(routes[k : k + 1, :] * capacity + ranked.astype(jnp.int32))
    return targets, hits


def tables_of(targets, row_keys):
    return [(row_keys == target).astype(F32) for target in targets]


def normalise(tokens, gain):
    widened = tokens.astype(F32)
    inv_rms = lax.rsqrt(jnp.mean(widened * widened, axis=-1, keepdims=True) + EPS)
    return widened, inv_rms, (widened * inv_rms * gain.astype(F32)).astype(BF16)


def route_shares(normed, router, hits):
    logits = dot(router, normed, NT)
    exponents = [jnp.exp(jnp.sum(logits * hit, axis=0, keepdims=True)) for hit in hits]
    total = sum(exponents)
    return [exponent / total for exponent in exponents]


def keys_of_part(sizes, me, columns, part):
    device = partners(me, columns[:, 0:1], sizes["sources"], 1, sizes["turned"])
    return columns[:, 2 + part : 3 + part] + device * sizes["share"]


def first_send_kernel(
    sizes, place, arrived_f, arrived_b, embedded, loss, gain, routes_f, routes_b,
    columns, tokens, upstream, data, *send,
):
    experts, capacity = sizes["experts"], sizes["capacity"]
    count = embedded.shape[0]
    chosen = jnp.where(place[0] == 0, embedded[...], arrived_f[...])
    tokens[...] = chosen
    data[:count, :] = normalise(chosen, gain[...])[2]
    chosen = jnp.where(place[0] == place[1], loss[...], arrived_b[...])
    upstream[...] = chosen
    data[count:, :] = chosen
    targets_f, _ = slot_targets(routes_f[...], experts, capacity)
    targets_b, _ = slot_targets(routes_b[...], experts, capacity)
    keys = keys_of_part(sizes, place[2], columns, 0)
    table_f = sum(tables_of(targets_f, keys))
    table_b = sum(tables_of([t + experts * capacity for t in targets_b], keys))
    table = jnp.concatenate([table_f, table_b], axis=1).astype(BF16)
    parted(dot(table, data[...]), send)


def mixing_kernel(
    sizes, place, data, saved, gain, router, routes_f, routes_b, columns,
    mixing_f, mixing_b, tables_b, shares_b, *sends,
):
    experts, capacity = sizes["experts"], sizes["capacity"]
    count = saved.shape[0]
    targets_f, hits = slot_targets(routes_f[...], experts, capacity)
    shares_f = route_shares(data[:count, :], router[...], hits)
    targets_b, hits = slot_targets(routes_b[...], experts, capacity)
    targets_b = [t + experts * capacity for t in targets_b]
    _, _, rows = normalise(saved[...], gain[...])
    own_shares = route_shares(rows, router[...], hits)
    for k, share in enumerate(own_shares):
        shares_b[k] = jnp.broadcast_to(share, shares_b.shape[1:])
    parts = mixing_f.shape[0]
    for part in range(parts):
        keys = keys_of_part(sizes, place[2], columns, part)
        found_f, found_b = tables_of(targets_f, keys), tables_of(targets_b, keys)
        mixing_f[part] = sum(t * s.astype(BF16).astype(F32) for t, s in zip(found_f, shares_f))
        mixing_b[part] = sum(t * s.astype(BF16).astype(F32) for t, s in zip(found_b, own_shares))
        for k, table in enumerate(found_b):
            tables_b[part, k] = table
        if part > 0:
            blocks = len(sends) // (parts - 1)
            table = jnp.concatenate([sum(found_f), sum(found_b)], axis=1).astype(BF16)
            parted(dot(table, data[...]), sends[(part - 1) * blocks : part * blocks])


def expert_kernel(sizes, steps, blocks, place, columns, lanes, wanted, wanted_lanes, *refs):
    got, (saved_pre, up, down) = refs[:blocks], refs[blocks : blocks + 3]
    out = refs[blocks + 3 : 2 * blocks + 3]
    rows, total_f, total_b, inner, results = refs[2 * blocks + 3 :]
    expert, step = pl.program_id(0), pl.program_id(1)
    held = pl.num_programs(0)
    width = rows.shape[1]
    padded, block_rows = sizes["padded"], sizes["block_rows"]
    source = (sizes["sources"], -1, sizes["turned"])

    @pl.when((expert == 0) & (step == 0))
    def _():
        have = partners(place[2], lanes[0:1, :], *source) * block_rows + lanes[1:2, :]
        order = (wanted[...] == have).astype(F32).astype(BF16)
        rows[...] = dot(order, joined(got)).astype(BF16)
        results[:, width:] = jnp.zeros((results.shape[0], results.shape[1] - width), BF16)

    own_f = pl.ds(pl.multiple_of(expert * padded, ROWS), padded)
    own_b = pl.ds(pl.multiple_of((held + expert) * padded, ROWS), padded)
    pre_act = dot(rows[own_f, :], up[0])
    hidden_grad = dot(rows[own_b, :], down[0], NT)
    hidden = (pre_act / (1.0 + jnp.exp(-pre_act))).astype(BF16)
    pre = saved_pre[0].astype(F32)
    gate = 1.0 / (1.0 + jnp.exp(-pre))
    inner_part = jnp.sum(hidden_grad * (pre * gate).astype(BF16).astype(F32), axis=1, keepdims=True)
    pre_grad = (hidden_grad * gate * (1.0 + pre * (1.0 - gate))).astype(BF16)
    part_f = dot(hidden, down[0])
    part_b = dot(pre_grad, up[0], NT)

    @pl.when(step == 0)
    def _():
        total_f[...] = part_f
        total_b[...] = part_b
        inner[...] = jnp.broadcast_to(inner_part, inner.shape)

    @pl.when(step > 0)
    def _():
        total_f[...] += part_f
        total_b[...] += part_b
        inner[...] += jnp.broadcast_to(inner_part, inner.shape)

    @pl.when(step == steps - 1)
    def _():
        results[own_f, :width] = total_f[...].astype(BF16)
        results[own_b, :width] = total_b[...].astype(BF16)
        results[own_b, width:] = inner[...].astype(BF16)

    @pl.when((expert == held - 1) & (step == steps - 1))
    def _():
        have = partners(place[2], columns[:, 0:1], *source) * block_rows + columns[:, 1:2]
        order = (have == wanted_lanes[...]).astype(F32).astype(BF16)
        parted(dot(order, results[...]), out)


def combine_kernel(
    experts, tokens, saved, upstream, gain, router, routes, mixing_f, mixing_b, tables, shares, *refs
):
    *backs, output, gradient = refs
    width = tokens.shape[1]
    parts = range(mixing_f.shape[0])
    blocks = len(backs) // len(parts)
    back = [joined(backs[p * blocks : (p + 1) * blocks]) for p in parts]
    widened = saved[...].astype(F32)
    inv_rms = lax.rsqrt(jnp.mean(widened * widened, axis=-1, keepdims=True) + EPS)
    hits = expert_hits(routes[...], experts)
    top = len(hits)
    share = [shares[k][:1, :] for k in range(top)]
    sums = [back[p][:, width:].astype(F32)[:, :1] for p in parts]
    inner = [
        sum(jnp.sum(tables[p, k] * sums[p], axis=0, keepdims=True) for p in parts)
        for k in range(top)
    ]
    mean = sum(share[k] * inner[k] for k in range(top))
    logit_grad = sum(share[k] * (inner[k] - mean) * hits[k] for k in range(top))
    high = logit_grad.astype(BF16)
    rest = logit_grad - high.astype(F32)
    middle = rest.astype(BF16)
    low = (rest - middle.astype(F32)).astype(BF16)
    output[0] = (
        tokens[...].astype(F32)
        + sum(dot(mixing_f[p].astype(BF16), back[p][:, :width], TN) for p in parts)
    ).astype(BF16)
    normed_grad = sum(dot(mixing_b[p].astype(BF16), back[p][:, :width], TN) for p in parts)
    for piece in (high, middle, low):
        normed_grad += dot(piece, router[...], TN)
    gained = normed_grad * gain[...].astype(F32)
    projected = jnp.mean(widened * gained, axis=-1, keepdims=True)
    grad = inv_rms * gained - widened * (inv_rms * inv_rms * inv_rms * projected)
    gradient[0] = (upstream[...].astype(F32) + grad).astype(BF16)


def exchange_order(parts, sources, local, capacity, padded):
    held = local // parts
    slots = sources * local * capacity
    block_rows = 2 * held * capacity
    columns = np.zeros((sources * block_rows, 2 + parts), np.int32)
    wanted = np.full((2 * held * padded, 1), -1, np.int32)
    for source in range(sources):
        for batch in range(2):
            for expert in range(held):
                for slot in range(capacity):
                    within = (batch * held + expert) * capacity + slot
                    row = source * block_rows + within
                    columns[row, :2] = source, within
                    for part in range(parts):
                        own = (part * held + expert) * capacity + slot
                        columns[row, 2 + part] = batch * slots + own
                    wanted[(batch * held + expert) * padded + source * capacity + slot] = row
    return columns, wanted


def on_device(
    forward_sent,
    embedded,
    forward_routes,
    backward_sent,
    loss_gradient,
    saved_inputs,
    backward_routes,
    pre_activation,
    norm_gain,
    router,
    up_weight,
    down_weight,
):
    section = lax.axis_index("section")
    last = lax.axis_size("section") - 1
    sources = lax.axis_size("expert")
    experts = router.shape[2]
    capacity = pre_activation.shape[3]
    local, width, hidden = up_weight.shape
    count = embedded.shape[0]
    top = forward_routes.shape[2]
    slots = experts * capacity
    rows = sources * capacity
    padded = -(-rows // ROWS) * ROWS
    steps = 2
    chunk = hidden // steps
    shape = jax.ShapeDtypeStruct
    parts = 2 if local % 2 == 0 else 1
    held = local // parts
    moved = 2 * slots // parts
    turned = sources <= 8
    blocks = sources if turned else 1
    columns, wanted = exchange_order(parts, sources, local, capacity, padded)
    lanes, wanted_lanes = np.ascontiguousarray(columns.T), np.ascontiguousarray(wanted.T)
    sizes = {
        "experts": experts,
        "capacity": capacity,
        "sources": sources,
        "share": local * capacity,
        "turned": turned,
        "padded": padded,
        "block_rows": moved // sources,
    }
    place = jnp.stack([section, jnp.full_like(section, last), lax.axis_index("expert")])
    place = place.astype(jnp.int32)
    sent = (shape((moved // blocks, width), BF16),) * blocks
    result = (shape((moved // blocks, width + LANES), BF16),) * blocks

    router_t = router[0].T
    routes_f, routes_b = forward_routes[0].T, backward_routes[0].T
    arrived_f = from_behind(forward_sent[0], "section", 1)
    arrived_b = from_behind(backward_sent[0], "section", -1)
    tokens, upstream, data, *send = call(
        functools.partial(first_send_kernel, sizes),
        (
            shape((count, width), BF16),
            shape((count, width), BF16),
            shape((2 * count, width), BF16),
            *sent,
        ),
        (4 * moved * count * width, 2 * (8 * count + moved) * width),
        in_specs=[SMEM] + [VMEM] * 8,
    )(
        place, arrived_f, arrived_b, embedded, loss_gradient, norm_gain, routes_f, routes_b, columns
    )
    mixing_f, mixing_b, tables_b, shares_b, *sends = call(
        functools.partial(mixing_kernel, sizes),
        (
            shape((parts, moved, count), F32),
            shape((parts, moved, count), F32),
            shape((parts, top, moved, count), F32),
            shape((top, 8, count), F32),
            *(sent * (parts - 1)),
        ),
        (4 * moved * count * width, 2 * (4 * count + moved) * width),
        in_specs=[SMEM] + [VMEM] * 7,
    )(place, data, saved_inputs[0], norm_gain, router_t, routes_f, routes_b, columns)
    saved_pre = jnp.transpose(pre_activation[0], (1, 0, 2, 3)).reshape(local, rows, hidden)
    saved_pre = jnp.pad(saved_pre, ((0, 0), (0, padded - rows), (0, 0)))
    sends, saved_pre = lax.optimization_barrier((sends, saved_pre))

    sends = [send] + [sends[p * blocks : (p + 1) * blocks] for p in range(parts - 1)]
    received = [exchange(blocks_out, 1) for blocks_out in sends]
    backs = []
    for part, got in enumerate(received):
        done = call(
            functools.partial(expert_kernel, sizes, steps, blocks),
            result,
            (8 * held * padded * width * hidden, 4 * held * width * hidden),
            grid=(held, steps),
            in_specs=[
                SMEM,
                full_spec(columns.shape),
                full_spec(lanes.shape),
                full_spec(wanted.shape),
                full_spec(wanted_lanes.shape),
                *[full_spec(block.shape) for block in got],
                pl.BlockSpec((1, padded, chunk), lambda e, f, p=part: (p * held + e, 0, f)),
                pl.BlockSpec((1, width, chunk), lambda e, f, p=part: (p * held + e, 0, f)),
                pl.BlockSpec((1, chunk, width), lambda e, f, p=part: (p * held + e, f, 0)),
            ],
            out_specs=tuple(full_spec(block.shape) for block in result),
            scratch_shapes=[
                pltpu.VMEM((2 * held * padded, width), BF16),
                pltpu.VMEM((padded, width), F32),
                pltpu.VMEM((padded, width), F32),
                pltpu.VMEM((padded, LANES), F32),
                pltpu.VMEM((2 * held * padded, width + LANES), BF16),
            ],
        )(place, columns, lanes, wanted, wanted_lanes, *got, saved_pre, up_weight, down_weight)
        backs += exchange(list(done), -1)
    return tuple(
        call(
            functools.partial(combine_kernel, experts),
            (shape((1, count, width), BF16),) * 2,
            (8 * moved * count * width, 2 * (5 * count + 2 * moved) * width),
        )(
            tokens, saved_inputs[0], upstream, norm_gain, router_t, routes_b,
            mixing_f, mixing_b, tables_b, shares_b, *backs,
        )
    )


def solution(mesh):
    return jax.shard_map(
        on_device,
        mesh=mesh,
        in_specs=(
            P("section", "expert", None),
            P("expert", None),
            P("section", "expert", None),
            P("section", "expert", None),
            P("expert", None),
            P("section", "expert", None),
            P("section", "expert", None),
            P("section", None, "expert", None, None),
            P("section", None),
            P("section", None, None),
            P("expert", None, None),
            P("expert", None, None),
        ),
        out_specs=(P("section", "expert", None), P("section", "expert", None)),
        check_vma=False,
    )
```

time: 142 us -> 134 us (0.944)
  blocking collectives: 26.9 us -> 0 us
  starting transfers between devices: 19.6 us -> 37.9 us
  local copies, waits for them, and re-layouts: 22.2 us -> 4.07 us
  waiting for transfers between devices: 23.8 us -> 35.3 us
  Pallas kernels: 47.8 us -> 55.1 us
    ppermute x0 -> x28, starting transfers between devices: none -> 31.7 us  [exchange(): got[d] = lax.ppermute(blocks[d], 'expert', route)]
    all_to_all x1 -> x0, blocking collectives: 26.9 us -> none  [exchange(): lax.all_to_all(rows, 'expert', split_axis=0, concat_axis=0, tiled=True)]
    ppermute x0 -> x28, waiting for transfers between devices: none -> 26 us  [exchange(): got[d] = lax.ppermute(blocks[d], 'expert', route)]
    unnamed x54 -> x64, local copies, waits for them, and re-layouts: 19.4 us -> 1.99 us
    all_to_all x3 -> x0, starting transfers between devices: 13.5 us -> none  [exchange(): lax.all_to_all(rows, 'expert', split_axis=0, concat_axis=0, tiled=True)]
    all_to_all x3 -> x0, waiting for transfers between devices: 13.5 us -> none  [exchange(): lax.all_to_all(rows, 'expert', split_axis=0, concat_axis=0, tiled=True)]
    pallas_call x4, Pallas kernels: 45.9 us -> 51.2 us  [the longest x2 45.5 us: on_device(): call(functools.partial(expert_kernel, sizes, steps, blocks), result, (8 *...]
    pallas_call x1, Pallas kernels: 1.86 us -> 3.85 us  [on_device(): call(functools.partial(combine_kernel, experts), (shape((1, count, width)...]
  transfers between devices with their start and end apart: 5 -> 30, of which waited for: 3 -> 10; matrix products, arithmetic and copies ran while one was open for 2% -> 2% of each run, Pallas kernels for 31% -> 36%
where the time goes in v4:
time: 134 us
  Pallas kernels  55.1 us (41%)
  starting transfers between devices  37.9 us (28%)
  waiting for transfers between devices  35.3 us (26%)
  local copies, waits for them, and re-layouts  4.07 us (3%)
    pallas_call x2, Pallas kernels, on_device(): call(functools.partial(expert_kernel, sizes, steps, blocks), result, (8 *...  45.5 us
    ppermute x28, starting transfers between devices, exchange(): got[d] = lax.ppermute(blocks[d], 'expert', route)  31.7 us
    ppermute x28, waiting for transfers between devices, exchange(): got[d] = lax.ppermute(blocks[d], 'expert', route)  26 us
    ppermute x2, waiting for transfers between devices, from_behind(): return lax.ppermute(block, axis, route)  9.31 us
    ppermute x2, starting transfers between devices, from_behind(): return lax.ppermute(block, axis, route)  6.15 us
    pallas_call x1, Pallas kernels, on_device(): call(functools.partial(combine_kernel, experts), (shape((1, count, width)...  3.85 us
    pallas_call x1, Pallas kernels, on_device(): call(functools.partial(mixing_kernel, sizes), (shape((parts, moved, count...  2.93 us
    pallas_call x1, Pallas kernels, on_device(): call(functools.partial(first_send_kernel, sizes), (shape((count, width),...  2.82 us
  transfers between devices with their start and end apart: 30, of which 10 were waited for; matrix products, arithmetic and copies ran while one was open for 2% of the time, Pallas kernels for 36%

profile of v4, /device:TPU:0, one launch (start us, length us, event | category | flops | bytes accessed | tf_op | source)
XLA Modules:
  0.0 134.0 jit_solution(9808930526438953203)
XLA Ops:
  0.6 4.9 %collective-permute-start = (bf16[64,2048]{1,0:T(8,128)(2,1)}, bf16[64,2048]{1,0:T(8,128)(2,1)S(1)}, u32[]{:S(2)}, u32[]{:S(2)}) collective-permute-start(bf16[64,2048]{1,0:T(8,128)(2,1)} %bitcast.29), channel_id=1, source_target_pairs={{0,8},{8,16},{16,24},{1,9},{9,17},{17,25},{2,10},{10,18},{18,26},{... | collective-permute-start | bytes 786440 | tf_op jit(solution)/shard_map/ppermute | solution.py:47
  5.5 1.3 collective-permute-start.1
  6.8 1.2 copy.19
  8.0 0.9 pad.4.refs_8_
  8.9 0.6 pad_add_fusion.place
  9.5 1.9 %collective-permute-done.arrived_f = bf16[64,2048]{1,0:T(8,128)(2,1)S(1)} collective-permute-done((bf16[64,2048]{1,0:T(8,128)(2,1)}, bf16[64,2048]{1,0:T(8,128)(2,1)S(1)}, u32[]{:S(2)}, u32[]{:S(2)}) %collective-permute-start) | collective-permute-done | bytes 262176 | tf_op jit(solution)/shard_map/ppermute | solution.py:47
  11.3 7.5 %collective-permute-done.1.arrived_b = bf16[64,2048]{1,0:T(8,128)(2,1)S(1)} collective-permute-done((bf16[64,2048]{1,0:T(8,128)(2,1)}, bf16[64,2048]{1,0:T(8,128)(2,1)S(1)}, u32[]{:S(2)}, u32[]{:S(2)}) %collective-permute-start.1) | collective-permute-done | bytes 262176 | tf_op jit(solution)/shard_map/ppermute | solution.py:47
  18.8 0.7 copy-done.1
  19.5 2.8 %shard_map.167 = (bf16[64,2048]{1,0:T(8,128)(2,1)}, bf16[64,2048]{1,0:T(8,128)(2,1)}, bf16[128,2048]{1,0:T(8,128)(2,1)}, bf16[24,2048]{1,0:T(8,128)(2,1)}, bf16[...) custom-call(s32[3]{0:T(128)} %pad_add_fusion.place, ...), custom_call_target="tpu_custom_call" | custom-call | flops 100663296 | bytes 2883584 | tf_op jit(solution)/shard_map/pallas_call | solution.py:335
  22.3 0.0 collective-permute-start.2
  22.3 1.6 %collective-permute-start.3 = (bf16[24,2048]{1,0:T(8,128)(2,1)}, bf16[24,2048]{1,0:T(8,128)(2,1)S(1)}, u32[]{:S(2)}, u32[]{:S(2)}) collective-permute-start(bf16[24,2048]{1,0:T(8,128)(2,1)} %get-tuple-element.59), channel_id=1, source_target_pairs={{0,2},{1,3},{2,4},{3,5},{4,6},{5,7},{6,0},{7,1},{8,10},{9,11},{10,... | collective-permute-start | bytes 294920 | tf_op jit(solution)/shard_map/ppermute | solution.py:57
  24.0 2.9 %shard_map.168 = (f32[2,192,64]{2,1,0:T(8,128)}, f32[2,192,64]{2,1,0:T(8,128)}, f32[2,2,192,64]{3,2,1,0:T(8,128)}, f32[2,8,64]{2,1,0:T(8,128)}, bf16[24,2048]{1,...) custom-call(s32[3]{0:T(128)} %pad_add_fusion.place, ...), custom_call_target="tpu_custom_call" | custom-call | flops 100663296 | bytes 1835008 | tf_op jit(solution)/shard_map/pallas_call | solution.py:348
  26.9 1.4 %collective-permute-start.16 = (bf16[24,2048]{1,0:T(8,128)(2,1)}, bf16[24,2048]{1,0:T(8,128)(2,1)S(1)}, u32[]{:S(2)}, u32[]{:S(2)}) collective-permute-start(bf16[24,2048]{1,0:T(8,128)(2,1)} %get-tuple-element.83), channel_id=1, source_target_pairs={{0,1},{1,2},{2,3},{3,4},{4,5},{5,6},{6,7},{7,0},{8,9},{9,10},{10,1... | collective-permute-start | bytes 294920 | tf_op jit(solution)/shard_map/ppermute | solution.py:57
  28.2 1.6 %collective-permute-start.17 = (bf16[24,2048]{1,0:T(8,128)(2,1)}, bf16[24,2048]{1,0:T(8,128)(2,1)S(1)}, u32[]{:S(2)}, u32[]{:S(2)}) collective-permute-start(bf16[24,2048]{1,0:T(8,128)(2,1)} %get-tuple-element.84), channel_id=1, source_target_pairs={{0,2},{1,3},{2,4},{3,5},{4,6},{5,7},{6,0},{7,1},{8,10},{9,11},{10,... | collective-permute-start | bytes 294920 | tf_op jit(solution)/shard_map/ppermute | solution.py:57
  29.8 0.0 collective-permute-start.18
  29.8 0.0 collective-permute-done.2.refs_1_
  29.8 2.5 %collective-permute-start.19 = (bf16[24,2048]{1,0:T(8,128)(2,1)}, bf16[24,2048]{1,0:T(8,128)(2,1)S(1)}, u32[]{:S(2)}, u32[]{:S(2)}) collective-permute-start(bf16[24,2048]{1,0:T(8,128)(2,1)} %get-tuple-element.86), channel_id=1, source_target_pairs={{0,4},{1,5},{2,6},{3,7},{4,0},{5,1},{6,2},{7,3},{8,12},{9,13},{10,... | collective-permute-start | bytes 294920 | tf_op jit(solution)/shard_map/ppermute | solution.py:57
  32.3 0.0 collective-permute-done.3.refs_2_
  32.3 1.1 collective-permute-start.20
  33.4 0.0 collective-permute-done.16.refs_1_
  33.4 1.4 %collective-permute-start.21 = (bf16[24,2048]{1,0:T(8,128)(2,1)}, bf16[24,2048]{1,0:T(8,128)(2,1)S(1)}, u32[]{:S(2)}, u32[]{:S(2)}) collective-permute-start(bf16[24,2048]{1,0:T(8,128)(2,1)} %get-tuple-element.88), channel_id=1, source_target_pairs={{0,6},{1,7},{2,0},{3,1},{4,2},{5,3},{6,4},{7,5},{8,14},{9,15},{10,... | collective-permute-start | bytes 294920 | tf_op jit(solution)/shard_map/ppermute | solution.py:57
  34.9 1.1 collective-permute-done.17.refs_2_
  36.0 0.3 collective-permute-start.22
  36.3 6.4 %collective-permute-done.18.refs_3_ = bf16[24,2048]{1,0:T(8,128)(2,1)S(1)} collective-permute-done((bf16[24,2048]{1,0:T(8,128)(2,1)}, bf16[24,2048]{1,0:T(8,128)(2,1)S(1)}, u32[]{:S(2)}, u32[]{:S(2)}) %collective-permute-start.18) | collective-permute-done | bytes 98336 | tf_op jit(solution)/shard_map/ppermute | solution.py:57
  42.7 3.1 %collective-permute-start.4 = (bf16[24,2048]{1,0:T(8,128)(2,1)}, bf16[24,2048]{1,0:T(8,128)(2,1)S(1)}, u32[]{:S(2)}, u32[]{:S(2)}) collective-permute-start(bf16[24,2048]{1,0:T(8,128)(2,1)} %get-tuple-element.60), channel_id=1, source_target_pairs={{0,3},{1,4},{2,5},{3,6},{4,7},{5,0},{6,1},{7,2},{8,11},{9,12},{10,... | collective-permute-start | bytes 294920 | tf_op jit(solution)/shard_map/ppermute | solution.py:57
  45.8 0.0 collective-permute-done.19.refs_4_
  45.8 0.0 collective-permute-start.5
  45.8 0.0 collective-permute-done.20.refs_5_
  45.8 2.0 %collective-permute-start.6 = (bf16[24,2048]{1,0:T(8,128)(2,1)}, bf16[24,2048]{1,0:T(8,128)(2,1)S(1)}, u32[]{:S(2)}, u32[]{:S(2)}) collective-permute-start(bf16[24,2048]{1,0:T(8,128)(2,1)} %get-tuple-element.62), channel_id=1, source_target_pairs={{0,5},{1,6},{2,7},{3,0},{4,1},{5,2},{6,3},{7,4},{8,13},{9,14},{10,... | collective-permute-start | bytes 294920 | tf_op jit(solution)/shard_map/ppermute | solution.py:57
  47.9 0.0 collective-permute-done.21.refs_6_
  47.9 5.1 %collective-permute-start.7 = (bf16[24,2048]{1,0:T(8,128)(2,1)}, bf16[24,2048]{1,0:T(8,128)(2,1)S(1)}, u32[]{:S(2)}, u32[]{:S(2)}) collective-permute-start(bf16[24,2048]{1,0:T(8,128)(2,1)} %get-tuple-element.63), channel_id=1, source_target_pairs={{0,6},{1,7},{2,0},{3,1},{4,2},{5,3},{6,4},{7,5},{8,14},{9,15},{10,... | collective-permute-start | bytes 294920 | tf_op jit(solution)/shard_map/ppermute | solution.py:57
  53.0 0.0 collective-permute-start.8
  53.1 0.6 copy-done.29
  53.6 22.8 %shard_map.170 = (bf16[24,2176]{1,0:T(8,128)(2,1)}, bf16[24,2176]{1,0:T(8,128)(2,1)}, bf16[24,2176]{1,0:T(8,128)(2,1)}, bf16[24,2176]{1,0:T(8,128)(2,1)}, bf16[2...) custom-call(s32[3]{0:T(128)} %pad_add_fusion.place, ...), custom_call_target="tpu_custom_call" | custom-call | flops 2147483648 | bytes 33554432 | tf_op jit(solution)/shard_map/pallas_call | solution.py:368
  76.4 0.1 collective-permute-start.23
  76.5 0.0 collective-permute-done.5.refs_4_
  76.5 1.2 collective-permute-start.24
  77.7 0.0 collective-permute-start.25
  77.7 1.9 %collective-permute-start.26 = (bf16[24,2176]{1,0:T(8,128)(2,1)}, bf16[24,2176]{1,0:T(8,128)(2,1)S(1)}, u32[]{:S(2)}, u32[]{:S(2)}) collective-permute-start(bf16[24,2176]{1,0:T(8,128)(2,1)} %get-tuple-element.94), channel_id=1, source_target_pairs={{0,4},{1,5},{2,6},{3,7},{4,0},{5,1},{6,2},{7,3},{8,12},{9,13},{10,... | collective-permute-start | bytes 313352 | tf_op jit(solution)/shard_map/ppermute | solution.py:57
  79.6 1.4 %collective-permute-start.27 = (bf16[24,2176]{1,0:T(8,128)(2,1)}, bf16[24,2176]{1,0:T(8,128)(2,1)S(1)}, u32[]{:S(2)}, u32[]{:S(2)}) collective-permute-start(bf16[24,2176]{1,0:T(8,128)(2,1)} %get-tuple-element.95), channel_id=1, source_target_pairs={{0,3},{1,4},{2,5},{3,6},{4,7},{5,0},{6,1},{7,2},{8,11},{9,12},{10,... | collective-permute-start | bytes 313352 | tf_op jit(solution)/shard_map/ppermute | solution.py:57
  81.0 22.7 %shard_map.169 = (bf16[24,2176]{1,0:T(8,128)(2,1)}, bf16[24,2176]{1,0:T(8,128)(2,1)}, bf16[24,2176]{1,0:T(8,128)(2,1)}, bf16[24,2176]{1,0:T(8,128)(2,1)}, bf16[2...) custom-call(s32[3]{0:T(128)} %pad_add_fusion.place, ...), custom_call_target="tpu_custom_call" | custom-call | flops 2147483648 | bytes 33554432 | tf_op jit(solution)/shard_map/pallas_call | solution.py:368
  103.8 0.0 collective-permute-done.23.refs_9_
  103.8 1.0 collective-permute-start.28
  104.8 0.1 collective-permute-start.29
  104.8 0.0 collective-permute-done.25.refs_11_
  104.8 3.5 %collective-permute-start.9 = (bf16[24,2176]{1,0:T(8,128)(2,1)}, bf16[24,2176]{1,0:T(8,128)(2,1)S(1)}, u32[]{:S(2)}, u32[]{:S(2)}) collective-permute-start(bf16[24,2176]{1,0:T(8,128)(2,1)} %get-tuple-element.75), channel_id=1, source_target_pairs={{0,7},{1,0},{2,1},{3,2},{4,3},{5,4},{6,5},{7,6},{8,15},{9,8},{10,9... | collective-permute-start | bytes 313352 | tf_op jit(solution)/shard_map/ppermute | solution.py:57
  108.3 0.0 collective-permute-done.26.refs_12_
  108.4 1.1 collective-permute-start.10
  109.5 1.8 %collective-permute-done.28.refs_14_ = bf16[24,2176]{1,0:T(8,128)(2,1)S(1)} collective-permute-done((bf16[24,2176]{1,0:T(8,128)(2,1)S(1)}, bf16[24,2176]{1,0:T(8,128)(2,1)S(1)}, u32[]{:S(2)}, u32[]{:S(2)}) %collective-permute-start.28) | collective-permute-done | bytes 104480 | tf_op jit(solution)/shard_map/ppermute | solution.py:57
  111.3 0.3 collective-permute-done.29.refs_15_
  111.6 0.0 collective-permute-start.13
  111.6 0.3 collective-permute-done.9.refs_1_
  111.9 1.4 %collective-permute-start.14 = (bf16[24,2176]{1,0:T(8,128)(2,1)}, bf16[24,2176]{1,0:T(8,128)(2,1)S(1)}, u32[]{:S(2)}, u32[]{:S(2)}) collective-permute-start(bf16[24,2176]{1,0:T(8,128)(2,1)} %get-tuple-element.80), channel_id=1, source_target_pairs={{0,2},{1,3},{2,4},{3,5},{4,6},{5,7},{6,0},{7,1},{8,10},{9,11},{10,... | collective-permute-start | bytes 313352 | tf_op jit(solution)/shard_map/ppermute | solution.py:57
  113.4 2.5 %collective-permute-done.10.refs_2_ = bf16[24,2176]{1,0:T(8,128)(2,1)S(1)} collective-permute-done((bf16[24,2176]{1,0:T(8,128)(2,1)}, bf16[24,2176]{1,0:T(8,128)(2,1)S(1)}, u32[]{:S(2)}, u32[]{:S(2)}) %collective-permute-start.10) | collective-permute-done | bytes 104480 | tf_op jit(solution)/shard_map/ppermute | solution.py:57
  115.9 0.0 collective-permute-start.15
  115.9 0.5 collective-permute-done.11.refs_3_
  116.4 12.9 %collective-permute-done.12.refs_4_ = bf16[24,2176]{1,0:T(8,128)(2,1)S(1)} collective-permute-done((bf16[24,2176]{1,0:T(8,128)(2,1)}, bf16[24,2176]{1,0:T(8,128)(2,1)S(1)}, u32[]{:S(2)}, u32[]{:S(2)}) %collective-permute-start.12) | collective-permute-done | bytes 104480 | tf_op jit(solution)/shard_map/ppermute | solution.py:57
  129.3 0.0 collective-permute-done.13.refs_5_
  129.4 0.0 collective-permute-done.15.refs_7_
  129.5 0.5 copy-done.12
  130.0 0.0 copy-done.13
  130.0 0.1 copy-done.14
  130.1 0.0 copy-done.15
  130.1 3.9 %shard_map.171 = (bf16[1,64,2048]{2,1,0:T(8,128)(2,1)}, bf16[1,64,2048]{2,1,0:T(8,128)(2,1)}) custom-call(bf16[64,2048]{1,0:T(8,128)(2,1)} %get-tuple-element.50.tokens, bf16[64,2048]{1,0:T(8,128)(2,1)} %bitcast.20, bf16[64,2048]{1,0:T(8,128)(2,1)} %get-tuple-element.51.upstream, bf16[1,2048]{1,0:T(2,128)(2,1)} %gain.5, bf16[64,2048]{1,0:T(8,128)(2,1)} %bitcast.22, ...), custom_call_target="tpu_custom_call" | custom-call | flops 201326592 | bytes 2883584 | tf_op jit(solution)/shard_map/pallas_call | solution.py:395
  (68 shorter events, 0.1 us)
Async XLA Ops:
  0.6 10.7 %collective-permute-start = (bf16[64,2048]{1,0:T(8,128)(2,1)}, bf16[64,2048]{1,0:T(8,128)(2,1)S(1)}, u32[]{:S(2)}, u32[]{:S(2)}) collective-permute-start(bf16[64,2048]{1,0:T(8,128)(2,1)} %bitcast.29), channel_id=1, source_target_pairs={{0,8},{8,16},{16,24},{1,9},{9,17},{17,25},{2,10},{10,18},{18,26},{... | collective-permute-start | bytes 786440 | tf_op jit(solution)/shard_map/ppermute | solution.py:47
  5.5 13.3 %collective-permute-start.1 = (bf16[64,2048]{1,0:T(8,128)(2,1)}, bf16[64,2048]{1,0:T(8,128)(2,1)S(1)}, u32[]{:S(2)}, u32[]{:S(2)}) collective-permute-start(bf16[64,2048]{1,0:T(8,128)(2,1)} %bitcast.30), channel_id=1, source_target_pairs={{8,0},{16,8},{24,16},{9,1},{17,9},{25,17},{10,2},{18,10},{26,18},{... | collective-permute-start | bytes 786440 | tf_op jit(solution)/shard_map/ppermute | solution.py:47
  11.3 7.5 %copy-start = (bf16[64,2048]{1,0:T(8,128)(2,1)}, bf16[64,2048]{1,0:T(8,128)(2,1)S(1)}, u32[]{:S(2)}) copy-start(bf16[64,2048]{1,0:T(8,128)(2,1)S(1)} %collective-permute-done.arrived_f) | copy-start | bytes 786436
  18.8 0.7 copy-start.1
  22.3 7.5 %collective-permute-start.2 = (bf16[24,2048]{1,0:T(8,128)(2,1)}, bf16[24,2048]{1,0:T(8,128)(2,1)S(1)}, u32[]{:S(2)}, u32[]{:S(2)}) collective-permute-start(bf16[24,2048]{1,0:T(8,128)(2,1)} %get-tuple-element.58), channel_id=1, source_target_pairs={{0,1},{1,2},{2,3},{3,4},{4,5},{5,6},{6,7},{7,0},{8,9},{9,10},{10,1... | collective-permute-start | bytes 294920 | tf_op jit(solution)/shard_map/ppermute | solution.py:57
  22.3 10.0 %collective-permute-start.3 = (bf16[24,2048]{1,0:T(8,128)(2,1)}, bf16[24,2048]{1,0:T(8,128)(2,1)S(1)}, u32[]{:S(2)}, u32[]{:S(2)}) collective-permute-start(bf16[24,2048]{1,0:T(8,128)(2,1)} %get-tuple-element.59), channel_id=1, source_target_pairs={{0,2},{1,3},{2,4},{3,5},{4,6},{5,7},{6,0},{7,1},{8,10},{9,11},{10,... | collective-permute-start | bytes 294920 | tf_op jit(solution)/shard_map/ppermute | solution.py:57
  26.9 6.5 %collective-permute-start.16 = (bf16[24,2048]{1,0:T(8,128)(2,1)}, bf16[24,2048]{1,0:T(8,128)(2,1)S(1)}, u32[]{:S(2)}, u32[]{:S(2)}) collective-permute-start(bf16[24,2048]{1,0:T(8,128)(2,1)} %get-tuple-element.83), channel_id=1, source_target_pairs={{0,1},{1,2},{2,3},{3,4},{4,5},{5,6},{6,7},{7,0},{8,9},{9,10},{10,1... | collective-permute-start | bytes 294920 | tf_op jit(solution)/shard_map/ppermute | solution.py:57
  28.2 7.7 %collective-permute-start.17 = (bf16[24,2048]{1,0:T(8,128)(2,1)}, bf16[24,2048]{1,0:T(8,128)(2,1)S(1)}, u32[]{:S(2)}, u32[]{:S(2)}) collective-permute-start(bf16[24,2048]{1,0:T(8,128)(2,1)} %get-tuple-element.84), channel_id=1, source_target_pairs={{0,2},{1,3},{2,4},{3,5},{4,6},{5,7},{6,0},{7,1},{8,10},{9,11},{10,... | collective-permute-start | bytes 294920 | tf_op jit(solution)/shard_map/ppermute | solution.py:57
  29.8 12.9 %collective-permute-start.18 = (bf16[24,2048]{1,0:T(8,128)(2,1)}, bf16[24,2048]{1,0:T(8,128)(2,1)S(1)}, u32[]{:S(2)}, u32[]{:S(2)}) collective-permute-start(bf16[24,2048]{1,0:T(8,128)(2,1)} %get-tuple-element.85), channel_id=1, source_target_pairs={{0,3},{1,4},{2,5},{3,6},{4,7},{5,0},{6,1},{7,2},{8,11},{9,12},{10,... | collective-permute-start | bytes 294920 | tf_op jit(solution)/shard_map/ppermute | solution.py:57
  29.8 46.5 %copy-start.16 = (bf16[24,2048]{1,0:T(8,128)(2,1)}, bf16[24,2048]{1,0:T(8,128)(2,1)S(1)}, u32[]{:S(2)}) copy-start(bf16[24,2048]{1,0:T(8,128)(2,1)S(1)} %collective-permute-done.2.refs_1_) | copy-start | bytes 294916
  29.8 16.0 %collective-permute-start.19 = (bf16[24,2048]{1,0:T(8,128)(2,1)}, bf16[24,2048]{1,0:T(8,128)(2,1)S(1)}, u32[]{:S(2)}, u32[]{:S(2)}) collective-permute-start(bf16[24,2048]{1,0:T(8,128)(2,1)} %get-tuple-element.86), channel_id=1, source_target_pairs={{0,4},{1,5},{2,6},{3,7},{4,0},{5,1},{6,2},{7,3},{8,12},{9,13},{10,... | collective-permute-start | bytes 294920 | tf_op jit(solution)/shard_map/ppermute | solution.py:57
  32.3 44.1 %copy-start.17 = (bf16[24,2048]{1,0:T(8,128)(2,1)}, bf16[24,2048]{1,0:T(8,128)(2,1)S(1)}, u32[]{:S(2)}) copy-start(bf16[24,2048]{1,0:T(8,128)(2,1)S(1)} %collective-permute-done.3.refs_2_) | copy-start | bytes 294916
  32.3 13.5 %collective-permute-start.20 = (bf16[24,2048]{1,0:T(8,128)(2,1)}, bf16[24,2048]{1,0:T(8,128)(2,1)S(1)}, u32[]{:S(2)}, u32[]{:S(2)}) collective-permute-start(bf16[24,2048]{1,0:T(8,128)(2,1)} %get-tuple-element.87), channel_id=1, source_target_pairs={{0,5},{1,6},{2,7},{3,0},{4,1},{5,2},{6,3},{7,4},{8,13},{9,14},{10,... | collective-permute-start | bytes 294920 | tf_op jit(solution)/shard_map/ppermute | solution.py:57
  33.4 19.6 %copy-start.21 = (bf16[24,2048]{1,0:T(8,128)(2,1)}, bf16[24,2048]{1,0:T(8,128)(2,1)S(1)}, u32[]{:S(2)}) copy-start(bf16[24,2048]{1,0:T(8,128)(2,1)S(1)} %collective-permute-done.16.refs_1_) | copy-start | bytes 294916
  33.4 14.4 %collective-permute-start.21 = (bf16[24,2048]{1,0:T(8,128)(2,1)}, bf16[24,2048]{1,0:T(8,128)(2,1)S(1)}, u32[]{:S(2)}, u32[]{:S(2)}) collective-permute-start(bf16[24,2048]{1,0:T(8,128)(2,1)} %get-tuple-element.88), channel_id=1, source_target_pairs={{0,6},{1,7},{2,0},{3,1},{4,2},{5,3},{6,4},{7,5},{8,14},{9,15},{10,... | collective-permute-start | bytes 294920 | tf_op jit(solution)/shard_map/ppermute | solution.py:57
  36.0 17.0 %copy-start.22 = (bf16[24,2048]{1,0:T(8,128)(2,1)}, bf16[24,2048]{1,0:T(8,128)(2,1)S(1)}, u32[]{:S(2)}) copy-start(bf16[24,2048]{1,0:T(8,128)(2,1)S(1)} %collective-permute-done.17.refs_2_) | copy-start | bytes 294916
  36.0 17.0 %collective-permute-start.22 = (bf16[24,2048]{1,0:T(8,128)(2,1)}, bf16[24,2048]{1,0:T(8,128)(2,1)S(1)}, u32[]{:S(2)}, u32[]{:S(2)}) collective-permute-start(bf16[24,2048]{1,0:T(8,128)(2,1)} %get-tuple-element.89), channel_id=1, source_target_pairs={{0,7},{1,0},{2,1},{3,2},{4,3},{5,4},{6,5},{7,6},{8,15},{9,8},{10,9... | collective-permute-start | bytes 294920 | tf_op jit(solution)/shard_map/ppermute | solution.py:57
  42.7 10.3 %copy-start.24 = (bf16[24,2048]{1,0:T(8,128)(2,1)}, bf16[24,2048]{1,0:T(8,128)(2,1)S(1)}, u32[]{:S(2)}) copy-start(bf16[24,2048]{1,0:T(8,128)(2,1)S(1)} %collective-permute-done.18.refs_3_) | copy-start | bytes 294916
  42.7 33.7 %collective-permute-start.4 = (bf16[24,2048]{1,0:T(8,128)(2,1)}, bf16[24,2048]{1,0:T(8,128)(2,1)S(1)}, u32[]{:S(2)}, u32[]{:S(2)}) collective-permute-start(bf16[24,2048]{1,0:T(8,128)(2,1)} %get-tuple-element.60), channel_id=1, source_target_pairs={{0,3},{1,4},{2,5},{3,6},{4,7},{5,0},{6,1},{7,2},{8,11},{9,12},{10,... | collective-permute-start | bytes 294920 | tf_op jit(solution)/shard_map/ppermute | solution.py:57
  45.8 7.2 %copy-start.26 = (bf16[24,2048]{1,0:T(8,128)(2,1)}, bf16[24,2048]{1,0:T(8,128)(2,1)S(1)}, u32[]{:S(2)}) copy-start(bf16[24,2048]{1,0:T(8,128)(2,1)S(1)} %collective-permute-done.19.refs_4_) | copy-start | bytes 294916
  45.8 30.7 %collective-permute-start.5 = (bf16[24,2048]{1,0:T(8,128)(2,1)}, bf16[24,2048]{1,0:T(8,128)(2,1)S(1)}, u32[]{:S(2)}, u32[]{:S(2)}) collective-permute-start(bf16[24,2048]{1,0:T(8,128)(2,1)} %get-tuple-element.61), channel_id=1, source_target_pairs={{0,4},{1,5},{2,6},{3,7},{4,0},{5,1},{6,2},{7,3},{8,12},{9,13},{10,... | collective-permute-start | bytes 294920 | tf_op jit(solution)/shard_map/ppermute | solution.py:57
  45.8 7.2 %copy-start.27 = (bf16[24,2048]{1,0:T(8,128)(2,1)}, bf16[24,2048]{1,0:T(8,128)(2,1)S(1)}, u32[]{:S(2)}) copy-start(bf16[24,2048]{1,0:T(8,128)(2,1)S(1)} %collective-permute-done.20.refs_5_) | copy-start | bytes 294916
  45.8 31.9 %collective-permute-start.6 = (bf16[24,2048]{1,0:T(8,128)(2,1)}, bf16[24,2048]{1,0:T(8,128)(2,1)S(1)}, u32[]{:S(2)}, u32[]{:S(2)}) collective-permute-start(bf16[24,2048]{1,0:T(8,128)(2,1)} %get-tuple-element.62), channel_id=1, source_target_pairs={{0,5},{1,6},{2,7},{3,0},{4,1},{5,2},{6,3},{7,4},{8,13},{9,14},{10,... | collective-permute-start | bytes 294920 | tf_op jit(solution)/shard_map/ppermute | solution.py:57
  47.9 5.2 %copy-start.28 = (bf16[24,2048]{1,0:T(8,128)(2,1)}, bf16[24,2048]{1,0:T(8,128)(2,1)S(1)}, u32[]{:S(2)}) copy-start(bf16[24,2048]{1,0:T(8,128)(2,1)S(1)} %collective-permute-done.21.refs_6_) | copy-start | bytes 294916
  47.9 29.9 %collective-permute-start.7 = (bf16[24,2048]{1,0:T(8,128)(2,1)}, bf16[24,2048]{1,0:T(8,128)(2,1)S(1)}, u32[]{:S(2)}, u32[]{:S(2)}) collective-permute-start(bf16[24,2048]{1,0:T(8,128)(2,1)} %get-tuple-element.63), channel_id=1, source_target_pairs={{0,6},{1,7},{2,0},{3,1},{4,2},{5,3},{6,4},{7,5},{8,14},{9,15},{10,... | collective-permute-start | bytes 294920 | tf_op jit(solution)/shard_map/ppermute | solution.py:57
  53.0 0.6 copy-start.29
  53.0 26.6 %collective-permute-start.8 = (bf16[24,2048]{1,0:T(8,128)(2,1)}, bf16[24,2048]{1,0:T(8,128)(2,1)S(1)}, u32[]{:S(2)}, u32[]{:S(2)}) collective-permute-start(bf16[24,2048]{1,0:T(8,128)(2,1)} %get-tuple-element.64), channel_id=1, source_target_pairs={{0,7},{1,0},{2,1},{3,2},{4,3},{5,4},{6,5},{7,6},{8,15},{9,8},{10,9... | collective-permute-start | bytes 294920 | tf_op jit(solution)/shard_map/ppermute | solution.py:57
  76.4 4.6 %copy-start.18 = (bf16[24,2048]{1,0:T(8,128)(2,1)}, bf16[24,2048]{1,0:T(8,128)(2,1)S(1)}, u32[]{:S(2)}) copy-start(bf16[24,2048]{1,0:T(8,128)(2,1)S(1)} %collective-permute-done.4.refs_3_) | copy-start | bytes 294916
  76.4 27.3 %collective-permute-start.23 = (bf16[24,2176]{1,0:T(8,128)(2,1)}, bf16[24,2176]{1,0:T(8,128)(2,1)S(1)}, u32[]{:S(2)}, u32[]{:S(2)}) collective-permute-start(bf16[24,2176]{1,0:T(8,128)(2,1)} %get-tuple-element.91), channel_id=1, source_target_pairs={{0,7},{1,0},{2,1},{3,2},{4,3},{5,4},{6,5},{7,6},{8,15},{9,8},{10,9... | collective-permute-start | bytes 313352 | tf_op jit(solution)/shard_map/ppermute | solution.py:57
  76.5 4.5 %copy-start.19 = (bf16[24,2048]{1,0:T(8,128)(2,1)}, bf16[24,2048]{1,0:T(8,128)(2,1)S(1)}, u32[]{:S(2)}) copy-start(bf16[24,2048]{1,0:T(8,128)(2,1)S(1)} %collective-permute-done.5.refs_4_) | copy-start | bytes 294916
  76.5 28.2 %collective-permute-start.24 = (bf16[24,2176]{1,0:T(8,128)(2,1)}, bf16[24,2176]{1,0:T(8,128)(2,1)S(1)}, u32[]{:S(2)}, u32[]{:S(2)}) collective-permute-start(bf16[24,2176]{1,0:T(8,128)(2,1)} %get-tuple-element.92), channel_id=1, source_target_pairs={{0,6},{1,7},{2,0},{3,1},{4,2},{5,3},{6,4},{7,5},{8,14},{9,15},{10,... | collective-permute-start | bytes 313352 | tf_op jit(solution)/shard_map/ppermute | solution.py:57
  77.7 3.3 %copy-start.20 = (bf16[24,2048]{1,0:T(8,128)(2,1)}, bf16[24,2048]{1,0:T(8,128)(2,1)S(1)}, u32[]{:S(2)}) copy-start(bf16[24,2048]{1,0:T(8,128)(2,1)S(1)} %collective-permute-done.6.refs_5_) | copy-start | bytes 294916
  77.7 27.1 %collective-permute-start.25 = (bf16[24,2176]{1,0:T(8,128)(2,1)}, bf16[24,2176]{1,0:T(8,128)(2,1)S(1)}, u32[]{:S(2)}, u32[]{:S(2)}) collective-permute-start(bf16[24,2176]{1,0:T(8,128)(2,1)} %get-tuple-element.93), channel_id=1, source_target_pairs={{0,5},{1,6},{2,7},{3,0},{4,1},{5,2},{6,3},{7,4},{8,13},{9,14},{10,... | collective-permute-start | bytes 313352 | tf_op jit(solution)/shard_map/ppermute | solution.py:57
  77.7 3.3 %copy-start.23 = (bf16[24,2048]{1,0:T(8,128)(2,1)}, bf16[24,2048]{1,0:T(8,128)(2,1)S(1)}, u32[]{:S(2)}) copy-start(bf16[24,2048]{1,0:T(8,128)(2,1)S(1)} %collective-permute-done.7.refs_6_) | copy-start | bytes 294916
  77.7 30.6 %collective-permute-start.26 = (bf16[24,2176]{1,0:T(8,128)(2,1)}, bf16[24,2176]{1,0:T(8,128)(2,1)S(1)}, u32[]{:S(2)}, u32[]{:S(2)}) collective-permute-start(bf16[24,2176]{1,0:T(8,128)(2,1)} %get-tuple-element.94), channel_id=1, source_target_pairs={{0,4},{1,5},{2,6},{3,7},{4,0},{5,1},{6,2},{7,3},{8,12},{9,13},{10,... | collective-permute-start | bytes 313352 | tf_op jit(solution)/shard_map/ppermute | solution.py:57
  79.6 1.4 %copy-start.25 = (bf16[24,2048]{1,0:T(8,128)(2,1)}, bf16[24,2048]{1,0:T(8,128)(2,1)S(1)}, u32[]{:S(2)}) copy-start(bf16[24,2048]{1,0:T(8,128)(2,1)S(1)} %collective-permute-done.8.refs_7_) | copy-start | bytes 294916
  79.6 29.9 %collective-permute-start.27 = (bf16[24,2176]{1,0:T(8,128)(2,1)}, bf16[24,2176]{1,0:T(8,128)(2,1)S(1)}, u32[]{:S(2)}, u32[]{:S(2)}) collective-permute-start(bf16[24,2176]{1,0:T(8,128)(2,1)} %get-tuple-element.95), channel_id=1, source_target_pairs={{0,3},{1,4},{2,5},{3,6},{4,7},{5,0},{6,1},{7,2},{8,11},{9,12},{10,... | collective-permute-start | bytes 313352 | tf_op jit(solution)/shard_map/ppermute | solution.py:57
  81.0 22.7 %copy-start.31 = (bf16[24,2176]{1,0:T(8,128)(2,1)S(1)}, bf16[24,2176]{1,0:T(8,128)(2,1)}, u32[]{:S(2)}) copy-start(bf16[24,2176]{1,0:T(8,128)(2,1)} %get-tuple-element.96) | copy-start | bytes 313348
  81.0 23.7 %copy-start.30 = (bf16[24,2176]{1,0:T(8,128)(2,1)S(1)}, bf16[24,2176]{1,0:T(8,128)(2,1)}, u32[]{:S(2)}) copy-start(bf16[24,2176]{1,0:T(8,128)(2,1)} %get-tuple-element.97) | copy-start | bytes 313348
  103.8 25.6 %copy-start.2 = (bf16[24,2176]{1,0:T(8,128)(2,1)}, bf16[24,2176]{1,0:T(8,128)(2,1)S(1)}, u32[]{:S(2)}) copy-start(bf16[24,2176]{1,0:T(8,128)(2,1)S(1)} %collective-permute-done.23.refs_9_) | copy-start | bytes 313348
  103.8 7.5 %collective-permute-start.28 = (bf16[24,2176]{1,0:T(8,128)(2,1)S(1)}, bf16[24,2176]{1,0:T(8,128)(2,1)S(1)}, u32[]{:S(2)}, u32[]{:S(2)}) collective-permute-start(bf16[24,2176]{1,0:T(8,128)(2,1)S(1)} %copy-done.31), channel_id=1, source_target_pairs={{0,2},{1,3},{2,4},{3,5},{4,6},{5,7},{6,0},{7,1},{8,10},{9,11},{10,... | collective-permute-start | bytes 313352 | tf_op jit(solution)/shard_map/ppermute | solution.py:57
  104.7 24.7 %copy-start.3 = (bf16[24,2176]{1,0:T(8,128)(2,1)}, bf16[24,2176]{1,0:T(8,128)(2,1)S(1)}, u32[]{:S(2)}) copy-start(bf16[24,2176]{1,0:T(8,128)(2,1)S(1)} %collective-permute-done.24.refs_10_) | copy-start | bytes 313348
  104.8 6.9 %collective-permute-start.29 = (bf16[24,2176]{1,0:T(8,128)(2,1)S(1)}, bf16[24,2176]{1,0:T(8,128)(2,1)S(1)}, u32[]{:S(2)}, u32[]{:S(2)}) collective-permute-start(bf16[24,2176]{1,0:T(8,128)(2,1)S(1)} %copy-done.30), channel_id=1, source_target_pairs={{0,1},{1,2},{2,3},{3,4},{4,5},{5,6},{6,7},{7,0},{8,9},{9,10},{10,1... | collective-permute-start | bytes 313352 | tf_op jit(solution)/shard_map/ppermute | solution.py:57
  104.8 24.6 %copy-start.4 = (bf16[24,2176]{1,0:T(8,128)(2,1)}, bf16[24,2176]{1,0:T(8,128)(2,1)S(1)}, u32[]{:S(2)}) copy-start(bf16[24,2176]{1,0:T(8,128)(2,1)S(1)} %collective-permute-done.25.refs_11_) | copy-start | bytes 313348
  104.8 7.1 %collective-permute-start.9 = (bf16[24,2176]{1,0:T(8,128)(2,1)}, bf16[24,2176]{1,0:T(8,128)(2,1)S(1)}, u32[]{:S(2)}, u32[]{:S(2)}) collective-permute-start(bf16[24,2176]{1,0:T(8,128)(2,1)} %get-tuple-element.75), channel_id=1, source_target_pairs={{0,7},{1,0},{2,1},{3,2},{4,3},{5,4},{6,5},{7,6},{8,15},{9,8},{10,9... | collective-permute-start | bytes 313352 | tf_op jit(solution)/shard_map/ppermute | solution.py:57
  108.4 21.1 %copy-start.5 = (bf16[24,2176]{1,0:T(8,128)(2,1)}, bf16[24,2176]{1,0:T(8,128)(2,1)S(1)}, u32[]{:S(2)}) copy-start(bf16[24,2176]{1,0:T(8,128)(2,1)S(1)} %collective-permute-done.26.refs_12_) | copy-start | bytes 313348
  108.4 7.6 %collective-permute-start.10 = (bf16[24,2176]{1,0:T(8,128)(2,1)}, bf16[24,2176]{1,0:T(8,128)(2,1)S(1)}, u32[]{:S(2)}, u32[]{:S(2)}) collective-permute-start(bf16[24,2176]{1,0:T(8,128)(2,1)} %get-tuple-element.76), channel_id=1, source_target_pairs={{0,6},{1,7},{2,0},{3,1},{4,2},{5,3},{6,4},{7,5},{8,14},{9,15},{10,... | collective-permute-start | bytes 313352 | tf_op jit(solution)/shard_map/ppermute | solution.py:57
  109.5 20.0 %copy-start.6 = (bf16[24,2176]{1,0:T(8,128)(2,1)}, bf16[24,2176]{1,0:T(8,128)(2,1)S(1)}, u32[]{:S(2)}) copy-start(bf16[24,2176]{1,0:T(8,128)(2,1)S(1)} %collective-permute-done.27.refs_13_) | copy-start | bytes 313348
  109.5 6.9 %collective-permute-start.11 = (bf16[24,2176]{1,0:T(8,128)(2,1)}, bf16[24,2176]{1,0:T(8,128)(2,1)S(1)}, u32[]{:S(2)}, u32[]{:S(2)}) collective-permute-start(bf16[24,2176]{1,0:T(8,128)(2,1)} %get-tuple-element.77), channel_id=1, source_target_pairs={{0,5},{1,6},{2,7},{3,0},{4,1},{5,2},{6,3},{7,4},{8,13},{9,14},{10,... | collective-permute-start | bytes 313352 | tf_op jit(solution)/shard_map/ppermute | solution.py:57
  111.3 18.2 %copy-start.7 = (bf16[24,2176]{1,0:T(8,128)(2,1)}, bf16[24,2176]{1,0:T(8,128)(2,1)S(1)}, u32[]{:S(2)}) copy-start(bf16[24,2176]{1,0:T(8,128)(2,1)S(1)} %collective-permute-done.28.refs_14_) | copy-start | bytes 313348
  111.3 18.1 %collective-permute-start.12 = (bf16[24,2176]{1,0:T(8,128)(2,1)}, bf16[24,2176]{1,0:T(8,128)(2,1)S(1)}, u32[]{:S(2)}, u32[]{:S(2)}) collective-permute-start(bf16[24,2176]{1,0:T(8,128)(2,1)} %get-tuple-element.78), channel_id=1, source_target_pairs={{0,4},{1,5},{2,6},{3,7},{4,0},{5,1},{6,2},{7,3},{8,12},{9,13},{10,... | collective-permute-start | bytes 313352 | tf_op jit(solution)/shard_map/ppermute | solution.py:57
  111.6 17.8 %copy-start.8 = (bf16[24,2176]{1,0:T(8,128)(2,1)}, bf16[24,2176]{1,0:T(8,128)(2,1)S(1)}, u32[]{:S(2)}) copy-start(bf16[24,2176]{1,0:T(8,128)(2,1)S(1)} %collective-permute-done.29.refs_15_) | copy-start | bytes 313348
  111.6 17.7 %collective-permute-start.13 = (bf16[24,2176]{1,0:T(8,128)(2,1)}, bf16[24,2176]{1,0:T(8,128)(2,1)S(1)}, u32[]{:S(2)}, u32[]{:S(2)}) collective-permute-start(bf16[24,2176]{1,0:T(8,128)(2,1)} %get-tuple-element.79), channel_id=1, source_target_pairs={{0,3},{1,4},{2,5},{3,6},{4,7},{5,0},{6,1},{7,2},{8,11},{9,12},{10,... | collective-permute-start | bytes 313352 | tf_op jit(solution)/shard_map/ppermute | solution.py:57
  111.9 17.5 %copy-start.9 = (bf16[24,2176]{1,0:T(8,128)(2,1)}, bf16[24,2176]{1,0:T(8,128)(2,1)S(1)}, u32[]{:S(2)}) copy-start(bf16[24,2176]{1,0:T(8,128)(2,1)S(1)} %collective-permute-done.9.refs_1_) | copy-start | bytes 313348
  111.9 17.4 %collective-permute-start.14 = (bf16[24,2176]{1,0:T(8,128)(2,1)}, bf16[24,2176]{1,0:T(8,128)(2,1)S(1)}, u32[]{:S(2)}, u32[]{:S(2)}) collective-permute-start(bf16[24,2176]{1,0:T(8,128)(2,1)} %get-tuple-element.80), channel_id=1, source_target_pairs={{0,2},{1,3},{2,4},{3,5},{4,6},{5,7},{6,0},{7,1},{8,10},{9,11},{10,... | collective-permute-start | bytes 313352 | tf_op jit(solution)/shard_map/ppermute | solution.py:57
  115.9 13.6 %copy-start.10 = (bf16[24,2176]{1,0:T(8,128)(2,1)}, bf16[24,2176]{1,0:T(8,128)(2,1)S(1)}, u32[]{:S(2)}) copy-start(bf16[24,2176]{1,0:T(8,128)(2,1)S(1)} %collective-permute-done.10.refs_2_) | copy-start | bytes 313348
  115.9 13.5 %collective-permute-start.15 = (bf16[24,2176]{1,0:T(8,128)(2,1)}, bf16[24,2176]{1,0:T(8,128)(2,1)S(1)}, u32[]{:S(2)}, u32[]{:S(2)}) collective-permute-start(bf16[24,2176]{1,0:T(8,128)(2,1)} %get-tuple-element.81), channel_id=1, source_target_pairs={{0,1},{1,2},{2,3},{3,4},{4,5},{5,6},{6,7},{7,0},{8,9},{9,10},{10,1... | collective-permute-start | bytes 313352 | tf_op jit(solution)/shard_map/ppermute | solution.py:57
  116.4 13.1 %copy-start.11 = (bf16[24,2176]{1,0:T(8,128)(2,1)}, bf16[24,2176]{1,0:T(8,128)(2,1)S(1)}, u32[]{:S(2)}) copy-start(bf16[24,2176]{1,0:T(8,128)(2,1)S(1)} %collective-permute-done.11.refs_3_) | copy-start | bytes 313348
  129.3 0.6 copy-start.12
  129.3 0.7 copy-start.13
  129.4 0.7 copy-start.14
  129.4 0.7 copy-start.15

commit v5 on v4

--- a/solution.py
+++ b/solution.py
@@ -114,8 +114,8 @@
     return [exponent / total for exponent in exponents]
 
 
-def keys_of_part(sizes, me, columns, part):
-    device = partners(me, columns[:, 0:1], sizes["sources"], 1, sizes["turned"])
+def keys_of_part(sizes, me, columns, part, turned):
+    device = partners(me, columns[:, 0:1], sizes["sources"], 1, turned)
     return columns[:, 2 + part : 3 + part] + device * sizes["share"]
 
 
@@ -133,7 +133,7 @@
     data[count:, :] = chosen
     targets_f, _ = slot_targets(routes_f[...], experts, capacity)
     targets_b, _ = slot_targets(routes_b[...], experts, capacity)
-    keys = keys_of_part(sizes, place[2], columns, 0)
+    keys = keys_of_part(sizes, place[2], columns, 0, sizes["there"][0])
     table_f = sum(tables_of(targets_f, keys))
     table_b = sum(tables_of([t + experts * capacity for t in targets_b], keys))
     table = jnp.concatenate([table_f, table_b], axis=1).astype(BF16)
@@ -154,33 +154,39 @@
     own_shares = route_shares(rows, router[...], hits)
     for k, share in enumerate(own_shares):
         shares_b[k] = jnp.broadcast_to(share, shares_b.shape[1:])
-    parts = mixing_f.shape[0]
-    for part in range(parts):
-        keys = keys_of_part(sizes, place[2], columns, part)
+    sends = list(sends)
+    for part in range(mixing_f.shape[0]):
+        there, back = sizes["there"][part], sizes["back"][part]
+        keys = keys_of_part(sizes, place[2], columns, part, back)
         found_f, found_b = tables_of(targets_f, keys), tables_of(targets_b, keys)
         mixing_f[part] = sum(t * s.astype(BF16).astype(F32) for t, s in zip(found_f, shares_f))
         mixing_b[part] = sum(t * s.astype(BF16).astype(F32) for t, s in zip(found_b, own_shares))
         for k, table in enumerate(found_b):
             tables_b[part, k] = table
         if part > 0:
-            blocks = len(sends) // (parts - 1)
+            if there != back:
+                keys = keys_of_part(sizes, place[2], columns, part, there)
+                found_f, found_b = tables_of(targets_f, keys), tables_of(targets_b, keys)
+            blocks = sizes["sources"] if there else 1
             table = jnp.concatenate([sum(found_f), sum(found_b)], axis=1).astype(BF16)
-            parted(dot(table, data[...]), sends[(part - 1) * blocks : part * blocks])
-
-
-def expert_kernel(sizes, steps, blocks, place, columns, lanes, wanted, wanted_lanes, *refs):
+            parted(dot(table, data[...]), sends[:blocks])
+            sends = sends[blocks:]
+
+
+def expert_kernel(sizes, steps, part, place, columns, lanes, wanted, wanted_lanes, *refs):
+    there, back = sizes["there"][part], sizes["back"][part]
+    blocks = sizes["sources"] if there else 1
     got, (saved_pre, up, down) = refs[:blocks], refs[blocks : blocks + 3]
-    out = refs[blocks + 3 : 2 * blocks + 3]
-    rows, total_f, total_b, inner, results = refs[2 * blocks + 3 :]
+    out, (rows, total_f, total_b, inner, results) = refs[blocks + 3 : -5], refs[-5:]
     expert, step = pl.program_id(0), pl.program_id(1)
     held = pl.num_programs(0)
     width = rows.shape[1]
     padded, block_rows = sizes["padded"], sizes["block_rows"]
-    source = (sizes["sources"], -1, sizes["turned"])
+    source = (sizes["sources"], -1)
 
     @pl.when((expert == 0) & (step == 0))
     def _():
-        have = partners(place[2], lanes[0:1, :], *source) * block_rows + lanes[1:2, :]
+        have = partners(place[2], lanes[0:1, :], *source, there) * block_rows + lanes[1:2, :]
         order = (wanted[...] == have).astype(F32).astype(BF16)
         rows[...] = dot(order, joined(got)).astype(BF16)
         results[:, width:] = jnp.zeros((results.shape[0], results.shape[1] - width), BF16)
@@ -217,40 +223,62 @@
 
     @pl.when((expert == held - 1) & (step == steps - 1))
     def _():
-        have = partners(place[2], columns[:, 0:1], *source) * block_rows + columns[:, 1:2]
+        have = partners(place[2], columns[:, 0:1], *source, back) * block_rows + columns[:, 1:2]
         order = (have == wanted_lanes[...]).astype(F32).astype(BF16)
         parted(dot(order, results[...]), out)
 
 
-def combine_kernel(
-    experts, tokens, saved, upstream, gain, router, routes, mixing_f, mixing_b, tables, shares, *refs
+def add_up(part, blocks, mixing_f, mixing_b, tables):
+    back = joined(blocks)
+    width = back.shape[1] - LANES
+    sums = back[:, width:].astype(F32)[:, :1]
+    return (
+        dot(mixing_f[part].astype(BF16), back[:, :width], TN),
+        dot(mixing_b[part].astype(BF16), back[:, :width], TN),
+        [jnp.sum(tables[part, k] * sums, axis=0, keepdims=True) for k in range(tables.shape[1])],
+    )
+
+
+def early_kernel(sizes, tokens, mixing_f, mixing_b, tables, *refs):
+    *backs, output, gradient, inner = refs
+    sum_f, sum_b, sums = tokens[...].astype(F32), None, None
+    for part, turned in enumerate(sizes["back"][:-1]):
+        blocks = sizes["sources"] if turned else 1
+        more_f, more_b, more = add_up(part, backs[:blocks], mixing_f, mixing_b, tables)
+        backs = backs[blocks:]
+        sum_f += more_f
+        sum_b = more_b if sum_b is None else sum_b + more_b
+        sums = more if sums is None else [a + b for a, b in zip(sums, more)]
+    output[...] = sum_f
+    if sums is None:
+        gradient[...] = jnp.zeros(gradient.shape, F32)
+        inner[...] = jnp.zeros(inner.shape, F32)
+    else:
+        gradient[...] = sum_b
+        for k, row in enumerate(sums):
+            inner[k] = jnp.broadcast_to(row, inner.shape[1:])
+
+
+def late_kernel(
+    experts, early_f, early_b, early_inner, saved, upstream, gain, router, routes,
+    mixing_f, mixing_b, tables, shares, *refs,
 ):
     *backs, output, gradient = refs
-    width = tokens.shape[1]
-    parts = range(mixing_f.shape[0])
-    blocks = len(backs) // len(parts)
-    back = [joined(backs[p * blocks : (p + 1) * blocks]) for p in parts]
+    more_f, more_b, more = add_up(mixing_f.shape[0] - 1, backs, mixing_f, mixing_b, tables)
     widened = saved[...].astype(F32)
     inv_rms = lax.rsqrt(jnp.mean(widened * widened, axis=-1, keepdims=True) + EPS)
     hits = expert_hits(routes[...], experts)
     top = len(hits)
     share = [shares[k][:1, :] for k in range(top)]
-    sums = [back[p][:, width:].astype(F32)[:, :1] for p in parts]
-    inner = [
-        sum(jnp.sum(tables[p, k] * sums[p], axis=0, keepdims=True) for p in parts)
-        for k in range(top)
-    ]
+    inner = [early_inner[k][:1, :] + more[k] for k in range(top)]
     mean = sum(share[k] * inner[k] for k in range(top))
     logit_grad = sum(share[k] * (inner[k] - mean) * hits[k] for k in range(top))
     high = logit_grad.astype(BF16)
     rest = logit_grad - high.astype(F32)
     middle = rest.astype(BF16)
     low = (rest - middle.astype(F32)).astype(BF16)
-    output[0] = (
-        tokens[...].astype(F32)
-        + sum(dot(mixing_f[p].astype(BF16), back[p][:, :width], TN) for p in parts)
-    ).astype(BF16)
-    normed_grad = sum(dot(mixing_b[p].astype(BF16), back[p][:, :width], TN) for p in parts)
+    output[0] = (early_f[...] + more_f).astype(BF16)
+    normed_grad = early_b[...] + more_b
     for piece in (high, middle, low):
         normed_grad += dot(piece, router[...], TN)
     gained = normed_grad * gain[...].astype(F32)
@@ -310,8 +338,9 @@
     parts = 2 if local % 2 == 0 else 1
     held = local // parts
     moved = 2 * slots // parts
-    turned = sources <= 8
-    blocks = sources if turned else 1
+    few = sources <= 8
+    there = [few and part == 0 for part in range(parts)]
+    back = [few and part == parts - 1 for part in range(parts)]
     columns, wanted = exchange_order(parts, sources, local, capacity, padded)
     lanes, wanted_lanes = np.ascontiguousarray(columns.T), np.ascontiguousarray(wanted.T)
     sizes = {
@@ -319,14 +348,19 @@
         "capacity": capacity,
         "sources": sources,
         "share": local * capacity,
-        "turned": turned,
+        "there": there,
+        "back": back,
         "padded": padded,
         "block_rows": moved // sources,
     }
     place = jnp.stack([section, jnp.full_like(section, last), lax.axis_index("expert")])
     place = place.astype(jnp.int32)
-    sent = (shape((moved // blocks, width), BF16),) * blocks
-    result = (shape((moved // blocks, width + LANES), BF16),) * blocks
+
+    def blocks_of(turned, columns):
+        blocks = sources if turned else 1
+        return [shape((moved // blocks, columns), BF16)] * blocks
+
+    later = [block for turned in there[1:] for block in blocks_of(turned, width)]
 
     router_t = router[0].T
     routes_f, routes_b = forward_routes[0].T, backward_routes[0].T
@@ -338,7 +372,7 @@
             shape((count, width), BF16),
             shape((count, width), BF16),
             shape((2 * count, width), BF16),
-            *sent,
+            *blocks_of(there[0], width),
         ),
         (4 * moved * count * width, 2 * (8 * count + moved) * width),
         in_specs=[SMEM] + [VMEM] * 8,
@@ -352,22 +386,25 @@
             shape((parts, moved, count), F32),
             shape((parts, top, moved, count), F32),
             shape((top, 8, count), F32),
-            *(sent * (parts - 1)),
+            *later,
         ),
         (4 * moved * count * width, 2 * (4 * count + moved) * width),
         in_specs=[SMEM] + [VMEM] * 7,
     )(place, data, saved_inputs[0], norm_gain, router_t, routes_f, routes_b, columns)
     saved_pre = jnp.transpose(pre_activation[0], (1, 0, 2, 3)).reshape(local, rows, hidden)
     saved_pre = jnp.pad(saved_pre, ((0, 0), (0, padded - rows), (0, 0)))
-    sends, saved_pre = lax.optimization_barrier((sends, saved_pre))
-
-    sends = [send] + [sends[p * blocks : (p + 1) * blocks] for p in range(parts - 1)]
-    received = [exchange(blocks_out, 1) for blocks_out in sends]
     backs = []
-    for part, got in enumerate(received):
+    got = exchange(send, 1)
+    for part in range(parts):
+        if part + 1 < parts:
+            sends, saved_pre, got = lax.optimization_barrier((sends, saved_pre, got))
+            blocks = len(blocks_of(there[part + 1], width))
+            coming = exchange(sends[:blocks], 1)
+            sends = sends[blocks:]
+        result = blocks_of(back[part], width + LANES)
         done = call(
-            functools.partial(expert_kernel, sizes, steps, blocks),
-            result,
+            functools.partial(expert_kernel, sizes, steps, part),
+            tuple(result),
             (8 * held * padded * width * hidden, 4 * held * width * hidden),
             grid=(held, steps),
             in_specs=[
@@ -390,15 +427,25 @@
                 pltpu.VMEM((2 * held * padded, width + LANES), BF16),
             ],
         )(place, columns, lanes, wanted, wanted_lanes, *got, saved_pre, up_weight, down_weight)
-        backs += exchange(list(done), -1)
+        backs.append(exchange(list(done), -1))
+        got = coming if part + 1 < parts else None
+    early = call(
+        functools.partial(early_kernel, sizes),
+        (
+            shape((count, width), F32),
+            shape((count, width), F32),
+            shape((top, 8, count), F32),
+        ),
+        (4 * moved * count * width, 2 * (5 * count + moved) * width),
+    )(tokens, mixing_f, mixing_b, tables_b, *[block for got in backs[:-1] for block in got])
     return tuple(
         call(
-            functools.partial(combine_kernel, experts),
+            functools.partial(late_kernel, experts),
             (shape((1, count, width), BF16),) * 2,
-            (8 * moved * count * width, 2 * (5 * count + 2 * moved) * width),
+            (4 * moved * count * width, 2 * (8 * count + moved) * width),
         )(
-            tokens, saved_inputs[0], upstream, norm_gain, router_t, routes_b,
-            mixing_f, mixing_b, tables_b, shares_b, *backs,
+            *early, saved_inputs[0], upstream, norm_gain, router_t, routes_b,
+            mixing_f, mixing_b, tables_b, shares_b, *backs[-1],
         )
     )
 

time: 134 us -> 125 us (0.933)
  waiting for transfers between devices: 35.3 us -> 24.1 us
  Pallas kernels: 55.1 us -> 57.6 us
    ppermute x28 -> x14, starting transfers between devices: 31.7 us -> 16.8 us  [exchange(): got[d] = lax.ppermute(blocks[d], 'expert', route)]
    all_to_all x0 -> x2, starting transfers between devices: none -> 13.6 us  [exchange(): lax.all_to_all(blocks[0], 'expert', split_axis=0, concat_axis=0, tiled=True)]
    ppermute x28 -> x14, waiting for transfers between devices: 26 us -> 12.7 us  [exchange(): got[d] = lax.ppermute(blocks[d], 'expert', route)]
    pallas_call x3 -> x4, Pallas kernels: 49.3 us -> 51.7 us  [the longest x2 45.3 us: on_device(): call(functools.partial(expert_kernel, sizes, steps, part), tuple(result),...]
    ppermute x2, waiting for transfers between devices: 9.31 us -> 11.3 us  [from_behind(): return lax.ppermute(block, axis, route)]
  transfers between devices with their start and end apart: 30 -> 18, of which waited for: 10 -> 8; matrix products, arithmetic and copies ran while one was open for 2% -> 2% of each run, Pallas kernels for 36% -> 41%
where the time goes in v5:
time: 125 us; the launch traced here: 124 us
  Pallas kernels  57.6 us (46%)
  starting transfers between devices  36.6 us (29%)
  waiting for transfers between devices  24.1 us (19%)
  local copies, waits for them, and re-layouts  4.43 us (4%)
    pallas_call x2, Pallas kernels, on_device(): call(functools.partial(expert_kernel, sizes, steps, part), tuple(result),...  45.3 us
    ppermute x14, starting transfers between devices, exchange(): got[d] = lax.ppermute(blocks[d], 'expert', route)  16.8 us
    all_to_all x2, starting transfers between devices, exchange(): lax.all_to_all(blocks[0], 'expert', split_axis=0, concat_axis=0, tiled=True)  13.6 us
    ppermute x14, waiting for transfers between devices, exchange(): got[d] = lax.ppermute(blocks[d], 'expert', route)  12.7 us
    ppermute x2, waiting for transfers between devices, from_behind(): return lax.ppermute(block, axis, route)  11.3 us
    ppermute x2, starting transfers between devices, from_behind(): return lax.ppermute(block, axis, route)  6.15 us
    pallas_call x1, Pallas kernels, on_device(): call(functools.partial(late_kernel, experts), (shape((1, count, width), B...  3.49 us
    pallas_call x1, Pallas kernels, on_device(): call(functools.partial(mixing_kernel, sizes), (shape((parts, moved, count...  3.06 us
  transfers between devices with their start and end apart: 18, of which 8 were waited for; matrix products, arithmetic and copies ran while one was open for 2% of the time, Pallas kernels for 41%

profile of v5, /device:TPU:0, one launch (start us, length us, event | category | flops | bytes accessed | tf_op | source)
XLA Modules:
  0.0 124.2 jit_solution(10109134433321576280)
XLA Ops:
  0.6 4.9 %collective-permute-start = (bf16[64,2048]{1,0:T(8,128)(2,1)}, bf16[64,2048]{1,0:T(8,128)(2,1)S(1)}, u32[]{:S(2)}, u32[]{:S(2)}) collective-permute-start(bf16[64,2048]{1,0:T(8,128)(2,1)} %bitcast.37), channel_id=1, source_target_pairs={{0,8},{8,16},{16,24},{1,9},{9,17},{17,25},{2,10},{10,18},{18,26},{... | collective-permute-start | bytes 786440 | tf_op jit(solution)/shard_map/ppermute | solution.py:47
  5.5 1.3 %collective-permute-start.1 = (bf16[64,2048]{1,0:T(8,128)(2,1)}, bf16[64,2048]{1,0:T(8,128)(2,1)S(1)}, u32[]{:S(2)}, u32[]{:S(2)}) collective-permute-start(bf16[64,2048]{1,0:T(8,128)(2,1)} %bitcast.38), channel_id=1, source_target_pairs={{8,0},{16,8},{24,16},{9,1},{17,9},{25,17},{10,2},{18,10},{26,18},{... | collective-permute-start | bytes 786440 | tf_op jit(solution)/shard_map/ppermute | solution.py:47
  6.8 0.7 pad_add_fusion.place
  7.5 3.9 %collective-permute-done.arrived_f = bf16[64,2048]{1,0:T(8,128)(2,1)S(1)} collective-permute-done((bf16[64,2048]{1,0:T(8,128)(2,1)}, bf16[64,2048]{1,0:T(8,128)(2,1)S(1)}, u32[]{:S(2)}, u32[]{:S(2)}) %collective-permute-start) | collective-permute-done | bytes 262176 | tf_op jit(solution)/shard_map/ppermute | solution.py:47
  11.3 7.5 %collective-permute-done.1.arrived_b = bf16[64,2048]{1,0:T(8,128)(2,1)S(1)} collective-permute-done((bf16[64,2048]{1,0:T(8,128)(2,1)}, bf16[64,2048]{1,0:T(8,128)(2,1)S(1)}, u32[]{:S(2)}, u32[]{:S(2)}) %collective-permute-start.1) | collective-permute-done | bytes 262176 | tf_op jit(solution)/shard_map/ppermute | solution.py:47
  18.8 0.0 copy-done.2
  18.8 0.7 copy-done.3
  19.5 2.8 %shard_map.167 = (bf16[64,2048]{1,0:T(8,128)(2,1)}, bf16[64,2048]{1,0:T(8,128)(2,1)}, bf16[128,2048]{1,0:T(8,128)(2,1)}, bf16[24,2048]{1,0:T(8,128)(2,1)}, bf16[...) custom-call(s32[3]{0:T(128)} %pad_add_fusion.place, ...), custom_call_target="tpu_custom_call" | custom-call | flops 100663296 | bytes 2883584 | tf_op jit(solution)/shard_map/pallas_call | solution.py:369
  22.3 0.0 collective-permute-start.2
  22.3 1.6 %collective-permute-start.3 = (bf16[24,2048]{1,0:T(8,128)(2,1)}, bf16[24,2048]{1,0:T(8,128)(2,1)S(1)}, u32[]{:S(2)}, u32[]{:S(2)}) collective-permute-start(bf16[24,2048]{1,0:T(8,128)(2,1)} %get-tuple-element.47), channel_id=1, source_target_pairs={{0,2},{1,3},{2,4},{3,5},{4,6},{5,7},{6,0},{7,1},{8,10},{9,11},{10,... | collective-permute-start | bytes 294920 | tf_op jit(solution)/shard_map/ppermute | solution.py:57
  24.0 2.5 %collective-permute-start.4 = (bf16[24,2048]{1,0:T(8,128)(2,1)}, bf16[24,2048]{1,0:T(8,128)(2,1)S(1)}, u32[]{:S(2)}, u32[]{:S(2)}) collective-permute-start(bf16[24,2048]{1,0:T(8,128)(2,1)} %get-tuple-element.48), channel_id=1, source_target_pairs={{0,3},{1,4},{2,5},{3,6},{4,7},{5,0},{6,1},{7,2},{8,11},{9,12},{10,... | collective-permute-start | bytes 294920 | tf_op jit(solution)/shard_map/ppermute | solution.py:57
  26.5 1.2 collective-permute-start.5
  27.7 1.2 collective-permute-start.6
  28.9 0.0 collective-permute-done.2.refs_1_
  29.0 1.7 %collective-permute-start.7 = (bf16[24,2048]{1,0:T(8,128)(2,1)}, bf16[24,2048]{1,0:T(8,128)(2,1)S(1)}, u32[]{:S(2)}, u32[]{:S(2)}) collective-permute-start(bf16[24,2048]{1,0:T(8,128)(2,1)} %get-tuple-element.51), channel_id=1, source_target_pairs={{0,6},{1,7},{2,0},{3,1},{4,2},{5,3},{6,4},{7,5},{8,14},{9,15},{10,... | collective-permute-start | bytes 294920 | tf_op jit(solution)/shard_map/ppermute | solution.py:57
  30.7 0.0 collective-permute-done.3.refs_2_
  30.7 1.5 %collective-permute-start.8 = (bf16[24,2048]{1,0:T(8,128)(2,1)}, bf16[24,2048]{1,0:T(8,128)(2,1)S(1)}, u32[]{:S(2)}, u32[]{:S(2)}) collective-permute-start(bf16[24,2048]{1,0:T(8,128)(2,1)} %get-tuple-element.52), channel_id=1, source_target_pairs={{0,7},{1,0},{2,1},{3,2},{4,3},{5,4},{6,5},{7,6},{8,15},{9,8},{10,9... | collective-permute-start | bytes 294920 | tf_op jit(solution)/shard_map/ppermute | solution.py:57
  32.2 1.2 copy.19
  33.4 0.9 pad.4.refs_8_.refs_1_
  34.3 3.1 %shard_map.168 = (f32[2,192,64]{2,1,0:T(8,128)}, f32[2,192,64]{2,1,0:T(8,128)}, f32[2,2,192,64]{3,2,1,0:T(8,128)}, f32[2,8,64]{2,1,0:T(8,128)}, bf16[192,2048]{1,0:T(8,128)(2,1)}) custom-call(s32[3]{0:T(128)} %pad_add_fusion.place, bf16[128,2048]{1,0:T(8,128)(2,1)} %get-tuple-element.40.data, bf16[64,2048]{1,0:T(8,128)(2,1)} %bitcast.26, ...), custom_call_target="tpu_custom_call" | custom-call | flops 100663296 | bytes 1835008 | tf_op jit(solution)/shard_map/pallas_call | solution.py:382
  37.4 0.5 collective-permute-done.4.refs_3_
  37.9 0.2 collective-permute-done.5.refs_4_
  38.1 0.0 collective-permute-done.6.refs_5_
  38.1 0.0 collective-permute-done.7.refs_6_
  38.1 0.0 copy-start.16
  38.1 0.0 collective-permute-done.8.refs_7_
  38.1 0.0 copy-start.17
  38.1 8.5 %all-to-all-start.1 = ((bf16[8,24,2048]{2,1,0:T(8,128)(2,1)}), bf16[8,24,2048]{2,1,0:T(8,128)(2,1)S(1)}, u32[]{:S(2)}, u32[]{:S(2)}) async-start(bf16[8,24,2048]{2,1,0:T(8,128)(2,1)} %bitcast.30), calls=%async_computation.1 | async-start | bytes 1572864 | tf_op jit(solution)/shard_map/all_to_all | solution.py:53
  46.6 0.0 copy-done.11
  46.6 0.0 copy-done.12
  46.6 0.0 copy-done.13
  46.6 0.0 copy-done.14
  46.7 0.0 copy-done.15
  46.7 0.0 copy-done.16
  46.7 0.0 copy-done.17
  46.7 22.6 %shard_map.169 = bf16[192,2176]{1,0:T(8,128)(2,1)} custom-call(s32[3]{0:T(128)} %pad_add_fusion.place, s32[192,4]{1,0:T(8,128)} %constant.21.clone.columns, s32[4,192]{1,0:T(4,128)} %constant.22.clone.lanes, s32[256,1]{1,0:T(8,128)} %constant.23.clone.wanted, s32[1,256]{1,0:T(1,128)} %constant.24.clone.wanted_lanes, ...), custom_call_target="tpu_custom_call" | custom-call | flops 2147483648 | bytes 33554432 | tf_op jit(solution)/shard_map/pallas_call | solution.py:405
  69.3 0.0 all-to-all-done.1
  69.3 0.0 copy-start.1
  69.3 5.1 %all-to-all-start = ((bf16[8,24,2176]{2,1,0:T(8,128)(2,1)}), bf16[8,24,2176]{2,1,0:T(8,128)(2,1)S(1)}, u32[]{:S(2)}, u32[]{:S(2)}) async-start(bf16[8,24,2176]{2,1,0:T(8,128)(2,1)} %bitcast.23), calls=%async_computation | async-start | bytes 1671168 | tf_op jit(solution)/shard_map/all_to_all | solution.py:53
  74.4 0.0 copy-done.1
  74.4 22.7 %shard_map.171 = (bf16[24,2176]{1,0:T(8,128)(2,1)}, bf16[24,2176]{1,0:T(8,128)(2,1)}, bf16[24,2176]{1,0:T(8,128)(2,1)}, bf16[24,2176]{1,0:T(8,128)(2,1)}, bf16[2...) custom-call(s32[3]{0:T(128)} %pad_add_fusion.place, ...), custom_call_target="tpu_custom_call" | custom-call | flops 2147483648 | bytes 33554432 | tf_op jit(solution)/shard_map/pallas_call | solution.py:405
  97.2 3.6 %collective-permute-start.9 = (bf16[24,2176]{1,0:T(8,128)(2,1)}, bf16[24,2176]{1,0:T(8,128)(2,1)S(1)}, u32[]{:S(2)}, u32[]{:S(2)}) collective-permute-start(bf16[24,2176]{1,0:T(8,128)(2,1)} %get-tuple-element.69), channel_id=1, source_target_pairs={{0,7},{1,0},{2,1},{3,2},{4,3},{5,4},{6,5},{7,6},{8,15},{9,8},{10,9... | collective-permute-start | bytes 313352 | tf_op jit(solution)/shard_map/ppermute | solution.py:57
  100.7 0.6 collective-permute-start.10
  101.3 0.0 collective-permute-start.11
  101.3 2.4 %collective-permute-start.12 = (bf16[24,2176]{1,0:T(8,128)(2,1)}, bf16[24,2176]{1,0:T(8,128)(2,1)S(1)}, u32[]{:S(2)}, u32[]{:S(2)}) collective-permute-start(bf16[24,2176]{1,0:T(8,128)(2,1)} %get-tuple-element.72), channel_id=1, source_target_pairs={{0,4},{1,5},{2,6},{3,7},{4,0},{5,1},{6,2},{7,3},{8,12},{9,13},{10,... | collective-permute-start | bytes 313352 | tf_op jit(solution)/shard_map/ppermute | solution.py:57
  103.7 0.0 collective-permute-start.13
  103.7 0.6 collective-permute-done.9.refs_1_
  104.4 0.4 collective-permute-start.14
  104.8 2.9 %collective-permute-done.10.refs_2_ = bf16[24,2176]{1,0:T(8,128)(2,1)S(1)} collective-permute-done((bf16[24,2176]{1,0:T(8,128)(2,1)}, bf16[24,2176]{1,0:T(8,128)(2,1)S(1)}, u32[]{:S(2)}, u32[]{:S(2)}) %collective-permute-start.10) | collective-permute-done | bytes 104480 | tf_op jit(solution)/shard_map/ppermute | solution.py:57
  107.7 0.0 collective-permute-start.15
  107.7 0.0 all-to-all-done
  107.7 0.0 copy-start
  107.7 0.9 copy-done
  108.6 2.8 %shard_map.170 = (f32[64,2048]{1,0:T(8,128)}, f32[64,2048]{1,0:T(8,128)}, f32[2,8,64]{2,1,0:T(8,128)}) custom-call(bf16[64,2048]{1,0:T(8,128)(2,1)} %get-tuple-element.39.tokens, f32[2,192,64]{2,1,0:T(8,128)} %get-tuple-element.41.mixing_f, f32[2,192,64]{2,1,0:T(8,128)} %get-tuple-element.42.mixing_b, f32[2,2,192,64]{3,2,1,0:T(8,128)} %get-tuple-element.43.tables, ...), custom_call_target="tpu_custom_call" | custom-call | flops 100663296 | bytes 2097152 | tf_op jit(solution)/shard_map/pallas_call | solution.py:432
  111.5 0.0 collective-permute-done.11.refs_3_
  111.5 7.4 %collective-permute-done.12.refs_4_ = bf16[24,2176]{1,0:T(8,128)(2,1)S(1)} collective-permute-done((bf16[24,2176]{1,0:T(8,128)(2,1)}, bf16[24,2176]{1,0:T(8,128)(2,1)S(1)}, u32[]{:S(2)}, u32[]{:S(2)}) %collective-permute-start.12) | collective-permute-done | bytes 104480 | tf_op jit(solution)/shard_map/ppermute | solution.py:57
  118.9 1.0 collective-permute-done.13.refs_5_
  119.9 0.0 collective-permute-done.14.refs_6_
  119.9 0.0 collective-permute-done.15.refs_7_
  119.9 0.0 copy-start.10
  120.0 0.6 copy-done.8
  120.6 0.0 copy-done.9
  120.6 0.0 copy-done.10
  120.7 3.5 %shard_map.172 = (bf16[1,64,2048]{2,1,0:T(8,128)(2,1)}, bf16[1,64,2048]{2,1,0:T(8,128)(2,1)}) custom-call(f32[64,2048]{1,0:T(8,128)} %get-tuple-element.62.early_f, f32[64,2048]{1,0:T(8,128)} %get-tuple-element.63.early_b, f32[2,8,64]{2,1,0:T(8,128)} %get-tuple-element.64.early_inner, bf16[64,2048]{1,0:T(8,128)(2,1)} %bitcast.27, ...), custom_call_target="tpu_custom_call" | custom-call | flops 100663296 | bytes 2883584 | tf_op jit(solution)/shard_map/pallas_call | solution.py:442
  (17 shorter events, 0.0 us)
Async XLA Ops:
  0.6 10.7 %collective-permute-start = (bf16[64,2048]{1,0:T(8,128)(2,1)}, bf16[64,2048]{1,0:T(8,128)(2,1)S(1)}, u32[]{:S(2)}, u32[]{:S(2)}) collective-permute-start(bf16[64,2048]{1,0:T(8,128)(2,1)} %bitcast.37), channel_id=1, source_target_pairs={{0,8},{8,16},{16,24},{1,9},{9,17},{17,25},{2,10},{10,18},{18,26},{... | collective-permute-start | bytes 786440 | tf_op jit(solution)/shard_map/ppermute | solution.py:47
  5.5 13.3 %collective-permute-start.1 = (bf16[64,2048]{1,0:T(8,128)(2,1)}, bf16[64,2048]{1,0:T(8,128)(2,1)S(1)}, u32[]{:S(2)}, u32[]{:S(2)}) collective-permute-start(bf16[64,2048]{1,0:T(8,128)(2,1)} %bitcast.38), channel_id=1, source_target_pairs={{8,0},{16,8},{24,16},{9,1},{17,9},{25,17},{10,2},{18,10},{26,18},{... | collective-permute-start | bytes 786440 | tf_op jit(solution)/shard_map/ppermute | solution.py:47
  11.3 7.5 %copy-start.2 = (bf16[64,2048]{1,0:T(8,128)(2,1)}, bf16[64,2048]{1,0:T(8,128)(2,1)S(1)}, u32[]{:S(2)}) copy-start(bf16[64,2048]{1,0:T(8,128)(2,1)S(1)} %collective-permute-done.arrived_f) | copy-start | bytes 786436
  18.8 0.7 copy-start.3
  22.3 6.6 %collective-permute-start.2 = (bf16[24,2048]{1,0:T(8,128)(2,1)}, bf16[24,2048]{1,0:T(8,128)(2,1)S(1)}, u32[]{:S(2)}, u32[]{:S(2)}) collective-permute-start(bf16[24,2048]{1,0:T(8,128)(2,1)} %get-tuple-element.46), channel_id=1, source_target_pairs={{0,1},{1,2},{2,3},{3,4},{4,5},{5,6},{6,7},{7,0},{8,9},{9,10},{10,1... | collective-permute-start | bytes 294920 | tf_op jit(solution)/shard_map/ppermute | solution.py:57
  22.3 8.3 %collective-permute-start.3 = (bf16[24,2048]{1,0:T(8,128)(2,1)}, bf16[24,2048]{1,0:T(8,128)(2,1)S(1)}, u32[]{:S(2)}, u32[]{:S(2)}) collective-permute-start(bf16[24,2048]{1,0:T(8,128)(2,1)} %get-tuple-element.47), channel_id=1, source_target_pairs={{0,2},{1,3},{2,4},{3,5},{4,6},{5,7},{6,0},{7,1},{8,10},{9,11},{10,... | collective-permute-start | bytes 294920 | tf_op jit(solution)/shard_map/ppermute | solution.py:57
  24.0 13.9 %collective-permute-start.4 = (bf16[24,2048]{1,0:T(8,128)(2,1)}, bf16[24,2048]{1,0:T(8,128)(2,1)S(1)}, u32[]{:S(2)}, u32[]{:S(2)}) collective-permute-start(bf16[24,2048]{1,0:T(8,128)(2,1)} %get-tuple-element.48), channel_id=1, source_target_pairs={{0,3},{1,4},{2,5},{3,6},{4,7},{5,0},{6,1},{7,2},{8,11},{9,12},{10,... | collective-permute-start | bytes 294920 | tf_op jit(solution)/shard_map/ppermute | solution.py:57
  26.5 11.6 %collective-permute-start.5 = (bf16[24,2048]{1,0:T(8,128)(2,1)}, bf16[24,2048]{1,0:T(8,128)(2,1)S(1)}, u32[]{:S(2)}, u32[]{:S(2)}) collective-permute-start(bf16[24,2048]{1,0:T(8,128)(2,1)} %get-tuple-element.49), channel_id=1, source_target_pairs={{0,4},{1,5},{2,6},{3,7},{4,0},{5,1},{6,2},{7,3},{8,12},{9,13},{10,... | collective-permute-start | bytes 294920 | tf_op jit(solution)/shard_map/ppermute | solution.py:57
  27.7 10.3 %collective-permute-start.6 = (bf16[24,2048]{1,0:T(8,128)(2,1)}, bf16[24,2048]{1,0:T(8,128)(2,1)S(1)}, u32[]{:S(2)}, u32[]{:S(2)}) collective-permute-start(bf16[24,2048]{1,0:T(8,128)(2,1)} %get-tuple-element.50), channel_id=1, source_target_pairs={{0,5},{1,6},{2,7},{3,0},{4,1},{5,2},{6,3},{7,4},{8,13},{9,14},{10,... | collective-permute-start | bytes 294920 | tf_op jit(solution)/shard_map/ppermute | solution.py:57
  28.9 17.7 %copy-start.11 = (bf16[24,2048]{1,0:T(8,128)(2,1)}, bf16[24,2048]{1,0:T(8,128)(2,1)S(1)}, u32[]{:S(2)}) copy-start(bf16[24,2048]{1,0:T(8,128)(2,1)S(1)} %collective-permute-done.2.refs_1_) | copy-start | bytes 294916
  29.0 9.1 %collective-permute-start.7 = (bf16[24,2048]{1,0:T(8,128)(2,1)}, bf16[24,2048]{1,0:T(8,128)(2,1)S(1)}, u32[]{:S(2)}, u32[]{:S(2)}) collective-permute-start(bf16[24,2048]{1,0:T(8,128)(2,1)} %get-tuple-element.51), channel_id=1, source_target_pairs={{0,6},{1,7},{2,0},{3,1},{4,2},{5,3},{6,4},{7,5},{8,14},{9,15},{10,... | collective-permute-start | bytes 294920 | tf_op jit(solution)/shard_map/ppermute | solution.py:57
  30.7 16.0 %copy-start.12 = (bf16[24,2048]{1,0:T(8,128)(2,1)}, bf16[24,2048]{1,0:T(8,128)(2,1)S(1)}, u32[]{:S(2)}) copy-start(bf16[24,2048]{1,0:T(8,128)(2,1)S(1)} %collective-permute-done.3.refs_2_) | copy-start | bytes 294916
  30.7 7.4 %collective-permute-start.8 = (bf16[24,2048]{1,0:T(8,128)(2,1)}, bf16[24,2048]{1,0:T(8,128)(2,1)S(1)}, u32[]{:S(2)}, u32[]{:S(2)}) collective-permute-start(bf16[24,2048]{1,0:T(8,128)(2,1)} %get-tuple-element.52), channel_id=1, source_target_pairs={{0,7},{1,0},{2,1},{3,2},{4,3},{5,4},{6,5},{7,6},{8,15},{9,8},{10,9... | collective-permute-start | bytes 294920 | tf_op jit(solution)/shard_map/ppermute | solution.py:57
  37.9 8.8 %copy-start.13 = (bf16[24,2048]{1,0:T(8,128)(2,1)}, bf16[24,2048]{1,0:T(8,128)(2,1)S(1)}, u32[]{:S(2)}) copy-start(bf16[24,2048]{1,0:T(8,128)(2,1)S(1)} %collective-permute-done.4.refs_3_) | copy-start | bytes 294916
  38.1 8.6 %copy-start.14 = (bf16[24,2048]{1,0:T(8,128)(2,1)}, bf16[24,2048]{1,0:T(8,128)(2,1)S(1)}, u32[]{:S(2)}) copy-start(bf16[24,2048]{1,0:T(8,128)(2,1)S(1)} %collective-permute-done.5.refs_4_) | copy-start | bytes 294916
  38.1 8.6 %copy-start.15 = (bf16[24,2048]{1,0:T(8,128)(2,1)}, bf16[24,2048]{1,0:T(8,128)(2,1)S(1)}, u32[]{:S(2)}) copy-start(bf16[24,2048]{1,0:T(8,128)(2,1)S(1)} %collective-permute-done.6.refs_5_) | copy-start | bytes 294916
  38.1 8.6 %copy-start.16 = (bf16[24,2048]{1,0:T(8,128)(2,1)}, bf16[24,2048]{1,0:T(8,128)(2,1)S(1)}, u32[]{:S(2)}) copy-start(bf16[24,2048]{1,0:T(8,128)(2,1)S(1)} %collective-permute-done.7.refs_6_) | copy-start | bytes 294916
  38.1 8.6 %copy-start.17 = (bf16[24,2048]{1,0:T(8,128)(2,1)}, bf16[24,2048]{1,0:T(8,128)(2,1)S(1)}, u32[]{:S(2)}) copy-start(bf16[24,2048]{1,0:T(8,128)(2,1)S(1)} %collective-permute-done.8.refs_7_) | copy-start | bytes 294916
  38.1 31.2 %all-to-all-start.1 = ((bf16[8,24,2048]{2,1,0:T(8,128)(2,1)}), bf16[8,24,2048]{2,1,0:T(8,128)(2,1)S(1)}, u32[]{:S(2)}, u32[]{:S(2)}) async-start(bf16[8,24,2048]{2,1,0:T(8,128)(2,1)} %bitcast.30), calls=%async_computation.1 | async-start | bytes 1572864 | tf_op jit(solution)/shard_map/all_to_all | solution.py:53
  69.3 5.1 %copy-start.1 = (bf16[8,24,2048]{2,1,0:T(8,128)(2,1)}, bf16[8,24,2048]{2,1,0:T(8,128)(2,1)S(1)}, u32[]{:S(2)}) copy-start(bf16[8,24,2048]{2,1,0:T(8,128)(2,1)S(1)} %all-to-all-done.1) | copy-start | bytes 2359300
  69.3 38.4 %all-to-all-start = ((bf16[8,24,2176]{2,1,0:T(8,128)(2,1)}), bf16[8,24,2176]{2,1,0:T(8,128)(2,1)S(1)}, u32[]{:S(2)}, u32[]{:S(2)}) async-start(bf16[8,24,2176]{2,1,0:T(8,128)(2,1)} %bitcast.23), calls=%async_computation | async-start | bytes 1671168 | tf_op jit(solution)/shard_map/all_to_all | solution.py:53
  97.2 7.2 %collective-permute-start.9 = (bf16[24,2176]{1,0:T(8,128)(2,1)}, bf16[24,2176]{1,0:T(8,128)(2,1)S(1)}, u32[]{:S(2)}, u32[]{:S(2)}) collective-permute-start(bf16[24,2176]{1,0:T(8,128)(2,1)} %get-tuple-element.69), channel_id=1, source_target_pairs={{0,7},{1,0},{2,1},{3,2},{4,3},{5,4},{6,5},{7,6},{8,15},{9,8},{10,9... | collective-permute-start | bytes 313352 | tf_op jit(solution)/shard_map/ppermute | solution.py:57
  100.7 7.0 %collective-permute-start.10 = (bf16[24,2176]{1,0:T(8,128)(2,1)}, bf16[24,2176]{1,0:T(8,128)(2,1)S(1)}, u32[]{:S(2)}, u32[]{:S(2)}) collective-permute-start(bf16[24,2176]{1,0:T(8,128)(2,1)} %get-tuple-element.70), channel_id=1, source_target_pairs={{0,6},{1,7},{2,0},{3,1},{4,2},{5,3},{6,4},{7,5},{8,14},{9,15},{10,... | collective-permute-start | bytes 313352 | tf_op jit(solution)/shard_map/ppermute | solution.py:57
  101.3 10.2 %collective-permute-start.11 = (bf16[24,2176]{1,0:T(8,128)(2,1)}, bf16[24,2176]{1,0:T(8,128)(2,1)S(1)}, u32[]{:S(2)}, u32[]{:S(2)}) collective-permute-start(bf16[24,2176]{1,0:T(8,128)(2,1)} %get-tuple-element.71), channel_id=1, source_target_pairs={{0,5},{1,6},{2,7},{3,0},{4,1},{5,2},{6,3},{7,4},{8,13},{9,14},{10,... | collective-permute-start | bytes 313352 | tf_op jit(solution)/shard_map/ppermute | solution.py:57
  101.3 17.6 %collective-permute-start.12 = (bf16[24,2176]{1,0:T(8,128)(2,1)}, bf16[24,2176]{1,0:T(8,128)(2,1)S(1)}, u32[]{:S(2)}, u32[]{:S(2)}) collective-permute-start(bf16[24,2176]{1,0:T(8,128)(2,1)} %get-tuple-element.72), channel_id=1, source_target_pairs={{0,4},{1,5},{2,6},{3,7},{4,0},{5,1},{6,2},{7,3},{8,12},{9,13},{10,... | collective-permute-start | bytes 313352 | tf_op jit(solution)/shard_map/ppermute | solution.py:57
  103.7 16.2 %collective-permute-start.13 = (bf16[24,2176]{1,0:T(8,128)(2,1)}, bf16[24,2176]{1,0:T(8,128)(2,1)S(1)}, u32[]{:S(2)}, u32[]{:S(2)}) collective-permute-start(bf16[24,2176]{1,0:T(8,128)(2,1)} %get-tuple-element.73), channel_id=1, source_target_pairs={{0,3},{1,4},{2,5},{3,6},{4,7},{5,0},{6,1},{7,2},{8,11},{9,12},{10,... | collective-permute-start | bytes 313352 | tf_op jit(solution)/shard_map/ppermute | solution.py:57
  104.4 15.6 %copy-start.4 = (bf16[24,2176]{1,0:T(8,128)(2,1)}, bf16[24,2176]{1,0:T(8,128)(2,1)S(1)}, u32[]{:S(2)}) copy-start(bf16[24,2176]{1,0:T(8,128)(2,1)S(1)} %collective-permute-done.9.refs_1_) | copy-start | bytes 313348
  104.4 15.6 %collective-permute-start.14 = (bf16[24,2176]{1,0:T(8,128)(2,1)}, bf16[24,2176]{1,0:T(8,128)(2,1)S(1)}, u32[]{:S(2)}, u32[]{:S(2)}) collective-permute-start(bf16[24,2176]{1,0:T(8,128)(2,1)} %get-tuple-element.74), channel_id=1, source_target_pairs={{0,2},{1,3},{2,4},{3,5},{4,6},{5,7},{6,0},{7,1},{8,10},{9,11},{10,... | collective-permute-start | bytes 313352 | tf_op jit(solution)/shard_map/ppermute | solution.py:57
  107.7 12.3 %copy-start.5 = (bf16[24,2176]{1,0:T(8,128)(2,1)}, bf16[24,2176]{1,0:T(8,128)(2,1)S(1)}, u32[]{:S(2)}) copy-start(bf16[24,2176]{1,0:T(8,128)(2,1)S(1)} %collective-permute-done.10.refs_2_) | copy-start | bytes 313348
  107.7 12.3 %collective-permute-start.15 = (bf16[24,2176]{1,0:T(8,128)(2,1)}, bf16[24,2176]{1,0:T(8,128)(2,1)S(1)}, u32[]{:S(2)}, u32[]{:S(2)}) collective-permute-start(bf16[24,2176]{1,0:T(8,128)(2,1)} %get-tuple-element.75), channel_id=1, source_target_pairs={{0,1},{1,2},{2,3},{3,4},{4,5},{5,6},{6,7},{7,0},{8,9},{9,10},{10,1... | collective-permute-start | bytes 313352 | tf_op jit(solution)/shard_map/ppermute | solution.py:57
  107.7 0.9 copy-start
  111.5 8.5 %copy-start.6 = (bf16[24,2176]{1,0:T(8,128)(2,1)}, bf16[24,2176]{1,0:T(8,128)(2,1)S(1)}, u32[]{:S(2)}) copy-start(bf16[24,2176]{1,0:T(8,128)(2,1)S(1)} %collective-permute-done.11.refs_3_) | copy-start | bytes 313348
  118.9 1.1 copy-start.7
  119.9 0.6 copy-start.8
  119.9 0.7 copy-start.9
  119.9 0.7 copy-start.10

commit v6 on v5

--- a/solution.py
+++ b/solution.py
@@ -45,6 +45,11 @@
     devices = range(lax.axis_size(axis))
     route = [(i - distance, i) for i in devices if i - distance in devices]
     return lax.ppermute(block, axis, route)
+
+
+def rotate(block, axis, distance):
+    size = lax.axis_size(axis)
+    return lax.ppermute(block, axis, [(i, (i + distance) % size) for i in range(size)])
 
 
 def exchange(blocks, direction):
@@ -119,58 +124,66 @@
     return columns[:, 2 + part : 3 + part] + device * sizes["share"]
 
 
-def first_send_kernel(
-    sizes, place, arrived_f, arrived_b, embedded, loss, gain, routes_f, routes_b,
-    columns, tokens, upstream, data, *send,
+def forward_rows_kernel(
+    sizes, place, sent, embedded, gain, routes, columns, tokens, normed, rows
+):
+    chosen = jnp.where(place[0] == place[1], embedded[...], sent[...])
+    tokens[...] = chosen
+    data = normalise(chosen, gain[...])[2]
+    normed[...] = data
+    targets, _ = slot_targets(routes[...], sizes["experts"], sizes["capacity"])
+    keys = keys_of_part(sizes, place[2], columns, 0, sizes["there"][0])
+    rows[...] = dot(sum(tables_of(targets, keys)).astype(BF16), data).astype(BF16)
+
+
+def first_send_kernel(sizes, place, arrived, loss, routes, columns, rows, upstream, *send):
+    experts, capacity = sizes["experts"], sizes["capacity"]
+    chosen = jnp.where(place[0] == place[1], loss[...], arrived[...])
+    upstream[...] = chosen
+    targets, _ = slot_targets(routes[...], experts, capacity)
+    keys = keys_of_part(sizes, place[2], columns, 0, sizes["there"][0])
+    table = sum(tables_of([t + experts * capacity for t in targets], keys)).astype(BF16)
+    parted(rows[...].astype(F32) + dot(table, chosen), send)
+
+
+def later_send_kernel(sizes, place, normed, upstream, routes_f, routes_b, columns, *sends):
+    experts, capacity = sizes["experts"], sizes["capacity"]
+    targets_f, _ = slot_targets(routes_f[...], experts, capacity)
+    targets_b, _ = slot_targets(routes_b[...], experts, capacity)
+    targets_b = [t + experts * capacity for t in targets_b]
+    data = jnp.concatenate([normed[...], upstream[...]], axis=0)
+    for part, there in enumerate(sizes["there"]):
+        if part > 0:
+            keys = keys_of_part(sizes, place[2], columns, part, there)
+            found = [sum(tables_of(targets, keys)) for targets in (targets_f, targets_b)]
+            blocks = sizes["sources"] if there else 1
+            parted(dot(jnp.concatenate(found, axis=1).astype(BF16), data), sends[:blocks])
+            sends = sends[blocks:]
+
+
+def mixing_kernel(
+    sizes, place, normed, saved, router_f, routes_f, gain, router_b, routes_b, columns,
+    shares_b, *refs,
 ):
     experts, capacity = sizes["experts"], sizes["capacity"]
-    count = embedded.shape[0]
-    chosen = jnp.where(place[0] == 0, embedded[...], arrived_f[...])
-    tokens[...] = chosen
-    data[:count, :] = normalise(chosen, gain[...])[2]
-    chosen = jnp.where(place[0] == place[1], loss[...], arrived_b[...])
-    upstream[...] = chosen
-    data[count:, :] = chosen
-    targets_f, _ = slot_targets(routes_f[...], experts, capacity)
-    targets_b, _ = slot_targets(routes_b[...], experts, capacity)
-    keys = keys_of_part(sizes, place[2], columns, 0, sizes["there"][0])
-    table_f = sum(tables_of(targets_f, keys))
-    table_b = sum(tables_of([t + experts * capacity for t in targets_b], keys))
-    table = jnp.concatenate([table_f, table_b], axis=1).astype(BF16)
-    parted(dot(table, data[...]), send)
-
-
-def mixing_kernel(
-    sizes, place, data, saved, gain, router, routes_f, routes_b, columns,
-    mixing_f, mixing_b, tables_b, shares_b, *sends,
-):
-    experts, capacity = sizes["experts"], sizes["capacity"]
-    count = saved.shape[0]
     targets_f, hits = slot_targets(routes_f[...], experts, capacity)
-    shares_f = route_shares(data[:count, :], router[...], hits)
+    shares_f = route_shares(normed[...], router_f[...], hits)
     targets_b, hits = slot_targets(routes_b[...], experts, capacity)
     targets_b = [t + experts * capacity for t in targets_b]
-    _, _, rows = normalise(saved[...], gain[...])
-    own_shares = route_shares(rows, router[...], hits)
+    own_shares = route_shares(normalise(saved[...], gain[...])[2], router_b[...], hits)
     for k, share in enumerate(own_shares):
         shares_b[k] = jnp.broadcast_to(share, shares_b.shape[1:])
-    sends = list(sends)
-    for part in range(mixing_f.shape[0]):
-        there, back = sizes["there"][part], sizes["back"][part]
+    for part, back in enumerate(sizes["back"]):
+        mixing_f, mixing_b, tables_b = refs[3 * part : 3 * part + 3]
         keys = keys_of_part(sizes, place[2], columns, part, back)
         found_f, found_b = tables_of(targets_f, keys), tables_of(targets_b, keys)
-        mixing_f[part] = sum(t * s.astype(BF16).astype(F32) for t, s in zip(found_f, shares_f))
-        mixing_b[part] = sum(t * s.astype(BF16).astype(F32) for t, s in zip(found_b, own_shares))
+        for mixing, found, shares in (
+            (mixing_f, found_f, shares_f), (mixing_b, found_b, own_shares)
+        ):
+            mixed = sum(t * s.astype(BF16).astype(F32) for t, s in zip(found, shares))
+            mixing[...] = jnp.transpose(mixed).astype(BF16)
         for k, table in enumerate(found_b):
-            tables_b[part, k] = table
-        if part > 0:
-            if there != back:
-                keys = keys_of_part(sizes, place[2], columns, part, there)
-                found_f, found_b = tables_of(targets_f, keys), tables_of(targets_b, keys)
-            blocks = sizes["sources"] if there else 1
-            table = jnp.concatenate([sum(found_f), sum(found_b)], axis=1).astype(BF16)
-            parted(dot(table, data[...]), sends[:blocks])
-            sends = sends[blocks:]
+            tables_b[k] = table
 
 
 def expert_kernel(sizes, steps, part, place, columns, lanes, wanted, wanted_lanes, *refs):
@@ -228,57 +241,56 @@
         parted(dot(order, results[...]), out)
 
 
-def add_up(part, blocks, mixing_f, mixing_b, tables):
-    back = joined(blocks)
+def inner_of(back, tables):
     width = back.shape[1] - LANES
     sums = back[:, width:].astype(F32)[:, :1]
-    return (
-        dot(mixing_f[part].astype(BF16), back[:, :width], TN),
-        dot(mixing_b[part].astype(BF16), back[:, :width], TN),
-        [jnp.sum(tables[part, k] * sums, axis=0, keepdims=True) for k in range(tables.shape[1])],
-    )
-
-
-def early_kernel(sizes, tokens, mixing_f, mixing_b, tables, *refs):
-    *backs, output, gradient, inner = refs
-    sum_f, sum_b, sums = tokens[...].astype(F32), None, None
-    for part, turned in enumerate(sizes["back"][:-1]):
+    return [jnp.sum(tables[k] * sums, axis=0, keepdims=True) for k in range(tables.shape[0])]
+
+
+def early_kernel(sizes, tokens, *refs):
+    *refs, output, gradient, inner = refs
+    width = tokens.shape[1]
+    sum_f, sum_b = tokens[...].astype(F32), jnp.zeros(tokens.shape, F32)
+    sums = [jnp.zeros((1, inner.shape[2]), F32)] * inner.shape[0]
+    for turned in sizes["back"][:-1]:
         blocks = sizes["sources"] if turned else 1
-        more_f, more_b, more = add_up(part, backs[:blocks], mixing_f, mixing_b, tables)
-        backs = backs[blocks:]
-        sum_f += more_f
-        sum_b = more_b if sum_b is None else sum_b + more_b
-        sums = more if sums is None else [a + b for a, b in zip(sums, more)]
+        back = joined(refs[3 : 3 + blocks])
+        mixing_f, mixing_b, tables = refs[:3]
+        refs = refs[3 + blocks :]
+        sum_f += dot(mixing_f[...], back[:, :width])
+        sum_b += dot(mixing_b[...], back[:, :width])
+        sums = [a + b for a, b in zip(sums, inner_of(back, tables))]
     output[...] = sum_f
-    if sums is None:
-        gradient[...] = jnp.zeros(gradient.shape, F32)
-        inner[...] = jnp.zeros(inner.shape, F32)
-    else:
-        gradient[...] = sum_b
-        for k, row in enumerate(sums):
-            inner[k] = jnp.broadcast_to(row, inner.shape[1:])
-
-
-def late_kernel(
-    experts, early_f, early_b, early_inner, saved, upstream, gain, router, routes,
-    mixing_f, mixing_b, tables, shares, *refs,
+    gradient[...] = sum_b
+    for k, row in enumerate(sums):
+        inner[k] = jnp.broadcast_to(row, inner.shape[1:])
+
+
+def late_forward_kernel(early, mixing, *refs):
+    *blocks, output = refs
+    output[...] = (
+        early[...] + dot(mixing[...], joined(blocks)[:, : early.shape[1]])
+    ).astype(BF16)
+
+
+def late_backward_kernel(
+    experts, early, early_inner, mixing, tables, saved, upstream, gain, router, routes, shares, *refs
 ):
-    *backs, output, gradient = refs
-    more_f, more_b, more = add_up(mixing_f.shape[0] - 1, backs, mixing_f, mixing_b, tables)
+    *blocks, gradient = refs
+    back = joined(blocks)
     widened = saved[...].astype(F32)
     inv_rms = lax.rsqrt(jnp.mean(widened * widened, axis=-1, keepdims=True) + EPS)
     hits = expert_hits(routes[...], experts)
     top = len(hits)
     share = [shares[k][:1, :] for k in range(top)]
-    inner = [early_inner[k][:1, :] + more[k] for k in range(top)]
+    inner = [early_inner[k][:1, :] + row for k, row in enumerate(inner_of(back, tables))]
     mean = sum(share[k] * inner[k] for k in range(top))
     logit_grad = sum(share[k] * (inner[k] - mean) * hits[k] for k in range(top))
     high = logit_grad.astype(BF16)
     rest = logit_grad - high.astype(F32)
     middle = rest.astype(BF16)
     low = (rest - middle.astype(F32)).astype(BF16)
-    output[0] = (early_f[...] + more_f).astype(BF16)
-    normed_grad = early_b[...] + more_b
+    normed_grad = early[...] + dot(mixing[...], back[:, : early.shape[1]])
     for piece in (high, middle, low):
         normed_grad += dot(piece, router[...], TN)
     gained = normed_grad * gain[...].astype(F32)
@@ -363,41 +375,63 @@
     later = [block for turned in there[1:] for block in blocks_of(turned, width)]
 
     router_t = router[0].T
-    routes_f, routes_b = forward_routes[0].T, backward_routes[0].T
-    arrived_f = from_behind(forward_sent[0], "section", 1)
-    arrived_b = from_behind(backward_sent[0], "section", -1)
-    tokens, upstream, data, *send = call(
-        functools.partial(first_send_kernel, sizes),
+    routes_b = backward_routes[0].T
+    arrived = from_behind(backward_sent[0], "section", -1)
+    routes_f = rotate(forward_routes[0].T, "section", -1)
+    gain_f = rotate(norm_gain, "section", -1)
+    tokens, normed, first_rows = call(
+        functools.partial(forward_rows_kernel, sizes),
         (
             shape((count, width), BF16),
             shape((count, width), BF16),
-            shape((2 * count, width), BF16),
-            *blocks_of(there[0], width),
+            shape((moved, width), BF16),
         ),
-        (4 * moved * count * width, 2 * (8 * count + moved) * width),
+        (2 * moved * count * width, 2 * (4 * count + moved) * width),
+        in_specs=[SMEM] + [VMEM] * 5,
+    )(place, forward_sent[0], embedded, gain_f, routes_f, columns)
+    arrived, first_rows = lax.optimization_barrier((arrived, first_rows))
+    upstream, *send = call(
+        functools.partial(first_send_kernel, sizes),
+        (shape((count, width), BF16), *blocks_of(there[0], width)),
+        (2 * moved * count * width, 2 * (3 * count + 2 * moved) * width),
+        in_specs=[SMEM] + [VMEM] * 5,
+    )(place, arrived, loss_gradient, routes_b, columns, first_rows)
+    sends = []
+    if parts > 1:
+        sends = call(
+            functools.partial(later_send_kernel, sizes),
+            tuple(later),
+            (4 * moved * count * width, 2 * (2 * count + moved) * width),
+            in_specs=[SMEM] + [VMEM] * 5,
+        )(place, normed, upstream, routes_f, routes_b, columns)
+    router_late, _ = lax.optimization_barrier((router_t, send[0]))
+    router_f = rotate(router_late, "section", -1)
+    shares_b, *mixing = call(
+        functools.partial(mixing_kernel, sizes),
+        (
+            shape((top, 8, count), F32),
+            *[
+                shape((count, moved), BF16),
+                shape((count, moved), BF16),
+                shape((top, moved, count), F32),
+            ]
+            * parts,
+        ),
+        (4 * count * width * experts, 2 * (2 * count + 2 * experts) * width),
         in_specs=[SMEM] + [VMEM] * 8,
     )(
-        place, arrived_f, arrived_b, embedded, loss_gradient, norm_gain, routes_f, routes_b, columns
+        place, normed, saved_inputs[0], router_f, routes_f, norm_gain, router_t, routes_b, columns
     )
-    mixing_f, mixing_b, tables_b, shares_b, *sends = call(
-        functools.partial(mixing_kernel, sizes),
-        (
-            shape((parts, moved, count), F32),
-            shape((parts, moved, count), F32),
-            shape((parts, top, moved, count), F32),
-            shape((top, 8, count), F32),
-            *later,
-        ),
-        (4 * moved * count * width, 2 * (4 * count + moved) * width),
-        in_specs=[SMEM] + [VMEM] * 7,
-    )(place, data, saved_inputs[0], norm_gain, router_t, routes_f, routes_b, columns)
+    mixing = [mixing[3 * part : 3 * part + 3] for part in range(parts)]
     saved_pre = jnp.transpose(pre_activation[0], (1, 0, 2, 3)).reshape(local, rows, hidden)
     saved_pre = jnp.pad(saved_pre, ((0, 0), (0, padded - rows), (0, 0)))
     backs = []
     got = exchange(send, 1)
     for part in range(parts):
         if part + 1 < parts:
-            sends, saved_pre, got = lax.optimization_barrier((sends, saved_pre, got))
+            sends, saved_pre, got, mixing = lax.optimization_barrier(
+                (sends, saved_pre, got, mixing)
+            )
             blocks = len(blocks_of(there[part + 1], width))
             coming = exchange(sends[:blocks], 1)
             sends = sends[blocks:]
@@ -429,7 +463,7 @@
         )(place, columns, lanes, wanted, wanted_lanes, *got, saved_pre, up_weight, down_weight)
         backs.append(exchange(list(done), -1))
         got = coming if part + 1 < parts else None
-    early = call(
+    early_f, early_b, early_inner = call(
         functools.partial(early_kernel, sizes),
         (
             shape((count, width), F32),
@@ -437,17 +471,23 @@
             shape((top, 8, count), F32),
         ),
         (4 * moved * count * width, 2 * (5 * count + moved) * width),
-    )(tokens, mixing_f, mixing_b, tables_b, *[block for got in backs[:-1] for block in got])
-    return tuple(
-        call(
-            functools.partial(late_kernel, experts),
-            (shape((1, count, width), BF16),) * 2,
-            (4 * moved * count * width, 2 * (8 * count + moved) * width),
-        )(
-            *early, saved_inputs[0], upstream, norm_gain, router_t, routes_b,
-            mixing_f, mixing_b, tables_b, shares_b, *backs[-1],
-        )
+    )(tokens, *[ref for part in range(parts - 1) for ref in (*mixing[part], *backs[part])])
+    mixing_f, mixing_b, tables_b = mixing[-1]
+    output = call(
+        late_forward_kernel,
+        shape((count, width), BF16),
+        (2 * moved * count * width, 2 * (3 * count + moved) * width),
+    )(early_f, mixing_f, *backs[-1])
+    output = rotate(output, "section", 1)
+    gradient = call(
+        functools.partial(late_backward_kernel, experts),
+        shape((1, count, width), BF16),
+        (2 * moved * count * width, 2 * (7 * count + moved) * width),
+    )(
+        early_b, early_inner, mixing_b, tables_b, saved_inputs[0], upstream, norm_gain, router_t,
+        routes_b, shares_b, *backs[-1],
     )
+    return (output[None], gradient)
 
 
 def solution(mesh):

time: 125 us -> 131 us (1.048)
  Pallas kernels: 57.6 us -> 63.9 us
  waiting for transfers between devices: 24.1 us -> 21.1 us
    ppermute x2 -> x1, waiting for transfers between devices: 11.3 us -> 0.01 us  [from_behind(): return lax.ppermute(block, axis, route)]
    ppermute x0 -> x4, starting transfers between devices: none -> 9.19 us  [rotate(): lax.ppermute(block, axis, [(i, (i + distance) % size) for i in range(size)])]
    ppermute x0 -> x4, waiting for transfers between devices: none -> 6.61 us  [rotate(): lax.ppermute(block, axis, [(i, (i + distance) % size) for i in range(size)])]
    pallas_call x2 -> x5, Pallas kernels: 6.55 us -> 13.1 us  [the longest x1 3.08 us: on_device(): call(functools.partial(late_backward_kernel, experts), shape((1, count, w...]
    ppermute x2 -> x1, starting transfers between devices: 6.15 us -> 1.29 us  [from_behind(): return lax.ppermute(block, axis, route)]
    all_to_all x2, starting transfers between devices: 13.6 us -> 11 us  [exchange(): lax.all_to_all(blocks[0], 'expert', split_axis=0, concat_axis=0, tiled=True)]
    ppermute x14, waiting for transfers between devices: 12.7 us -> 14.5 us  [exchange(): got[d] = lax.ppermute(blocks[d], 'expert', route)]
    unnamed x36 -> x41, local copies, waits for them, and re-layouts: 2.35 us -> 3.64 us
  transfers between devices with their start and end apart: 18 -> 21, of which waited for: 8 -> 8; matrix products, arithmetic and copies ran while one was open for 2% -> 2% of each run, Pallas kernels for 41% -> 45%
where the time goes in v6:
time: 131 us; the launch traced here: 129 us
  Pallas kernels  63.9 us (49%)
  starting transfers between devices  37.2 us (28%)
  waiting for transfers between devices  21.1 us (16%)
  local copies, waits for them, and re-layouts  5.71 us (4%)
    pallas_call x2, Pallas kernels, on_device(): call(functools.partial(expert_kernel, sizes, steps, part), tuple(result),...  45.4 us
    ppermute x14, starting transfers between devices, exchange(): got[d] = lax.ppermute(blocks[d], 'expert', route)  15.7 us
    ppermute x14, waiting for transfers between devices, exchange(): got[d] = lax.ppermute(blocks[d], 'expert', route)  14.5 us
    all_to_all x2, starting transfers between devices, exchange(): lax.all_to_all(blocks[0], 'expert', split_axis=0, concat_axis=0, tiled=True)  11 us
    ppermute x4, starting transfers between devices, rotate(): lax.ppermute(block, axis, [(i, (i + distance) % size) for i in range(size)])  9.19 us
    ppermute x4, waiting for transfers between devices, rotate(): lax.ppermute(block, axis, [(i, (i + distance) % size) for i in range(size)])  6.61 us
    unnamed x41, local copies, waits for them, and re-layouts  3.64 us
    pallas_call x1, Pallas kernels, on_device(): call(functools.partial(late_backward_kernel, experts), shape((1, count, w...  3.08 us
  transfers between devices with their start and end apart: 21, of which 8 were waited for; matrix products, arithmetic and copies ran while one was open for 2% of the time, Pallas kernels for 45%

profile of v6, /device:TPU:0, one launch (start us, length us, event | category | flops | bytes accessed | tf_op | source)
XLA Modules:
  0.0 129.4 jit_solution(18228431897765004349)
XLA Ops:
  0.6 1.3 collective-permute-start.2
  1.9 5.1 %collective-permute-start.1 = (s32[2,64]{1,0:T(2,128)}, s32[2,64]{1,0:T(2,128)S(1)}, u32[]{:S(2)}, u32[]{:S(2)}) collective-permute-start(s32[2,64]{1,0:T(2,128)} %bitcast.41), channel_id=1, source_target_pairs={{0,24},{8,0},{16,8},{24,16},{1,25},{9,1},{17,9},{25,17},{2,26},{10... | collective-permute-start | bytes 1544 | tf_op jit(solution)/shard_map/ppermute | solution.py:52
  7.0 1.4 %collective-permute-start = (bf16[1,2048]{1,0:T(2,128)(2,1)}, bf16[1,2048]{1,0:T(2,128)(2,1)S(1)}, u32[]{:S(2)}, u32[]{:S(2)}) collective-permute-start(bf16[1,2048]{1,0:T(2,128)(2,1)} %gain.3), channel_id=1, source_target_pairs={{0,24},{8,0},{16,8},{24,16},{1,25},{9,1},{17,9},{25,17},{2,26},{10... | collective-permute-start | bytes 12296 | tf_op jit(solution)/shard_map/ppermute | solution.py:52
  8.5 0.7 pad_add_fusion.place
  9.1 3.0 %collective-permute-done.1.routes.routes_f = s32[2,64]{1,0:T(2,128)S(1)} collective-permute-done((s32[2,64]{1,0:T(2,128)}, s32[2,64]{1,0:T(2,128)S(1)}, u32[]{:S(2)}, u32[]{:S(2)}) %collective-permute-start.1) | collective-permute-done | bytes 544 | tf_op jit(solution)/shard_map/ppermute | solution.py:52
  12.1 0.0 collective-permute-done.gain
  12.2 0.5 copy-done.18
  12.7 0.1 copy-done.19
  12.8 2.6 %shard_map.167 = (bf16[64,2048]{1,0:T(8,128)(2,1)}, bf16[64,2048]{1,0:T(8,128)(2,1)}, bf16[192,2048]{1,0:T(8,128)(2,1)}) custom-call(s32[3]{0:T(128)} %pad_add_fusion.place, bf16[64,2048]{1,0:T(8,128)(2,1)} %bitcast.34, bf16[64,2048]{1,0:T(8,128)(2,1)} %embedded.1, bf16[1,2048]{1,0:T(2,128)(2,1)} %copy-done.19, s32[2,64]{1,0:T(2,128)} %copy-done.18, ...), custom_call_target="tpu_custom_call" | custom-call | flops 50331648 | bytes 1835008 | tf_op jit(solution)/shard_map/pallas_call | solution.py:382
  15.3 0.0 collective-permute-done.2.arrived
  15.3 0.7 copy-done.10
  16.0 2.7 %shard_map.168 = (bf16[64,2048]{1,0:T(8,128)(2,1)}, bf16[24,2048]{1,0:T(8,128)(2,1)}, bf16[24,2048]{1,0:T(8,128)(2,1)}, bf16[24,2048]{1,0:T(8,128)(2,1)}, bf16[2...) custom-call(s32[3]{0:T(128)} %pad_add_fusion.place, ...), custom_call_target="tpu_custom_call" | custom-call | flops 50331648 | bytes 2359296 | tf_op jit(solution)/shard_map/pallas_call | solution.py:393
  18.8 1.0 collective-permute-start.10
  19.8 0.0 collective-permute-start.3
  19.8 1.6 %collective-permute-start.4 = (bf16[24,2048]{1,0:T(8,128)(2,1)}, bf16[24,2048]{1,0:T(8,128)(2,1)S(1)}, u32[]{:S(2)}, u32[]{:S(2)}) collective-permute-start(bf16[24,2048]{1,0:T(8,128)(2,1)} %get-tuple-element.59), channel_id=1, source_target_pairs={{0,2},{1,3},{2,4},{3,5},{4,6},{5,7},{6,0},{7,1},{8,10},{9,11},{10,... | collective-permute-start | bytes 294920 | tf_op jit(solution)/shard_map/ppermute | solution.py:62
  21.4 2.6 %collective-permute-start.5 = (bf16[24,2048]{1,0:T(8,128)(2,1)}, bf16[24,2048]{1,0:T(8,128)(2,1)S(1)}, u32[]{:S(2)}, u32[]{:S(2)}) collective-permute-start(bf16[24,2048]{1,0:T(8,128)(2,1)} %get-tuple-element.60), channel_id=1, source_target_pairs={{0,3},{1,4},{2,5},{3,6},{4,7},{5,0},{6,1},{7,2},{8,11},{9,12},{10,... | collective-permute-start | bytes 294920 | tf_op jit(solution)/shard_map/ppermute | solution.py:62
  24.0 1.2 collective-permute-start.6
  25.2 1.2 collective-permute-done.3.refs_1_
  26.5 0.0 collective-permute-start.7
  26.5 1.1 collective-permute-done.4.refs_2_
  27.6 1.7 %collective-permute-start.8 = (bf16[24,2048]{1,0:T(8,128)(2,1)}, bf16[24,2048]{1,0:T(8,128)(2,1)S(1)}, u32[]{:S(2)}, u32[]{:S(2)}) collective-permute-start(bf16[24,2048]{1,0:T(8,128)(2,1)} %get-tuple-element.63), channel_id=1, source_target_pairs={{0,6},{1,7},{2,0},{3,1},{4,2},{5,3},{6,4},{7,5},{8,14},{9,15},{10,... | collective-permute-start | bytes 294920 | tf_op jit(solution)/shard_map/ppermute | solution.py:62
  29.3 0.0 collective-permute-done.10.router_f
  29.3 1.6 %collective-permute-start.9 = (bf16[24,2048]{1,0:T(8,128)(2,1)}, bf16[24,2048]{1,0:T(8,128)(2,1)S(1)}, u32[]{:S(2)}, u32[]{:S(2)}) collective-permute-start(bf16[24,2048]{1,0:T(8,128)(2,1)} %get-tuple-element.64), channel_id=1, source_target_pairs={{0,7},{1,0},{2,1},{3,2},{4,3},{5,4},{6,5},{7,6},{8,15},{9,8},{10,9... | collective-permute-start | bytes 294920 | tf_op jit(solution)/shard_map/ppermute | solution.py:62
  30.9 1.2 copy.19
  32.1 0.9 pad.4.refs_8_.refs_1_
  32.9 2.6 %shard_map.169 = bf16[192,2048]{1,0:T(8,128)(2,1)} custom-call(s32[3]{0:T(128)} %pad_add_fusion.place, bf16[64,2048]{1,0:T(8,128)(2,1)} %get-tuple-element.52.normed, bf16[64,2048]{1,0:T(8,128)(2,1)} %get-tuple-element.56.upstream, s32[2,64]{1,0:T(2,128)} %copy-done.18, s32[2,64]{1,0:T(2,128)} %bitcast.37, s32[192,4]{1,0:T(8,128)} %constant.21.clone.columns), custom_call_target="tpu_custom_call" | custom-call | flops 100663296 | bytes 1310720 | tf_op jit(solution)/shard_map/pallas_call | solution.py:401
  35.5 2.6 %shard_map.170 = (f32[2,8,64]{2,1,0:T(8,128)}, bf16[64,192]{1,0:T(8,128)(2,1)}, bf16[64,192]{1,0:T(8,128)(2,1)}, f32[2,192,64]{2,1,0:T(8,128)}, bf16[64,192]{1,0...) custom-call(s32[3]{0:T(128)} %pad_add_fusion.place, bf16[64,2048]{1,0:T(8,128)(2,1)} %get-tuple-element.52.normed, ...), custom_call_target="tpu_custom_call" | custom-call | flops 33554432 | bytes 1048576 | tf_op jit(solution)/shard_map/pallas_call | solution.py:409
  38.1 0.0 collective-permute-done.5.refs_3_
  38.1 0.0 collective-permute-done.6.refs_4_
  38.1 0.0 collective-permute-done.7.refs_5_
  38.1 0.0 collective-permute-done.8.refs_6_
  38.2 0.0 collective-permute-done.9.refs_7_
  38.2 0.0 copy-start.17
  38.2 5.9 %all-to-all-start.1 = ((bf16[8,24,2048]{2,1,0:T(8,128)(2,1)}), bf16[8,24,2048]{2,1,0:T(8,128)(2,1)S(1)}, u32[]{:S(2)}, u32[]{:S(2)}) async-start(bf16[8,24,2048]{2,1,0:T(8,128)(2,1)} %bitcast.27), calls=%async_computation.1 | async-start | bytes 1572864 | tf_op jit(solution)/shard_map/all_to_all | solution.py:58
  44.2 22.6 %shard_map.171 = bf16[192,2176]{1,0:T(8,128)(2,1)} custom-call(s32[3]{0:T(128)} %pad_add_fusion.place, s32[192,4]{1,0:T(8,128)} %constant.21.clone.columns, s32[4,192]{1,0:T(4,128)} %constant.22.clone.lanes, s32[256,1]{1,0:T(8,128)} %constant.23.clone.wanted, s32[1,256]{1,0:T(1,128)} %constant.24.clone.wanted_lanes, ...), custom_call_target="tpu_custom_call" | custom-call | flops 2147483648 | bytes 33554432 | tf_op jit(solution)/shard_map/pallas_call | solution.py:439
  66.8 0.0 all-to-all-done.1
  66.8 5.1 %all-to-all-start = ((bf16[8,24,2176]{2,1,0:T(8,128)(2,1)}), bf16[8,24,2176]{2,1,0:T(8,128)(2,1)S(1)}, u32[]{:S(2)}, u32[]{:S(2)}) async-start(bf16[8,24,2176]{2,1,0:T(8,128)(2,1)} %bitcast.24), calls=%async_computation | async-start | bytes 1671168 | tf_op jit(solution)/shard_map/all_to_all | solution.py:58
  71.9 0.0 copy-done.1
  71.9 22.8 %shard_map.173 = (bf16[24,2176]{1,0:T(8,128)(2,1)}, bf16[24,2176]{1,0:T(8,128)(2,1)}, bf16[24,2176]{1,0:T(8,128)(2,1)}, bf16[24,2176]{1,0:T(8,128)(2,1)}, bf16[2...) custom-call(s32[3]{0:T(128)} %pad_add_fusion.place, ...), custom_call_target="tpu_custom_call" | custom-call | flops 2147483648 | bytes 33554432 | tf_op jit(solution)/shard_map/pallas_call | solution.py:439
  94.7 3.6 %collective-permute-start.11 = (bf16[24,2176]{1,0:T(8,128)(2,1)}, bf16[24,2176]{1,0:T(8,128)(2,1)S(1)}, u32[]{:S(2)}, u32[]{:S(2)}) collective-permute-start(bf16[24,2176]{1,0:T(8,128)(2,1)} %get-tuple-element.88), channel_id=1, source_target_pairs={{0,7},{1,0},{2,1},{3,2},{4,3},{5,4},{6,5},{7,6},{8,15},{9,8},{10,9... | collective-permute-start | bytes 313352 | tf_op jit(solution)/shard_map/ppermute | solution.py:62
  98.2 0.6 collective-permute-start.12
  98.8 0.0 collective-permute-start.13
  98.8 2.4 %collective-permute-start.14 = (bf16[24,2176]{1,0:T(8,128)(2,1)}, bf16[24,2176]{1,0:T(8,128)(2,1)S(1)}, u32[]{:S(2)}, u32[]{:S(2)}) collective-permute-start(bf16[24,2176]{1,0:T(8,128)(2,1)} %get-tuple-element.91), channel_id=1, source_target_pairs={{0,4},{1,5},{2,6},{3,7},{4,0},{5,1},{6,2},{7,3},{8,12},{9,13},{10,... | collective-permute-start | bytes 313352 | tf_op jit(solution)/shard_map/ppermute | solution.py:62
  101.3 0.0 collective-permute-start.15
  101.3 0.6 collective-permute-done.11.refs_1_
  101.9 0.4 collective-permute-start.16
  102.3 2.9 %collective-permute-done.12.refs_2_ = bf16[24,2176]{1,0:T(8,128)(2,1)S(1)} collective-permute-done((bf16[24,2176]{1,0:T(8,128)(2,1)}, bf16[24,2176]{1,0:T(8,128)(2,1)S(1)}, u32[]{:S(2)}, u32[]{:S(2)}) %collective-permute-start.12) | collective-permute-done | bytes 104480 | tf_op jit(solution)/shard_map/ppermute | solution.py:62
  105.2 0.0 collective-permute-start.17
  105.2 0.0 all-to-all-done
  105.2 0.9 copy-done
  106.2 2.7 %shard_map.172 = (f32[64,2048]{1,0:T(8,128)}, f32[64,2048]{1,0:T(8,128)}, f32[2,8,64]{2,1,0:T(8,128)}) custom-call(bf16[64,2048]{1,0:T(8,128)(2,1)} %get-tuple-element.51.tokens, bf16[64,192]{1,0:T(8,128)(2,1)} %get-tuple-element.72.refs_0_, bf16[64,192]{1,0:T(8,128)(2,1)} %get-tuple-element.73.refs_1_, f32[2,192,64]{2,1,0:T(8,128)} %get-tuple-element.74.refs_2_, ...), custom_call_target="tpu_custom_call" | custom-call | flops 100663296 | bytes 2097152 | tf_op jit(solution)/shard_map/pallas_call | solution.py:466
  108.8 0.0 collective-permute-done.13.refs_3_
  108.8 7.6 %collective-permute-done.14.refs_4_ = bf16[24,2176]{1,0:T(8,128)(2,1)S(1)} collective-permute-done((bf16[24,2176]{1,0:T(8,128)(2,1)}, bf16[24,2176]{1,0:T(8,128)(2,1)S(1)}, u32[]{:S(2)}, u32[]{:S(2)}) %collective-permute-start.14) | collective-permute-done | bytes 104480 | tf_op jit(solution)/shard_map/ppermute | solution.py:62
  116.4 1.0 collective-permute-done.15.refs_5_
  117.5 0.0 collective-permute-done.16.refs_6_
  117.5 0.0 collective-permute-done.17.refs_7_
  117.5 0.6 copy-done.6
  118.1 0.0 copy-done.7
  118.1 0.0 copy-done.8
  118.2 2.3 %shard_map.174 = bf16[64,2048]{1,0:T(8,128)(2,1)} custom-call(f32[64,2048]{1,0:T(8,128)} %get-tuple-element.84.early, bf16[64,192]{1,0:T(8,128)(2,1)} %get-tuple-element.85.mixing, bf16[24,2176]{1,0:T(8,128)(2,1)} %get-tuple-element.87.refs_0_, bf16[24,2176]{1,0:T(8,128)(2,1)} %copy-done.2, bf16[24,2176]{1,0:T(8,128)(2,1)} %copy-done.3, ...), custom_call_target="tpu_custom_call" | custom-call | flops 50331648 | bytes 1572864 | tf_op jit(solution)/shard_map/pallas_call | solution.py:476
  120.5 1.6 %collective-permute-start.18 = (bf16[64,2048]{1,0:T(8,128)(2,1)}, bf16[64,2048]{1,0:T(8,128)(2,1)S(1)}, u32[]{:S(2)}, u32[]{:S(2)}) collective-permute-start(bf16[64,2048]{1,0:T(8,128)(2,1)} %shard_map.174), channel_id=1, source_target_pairs={{0,8},{8,16},{16,24},{24,0},{1,9},{9,17},{17,25},{25,1},{2,10},{10... | collective-permute-start | bytes 786440 | tf_op jit(solution)/shard_map/ppermute | solution.py:52
  122.1 3.1 %shard_map.175 = bf16[1,64,2048]{2,1,0:T(8,128)(2,1)} custom-call(f32[64,2048]{1,0:T(8,128)} %get-tuple-element.95.early, f32[2,8,64]{2,1,0:T(8,128)} %get-tuple-element.96.early_inner, bf16[64,192]{1,0:T(8,128)(2,1)} %get-tuple-element.97.mixing, f32[2,192,64]{2,1,0:T(8,128)} %get-tuple-element.98.tables, bf16[64,2048]{1,0:T(8,128)(2,1)} %bitcast.29, ...), custom_call_target="tpu_custom_call" | custom-call | flops 50331648 | bytes 2621440 | tf_op jit(solution)/shard_map/pallas_call | solution.py:482
  125.2 3.5 %collective-permute-done.18 = bf16[64,2048]{1,0:T(8,128)(2,1)S(1)} collective-permute-done((bf16[64,2048]{1,0:T(8,128)(2,1)}, bf16[64,2048]{1,0:T(8,128)(2,1)S(1)}, u32[]{:S(2)}, u32[]{:S(2)}) %collective-permute-start.18) | collective-permute-done | bytes 262176 | tf_op jit(solution)/shard_map/ppermute | solution.py:52
  128.7 0.7 copy.21
  (31 shorter events, 0.1 us)
Async XLA Ops:
  0.6 14.7 %collective-permute-start.2 = (bf16[64,2048]{1,0:T(8,128)(2,1)}, bf16[64,2048]{1,0:T(8,128)(2,1)S(1)}, u32[]{:S(2)}, u32[]{:S(2)}) collective-permute-start(bf16[64,2048]{1,0:T(8,128)(2,1)} %bitcast.40), channel_id=1, source_target_pairs={{8,0},{16,8},{24,16},{9,1},{17,9},{25,17},{10,2},{18,10},{26,18},{... | collective-permute-start | bytes 786440 | tf_op jit(solution)/shard_map/ppermute | solution.py:47
  1.9 10.2 %collective-permute-start.1 = (s32[2,64]{1,0:T(2,128)}, s32[2,64]{1,0:T(2,128)S(1)}, u32[]{:S(2)}, u32[]{:S(2)}) collective-permute-start(s32[2,64]{1,0:T(2,128)} %bitcast.41), channel_id=1, source_target_pairs={{0,24},{8,0},{16,8},{24,16},{1,25},{9,1},{17,9},{25,17},{2,26},{10... | collective-permute-start | bytes 1544 | tf_op jit(solution)/shard_map/ppermute | solution.py:52
  7.0 5.1 %collective-permute-start = (bf16[1,2048]{1,0:T(2,128)(2,1)}, bf16[1,2048]{1,0:T(2,128)(2,1)S(1)}, u32[]{:S(2)}, u32[]{:S(2)}) collective-permute-start(bf16[1,2048]{1,0:T(2,128)(2,1)} %gain.3), channel_id=1, source_target_pairs={{0,24},{8,0},{16,8},{24,16},{1,25},{9,1},{17,9},{25,17},{2,26},{10... | collective-permute-start | bytes 12296 | tf_op jit(solution)/shard_map/ppermute | solution.py:52
  12.1 0.6 copy-start.18
  12.2 0.6 copy-start.19
  15.3 0.7 copy-start.10
  18.8 10.5 %collective-permute-start.10 = (bf16[64,2048]{1,0:T(8,128)(2,1)}, bf16[64,2048]{1,0:T(8,128)(2,1)S(1)}, u32[]{:S(2)}, u32[]{:S(2)}) collective-permute-start(bf16[64,2048]{1,0:T(8,128)(2,1)} %bitcast.30), channel_id=1, source_target_pairs={{0,24},{8,0},{16,8},{24,16},{1,25},{9,1},{17,9},{25,17},{2,26},{10... | collective-permute-start | bytes 786440 | tf_op jit(solution)/shard_map/ppermute | solution.py:52
  19.8 6.6 %collective-permute-start.3 = (bf16[24,2048]{1,0:T(8,128)(2,1)}, bf16[24,2048]{1,0:T(8,128)(2,1)S(1)}, u32[]{:S(2)}, u32[]{:S(2)}) collective-permute-start(bf16[24,2048]{1,0:T(8,128)(2,1)} %get-tuple-element.58), channel_id=1, source_target_pairs={{0,1},{1,2},{2,3},{3,4},{4,5},{5,6},{6,7},{7,0},{8,9},{9,10},{10,1... | collective-permute-start | bytes 294920 | tf_op jit(solution)/shard_map/ppermute | solution.py:62
  19.8 7.7 %collective-permute-start.4 = (bf16[24,2048]{1,0:T(8,128)(2,1)}, bf16[24,2048]{1,0:T(8,128)(2,1)S(1)}, u32[]{:S(2)}, u32[]{:S(2)}) collective-permute-start(bf16[24,2048]{1,0:T(8,128)(2,1)} %get-tuple-element.59), channel_id=1, source_target_pairs={{0,2},{1,3},{2,4},{3,5},{4,6},{5,7},{6,0},{7,1},{8,10},{9,11},{10,... | collective-permute-start | bytes 294920 | tf_op jit(solution)/shard_map/ppermute | solution.py:62
  21.4 16.7 %collective-permute-start.5 = (bf16[24,2048]{1,0:T(8,128)(2,1)}, bf16[24,2048]{1,0:T(8,128)(2,1)S(1)}, u32[]{:S(2)}, u32[]{:S(2)}) collective-permute-start(bf16[24,2048]{1,0:T(8,128)(2,1)} %get-tuple-element.60), channel_id=1, source_target_pairs={{0,3},{1,4},{2,5},{3,6},{4,7},{5,0},{6,1},{7,2},{8,11},{9,12},{10,... | collective-permute-start | bytes 294920 | tf_op jit(solution)/shard_map/ppermute | solution.py:62
  24.0 14.1 %collective-permute-start.6 = (bf16[24,2048]{1,0:T(8,128)(2,1)}, bf16[24,2048]{1,0:T(8,128)(2,1)S(1)}, u32[]{:S(2)}, u32[]{:S(2)}) collective-permute-start(bf16[24,2048]{1,0:T(8,128)(2,1)} %get-tuple-element.61), channel_id=1, source_target_pairs={{0,4},{1,5},{2,6},{3,7},{4,0},{5,1},{6,2},{7,3},{8,12},{9,13},{10,... | collective-permute-start | bytes 294920 | tf_op jit(solution)/shard_map/ppermute | solution.py:62
  26.5 17.6 %copy-start.11 = (bf16[24,2048]{1,0:T(8,128)(2,1)}, bf16[24,2048]{1,0:T(8,128)(2,1)S(1)}, u32[]{:S(2)}) copy-start(bf16[24,2048]{1,0:T(8,128)(2,1)S(1)} %collective-permute-done.3.refs_1_) | copy-start | bytes 294916
  26.5 11.7 %collective-permute-start.7 = (bf16[24,2048]{1,0:T(8,128)(2,1)}, bf16[24,2048]{1,0:T(8,128)(2,1)S(1)}, u32[]{:S(2)}, u32[]{:S(2)}) collective-permute-start(bf16[24,2048]{1,0:T(8,128)(2,1)} %get-tuple-element.62), channel_id=1, source_target_pairs={{0,5},{1,6},{2,7},{3,0},{4,1},{5,2},{6,3},{7,4},{8,13},{9,14},{10,... | collective-permute-start | bytes 294920 | tf_op jit(solution)/shard_map/ppermute | solution.py:62
  27.6 16.5 %copy-start.12 = (bf16[24,2048]{1,0:T(8,128)(2,1)}, bf16[24,2048]{1,0:T(8,128)(2,1)S(1)}, u32[]{:S(2)}) copy-start(bf16[24,2048]{1,0:T(8,128)(2,1)S(1)} %collective-permute-done.4.refs_2_) | copy-start | bytes 294916
  27.6 10.6 %collective-permute-start.8 = (bf16[24,2048]{1,0:T(8,128)(2,1)}, bf16[24,2048]{1,0:T(8,128)(2,1)S(1)}, u32[]{:S(2)}, u32[]{:S(2)}) collective-permute-start(bf16[24,2048]{1,0:T(8,128)(2,1)} %get-tuple-element.63), channel_id=1, source_target_pairs={{0,6},{1,7},{2,0},{3,1},{4,2},{5,3},{6,4},{7,5},{8,14},{9,15},{10,... | collective-permute-start | bytes 294920 | tf_op jit(solution)/shard_map/ppermute | solution.py:62
  29.3 6.2 %copy-start.9 = (bf16[64,2048]{1,0:T(8,128)(2,1)}, bf16[64,2048]{1,0:T(8,128)(2,1)S(1)}, u32[]{:S(2)}) copy-start(bf16[64,2048]{1,0:T(8,128)(2,1)S(1)} %collective-permute-done.10.router_f) | copy-start | bytes 786436
  29.3 8.9 %collective-permute-start.9 = (bf16[24,2048]{1,0:T(8,128)(2,1)}, bf16[24,2048]{1,0:T(8,128)(2,1)S(1)}, u32[]{:S(2)}, u32[]{:S(2)}) collective-permute-start(bf16[24,2048]{1,0:T(8,128)(2,1)} %get-tuple-element.64), channel_id=1, source_target_pairs={{0,7},{1,0},{2,1},{3,2},{4,3},{5,4},{6,5},{7,6},{8,15},{9,8},{10,9... | collective-permute-start | bytes 294920 | tf_op jit(solution)/shard_map/ppermute | solution.py:62
  38.1 6.0 %copy-start.13 = (bf16[24,2048]{1,0:T(8,128)(2,1)}, bf16[24,2048]{1,0:T(8,128)(2,1)S(1)}, u32[]{:S(2)}) copy-start(bf16[24,2048]{1,0:T(8,128)(2,1)S(1)} %collective-permute-done.5.refs_3_) | copy-start | bytes 294916
  38.1 6.0 %copy-start.14 = (bf16[24,2048]{1,0:T(8,128)(2,1)}, bf16[24,2048]{1,0:T(8,128)(2,1)S(1)}, u32[]{:S(2)}) copy-start(bf16[24,2048]{1,0:T(8,128)(2,1)S(1)} %collective-permute-done.6.refs_4_) | copy-start | bytes 294916
  38.1 6.0 %copy-start.15 = (bf16[24,2048]{1,0:T(8,128)(2,1)}, bf16[24,2048]{1,0:T(8,128)(2,1)S(1)}, u32[]{:S(2)}) copy-start(bf16[24,2048]{1,0:T(8,128)(2,1)S(1)} %collective-permute-done.7.refs_5_) | copy-start | bytes 294916
  38.1 6.0 %copy-start.16 = (bf16[24,2048]{1,0:T(8,128)(2,1)}, bf16[24,2048]{1,0:T(8,128)(2,1)S(1)}, u32[]{:S(2)}) copy-start(bf16[24,2048]{1,0:T(8,128)(2,1)S(1)} %collective-permute-done.8.refs_6_) | copy-start | bytes 294916
  38.2 6.0 %copy-start.17 = (bf16[24,2048]{1,0:T(8,128)(2,1)}, bf16[24,2048]{1,0:T(8,128)(2,1)S(1)}, u32[]{:S(2)}) copy-start(bf16[24,2048]{1,0:T(8,128)(2,1)S(1)} %collective-permute-done.9.refs_7_) | copy-start | bytes 294916
  38.2 28.6 %all-to-all-start.1 = ((bf16[8,24,2048]{2,1,0:T(8,128)(2,1)}), bf16[8,24,2048]{2,1,0:T(8,128)(2,1)S(1)}, u32[]{:S(2)}, u32[]{:S(2)}) async-start(bf16[8,24,2048]{2,1,0:T(8,128)(2,1)} %bitcast.27), calls=%async_computation.1 | async-start | bytes 1572864 | tf_op jit(solution)/shard_map/all_to_all | solution.py:58
  66.8 5.1 %copy-start.1 = (bf16[8,24,2048]{2,1,0:T(8,128)(2,1)}, bf16[8,24,2048]{2,1,0:T(8,128)(2,1)S(1)}, u32[]{:S(2)}) copy-start(bf16[8,24,2048]{2,1,0:T(8,128)(2,1)S(1)} %all-to-all-done.1) | copy-start | bytes 2359300
  66.8 38.4 %all-to-all-start = ((bf16[8,24,2176]{2,1,0:T(8,128)(2,1)}), bf16[8,24,2176]{2,1,0:T(8,128)(2,1)S(1)}, u32[]{:S(2)}, u32[]{:S(2)}) async-start(bf16[8,24,2176]{2,1,0:T(8,128)(2,1)} %bitcast.24), calls=%async_computation | async-start | bytes 1671168 | tf_op jit(solution)/shard_map/all_to_all | solution.py:58
  94.7 7.2 %collective-permute-start.11 = (bf16[24,2176]{1,0:T(8,128)(2,1)}, bf16[24,2176]{1,0:T(8,128)(2,1)S(1)}, u32[]{:S(2)}, u32[]{:S(2)}) collective-permute-start(bf16[24,2176]{1,0:T(8,128)(2,1)} %get-tuple-element.88), channel_id=1, source_target_pairs={{0,7},{1,0},{2,1},{3,2},{4,3},{5,4},{6,5},{7,6},{8,15},{9,8},{10,9... | collective-permute-start | bytes 313352 | tf_op jit(solution)/shard_map/ppermute | solution.py:62
  98.2 7.0 %collective-permute-start.12 = (bf16[24,2176]{1,0:T(8,128)(2,1)}, bf16[24,2176]{1,0:T(8,128)(2,1)S(1)}, u32[]{:S(2)}, u32[]{:S(2)}) collective-permute-start(bf16[24,2176]{1,0:T(8,128)(2,1)} %get-tuple-element.89), channel_id=1, source_target_pairs={{0,6},{1,7},{2,0},{3,1},{4,2},{5,3},{6,4},{7,5},{8,14},{9,15},{10,... | collective-permute-start | bytes 313352 | tf_op jit(solution)/shard_map/ppermute | solution.py:62
  98.8 10.0 %collective-permute-start.13 = (bf16[24,2176]{1,0:T(8,128)(2,1)}, bf16[24,2176]{1,0:T(8,128)(2,1)S(1)}, u32[]{:S(2)}, u32[]{:S(2)}) collective-permute-start(bf16[24,2176]{1,0:T(8,128)(2,1)} %get-tuple-element.90), channel_id=1, source_target_pairs={{0,5},{1,6},{2,7},{3,0},{4,1},{5,2},{6,3},{7,4},{8,13},{9,14},{10,... | collective-permute-start | bytes 313352 | tf_op jit(solution)/shard_map/ppermute | solution.py:62
  98.8 17.6 %collective-permute-start.14 = (bf16[24,2176]{1,0:T(8,128)(2,1)}, bf16[24,2176]{1,0:T(8,128)(2,1)S(1)}, u32[]{:S(2)}, u32[]{:S(2)}) collective-permute-start(bf16[24,2176]{1,0:T(8,128)(2,1)} %get-tuple-element.91), channel_id=1, source_target_pairs={{0,4},{1,5},{2,6},{3,7},{4,0},{5,1},{6,2},{7,3},{8,12},{9,13},{10,... | collective-permute-start | bytes 313352 | tf_op jit(solution)/shard_map/ppermute | solution.py:62
  101.3 16.2 %collective-permute-start.15 = (bf16[24,2176]{1,0:T(8,128)(2,1)}, bf16[24,2176]{1,0:T(8,128)(2,1)S(1)}, u32[]{:S(2)}, u32[]{:S(2)}) collective-permute-start(bf16[24,2176]{1,0:T(8,128)(2,1)} %get-tuple-element.92), channel_id=1, source_target_pairs={{0,3},{1,4},{2,5},{3,6},{4,7},{5,0},{6,1},{7,2},{8,11},{9,12},{10,... | collective-permute-start | bytes 313352 | tf_op jit(solution)/shard_map/ppermute | solution.py:62
  101.9 15.6 %copy-start.2 = (bf16[24,2176]{1,0:T(8,128)(2,1)}, bf16[24,2176]{1,0:T(8,128)(2,1)S(1)}, u32[]{:S(2)}) copy-start(bf16[24,2176]{1,0:T(8,128)(2,1)S(1)} %collective-permute-done.11.refs_1_) | copy-start | bytes 313348
  101.9 15.6 %collective-permute-start.16 = (bf16[24,2176]{1,0:T(8,128)(2,1)}, bf16[24,2176]{1,0:T(8,128)(2,1)S(1)}, u32[]{:S(2)}, u32[]{:S(2)}) collective-permute-start(bf16[24,2176]{1,0:T(8,128)(2,1)} %get-tuple-element.93), channel_id=1, source_target_pairs={{0,2},{1,3},{2,4},{3,5},{4,6},{5,7},{6,0},{7,1},{8,10},{9,11},{10,... | collective-permute-start | bytes 313352 | tf_op jit(solution)/shard_map/ppermute | solution.py:62
  105.2 12.3 %copy-start.3 = (bf16[24,2176]{1,0:T(8,128)(2,1)}, bf16[24,2176]{1,0:T(8,128)(2,1)S(1)}, u32[]{:S(2)}) copy-start(bf16[24,2176]{1,0:T(8,128)(2,1)S(1)} %collective-permute-done.12.refs_2_) | copy-start | bytes 313348
  105.2 12.3 %collective-permute-start.17 = (bf16[24,2176]{1,0:T(8,128)(2,1)}, bf16[24,2176]{1,0:T(8,128)(2,1)S(1)}, u32[]{:S(2)}, u32[]{:S(2)}) collective-permute-start(bf16[24,2176]{1,0:T(8,128)(2,1)} %get-tuple-element.94), channel_id=1, source_target_pairs={{0,1},{1,2},{2,3},{3,4},{4,5},{5,6},{6,7},{7,0},{8,9},{9,10},{10,1... | collective-permute-start | bytes 313352 | tf_op jit(solution)/shard_map/ppermute | solution.py:62
  105.2 0.9 copy-start
  108.8 8.7 %copy-start.4 = (bf16[24,2176]{1,0:T(8,128)(2,1)}, bf16[24,2176]{1,0:T(8,128)(2,1)S(1)}, u32[]{:S(2)}) copy-start(bf16[24,2176]{1,0:T(8,128)(2,1)S(1)} %collective-permute-done.13.refs_3_) | copy-start | bytes 313348
  116.4 1.1 copy-start.5
  117.5 0.6 copy-start.6
  117.5 0.7 copy-start.7
  117.5 0.7 copy-start.8
  120.5 8.3 %collective-permute-start.18 = (bf16[64,2048]{1,0:T(8,128)(2,1)}, bf16[64,2048]{1,0:T(8,128)(2,1)S(1)}, u32[]{:S(2)}, u32[]{:S(2)}) collective-permute-start(bf16[64,2048]{1,0:T(8,128)(2,1)} %shard_map.174), channel_id=1, source_target_pairs={{0,8},{8,16},{16,24},{24,0},{1,9},{9,17},{17,25},{25,1},{2,10},{10... | collective-permute-start | bytes 786440 | tf_op jit(solution)/shard_map/ppermute | solution.py:52

commit v7 on v5

--- a/solution.py
+++ b/solution.py
@@ -33,12 +33,9 @@
     )
 
 
-def full_spec(shape):
-    return pl.BlockSpec(shape, lambda *_: (0,) * len(shape))
-
-
 SMEM = pl.BlockSpec(memory_space=pltpu.SMEM)
 VMEM = pl.BlockSpec(memory_space=pltpu.VMEM)
+HBM = pl.BlockSpec(memory_space=pl.ANY)
 
 
 def from_behind(block, axis, distance):
@@ -119,133 +116,159 @@
     return columns[:, 2 + part : 3 + part] + device * sizes["share"]
 
 
+def rows_to_send(place, arrived_f, arrived_b, embedded, loss, gain):
+    tokens = jnp.where(place[0] == 0, embedded[...], arrived_f[...])
+    upstream = jnp.where(place[0] == place[1], loss[...], arrived_b[...])
+    return tokens, normalise(tokens, gain[...])[2], upstream
+
+
 def first_send_kernel(
-    sizes, place, arrived_f, arrived_b, embedded, loss, gain, routes_f, routes_b,
-    columns, tokens, upstream, data, *send,
+    sizes, place, arrived_f, arrived_b, embedded, loss, gain, routes_f, routes_b, columns, *send
 ):
     experts, capacity = sizes["experts"], sizes["capacity"]
-    count = embedded.shape[0]
-    chosen = jnp.where(place[0] == 0, embedded[...], arrived_f[...])
-    tokens[...] = chosen
-    data[:count, :] = normalise(chosen, gain[...])[2]
-    chosen = jnp.where(place[0] == place[1], loss[...], arrived_b[...])
-    upstream[...] = chosen
-    data[count:, :] = chosen
+    _, normed, upstream = rows_to_send(place, arrived_f, arrived_b, embedded, loss, gain)
     targets_f, _ = slot_targets(routes_f[...], experts, capacity)
     targets_b, _ = slot_targets(routes_b[...], experts, capacity)
     keys = keys_of_part(sizes, place[2], columns, 0, sizes["there"][0])
     table_f = sum(tables_of(targets_f, keys))
     table_b = sum(tables_of([t + experts * capacity for t in targets_b], keys))
     table = jnp.concatenate([table_f, table_b], axis=1).astype(BF16)
-    parted(dot(table, data[...]), send)
+    parted(dot(table, jnp.concatenate([normed, upstream], axis=0)), send)
 
 
 def mixing_kernel(
-    sizes, place, data, saved, gain, router, routes_f, routes_b, columns,
-    mixing_f, mixing_b, tables_b, shares_b, *sends,
+    sizes, place, arrived_f, arrived_b, embedded, loss, gain, routes_f, routes_b, columns,
+    saved, router, tokens, upstream, shares_b, *refs,
 ):
     experts, capacity = sizes["experts"], sizes["capacity"]
-    count = saved.shape[0]
+    parts = len(sizes["back"])
+    mixing, sends = refs[: 3 * parts], refs[3 * parts :]
+    tokens[...], normed, upstream[...] = rows_to_send(
+        place, arrived_f, arrived_b, embedded, loss, gain
+    )
+    data = jnp.concatenate([normed, upstream[...]], axis=0)
     targets_f, hits = slot_targets(routes_f[...], experts, capacity)
-    shares_f = route_shares(data[:count, :], router[...], hits)
+    shares_f = route_shares(normed, router[...], hits)
     targets_b, hits = slot_targets(routes_b[...], experts, capacity)
     targets_b = [t + experts * capacity for t in targets_b]
-    _, _, rows = normalise(saved[...], gain[...])
-    own_shares = route_shares(rows, router[...], hits)
+    own_shares = route_shares(normalise(saved[...], gain[...])[2], router[...], hits)
     for k, share in enumerate(own_shares):
         shares_b[k] = jnp.broadcast_to(share, shares_b.shape[1:])
-    sends = list(sends)
-    for part in range(mixing_f.shape[0]):
+    for part in range(parts):
         there, back = sizes["there"][part], sizes["back"][part]
+        mixing_f, mixing_b, tables_b = mixing[3 * part : 3 * part + 3]
         keys = keys_of_part(sizes, place[2], columns, part, back)
         found_f, found_b = tables_of(targets_f, keys), tables_of(targets_b, keys)
-        mixing_f[part] = sum(t * s.astype(BF16).astype(F32) for t, s in zip(found_f, shares_f))
-        mixing_b[part] = sum(t * s.astype(BF16).astype(F32) for t, s in zip(found_b, own_shares))
+        for out, found, shares in ((mixing_f, found_f, shares_f), (mixing_b, found_b, own_shares)):
+            mixed = sum(t * s.astype(BF16).astype(F32) for t, s in zip(found, shares))
+            out[...] = jnp.transpose(mixed).astype(BF16)
         for k, table in enumerate(found_b):
-            tables_b[part, k] = table
+            tables_b[k] = table
         if part > 0:
             if there != back:
                 keys = keys_of_part(sizes, place[2], columns, part, there)
                 found_f, found_b = tables_of(targets_f, keys), tables_of(targets_b, keys)
             blocks = sizes["sources"] if there else 1
             table = jnp.concatenate([sum(found_f), sum(found_b)], axis=1).astype(BF16)
-            parted(dot(table, data[...]), sends[:blocks])
+            parted(dot(table, data), sends[:blocks])
             sends = sends[blocks:]
 
 
-def expert_kernel(sizes, steps, part, place, columns, lanes, wanted, wanted_lanes, *refs):
+def expert_kernel(
+    sizes, part, held, place, columns, lanes, wanted, wanted_lanes, saved_pre, up, down, *refs
+):
     there, back = sizes["there"][part], sizes["back"][part]
     blocks = sizes["sources"] if there else 1
-    got, (saved_pre, up, down) = refs[:blocks], refs[blocks : blocks + 3]
-    out, (rows, total_f, total_b, inner, results) = refs[blocks + 3 : -5], refs[-5:]
-    expert, step = pl.program_id(0), pl.program_id(1)
-    held = pl.num_programs(0)
+    got, out = refs[:blocks], refs[blocks:-5]
+    rows, results, up_held, down_held, sems = refs[-5:]
     width = rows.shape[1]
+    slots, halves = sems.shape[:2]
+    half = up.shape[2] // halves
     padded, block_rows = sizes["padded"], sizes["block_rows"]
     source = (sizes["sources"], -1)
 
-    @pl.when((expert == 0) & (step == 0))
-    def _():
-        have = partners(place[2], lanes[0:1, :], *source, there) * block_rows + lanes[1:2, :]
-        order = (wanted[...] == have).astype(F32).astype(BF16)
-        rows[...] = dot(order, joined(got)).astype(BF16)
-        results[:, width:] = jnp.zeros((results.shape[0], results.shape[1] - width), BF16)
-
-    own_f = pl.ds(pl.multiple_of(expert * padded, ROWS), padded)
-    own_b = pl.ds(pl.multiple_of((held + expert) * padded, ROWS), padded)
-    pre_act = dot(rows[own_f, :], up[0])
-    hidden_grad = dot(rows[own_b, :], down[0], NT)
-    hidden = (pre_act / (1.0 + jnp.exp(-pre_act))).astype(BF16)
-    pre = saved_pre[0].astype(F32)
-    gate = 1.0 / (1.0 + jnp.exp(-pre))
-    inner_part = jnp.sum(hidden_grad * (pre * gate).astype(BF16).astype(F32), axis=1, keepdims=True)
-    pre_grad = (hidden_grad * gate * (1.0 + pre * (1.0 - gate))).astype(BF16)
-    part_f = dot(hidden, down[0])
-    part_b = dot(pre_grad, up[0], NT)
-
-    @pl.when(step == 0)
-    def _():
-        total_f[...] = part_f
-        total_b[...] = part_b
-        inner[...] = jnp.broadcast_to(inner_part, inner.shape)
-
-    @pl.when(step > 0)
-    def _():
-        total_f[...] += part_f
-        total_b[...] += part_b
-        inner[...] += jnp.broadcast_to(inner_part, inner.shape)
-
-    @pl.when(step == steps - 1)
-    def _():
-        results[own_f, :width] = total_f[...].astype(BF16)
-        results[own_b, :width] = total_b[...].astype(BF16)
-        results[own_b, width:] = inner[...].astype(BF16)
-
-    @pl.when((expert == held - 1) & (step == steps - 1))
-    def _():
-        have = partners(place[2], columns[:, 0:1], *source, back) * block_rows + columns[:, 1:2]
-        order = (have == wanted_lanes[...]).astype(F32).astype(BF16)
-        parted(dot(order, results[...]), out)
-
-
-def add_up(part, blocks, mixing_f, mixing_b, tables):
+    def copies(expert, piece):
+        slot = lax.rem(expert, slots)
+        piece_of = pl.ds(piece * half, half)
+        return [
+            pltpu.make_async_copy(
+                up.at[part * held + expert, :, piece_of],
+                up_held.at[slot, :, piece_of],
+                sems.at[slot, piece, 0],
+            ),
+            pltpu.make_async_copy(
+                down.at[part * held + expert, piece_of, :],
+                down_held.at[slot, piece_of, :],
+                sems.at[slot, piece, 1],
+            ),
+        ]
+
+    for expert in range(min(slots, held)):
+        for piece in range(halves):
+            for copy in copies(jnp.int32(expert), piece):
+                copy.start()
+
+    have = partners(place[2], lanes[0:1, :], *source, there) * block_rows + lanes[1:2, :]
+    order = (wanted[...] == have).astype(F32).astype(BF16)
+    rows[...] = dot(order, joined(got)).astype(BF16)
+    results[:, width:] = jnp.zeros((results.shape[0], results.shape[1] - width), BF16)
+
+    def one_expert(expert, carry):
+        slot = lax.rem(expert, slots)
+        own_f = pl.ds(pl.multiple_of(expert * padded, ROWS), padded)
+        own_b = pl.ds(pl.multiple_of((held + expert) * padded, ROWS), padded)
+        hidden, pre_grad, inner = [], [], 0.0
+        for piece in range(halves):
+            for copy in copies(expert, piece):
+                copy.wait()
+            span = slice(piece * half, (piece + 1) * half)
+            pre_act = dot(rows[own_f, :], up_held[slot, :, span])
+            hidden_grad = dot(rows[own_b, :], down_held[slot, span, :], NT)
+            hidden.append((pre_act / (1.0 + jnp.exp(-pre_act))).astype(BF16))
+            pre = saved_pre[part * held + expert, :, span].astype(F32)
+            gate = 1.0 / (1.0 + jnp.exp(-pre))
+            inner += jnp.sum(
+                hidden_grad * (pre * gate).astype(BF16).astype(F32), axis=1, keepdims=True
+            )
+            pre_grad.append((hidden_grad * gate * (1.0 + pre * (1.0 - gate))).astype(BF16))
+        result_f = dot(jnp.concatenate(hidden, axis=1), down_held[slot])
+        result_b = dot(jnp.concatenate(pre_grad, axis=1), up_held[slot], NT)
+        results[own_f, :width] = result_f.astype(BF16)
+        results[own_b, :width] = result_b.astype(BF16)
+        results[own_b, width:] = jnp.broadcast_to(inner, (padded, LANES)).astype(BF16)
+
+        @pl.when(expert + slots < held)
+        def _():
+            for piece in range(halves):
+                for copy in copies(expert + slots, piece):
+                    copy.start()
+
+        return carry
+
+    lax.fori_loop(0, held, one_expert, 0)
+    have = partners(place[2], columns[:, 0:1], *source, back) * block_rows + columns[:, 1:2]
+    order = (have == wanted_lanes[...]).astype(F32).astype(BF16)
+    parted(dot(order, results[...]), out)
+
+
+def add_up(blocks, mixing_f, mixing_b, tables):
     back = joined(blocks)
     width = back.shape[1] - LANES
     sums = back[:, width:].astype(F32)[:, :1]
     return (
-        dot(mixing_f[part].astype(BF16), back[:, :width], TN),
-        dot(mixing_b[part].astype(BF16), back[:, :width], TN),
-        [jnp.sum(tables[part, k] * sums, axis=0, keepdims=True) for k in range(tables.shape[1])],
-    )
-
-
-def early_kernel(sizes, tokens, mixing_f, mixing_b, tables, *refs):
-    *backs, output, gradient, inner = refs
+        dot(mixing_f[...], back[:, :width]),
+        dot(mixing_b[...], back[:, :width]),
+        [jnp.sum(tables[k] * sums, axis=0, keepdims=True) for k in range(tables.shape[0])],
+    )
+
+
+def early_kernel(sizes, tokens, *refs):
+    *refs, output, gradient, inner = refs
     sum_f, sum_b, sums = tokens[...].astype(F32), None, None
-    for part, turned in enumerate(sizes["back"][:-1]):
+    for turned in sizes["back"][:-1]:
         blocks = sizes["sources"] if turned else 1
-        more_f, more_b, more = add_up(part, backs[:blocks], mixing_f, mixing_b, tables)
-        backs = backs[blocks:]
+        more_f, more_b, more = add_up(refs[3 : 3 + blocks], *refs[:3])
+        refs = refs[3 + blocks :]
         sum_f += more_f
         sum_b = more_b if sum_b is None else sum_b + more_b
         sums = more if sums is None else [a + b for a, b in zip(sums, more)]
@@ -264,7 +287,7 @@
     mixing_f, mixing_b, tables, shares, *refs,
 ):
     *backs, output, gradient = refs
-    more_f, more_b, more = add_up(mixing_f.shape[0] - 1, backs, mixing_f, mixing_b, tables)
+    more_f, more_b, more = add_up(backs, mixing_f, mixing_b, tables)
     widened = saved[...].astype(F32)
     inv_rms = lax.rsqrt(jnp.mean(widened * widened, axis=-1, keepdims=True) + EPS)
     hits = expert_hits(routes[...], experts)
@@ -332,8 +355,6 @@
     slots = experts * capacity
     rows = sources * capacity
     padded = -(-rows // ROWS) * ROWS
-    steps = 2
-    chunk = hidden // steps
     shape = jax.ShapeDtypeStruct
     parts = 2 if local % 2 == 0 else 1
     held = local // parts
@@ -366,31 +387,34 @@
     routes_f, routes_b = forward_routes[0].T, backward_routes[0].T
     arrived_f = from_behind(forward_sent[0], "section", 1)
     arrived_b = from_behind(backward_sent[0], "section", -1)
-    tokens, upstream, data, *send = call(
+    inputs = (
+        place, arrived_f, arrived_b, embedded, loss_gradient, norm_gain, routes_f, routes_b, columns
+    )
+    send = call(
         functools.partial(first_send_kernel, sizes),
+        tuple(blocks_of(there[0], width)),
+        (4 * moved * count * width, 2 * (4 * count + moved) * width),
+        in_specs=[SMEM] + [VMEM] * 8,
+    )(*inputs)
+    tokens, upstream, shares_b, *rest = call(
+        functools.partial(mixing_kernel, sizes),
         (
             shape((count, width), BF16),
             shape((count, width), BF16),
-            shape((2 * count, width), BF16),
-            *blocks_of(there[0], width),
+            shape((top, 8, count), F32),
+            *[
+                shape((count, moved), BF16),
+                shape((count, moved), BF16),
+                shape((top, moved, count), F32),
+            ]
+            * parts,
+            *later,
         ),
         (4 * moved * count * width, 2 * (8 * count + moved) * width),
-        in_specs=[SMEM] + [VMEM] * 8,
-    )(
-        place, arrived_f, arrived_b, embedded, loss_gradient, norm_gain, routes_f, routes_b, columns
-    )
-    mixing_f, mixing_b, tables_b, shares_b, *sends = call(
-        functools.partial(mixing_kernel, sizes),
-        (
-            shape((parts, moved, count), F32),
-            shape((parts, moved, count), F32),
-            shape((parts, top, moved, count), F32),
-            shape((top, 8, count), F32),
-            *later,
-        ),
-        (4 * moved * count * width, 2 * (4 * count + moved) * width),
-        in_specs=[SMEM] + [VMEM] * 7,
-    )(place, data, saved_inputs[0], norm_gain, router_t, routes_f, routes_b, columns)
+        in_specs=[SMEM] + [VMEM] * 10,
+    )(*inputs, saved_inputs[0], router_t)
+    mixing = [rest[3 * part : 3 * part + 3] for part in range(parts)]
+    sends = rest[3 * parts :]
     saved_pre = jnp.transpose(pre_activation[0], (1, 0, 2, 3)).reshape(local, rows, hidden)
     saved_pre = jnp.pad(saved_pre, ((0, 0), (0, padded - rows), (0, 0)))
     backs = []
@@ -403,30 +427,19 @@
             sends = sends[blocks:]
         result = blocks_of(back[part], width + LANES)
         done = call(
-            functools.partial(expert_kernel, sizes, steps, part),
+            functools.partial(expert_kernel, sizes, part, held),
             tuple(result),
             (8 * held * padded * width * hidden, 4 * held * width * hidden),
-            grid=(held, steps),
-            in_specs=[
-                SMEM,
-                full_spec(columns.shape),
-                full_spec(lanes.shape),
-                full_spec(wanted.shape),
-                full_spec(wanted_lanes.shape),
-                *[full_spec(block.shape) for block in got],
-                pl.BlockSpec((1, padded, chunk), lambda e, f, p=part: (p * held + e, 0, f)),
-                pl.BlockSpec((1, width, chunk), lambda e, f, p=part: (p * held + e, 0, f)),
-                pl.BlockSpec((1, chunk, width), lambda e, f, p=part: (p * held + e, f, 0)),
-            ],
-            out_specs=tuple(full_spec(block.shape) for block in result),
+            in_specs=[SMEM] + [VMEM] * 5 + [HBM] * 2 + [VMEM] * len(got),
+            out_specs=(VMEM,) * len(result),
             scratch_shapes=[
                 pltpu.VMEM((2 * held * padded, width), BF16),
-                pltpu.VMEM((padded, width), F32),
-                pltpu.VMEM((padded, width), F32),
-                pltpu.VMEM((padded, LANES), F32),
                 pltpu.VMEM((2 * held * padded, width + LANES), BF16),
+                pltpu.VMEM((min(2, held), width, hidden), BF16),
+                pltpu.VMEM((min(2, held), hidden, width), BF16),
+                pltpu.SemaphoreType.DMA((min(2, held), 2, 2)),
             ],
-        )(place, columns, lanes, wanted, wanted_lanes, *got, saved_pre, up_weight, down_weight)
+        )(place, columns, lanes, wanted, wanted_lanes, saved_pre, up_weight, down_weight, *got)
         backs.append(exchange(list(done), -1))
         got = coming if part + 1 < parts else None
     early = call(
@@ -437,7 +450,7 @@
             shape((top, 8, count), F32),
         ),
         (4 * moved * count * width, 2 * (5 * count + moved) * width),
-    )(tokens, mixing_f, mixing_b, tables_b, *[block for got in backs[:-1] for block in got])
+    )(tokens, *[ref for part in range(parts - 1) for ref in (*mixing[part], *backs[part])])
     return tuple(
         call(
             functools.partial(late_kernel, experts),
@@ -445,7 +458,7 @@
             (4 * moved * count * width, 2 * (8 * count + moved) * width),
         )(
             *early, saved_inputs[0], upstream, norm_gain, router_t, routes_b,
-            mixing_f, mixing_b, tables_b, shares_b, *backs[-1],
+            *mixing[-1], shares_b, *backs[-1],
         )
     )
 

time: 125 us -> 123 us (0.984)
  Pallas kernels: 57.6 us -> 56.2 us
where the time goes in v7:
time: 123 us
  Pallas kernels  56.2 us (46%)
  starting transfers between devices  36.6 us (30%)
  waiting for transfers between devices  24.2 us (20%)
  local copies, waits for them, and re-layouts  4.45 us (4%)
    pallas_call x2, Pallas kernels, on_device(): call(functools.partial(expert_kernel, sizes, part, held), tuple(result),...  44.2 us
    ppermute x14, starting transfers between devices, exchange(): got[d] = lax.ppermute(blocks[d], 'expert', route)  16.8 us
    all_to_all x2, starting transfers between devices, exchange(): lax.all_to_all(blocks[0], 'expert', split_axis=0, concat_axis=0, tiled=True)  13.6 us
    ppermute x14, waiting for transfers between devices, exchange(): got[d] = lax.ppermute(blocks[d], 'expert', route)  12.8 us
    ppermute x2, waiting for transfers between devices, from_behind(): return lax.ppermute(block, axis, route)  11.4 us
    ppermute x2, starting transfers between devices, from_behind(): return lax.ppermute(block, axis, route)  6.15 us
    pallas_call x1, Pallas kernels, on_device(): call(functools.partial(late_kernel, experts), (shape((1, count, width), B...  3.3 us
    pallas_call x1, Pallas kernels, on_device(): call(functools.partial(mixing_kernel, sizes), (shape((count, width), BF16...  3.25 us
  transfers between devices with their start and end apart: 18, of which 8 were waited for; matrix products, arithmetic and copies ran while one was open for 2% of the time, Pallas kernels for 41%

profile of v7, /device:TPU:0, one launch (start us, length us, event | category | flops | bytes accessed | tf_op | source)
XLA Modules:
  0.0 122.8 jit_solution(10256630343889651136)
XLA Ops:
  0.6 4.9 %collective-permute-start = (bf16[64,2048]{1,0:T(8,128)(2,1)}, bf16[64,2048]{1,0:T(8,128)(2,1)S(1)}, u32[]{:S(2)}, u32[]{:S(2)}) collective-permute-start(bf16[64,2048]{1,0:T(8,128)(2,1)} %bitcast.37), channel_id=1, source_target_pairs={{0,8},{8,16},{16,24},{1,9},{9,17},{17,25},{2,10},{10,18},{18,26},{... | collective-permute-start | bytes 786440 | tf_op jit(solution)/shard_map/ppermute | solution.py:44
  5.5 1.3 %collective-permute-start.1 = (bf16[64,2048]{1,0:T(8,128)(2,1)}, bf16[64,2048]{1,0:T(8,128)(2,1)S(1)}, u32[]{:S(2)}, u32[]{:S(2)}) collective-permute-start(bf16[64,2048]{1,0:T(8,128)(2,1)} %bitcast.38), channel_id=1, source_target_pairs={{8,0},{16,8},{24,16},{9,1},{17,9},{25,17},{10,2},{18,10},{26,18},{... | collective-permute-start | bytes 786440 | tf_op jit(solution)/shard_map/ppermute | solution.py:44
  6.8 0.6 pad_add_fusion.place
  7.4 4.0 %collective-permute-done.arrived_f = bf16[64,2048]{1,0:T(8,128)(2,1)S(1)} collective-permute-done((bf16[64,2048]{1,0:T(8,128)(2,1)}, bf16[64,2048]{1,0:T(8,128)(2,1)S(1)}, u32[]{:S(2)}, u32[]{:S(2)}) %collective-permute-start) | collective-permute-done | bytes 262176 | tf_op jit(solution)/shard_map/ppermute | solution.py:44
  11.3 7.5 %collective-permute-done.1.arrived_b = bf16[64,2048]{1,0:T(8,128)(2,1)S(1)} collective-permute-done((bf16[64,2048]{1,0:T(8,128)(2,1)}, bf16[64,2048]{1,0:T(8,128)(2,1)S(1)}, u32[]{:S(2)}, u32[]{:S(2)}) %collective-permute-start.1) | collective-permute-done | bytes 262176 | tf_op jit(solution)/shard_map/ppermute | solution.py:44
  18.8 0.0 copy-done.2
  18.8 0.7 copy-done.3
  19.5 2.8 %shard_map.168 = (bf16[24,2048]{1,0:T(8,128)(2,1)}, bf16[24,2048]{1,0:T(8,128)(2,1)}, bf16[24,2048]{1,0:T(8,128)(2,1)}, bf16[24,2048]{1,0:T(8,128)(2,1)}, bf16[2...) custom-call(s32[3]{0:T(128)} %pad_add_fusion.place, ...), custom_call_target="tpu_custom_call" | custom-call | flops 100663296 | bytes 1835008 | tf_op jit(solution)/shard_map/pallas_call | solution.py:393
  22.3 0.0 collective-permute-start.2
  22.3 1.6 %collective-permute-start.3 = (bf16[24,2048]{1,0:T(8,128)(2,1)}, bf16[24,2048]{1,0:T(8,128)(2,1)S(1)}, u32[]{:S(2)}, u32[]{:S(2)}) collective-permute-start(bf16[24,2048]{1,0:T(8,128)(2,1)} %get-tuple-element.48), channel_id=1, source_target_pairs={{0,2},{1,3},{2,4},{3,5},{4,6},{5,7},{6,0},{7,1},{8,10},{9,11},{10,... | collective-permute-start | bytes 294920 | tf_op jit(solution)/shard_map/ppermute | solution.py:54
  23.9 2.5 %collective-permute-start.4 = (bf16[24,2048]{1,0:T(8,128)(2,1)}, bf16[24,2048]{1,0:T(8,128)(2,1)S(1)}, u32[]{:S(2)}, u32[]{:S(2)}) collective-permute-start(bf16[24,2048]{1,0:T(8,128)(2,1)} %get-tuple-element.49), channel_id=1, source_target_pairs={{0,3},{1,4},{2,5},{3,6},{4,7},{5,0},{6,1},{7,2},{8,11},{9,12},{10,... | collective-permute-start | bytes 294920 | tf_op jit(solution)/shard_map/ppermute | solution.py:54
  26.4 1.2 %collective-permute-start.5 = (bf16[24,2048]{1,0:T(8,128)(2,1)}, bf16[24,2048]{1,0:T(8,128)(2,1)S(1)}, u32[]{:S(2)}, u32[]{:S(2)}) collective-permute-start(bf16[24,2048]{1,0:T(8,128)(2,1)} %get-tuple-element.50), channel_id=1, source_target_pairs={{0,4},{1,5},{2,6},{3,7},{4,0},{5,1},{6,2},{7,3},{8,12},{9,13},{10,... | collective-permute-start | bytes 294920 | tf_op jit(solution)/shard_map/ppermute | solution.py:54
  27.7 1.2 collective-permute-start.6
  28.8 0.0 collective-permute-done.2.refs_1_
  28.9 1.7 %collective-permute-start.7 = (bf16[24,2048]{1,0:T(8,128)(2,1)}, bf16[24,2048]{1,0:T(8,128)(2,1)S(1)}, u32[]{:S(2)}, u32[]{:S(2)}) collective-permute-start(bf16[24,2048]{1,0:T(8,128)(2,1)} %get-tuple-element.52), channel_id=1, source_target_pairs={{0,6},{1,7},{2,0},{3,1},{4,2},{5,3},{6,4},{7,5},{8,14},{9,15},{10,... | collective-permute-start | bytes 294920 | tf_op jit(solution)/shard_map/ppermute | solution.py:54
  30.6 0.0 collective-permute-done.3.refs_2_
  30.6 1.5 %collective-permute-start.8 = (bf16[24,2048]{1,0:T(8,128)(2,1)}, bf16[24,2048]{1,0:T(8,128)(2,1)S(1)}, u32[]{:S(2)}, u32[]{:S(2)}) collective-permute-start(bf16[24,2048]{1,0:T(8,128)(2,1)} %get-tuple-element.53), channel_id=1, source_target_pairs={{0,7},{1,0},{2,1},{3,2},{4,3},{5,4},{6,5},{7,6},{8,15},{9,8},{10,9... | collective-permute-start | bytes 294920 | tf_op jit(solution)/shard_map/ppermute | solution.py:54
  32.1 1.2 copy.19
  33.3 0.9 pad.4.saved_pre
  34.2 3.2 %shard_map.167 = (bf16[64,2048]{1,0:T(8,128)(2,1)}, bf16[64,2048]{1,0:T(8,128)(2,1)}, f32[2,8,64]{2,1,0:T(8,128)}, bf16[64,192]{1,0:T(8,128)(2,1)}, bf16[64,192]...) custom-call(s32[3]{0:T(128)} %pad_add_fusion.place, ...), custom_call_target="tpu_custom_call" | custom-call | flops 100663296 | bytes 2883584 | tf_op jit(solution)/shard_map/pallas_call | solution.py:399
  37.4 0.3 collective-permute-done.4.refs_3_
  37.8 0.2 collective-permute-done.5.refs_4_
  38.0 0.0 collective-permute-done.6.refs_5_
  38.0 0.0 collective-permute-done.7.refs_6_
  38.0 0.0 copy-start.16
  38.0 0.0 collective-permute-done.8.refs_7_
  38.0 0.0 copy-start.17
  38.0 8.5 %all-to-all-start.1 = ((bf16[8,24,2048]{2,1,0:T(8,128)(2,1)}), bf16[8,24,2048]{2,1,0:T(8,128)(2,1)S(1)}, u32[]{:S(2)}, u32[]{:S(2)}) async-start(bf16[8,24,2048]{2,1,0:T(8,128)(2,1)} %bitcast.30), calls=%async_computation.1 | async-start | bytes 1572864 | tf_op jit(solution)/shard_map/all_to_all | solution.py:50
  46.5 0.0 copy-done.11
  46.5 0.0 copy-done.12
  46.5 0.0 copy-done.13
  46.6 0.0 copy-done.14
  46.6 0.0 copy-done.15
  46.6 0.0 copy-done.16
  46.6 0.0 copy-done.17
  46.6 22.1 %shard_map.169 = bf16[192,2176]{1,0:T(8,128)(2,1)} custom-call(s32[3]{0:T(128)} %pad_add_fusion.place, s32[192,4]{1,0:T(8,128)} %constant.21.clone.columns, s32[4,192]{1,0:T(4,128)} %constant.22.clone.lanes, s32[256,1]{1,0:T(8,128)} %constant.23.clone.wanted, s32[1,256]{1,0:T(1,128)} %constant.24.clone.wanted_lanes, bf16[8,32,1024]{2,1,0:T(8,128)(2,1)} %pad.4.saved_pre, ...), custom_call_target="tpu_custom_call" | custom-call | flops 2147483648 | bytes 33554432 | tf_op jit(solution)/shard_map/pallas_call | solution.py:429
  68.7 0.0 all-to-all-done.1
  68.8 0.0 copy-start.1
  68.8 5.1 %all-to-all-start = ((bf16[8,24,2176]{2,1,0:T(8,128)(2,1)}), bf16[8,24,2176]{2,1,0:T(8,128)(2,1)S(1)}, u32[]{:S(2)}, u32[]{:S(2)}) async-start(bf16[8,24,2176]{2,1,0:T(8,128)(2,1)} %bitcast.23), calls=%async_computation | async-start | bytes 1671168 | tf_op jit(solution)/shard_map/all_to_all | solution.py:50
  73.9 0.0 copy-done.1
  73.9 22.1 %shard_map.171 = (bf16[24,2176]{1,0:T(8,128)(2,1)}, bf16[24,2176]{1,0:T(8,128)(2,1)}, bf16[24,2176]{1,0:T(8,128)(2,1)}, bf16[24,2176]{1,0:T(8,128)(2,1)}, bf16[2...) custom-call(s32[3]{0:T(128)} %pad_add_fusion.place, ...), custom_call_target="tpu_custom_call" | custom-call | flops 2147483648 | bytes 33554432 | tf_op jit(solution)/shard_map/pallas_call | solution.py:429
  96.0 3.6 %collective-permute-start.9 = (bf16[24,2176]{1,0:T(8,128)(2,1)}, bf16[24,2176]{1,0:T(8,128)(2,1)S(1)}, u32[]{:S(2)}, u32[]{:S(2)}) collective-permute-start(bf16[24,2176]{1,0:T(8,128)(2,1)} %get-tuple-element.73), channel_id=1, source_target_pairs={{0,7},{1,0},{2,1},{3,2},{4,3},{5,4},{6,5},{7,6},{8,15},{9,8},{10,9... | collective-permute-start | bytes 313352 | tf_op jit(solution)/shard_map/ppermute | solution.py:54
  99.6 0.6 collective-permute-start.10
  100.2 0.0 collective-permute-start.11
  100.2 2.4 %collective-permute-start.12 = (bf16[24,2176]{1,0:T(8,128)(2,1)}, bf16[24,2176]{1,0:T(8,128)(2,1)S(1)}, u32[]{:S(2)}, u32[]{:S(2)}) collective-permute-start(bf16[24,2176]{1,0:T(8,128)(2,1)} %get-tuple-element.76), channel_id=1, source_target_pairs={{0,4},{1,5},{2,6},{3,7},{4,0},{5,1},{6,2},{7,3},{8,12},{9,13},{10,... | collective-permute-start | bytes 313352 | tf_op jit(solution)/shard_map/ppermute | solution.py:54
  102.6 0.0 collective-permute-start.13
  102.6 0.6 collective-permute-done.9.refs_1_
  103.2 0.4 collective-permute-start.14
  103.6 2.9 %collective-permute-done.10.refs_2_ = bf16[24,2176]{1,0:T(8,128)(2,1)S(1)} collective-permute-done((bf16[24,2176]{1,0:T(8,128)(2,1)}, bf16[24,2176]{1,0:T(8,128)(2,1)S(1)}, u32[]{:S(2)}, u32[]{:S(2)}) %collective-permute-start.10) | collective-permute-done | bytes 104480 | tf_op jit(solution)/shard_map/ppermute | solution.py:54
  106.6 0.0 collective-permute-start.15
  106.6 0.0 all-to-all-done
  106.6 0.0 copy-start
  106.6 0.9 copy-done
  107.5 2.7 %shard_map.170 = (f32[64,2048]{1,0:T(8,128)}, f32[64,2048]{1,0:T(8,128)}, f32[2,8,64]{2,1,0:T(8,128)}) custom-call(bf16[64,2048]{1,0:T(8,128)(2,1)} %get-tuple-element.41.tokens, bf16[64,192]{1,0:T(8,128)(2,1)} %get-tuple-element.42.refs_0_, bf16[64,192]{1,0:T(8,128)(2,1)} %get-tuple-element.43.refs_1_, f32[2,192,64]{2,1,0:T(8,128)} %get-tuple-element.44.refs_2_, ...), custom_call_target="tpu_custom_call" | custom-call | flops 100663296 | bytes 2097152 | tf_op jit(solution)/shard_map/pallas_call | solution.py:445
  110.2 0.0 collective-permute-done.11.refs_3_
  110.2 7.6 %collective-permute-done.12.refs_4_ = bf16[24,2176]{1,0:T(8,128)(2,1)S(1)} collective-permute-done((bf16[24,2176]{1,0:T(8,128)(2,1)}, bf16[24,2176]{1,0:T(8,128)(2,1)S(1)}, u32[]{:S(2)}, u32[]{:S(2)}) %collective-permute-start.12) | collective-permute-done | bytes 104480 | tf_op jit(solution)/shard_map/ppermute | solution.py:54
  117.8 1.0 collective-permute-done.13.refs_5_
  118.8 0.0 collective-permute-done.14.refs_6_
  118.8 0.0 collective-permute-done.15.refs_7_
  118.8 0.0 copy-start.10
  118.9 0.6 copy-done.8
  119.4 0.0 copy-done.9
  119.5 0.1 copy-done.10
  119.5 3.3 %shard_map.172 = (bf16[1,64,2048]{2,1,0:T(8,128)(2,1)}, bf16[1,64,2048]{2,1,0:T(8,128)(2,1)}) custom-call(f32[64,2048]{1,0:T(8,128)} %get-tuple-element.63.early_f, f32[64,2048]{1,0:T(8,128)} %get-tuple-element.64.early_b, f32[2,8,64]{2,1,0:T(8,128)} %get-tuple-element.65.early_inner, bf16[64,2048]{1,0:T(8,128)(2,1)} %bitcast.27, ...), custom_call_target="tpu_custom_call" | custom-call | flops 100663296 | bytes 2883584 | tf_op jit(solution)/shard_map/pallas_call | solution.py:455
  (17 shorter events, 0.0 us)
Async XLA Ops:
  0.6 10.7 %collective-permute-start = (bf16[64,2048]{1,0:T(8,128)(2,1)}, bf16[64,2048]{1,0:T(8,128)(2,1)S(1)}, u32[]{:S(2)}, u32[]{:S(2)}) collective-permute-start(bf16[64,2048]{1,0:T(8,128)(2,1)} %bitcast.37), channel_id=1, source_target_pairs={{0,8},{8,16},{16,24},{1,9},{9,17},{17,25},{2,10},{10,18},{18,26},{... | collective-permute-start | bytes 786440 | tf_op jit(solution)/shard_map/ppermute | solution.py:44
  5.5 13.3 %collective-permute-start.1 = (bf16[64,2048]{1,0:T(8,128)(2,1)}, bf16[64,2048]{1,0:T(8,128)(2,1)S(1)}, u32[]{:S(2)}, u32[]{:S(2)}) collective-permute-start(bf16[64,2048]{1,0:T(8,128)(2,1)} %bitcast.38), channel_id=1, source_target_pairs={{8,0},{16,8},{24,16},{9,1},{17,9},{25,17},{10,2},{18,10},{26,18},{... | collective-permute-start | bytes 786440 | tf_op jit(solution)/shard_map/ppermute | solution.py:44
  11.3 7.5 %copy-start.2 = (bf16[64,2048]{1,0:T(8,128)(2,1)}, bf16[64,2048]{1,0:T(8,128)(2,1)S(1)}, u32[]{:S(2)}) copy-start(bf16[64,2048]{1,0:T(8,128)(2,1)S(1)} %collective-permute-done.arrived_f) | copy-start | bytes 786436
  18.8 0.7 copy-start.3
  22.3 6.6 %collective-permute-start.2 = (bf16[24,2048]{1,0:T(8,128)(2,1)}, bf16[24,2048]{1,0:T(8,128)(2,1)S(1)}, u32[]{:S(2)}, u32[]{:S(2)}) collective-permute-start(bf16[24,2048]{1,0:T(8,128)(2,1)} %get-tuple-element.47), channel_id=1, source_target_pairs={{0,1},{1,2},{2,3},{3,4},{4,5},{5,6},{6,7},{7,0},{8,9},{9,10},{10,1... | collective-permute-start | bytes 294920 | tf_op jit(solution)/shard_map/ppermute | solution.py:54
  22.3 8.3 %collective-permute-start.3 = (bf16[24,2048]{1,0:T(8,128)(2,1)}, bf16[24,2048]{1,0:T(8,128)(2,1)S(1)}, u32[]{:S(2)}, u32[]{:S(2)}) collective-permute-start(bf16[24,2048]{1,0:T(8,128)(2,1)} %get-tuple-element.48), channel_id=1, source_target_pairs={{0,2},{1,3},{2,4},{3,5},{4,6},{5,7},{6,0},{7,1},{8,10},{9,11},{10,... | collective-permute-start | bytes 294920 | tf_op jit(solution)/shard_map/ppermute | solution.py:54
  23.9 13.9 %collective-permute-start.4 = (bf16[24,2048]{1,0:T(8,128)(2,1)}, bf16[24,2048]{1,0:T(8,128)(2,1)S(1)}, u32[]{:S(2)}, u32[]{:S(2)}) collective-permute-start(bf16[24,2048]{1,0:T(8,128)(2,1)} %get-tuple-element.49), channel_id=1, source_target_pairs={{0,3},{1,4},{2,5},{3,6},{4,7},{5,0},{6,1},{7,2},{8,11},{9,12},{10,... | collective-permute-start | bytes 294920 | tf_op jit(solution)/shard_map/ppermute | solution.py:54
  26.4 11.6 %collective-permute-start.5 = (bf16[24,2048]{1,0:T(8,128)(2,1)}, bf16[24,2048]{1,0:T(8,128)(2,1)S(1)}, u32[]{:S(2)}, u32[]{:S(2)}) collective-permute-start(bf16[24,2048]{1,0:T(8,128)(2,1)} %get-tuple-element.50), channel_id=1, source_target_pairs={{0,4},{1,5},{2,6},{3,7},{4,0},{5,1},{6,2},{7,3},{8,12},{9,13},{10,... | collective-permute-start | bytes 294920 | tf_op jit(solution)/shard_map/ppermute | solution.py:54
  27.7 10.3 %collective-permute-start.6 = (bf16[24,2048]{1,0:T(8,128)(2,1)}, bf16[24,2048]{1,0:T(8,128)(2,1)S(1)}, u32[]{:S(2)}, u32[]{:S(2)}) collective-permute-start(bf16[24,2048]{1,0:T(8,128)(2,1)} %get-tuple-element.51), channel_id=1, source_target_pairs={{0,5},{1,6},{2,7},{3,0},{4,1},{5,2},{6,3},{7,4},{8,13},{9,14},{10,... | collective-permute-start | bytes 294920 | tf_op jit(solution)/shard_map/ppermute | solution.py:54
  28.9 17.7 %copy-start.11 = (bf16[24,2048]{1,0:T(8,128)(2,1)}, bf16[24,2048]{1,0:T(8,128)(2,1)S(1)}, u32[]{:S(2)}) copy-start(bf16[24,2048]{1,0:T(8,128)(2,1)S(1)} %collective-permute-done.2.refs_1_) | copy-start | bytes 294916
  28.9 9.1 %collective-permute-start.7 = (bf16[24,2048]{1,0:T(8,128)(2,1)}, bf16[24,2048]{1,0:T(8,128)(2,1)S(1)}, u32[]{:S(2)}, u32[]{:S(2)}) collective-permute-start(bf16[24,2048]{1,0:T(8,128)(2,1)} %get-tuple-element.52), channel_id=1, source_target_pairs={{0,6},{1,7},{2,0},{3,1},{4,2},{5,3},{6,4},{7,5},{8,14},{9,15},{10,... | collective-permute-start | bytes 294920 | tf_op jit(solution)/shard_map/ppermute | solution.py:54
  30.6 16.0 %copy-start.12 = (bf16[24,2048]{1,0:T(8,128)(2,1)}, bf16[24,2048]{1,0:T(8,128)(2,1)S(1)}, u32[]{:S(2)}) copy-start(bf16[24,2048]{1,0:T(8,128)(2,1)S(1)} %collective-permute-done.3.refs_2_) | copy-start | bytes 294916
  30.6 7.4 %collective-permute-start.8 = (bf16[24,2048]{1,0:T(8,128)(2,1)}, bf16[24,2048]{1,0:T(8,128)(2,1)S(1)}, u32[]{:S(2)}, u32[]{:S(2)}) collective-permute-start(bf16[24,2048]{1,0:T(8,128)(2,1)} %get-tuple-element.53), channel_id=1, source_target_pairs={{0,7},{1,0},{2,1},{3,2},{4,3},{5,4},{6,5},{7,6},{8,15},{9,8},{10,9... | collective-permute-start | bytes 294920 | tf_op jit(solution)/shard_map/ppermute | solution.py:54
  37.8 8.8 %copy-start.13 = (bf16[24,2048]{1,0:T(8,128)(2,1)}, bf16[24,2048]{1,0:T(8,128)(2,1)S(1)}, u32[]{:S(2)}) copy-start(bf16[24,2048]{1,0:T(8,128)(2,1)S(1)} %collective-permute-done.4.refs_3_) | copy-start | bytes 294916
  38.0 8.6 %copy-start.14 = (bf16[24,2048]{1,0:T(8,128)(2,1)}, bf16[24,2048]{1,0:T(8,128)(2,1)S(1)}, u32[]{:S(2)}) copy-start(bf16[24,2048]{1,0:T(8,128)(2,1)S(1)} %collective-permute-done.5.refs_4_) | copy-start | bytes 294916
  38.0 8.6 %copy-start.15 = (bf16[24,2048]{1,0:T(8,128)(2,1)}, bf16[24,2048]{1,0:T(8,128)(2,1)S(1)}, u32[]{:S(2)}) copy-start(bf16[24,2048]{1,0:T(8,128)(2,1)S(1)} %collective-permute-done.6.refs_5_) | copy-start | bytes 294916
  38.0 8.6 %copy-start.16 = (bf16[24,2048]{1,0:T(8,128)(2,1)}, bf16[24,2048]{1,0:T(8,128)(2,1)S(1)}, u32[]{:S(2)}) copy-start(bf16[24,2048]{1,0:T(8,128)(2,1)S(1)} %collective-permute-done.7.refs_6_) | copy-start | bytes 294916
  38.0 8.6 %copy-start.17 = (bf16[24,2048]{1,0:T(8,128)(2,1)}, bf16[24,2048]{1,0:T(8,128)(2,1)S(1)}, u32[]{:S(2)}) copy-start(bf16[24,2048]{1,0:T(8,128)(2,1)S(1)} %collective-permute-done.8.refs_7_) | copy-start | bytes 294916
  38.0 30.7 %all-to-all-start.1 = ((bf16[8,24,2048]{2,1,0:T(8,128)(2,1)}), bf16[8,24,2048]{2,1,0:T(8,128)(2,1)S(1)}, u32[]{:S(2)}, u32[]{:S(2)}) async-start(bf16[8,24,2048]{2,1,0:T(8,128)(2,1)} %bitcast.30), calls=%async_computation.1 | async-start | bytes 1572864 | tf_op jit(solution)/shard_map/all_to_all | solution.py:50
  68.8 5.1 %copy-start.1 = (bf16[8,24,2048]{2,1,0:T(8,128)(2,1)}, bf16[8,24,2048]{2,1,0:T(8,128)(2,1)S(1)}, u32[]{:S(2)}) copy-start(bf16[8,24,2048]{2,1,0:T(8,128)(2,1)S(1)} %all-to-all-done.1) | copy-start | bytes 2359300
  68.8 37.8 %all-to-all-start = ((bf16[8,24,2176]{2,1,0:T(8,128)(2,1)}), bf16[8,24,2176]{2,1,0:T(8,128)(2,1)S(1)}, u32[]{:S(2)}, u32[]{:S(2)}) async-start(bf16[8,24,2176]{2,1,0:T(8,128)(2,1)} %bitcast.23), calls=%async_computation | async-start | bytes 1671168 | tf_op jit(solution)/shard_map/all_to_all | solution.py:50
  96.0 7.3 %collective-permute-start.9 = (bf16[24,2176]{1,0:T(8,128)(2,1)}, bf16[24,2176]{1,0:T(8,128)(2,1)S(1)}, u32[]{:S(2)}, u32[]{:S(2)}) collective-permute-start(bf16[24,2176]{1,0:T(8,128)(2,1)} %get-tuple-element.73), channel_id=1, source_target_pairs={{0,7},{1,0},{2,1},{3,2},{4,3},{5,4},{6,5},{7,6},{8,15},{9,8},{10,9... | collective-permute-start | bytes 313352 | tf_op jit(solution)/shard_map/ppermute | solution.py:54
  99.6 7.0 %collective-permute-start.10 = (bf16[24,2176]{1,0:T(8,128)(2,1)}, bf16[24,2176]{1,0:T(8,128)(2,1)S(1)}, u32[]{:S(2)}, u32[]{:S(2)}) collective-permute-start(bf16[24,2176]{1,0:T(8,128)(2,1)} %get-tuple-element.74), channel_id=1, source_target_pairs={{0,6},{1,7},{2,0},{3,1},{4,2},{5,3},{6,4},{7,5},{8,14},{9,15},{10,... | collective-permute-start | bytes 313352 | tf_op jit(solution)/shard_map/ppermute | solution.py:54
  100.2 10.0 %collective-permute-start.11 = (bf16[24,2176]{1,0:T(8,128)(2,1)}, bf16[24,2176]{1,0:T(8,128)(2,1)S(1)}, u32[]{:S(2)}, u32[]{:S(2)}) collective-permute-start(bf16[24,2176]{1,0:T(8,128)(2,1)} %get-tuple-element.75), channel_id=1, source_target_pairs={{0,5},{1,6},{2,7},{3,0},{4,1},{5,2},{6,3},{7,4},{8,13},{9,14},{10,... | collective-permute-start | bytes 313352 | tf_op jit(solution)/shard_map/ppermute | solution.py:54
  100.2 17.6 %collective-permute-start.12 = (bf16[24,2176]{1,0:T(8,128)(2,1)}, bf16[24,2176]{1,0:T(8,128)(2,1)S(1)}, u32[]{:S(2)}, u32[]{:S(2)}) collective-permute-start(bf16[24,2176]{1,0:T(8,128)(2,1)} %get-tuple-element.76), channel_id=1, source_target_pairs={{0,4},{1,5},{2,6},{3,7},{4,0},{5,1},{6,2},{7,3},{8,12},{9,13},{10,... | collective-permute-start | bytes 313352 | tf_op jit(solution)/shard_map/ppermute | solution.py:54
  102.6 16.2 %collective-permute-start.13 = (bf16[24,2176]{1,0:T(8,128)(2,1)}, bf16[24,2176]{1,0:T(8,128)(2,1)S(1)}, u32[]{:S(2)}, u32[]{:S(2)}) collective-permute-start(bf16[24,2176]{1,0:T(8,128)(2,1)} %get-tuple-element.77), channel_id=1, source_target_pairs={{0,3},{1,4},{2,5},{3,6},{4,7},{5,0},{6,1},{7,2},{8,11},{9,12},{10,... | collective-permute-start | bytes 313352 | tf_op jit(solution)/shard_map/ppermute | solution.py:54
  103.2 15.6 %copy-start.4 = (bf16[24,2176]{1,0:T(8,128)(2,1)}, bf16[24,2176]{1,0:T(8,128)(2,1)S(1)}, u32[]{:S(2)}) copy-start(bf16[24,2176]{1,0:T(8,128)(2,1)S(1)} %collective-permute-done.9.refs_1_) | copy-start | bytes 313348
  103.2 15.6 %collective-permute-start.14 = (bf16[24,2176]{1,0:T(8,128)(2,1)}, bf16[24,2176]{1,0:T(8,128)(2,1)S(1)}, u32[]{:S(2)}, u32[]{:S(2)}) collective-permute-start(bf16[24,2176]{1,0:T(8,128)(2,1)} %get-tuple-element.78), channel_id=1, source_target_pairs={{0,2},{1,3},{2,4},{3,5},{4,6},{5,7},{6,0},{7,1},{8,10},{9,11},{10,... | collective-permute-start | bytes 313352 | tf_op jit(solution)/shard_map/ppermute | solution.py:54
  106.5 12.3 %copy-start.5 = (bf16[24,2176]{1,0:T(8,128)(2,1)}, bf16[24,2176]{1,0:T(8,128)(2,1)S(1)}, u32[]{:S(2)}) copy-start(bf16[24,2176]{1,0:T(8,128)(2,1)S(1)} %collective-permute-done.10.refs_2_) | copy-start | bytes 313348
  106.6 12.3 %collective-permute-start.15 = (bf16[24,2176]{1,0:T(8,128)(2,1)}, bf16[24,2176]{1,0:T(8,128)(2,1)S(1)}, u32[]{:S(2)}, u32[]{:S(2)}) collective-permute-start(bf16[24,2176]{1,0:T(8,128)(2,1)} %get-tuple-element.79), channel_id=1, source_target_pairs={{0,1},{1,2},{2,3},{3,4},{4,5},{5,6},{6,7},{7,0},{8,9},{9,10},{10,1... | collective-permute-start | bytes 313352 | tf_op jit(solution)/shard_map/ppermute | solution.py:54
  106.6 0.9 copy-start
  110.2 8.7 %copy-start.6 = (bf16[24,2176]{1,0:T(8,128)(2,1)}, bf16[24,2176]{1,0:T(8,128)(2,1)S(1)}, u32[]{:S(2)}) copy-start(bf16[24,2176]{1,0:T(8,128)(2,1)S(1)} %collective-permute-done.11.refs_3_) | copy-start | bytes 313348
  117.8 1.1 copy-start.7
  118.8 0.6 copy-start.8
  118.8 0.7 copy-start.9
  118.8 0.7 copy-start.10

commit v8 on v7

--- a/solution.py
+++ b/solution.py
@@ -13,7 +13,8 @@
 F32 = jnp.float32
 LANES = 128
 ROWS = 16
-VMEM_LIMIT = 60 * 1024 * 1024
+SMALL_VMEM = 16 * 1024 * 1024
+EXPERT_VMEM = 44 * 1024 * 1024
 NT = (((1,), (1,)), ((), ()))
 TN = (((0,), (0,)), ((), ()))
 
@@ -22,12 +23,12 @@
     return lax.dot_general(a, b, dims, preferred_element_type=F32)
 
 
-def call(kernel, out_shape, cost, **kwargs):
+def call(kernel, out_shape, cost, vmem=SMALL_VMEM, **kwargs):
     flops, moved = cost
     return pl.pallas_call(
         kernel,
         out_shape=out_shape,
-        compiler_params=pltpu.CompilerParams(vmem_limit_bytes=VMEM_LIMIT),
+        compiler_params=pltpu.CompilerParams(vmem_limit_bytes=vmem),
         cost_estimate=pl.CostEstimate(flops=flops, bytes_accessed=moved, transcendentals=0),
         **kwargs,
     )
@@ -122,27 +123,34 @@
     return tokens, normalise(tokens, gain[...])[2], upstream
 
 
-def first_send_kernel(
-    sizes, place, arrived_f, arrived_b, embedded, loss, gain, routes_f, routes_b, columns, *send
+def table_kernel(
+    sizes, place, embedded, loss, gain, routes_f, routes_b, columns,
+    table, embedded_out, loss_out, gain_out,
 ):
     experts, capacity = sizes["experts"], sizes["capacity"]
-    _, normed, upstream = rows_to_send(place, arrived_f, arrived_b, embedded, loss, gain)
     targets_f, _ = slot_targets(routes_f[...], experts, capacity)
     targets_b, _ = slot_targets(routes_b[...], experts, capacity)
     keys = keys_of_part(sizes, place[2], columns, 0, sizes["there"][0])
     table_f = sum(tables_of(targets_f, keys))
     table_b = sum(tables_of([t + experts * capacity for t in targets_b], keys))
-    table = jnp.concatenate([table_f, table_b], axis=1).astype(BF16)
-    parted(dot(table, jnp.concatenate([normed, upstream], axis=0)), send)
+    table[...] = jnp.concatenate([table_f, table_b], axis=1).astype(BF16)
+    embedded_out[...] = embedded[...]
+    loss_out[...] = loss[...]
+    gain_out[...] = gain[...]
+
+
+def first_send_kernel(place, arrived_f, arrived_b, embedded, loss, gain, table, *send):
+    _, normed, upstream = rows_to_send(place, arrived_f, arrived_b, embedded, loss, gain)
+    parted(dot(table[...], jnp.concatenate([normed, upstream], axis=0)), send)
 
 
 def mixing_kernel(
     sizes, place, arrived_f, arrived_b, embedded, loss, gain, routes_f, routes_b, columns,
-    saved, router, tokens, upstream, shares_b, *refs,
+    lanes, wanted, wanted_lanes, saved, router, tokens, upstream, shares_b, *refs,
 ):
     experts, capacity = sizes["experts"], sizes["capacity"]
     parts = len(sizes["back"])
-    mixing, sends = refs[: 3 * parts], refs[3 * parts :]
+    mixing, orders, sends = refs[: 3 * parts], refs[3 * parts : 5 * parts], refs[5 * parts :]
     tokens[...], normed, upstream[...] = rows_to_send(
         place, arrived_f, arrived_b, embedded, loss, gain
     )
@@ -164,6 +172,12 @@
             out[...] = jnp.transpose(mixed).astype(BF16)
         for k, table in enumerate(found_b):
             tables_b[k] = table
+        source = (sizes["sources"], -1)
+        have = partners(place[2], lanes[0:1, :], *source, there) * sizes["block_rows"] + lanes[1:2, :]
+        orders[2 * part][...] = (wanted[...] == have).astype(F32).astype(BF16)
+        have = partners(place[2], columns[:, 0:1], *source, back) * sizes["block_rows"]
+        have += columns[:, 1:2]
+        orders[2 * part + 1][...] = (have == wanted_lanes[...]).astype(F32).astype(BF16)
         if part > 0:
             if there != back:
                 keys = keys_of_part(sizes, place[2], columns, part, there)
@@ -174,18 +188,14 @@
             sends = sends[blocks:]
 
 
-def expert_kernel(
-    sizes, part, held, place, columns, lanes, wanted, wanted_lanes, saved_pre, up, down, *refs
-):
-    there, back = sizes["there"][part], sizes["back"][part]
-    blocks = sizes["sources"] if there else 1
+def expert_kernel(sizes, part, held, order, back_order, saved_pre, up, down, *refs):
+    blocks = sizes["sources"] if sizes["there"][part] else 1
     got, out = refs[:blocks], refs[blocks:-5]
     rows, results, up_held, down_held, sems = refs[-5:]
     width = rows.shape[1]
     slots, halves = sems.shape[:2]
     half = up.shape[2] // halves
-    padded, block_rows = sizes["padded"], sizes["block_rows"]
-    source = (sizes["sources"], -1)
+    padded = sizes["padded"]
 
     def copies(expert, piece):
         slot = lax.rem(expert, slots)
@@ -208,9 +218,7 @@
             for copy in copies(jnp.int32(expert), piece):
                 copy.start()
 
-    have = partners(place[2], lanes[0:1, :], *source, there) * block_rows + lanes[1:2, :]
-    order = (wanted[...] == have).astype(F32).astype(BF16)
-    rows[...] = dot(order, joined(got)).astype(BF16)
+    rows[...] = dot(order[...], joined(got)).astype(BF16)
     results[:, width:] = jnp.zeros((results.shape[0], results.shape[1] - width), BF16)
 
     def one_expert(expert, carry):
@@ -246,9 +254,7 @@
         return carry
 
     lax.fori_loop(0, held, one_expert, 0)
-    have = partners(place[2], columns[:, 0:1], *source, back) * block_rows + columns[:, 1:2]
-    order = (have == wanted_lanes[...]).astype(F32).astype(BF16)
-    parted(dot(order, results[...]), out)
+    parted(dot(back_order[...], results[...]), out)
 
 
 def add_up(blocks, mixing_f, mixing_b, tables):
@@ -262,8 +268,11 @@
     )
 
 
-def early_kernel(sizes, tokens, *refs):
-    *refs, output, gradient, inner = refs
+def early_kernel(sizes, handed, tokens, *refs):
+    output, gradient, inner, *copies = refs[-3 - handed :]
+    for given, copied in zip(refs, copies):
+        copied[...] = given[...]
+    refs = refs[handed : -3 - handed]
     sum_f, sum_b, sums = tokens[...].astype(F32), None, None
     for turned in sizes["back"][:-1]:
         blocks = sizes["sources"] if turned else 1
@@ -387,34 +396,47 @@
     routes_f, routes_b = forward_routes[0].T, backward_routes[0].T
     arrived_f = from_behind(forward_sent[0], "section", 1)
     arrived_b = from_behind(backward_sent[0], "section", -1)
-    inputs = (
-        place, arrived_f, arrived_b, embedded, loss_gradient, norm_gain, routes_f, routes_b, columns
-    )
+    row_shape = shape((count, width), BF16)
+    table, embedded_held, loss_held, gain_held = call(
+        functools.partial(table_kernel, sizes),
+        (shape((moved, 2 * count), BF16), row_shape, row_shape, shape((1, width), BF16)),
+        (4 * moved * count, 4 * (2 * count + moved) * width),
+        in_specs=[SMEM] + [VMEM] * 6,
+    )(place, embedded, loss_gradient, norm_gain, routes_f, routes_b, columns)
+    given = (place, arrived_f, arrived_b, embedded_held, loss_held, gain_held)
     send = call(
-        functools.partial(first_send_kernel, sizes),
+        first_send_kernel,
         tuple(blocks_of(there[0], width)),
         (4 * moved * count * width, 2 * (4 * count + moved) * width),
-        in_specs=[SMEM] + [VMEM] * 8,
-    )(*inputs)
+        in_specs=[SMEM] + [VMEM] * 6,
+    )(*given, table)
+    mixing_shapes = [
+        shape((count, moved), BF16),
+        shape((count, moved), BF16),
+        shape((top, moved, count), F32),
+    ]
+    order_shapes = [
+        shape((2 * held * padded, moved), BF16),
+        shape((moved, 2 * held * padded), BF16),
+    ]
     tokens, upstream, shares_b, *rest = call(
         functools.partial(mixing_kernel, sizes),
         (
-            shape((count, width), BF16),
-            shape((count, width), BF16),
+            row_shape,
+            row_shape,
             shape((top, 8, count), F32),
-            *[
-                shape((count, moved), BF16),
-                shape((count, moved), BF16),
-                shape((top, moved, count), F32),
-            ]
-            * parts,
+            *mixing_shapes * parts,
+            *order_shapes * parts,
             *later,
         ),
         (4 * moved * count * width, 2 * (8 * count + moved) * width),
-        in_specs=[SMEM] + [VMEM] * 10,
-    )(*inputs, saved_inputs[0], router_t)
+        in_specs=[SMEM] + [VMEM] * 13,
+    )(
+        *given, routes_f, routes_b, columns, lanes, wanted, wanted_lanes, saved_inputs[0], router_t
+    )
     mixing = [rest[3 * part : 3 * part + 3] for part in range(parts)]
-    sends = rest[3 * parts :]
+    orders = [rest[3 * parts + 2 * part : 3 * parts + 2 * part + 2] for part in range(parts)]
+    sends = rest[5 * parts :]
     saved_pre = jnp.transpose(pre_activation[0], (1, 0, 2, 3)).reshape(local, rows, hidden)
     saved_pre = jnp.pad(saved_pre, ((0, 0), (0, padded - rows), (0, 0)))
     backs = []
@@ -430,7 +452,8 @@
             functools.partial(expert_kernel, sizes, part, held),
             tuple(result),
             (8 * held * padded * width * hidden, 4 * held * width * hidden),
-            in_specs=[SMEM] + [VMEM] * 5 + [HBM] * 2 + [VMEM] * len(got),
+            vmem=EXPERT_VMEM,
+            in_specs=[VMEM] * 3 + [HBM] * 2 + [VMEM] * len(got),
             out_specs=(VMEM,) * len(result),
             scratch_shapes=[
                 pltpu.VMEM((2 * held * padded, width), BF16),
@@ -439,27 +462,28 @@
                 pltpu.VMEM((min(2, held), hidden, width), BF16),
                 pltpu.SemaphoreType.DMA((min(2, held), 2, 2)),
             ],
-        )(place, columns, lanes, wanted, wanted_lanes, saved_pre, up_weight, down_weight, *got)
+        )(*orders[part], saved_pre, up_weight, down_weight, *got)
         backs.append(exchange(list(done), -1))
         got = coming if part + 1 < parts else None
+    handed = (
+        saved_inputs[0], upstream, norm_gain, router_t, routes_b, *mixing[-1], shares_b,
+    )
     early = call(
-        functools.partial(early_kernel, sizes),
+        functools.partial(early_kernel, sizes, len(handed)),
         (
             shape((count, width), F32),
             shape((count, width), F32),
             shape((top, 8, count), F32),
+            *[shape(array.shape, array.dtype) for array in handed],
         ),
-        (4 * moved * count * width, 2 * (5 * count + moved) * width),
-    )(tokens, *[ref for part in range(parts - 1) for ref in (*mixing[part], *backs[part])])
+        (4 * moved * count * width, 2 * (10 * count + moved) * width),
+    )(tokens, *handed, *[ref for part in range(parts - 1) for ref in (*mixing[part], *backs[part])])
     return tuple(
         call(
             functools.partial(late_kernel, experts),
             (shape((1, count, width), BF16),) * 2,
             (4 * moved * count * width, 2 * (8 * count + moved) * width),
-        )(
-            *early, saved_inputs[0], upstream, norm_gain, router_t, routes_b,
-            *mixing[-1], shares_b, *backs[-1],
-        )
+        )(*early, *backs[-1])
     )
 
 

time: 123 us -> 125 us (1.016)
  local copies, waits for them, and re-layouts: 4.45 us -> 27.8 us
  Pallas kernels: 56.2 us -> 47.8 us
  waiting for transfers between devices: 24.2 us -> 16 us
  starting transfers between devices: 36.6 us -> 31.8 us
    unnamed x36 -> x74, local copies, waits for them, and re-layouts: 2.37 us -> 26.6 us
    ppermute x2, waiting for transfers between devices: 11.4 us -> 6.25 us  [from_behind(): return lax.ppermute(block, axis, route)]
    all_to_all x2, starting transfers between devices: 13.6 us -> 8.6 us  [exchange(): lax.all_to_all(blocks[0], 'expert', split_axis=0, concat_axis=0, tiled=True)]
    pallas_call x3 -> x4, Pallas kernels: 8.67 us -> 4.81 us  [the longest x1 2.47 us: on_device(): call(functools.partial(mixing_kernel, sizes), (row_shape, row_shape, shap...]
    ppermute x14, waiting for transfers between devices: 12.8 us -> 9.7 us  [exchange(): got[d] = lax.ppermute(blocks[d], 'expert', route)]
    pallas_call x2, Pallas kernels: 44.2 us -> 41.4 us  [on_device(): call(functools.partial(expert_kernel, sizes, part, held), tuple(result),...]
    pallas_call x1, Pallas kernels: 3.3 us -> 1.54 us  [on_device(): call(functools.partial(late_kernel, experts), (shape((1, count, width), B...]
  transfers between devices with their start and end apart: 18 -> 18, of which waited for: 8 -> 5; matrix products, arithmetic and copies ran while one was open for 2% -> 1% of each run, Pallas kernels for 41% -> 36%
where the time goes in v8:
time: 125 us; the launch traced here: 124 us
  Pallas kernels  47.8 us (38%)
  starting transfers between devices  31.8 us (25%)
  local copies, waits for them, and re-layouts  27.8 us (22%)
  waiting for transfers between devices  16 us (13%)
    pallas_call x2, Pallas kernels, on_device(): call(functools.partial(expert_kernel, sizes, part, held), tuple(result),...  41.4 us
    unnamed x74, local copies, waits for them, and re-layouts  26.6 us
    ppermute x14, starting transfers between devices, exchange(): got[d] = lax.ppermute(blocks[d], 'expert', route)  17 us
    ppermute x14, waiting for transfers between devices, exchange(): got[d] = lax.ppermute(blocks[d], 'expert', route)  9.7 us
    all_to_all x2, starting transfers between devices, exchange(): lax.all_to_all(blocks[0], 'expert', split_axis=0, concat_axis=0, tiled=True)  8.6 us
    ppermute x2, waiting for transfers between devices, from_behind(): return lax.ppermute(block, axis, route)  6.25 us
    ppermute x2, starting transfers between devices, from_behind(): return lax.ppermute(block, axis, route)  6.15 us
  transfers between devices with their start and end apart: 18, of which 5 were waited for; matrix products, arithmetic and copies ran while one was open for 1% of the time, Pallas kernels for 36%

profile of v8, /device:TPU:0, one launch (start us, length us, event | category | flops | bytes accessed | tf_op | source)
XLA Modules:
  0.0 124.3 jit_solution(10264848745076140725)
XLA Ops:
  0.6 4.9 %collective-permute-start = (bf16[64,2048]{1,0:T(8,128)(2,1)}, bf16[64,2048]{1,0:T(8,128)(2,1)S(1)}, u32[]{:S(2)}, u32[]{:S(2)}) collective-permute-start(bf16[64,2048]{1,0:T(8,128)(2,1)} %bitcast.35), channel_id=1, source_target_pairs={{0,8},{8,16},{16,24},{1,9},{9,17},{17,25},{2,10},{10,18},{18,26},{... | collective-permute-start | bytes 786440 | tf_op jit(solution)/shard_map/ppermute | solution.py:45
  5.5 1.3 %collective-permute-start.1 = (bf16[64,2048]{1,0:T(8,128)(2,1)}, bf16[64,2048]{1,0:T(8,128)(2,1)S(1)}, u32[]{:S(2)}, u32[]{:S(2)}) collective-permute-start(bf16[64,2048]{1,0:T(8,128)(2,1)} %bitcast.36), channel_id=1, source_target_pairs={{8,0},{16,8},{24,16},{9,1},{17,9},{25,17},{10,2},{18,10},{26,18},{... | collective-permute-start | bytes 786440 | tf_op jit(solution)/shard_map/ppermute | solution.py:45
  6.8 0.1 pad_add_fusion.place
  6.9 0.9 copy-done.4
  7.8 0.9 copy-done.6
  8.7 0.9 copy-done.7
  9.7 0.7 copy-done.27
  10.4 0.7 copy-done.29
  11.1 0.7 copy-done.34
  11.7 0.8 shard_map.167
  12.6 6.2 %collective-permute-done.1.arrived_b = bf16[64,2048]{1,0:T(8,128)(2,1)S(1)} collective-permute-done((bf16[64,2048]{1,0:T(8,128)(2,1)}, bf16[64,2048]{1,0:T(8,128)(2,1)S(1)}, u32[]{:S(2)}, u32[]{:S(2)}) %collective-permute-start.1) | collective-permute-done | bytes 262176 | tf_op jit(solution)/shard_map/ppermute | solution.py:45
  18.8 1.1 shard_map.169
  19.9 0.1 collective-permute-start.2
  19.9 1.6 %collective-permute-start.3 = (bf16[24,2048]{1,0:T(8,128)(2,1)S(1)}, bf16[24,2048]{1,0:T(8,128)(2,1)S(1)}, u32[]{:S(2)}, u32[]{:S(2)}) collective-permute-start(bf16[24,2048]{1,0:T(8,128)(2,1)S(1)} %get-tuple-element.76), channel_id=1, source_target_pairs={{0,2},{1,3},{2,4},{3,5},{4,6},{5,7},{6,0},{7,1},{8,10},{9,11},{10,... | collective-permute-start | bytes 294920 | tf_op jit(solution)/shard_map/ppermute | solution.py:55
  21.6 2.5 %collective-permute-start.4 = (bf16[24,2048]{1,0:T(8,128)(2,1)S(1)}, bf16[24,2048]{1,0:T(8,128)(2,1)S(1)}, u32[]{:S(2)}, u32[]{:S(2)}) collective-permute-start(bf16[24,2048]{1,0:T(8,128)(2,1)S(1)} %get-tuple-element.77), channel_id=1, source_target_pairs={{0,3},{1,4},{2,5},{3,6},{4,7},{5,0},{6,1},{7,2},{8,11},{9,12},{10,... | collective-permute-start | bytes 294920 | tf_op jit(solution)/shard_map/ppermute | solution.py:55
  24.1 1.2 collective-permute-start.5
  25.3 1.2 collective-permute-start.6
  26.5 1.5 %collective-permute-start.7 = (bf16[24,2048]{1,0:T(8,128)(2,1)S(1)}, bf16[24,2048]{1,0:T(8,128)(2,1)S(1)}, u32[]{:S(2)}, u32[]{:S(2)}) collective-permute-start(bf16[24,2048]{1,0:T(8,128)(2,1)S(1)} %get-tuple-element.80), channel_id=1, source_target_pairs={{0,6},{1,7},{2,0},{3,1},{4,2},{5,3},{6,4},{7,5},{8,14},{9,15},{10,... | collective-permute-start | bytes 294920 | tf_op jit(solution)/shard_map/ppermute | solution.py:55
  28.0 1.5 %collective-permute-start.8 = (bf16[24,2048]{1,0:T(8,128)(2,1)S(1)}, bf16[24,2048]{1,0:T(8,128)(2,1)S(1)}, u32[]{:S(2)}, u32[]{:S(2)}) collective-permute-start(bf16[24,2048]{1,0:T(8,128)(2,1)S(1)} %get-tuple-element.81), channel_id=1, source_target_pairs={{0,7},{1,0},{2,1},{3,2},{4,3},{5,4},{6,5},{7,6},{8,15},{9,8},{10,9... | collective-permute-start | bytes 294920 | tf_op jit(solution)/shard_map/ppermute | solution.py:55
  29.6 1.2 copy.19
  30.8 0.9 copy-done
  31.8 0.9 copy-done.2
  32.7 0.9 copy-done.5
  33.6 0.9 copy-done.10
  34.5 0.7 copy-done.33
  35.2 0.7 copy-done.35
  35.9 0.7 copy-done.36
  36.6 2.5 %shard_map.168 = (bf16[64,2048]{1,0:T(8,128)(2,1)S(1)}, bf16[64,2048]{1,0:T(8,128)(2,1)S(1)}, f32[2,8,64]{2,1,0:T(8,128)S(1)}, bf16[64,192]{1,0:T(8,128)(2,1)S(1...) custom-call(s32[3]{0:T(128)S(1)} %pad_add_fusion.place, ...), custom_call_target="tpu_custom_call" | custom-call | flops 100663296 | bytes 2883584 | tf_op jit(solution)/shard_map/pallas_call | solution.py:422
  39.1 0.7 copy-done.8
  39.7 0.6 copy-done.13
  40.4 0.6 copy-done.19
  41.0 0.6 copy-done.21
  41.6 0.6 copy-done.23
  42.2 0.6 copy-done.25
  42.8 0.6 copy-done.31
  43.5 0.6 copy-done.15
  44.1 0.6 copy-done.17
  44.7 3.5 %all-to-all-start.1 = ((bf16[8,24,2048]{2,1,0:T(8,128)(2,1)}), bf16[8,24,2048]{2,1,0:T(8,128)(2,1)S(1)}, u32[]{:S(2)}, u32[]{:S(2)}) async-start(bf16[8,24,2048]{2,1,0:T(8,128)(2,1)} %bitcast.16), calls=%async_computation.1 | async-start | bytes 1572864 | tf_op jit(solution)/shard_map/all_to_all | solution.py:51
  48.3 0.9 copy-done.16
  49.2 0.9 copy-done.18
  50.1 0.9 copy-done.20
  51.0 20.8 %shard_map.170 = bf16[192,2176]{1,0:T(8,128)(2,1)} custom-call(bf16[256,192]{1,0:T(8,128)(2,1)S(1)} %get-tuple-element.70.order, bf16[192,256]{1,0:T(8,128)(2,1)S(1)} %copy-done.20, bf16[8,32,1024]{2,1,0:T(8,128)(2,1)S(1)} %pad.4.saved_pre, bf16[8,2048,1024]{2,1,0:T(8,128)(2,1)} %up.3, bf16[8,1024,2048]{2,1,0:T(8,128)(2,1)} %down.3, ...), custom_call_target="tpu_custom_call" | custom-call | flops 2147483648 | bytes 33554432 | tf_op jit(solution)/shard_map/pallas_call | solution.py:451
  71.8 5.1 %all-to-all-start = ((bf16[8,24,2176]{2,1,0:T(8,128)(2,1)}), bf16[8,24,2176]{2,1,0:T(8,128)(2,1)S(1)}, u32[]{:S(2)}, u32[]{:S(2)}) async-start(bf16[8,24,2176]{2,1,0:T(8,128)(2,1)} %bitcast.14), calls=%async_computation | async-start | bytes 1671168 | tf_op jit(solution)/shard_map/all_to_all | solution.py:51
  76.8 0.9 copy-done.14
  77.7 20.6 %shard_map.172 = (bf16[24,2176]{1,0:T(8,128)(2,1)S(1)}, bf16[24,2176]{1,0:T(8,128)(2,1)S(1)}, bf16[24,2176]{1,0:T(8,128)(2,1)S(1)}, bf16[24,2176]{1,0:T(8,128)(2...) custom-call(bf16[256,192]{1,0:T(8,128)(2,1)S(1)} %get-tuple-element., ...), custom_call_target="tpu_custom_call" | custom-call | flops 2147483648 | bytes 33554432 | tf_op jit(solution)/shard_map/pallas_call | solution.py:451
  98.4 0.6 copy-done.11
  99.0 3.6 %collective-permute-start.9 = (bf16[24,2176]{1,0:T(8,128)(2,1)S(1)}, bf16[24,2176]{1,0:T(8,128)(2,1)S(1)}, u32[]{:S(2)}, u32[]{:S(2)}) collective-permute-start(bf16[24,2176]{1,0:T(8,128)(2,1)S(1)} %get-tuple-element.107), channel_id=1, source_target_pairs={{0,7},{1,0},{2,1},{3,2},{4,3},{5,4},{6,5},{7,6},{8,15},{9,8},{10,9... | collective-permute-start | bytes 313352 | tf_op jit(solution)/shard_map/ppermute | solution.py:55
  102.6 0.5 collective-permute-start.10
  103.2 2.4 %collective-permute-start.12 = (bf16[24,2176]{1,0:T(8,128)(2,1)}, bf16[24,2176]{1,0:T(8,128)(2,1)S(1)}, u32[]{:S(2)}, u32[]{:S(2)}) collective-permute-start(bf16[24,2176]{1,0:T(8,128)(2,1)} %get-tuple-element.110), channel_id=1, source_target_pairs={{0,4},{1,5},{2,6},{3,7},{4,0},{5,1},{6,2},{7,3},{8,12},{9,13},{10,... | collective-permute-start | bytes 313352 | tf_op jit(solution)/shard_map/ppermute | solution.py:55
  105.6 0.3 collective-permute-done.9.refs_1_
  105.9 0.7 collective-permute-start.14
  106.7 2.3 %collective-permute-done.10.refs_2_ = bf16[24,2176]{1,0:T(8,128)(2,1)S(1)} collective-permute-done((bf16[24,2176]{1,0:T(8,128)(2,1)S(1)}, bf16[24,2176]{1,0:T(8,128)(2,1)S(1)}, u32[]{:S(2)}, u32[]{:S(2)}) %collective-permute-start.10) | collective-permute-done | bytes 104480 | tf_op jit(solution)/shard_map/ppermute | solution.py:55
  109.0 0.9 copy-done.9
  109.9 0.8 copy-done.22
  110.7 0.8 copy-done.24
  111.4 0.8 copy-done.26
  112.2 0.7 copy-done.28
  112.9 0.7 copy-done.30
  113.6 0.7 copy-done.32
  114.3 0.5 shard_map.171
  114.8 6.0 %collective-permute-done.12.refs_4_ = bf16[24,2176]{1,0:T(8,128)(2,1)S(1)} collective-permute-done((bf16[24,2176]{1,0:T(8,128)(2,1)}, bf16[24,2176]{1,0:T(8,128)(2,1)S(1)}, u32[]{:S(2)}, u32[]{:S(2)}) %collective-permute-start.12) | collective-permute-done | bytes 104480 | tf_op jit(solution)/shard_map/ppermute | solution.py:55
  120.8 1.0 collective-permute-done.13.refs_5_
  121.8 0.9 copy-done.12
  122.7 1.5 %shard_map.173 = (bf16[1,64,2048]{2,1,0:T(8,128)(2,1)}, bf16[1,64,2048]{2,1,0:T(8,128)(2,1)}) custom-call(f32[64,2048]{1,0:T(8,128)S(1)} %get-tuple-element.91.early_f, f32[64,2048]{1,0:T(8,128)S(1)} %get-tuple-element.92.early_b, f32[2,8,64]{2,1,0:T(8,128)S(1)} %get-tuple-element.93.early_inner, bf16[64,2048]{1,0:T(8,128)(2,1)S(1)} %get-tuple-element.94.saved, ...), custom_call_target="tpu_custom_call" | custom-call | flops 100663296 | bytes 2883584 | tf_op jit(solution)/shard_map/pallas_call | solution.py:482
  (56 shorter events, 0.2 us)
Async XLA Ops:
  0.6 11.9 %collective-permute-start = (bf16[64,2048]{1,0:T(8,128)(2,1)}, bf16[64,2048]{1,0:T(8,128)(2,1)S(1)}, u32[]{:S(2)}, u32[]{:S(2)}) collective-permute-start(bf16[64,2048]{1,0:T(8,128)(2,1)} %bitcast.35), channel_id=1, source_target_pairs={{0,8},{8,16},{16,24},{1,9},{9,17},{17,25},{2,10},{10,18},{18,26},{... | collective-permute-start | bytes 786440 | tf_op jit(solution)/shard_map/ppermute | solution.py:45
  5.5 13.3 %collective-permute-start.1 = (bf16[64,2048]{1,0:T(8,128)(2,1)}, bf16[64,2048]{1,0:T(8,128)(2,1)S(1)}, u32[]{:S(2)}, u32[]{:S(2)}) collective-permute-start(bf16[64,2048]{1,0:T(8,128)(2,1)} %bitcast.36), channel_id=1, source_target_pairs={{8,0},{16,8},{24,16},{9,1},{17,9},{25,17},{10,2},{18,10},{26,18},{... | collective-permute-start | bytes 786440 | tf_op jit(solution)/shard_map/ppermute | solution.py:45
  6.9 0.9 copy-start.4
  7.8 0.9 copy-start.6
  8.7 0.9 copy-start.7
  9.7 0.7 copy-start.27
  10.4 0.7 copy-start.29
  11.0 0.7 copy-start.34
  19.9 6.7 %collective-permute-start.2 = (bf16[24,2048]{1,0:T(8,128)(2,1)S(1)}, bf16[24,2048]{1,0:T(8,128)(2,1)S(1)}, u32[]{:S(2)}, u32[]{:S(2)}) collective-permute-start(bf16[24,2048]{1,0:T(8,128)(2,1)S(1)} %get-tuple-element.75), channel_id=1, source_target_pairs={{0,1},{1,2},{2,3},{3,4},{4,5},{5,6},{6,7},{7,0},{8,9},{9,10},{10,1... | collective-permute-start | bytes 294920 | tf_op jit(solution)/shard_map/ppermute | solution.py:55
  19.9 8.1 %collective-permute-start.3 = (bf16[24,2048]{1,0:T(8,128)(2,1)S(1)}, bf16[24,2048]{1,0:T(8,128)(2,1)S(1)}, u32[]{:S(2)}, u32[]{:S(2)}) collective-permute-start(bf16[24,2048]{1,0:T(8,128)(2,1)S(1)} %get-tuple-element.76), channel_id=1, source_target_pairs={{0,2},{1,3},{2,4},{3,5},{4,6},{5,7},{6,0},{7,1},{8,10},{9,11},{10,... | collective-permute-start | bytes 294920 | tf_op jit(solution)/shard_map/ppermute | solution.py:55
  21.6 21.9 %collective-permute-start.4 = (bf16[24,2048]{1,0:T(8,128)(2,1)S(1)}, bf16[24,2048]{1,0:T(8,128)(2,1)S(1)}, u32[]{:S(2)}, u32[]{:S(2)}) collective-permute-start(bf16[24,2048]{1,0:T(8,128)(2,1)S(1)} %get-tuple-element.77), channel_id=1, source_target_pairs={{0,3},{1,4},{2,5},{3,6},{4,7},{5,0},{6,1},{7,2},{8,11},{9,12},{10,... | collective-permute-start | bytes 294920 | tf_op jit(solution)/shard_map/ppermute | solution.py:55
  24.1 19.4 %collective-permute-start.5 = (bf16[24,2048]{1,0:T(8,128)(2,1)S(1)}, bf16[24,2048]{1,0:T(8,128)(2,1)S(1)}, u32[]{:S(2)}, u32[]{:S(2)}) collective-permute-start(bf16[24,2048]{1,0:T(8,128)(2,1)S(1)} %get-tuple-element.78), channel_id=1, source_target_pairs={{0,4},{1,5},{2,6},{3,7},{4,0},{5,1},{6,2},{7,3},{8,12},{9,13},{10,... | collective-permute-start | bytes 294920 | tf_op jit(solution)/shard_map/ppermute | solution.py:55
  25.3 18.1 %collective-permute-start.6 = (bf16[24,2048]{1,0:T(8,128)(2,1)S(1)}, bf16[24,2048]{1,0:T(8,128)(2,1)S(1)}, u32[]{:S(2)}, u32[]{:S(2)}) collective-permute-start(bf16[24,2048]{1,0:T(8,128)(2,1)S(1)} %get-tuple-element.79), channel_id=1, source_target_pairs={{0,5},{1,6},{2,7},{3,0},{4,1},{5,2},{6,3},{7,4},{8,13},{9,14},{10,... | collective-permute-start | bytes 294920 | tf_op jit(solution)/shard_map/ppermute | solution.py:55
  26.5 16.9 %collective-permute-start.7 = (bf16[24,2048]{1,0:T(8,128)(2,1)S(1)}, bf16[24,2048]{1,0:T(8,128)(2,1)S(1)}, u32[]{:S(2)}, u32[]{:S(2)}) collective-permute-start(bf16[24,2048]{1,0:T(8,128)(2,1)S(1)} %get-tuple-element.80), channel_id=1, source_target_pairs={{0,6},{1,7},{2,0},{3,1},{4,2},{5,3},{6,4},{7,5},{8,14},{9,15},{10,... | collective-permute-start | bytes 294920 | tf_op jit(solution)/shard_map/ppermute | solution.py:55
  28.0 16.1 %collective-permute-start.8 = (bf16[24,2048]{1,0:T(8,128)(2,1)S(1)}, bf16[24,2048]{1,0:T(8,128)(2,1)S(1)}, u32[]{:S(2)}, u32[]{:S(2)}) collective-permute-start(bf16[24,2048]{1,0:T(8,128)(2,1)S(1)} %get-tuple-element.81), channel_id=1, source_target_pairs={{0,7},{1,0},{2,1},{3,2},{4,3},{5,4},{6,5},{7,6},{8,15},{9,8},{10,9... | collective-permute-start | bytes 294920 | tf_op jit(solution)/shard_map/ppermute | solution.py:55
  30.8 1.0 copy-start
  31.8 0.9 copy-start.2
  32.7 0.9 copy-start.5
  33.6 0.9 copy-start.10
  34.5 0.7 copy-start.33
  35.2 0.7 copy-start.35
  35.9 0.7 copy-start.36
  39.0 0.7 copy-start.8
  39.7 0.6 copy-start.13
  40.4 0.6 copy-start.19
  41.0 0.6 copy-start.21
  41.6 0.6 copy-start.23
  42.2 0.6 copy-start.25
  42.8 0.6 copy-start.31
  43.5 0.6 copy-start.15
  44.1 0.6 copy-start.17
  44.7 27.1 %all-to-all-start.1 = ((bf16[8,24,2048]{2,1,0:T(8,128)(2,1)}), bf16[8,24,2048]{2,1,0:T(8,128)(2,1)S(1)}, u32[]{:S(2)}, u32[]{:S(2)}) async-start(bf16[8,24,2048]{2,1,0:T(8,128)(2,1)} %bitcast.16), calls=%async_computation.1 | async-start | bytes 1572864 | tf_op jit(solution)/shard_map/all_to_all | solution.py:51
  48.3 0.9 copy-start.16
  49.2 0.9 copy-start.18
  50.1 0.9 copy-start.20
  71.8 37.2 %all-to-all-start = ((bf16[8,24,2176]{2,1,0:T(8,128)(2,1)}), bf16[8,24,2176]{2,1,0:T(8,128)(2,1)S(1)}, u32[]{:S(2)}, u32[]{:S(2)}) async-start(bf16[8,24,2176]{2,1,0:T(8,128)(2,1)} %bitcast.14), calls=%async_computation | async-start | bytes 1671168 | tf_op jit(solution)/shard_map/all_to_all | solution.py:51
  76.8 0.9 copy-start.14
  77.7 31.2 %copy-start.1 = (bf16[1,64,2048]{2,1,0:T(8,128)(2,1)S(1)}, bf16[1,64,2048]{2,1,0:T(8,128)(2,1)}, u32[]{:S(2)}) copy-start(bf16[1,64,2048]{2,1,0:T(8,128)(2,1)} %param.21) | copy-start | bytes 786436
  77.7 31.3 %copy-start.3 = (bf16[1,2048,64]{1,2,0:T(8,128)(2,1)S(1)}, bf16[1,2048,64]{1,2,0:T(8,128)(2,1)}, u32[]{:S(2)}) copy-start(bf16[1,2048,64]{1,2,0:T(8,128)(2,1)} %param.25) | copy-start | bytes 786436
  98.4 0.6 copy-start.11
  99.0 6.9 %collective-permute-start.9 = (bf16[24,2176]{1,0:T(8,128)(2,1)S(1)}, bf16[24,2176]{1,0:T(8,128)(2,1)S(1)}, u32[]{:S(2)}, u32[]{:S(2)}) collective-permute-start(bf16[24,2176]{1,0:T(8,128)(2,1)S(1)} %get-tuple-element.107), channel_id=1, source_target_pairs={{0,7},{1,0},{2,1},{3,2},{4,3},{5,4},{6,5},{7,6},{8,15},{9,8},{10,9... | collective-permute-start | bytes 313352 | tf_op jit(solution)/shard_map/ppermute | solution.py:55
  102.6 6.4 %collective-permute-start.10 = (bf16[24,2176]{1,0:T(8,128)(2,1)S(1)}, bf16[24,2176]{1,0:T(8,128)(2,1)S(1)}, u32[]{:S(2)}, u32[]{:S(2)}) collective-permute-start(bf16[24,2176]{1,0:T(8,128)(2,1)S(1)} %get-tuple-element.108), channel_id=1, source_target_pairs={{0,6},{1,7},{2,0},{3,1},{4,2},{5,3},{6,4},{7,5},{8,14},{9,15},{10,... | collective-permute-start | bytes 313352 | tf_op jit(solution)/shard_map/ppermute | solution.py:55
  103.2 11.6 %collective-permute-start.11 = (bf16[24,2176]{1,0:T(8,128)(2,1)}, bf16[24,2176]{1,0:T(8,128)(2,1)S(1)}, u32[]{:S(2)}, u32[]{:S(2)}) collective-permute-start(bf16[24,2176]{1,0:T(8,128)(2,1)} %get-tuple-element.109), channel_id=1, source_target_pairs={{0,5},{1,6},{2,7},{3,0},{4,1},{5,2},{6,3},{7,4},{8,13},{9,14},{10,... | collective-permute-start | bytes 313352 | tf_op jit(solution)/shard_map/ppermute | solution.py:55
  103.2 17.6 %collective-permute-start.12 = (bf16[24,2176]{1,0:T(8,128)(2,1)}, bf16[24,2176]{1,0:T(8,128)(2,1)S(1)}, u32[]{:S(2)}, u32[]{:S(2)}) collective-permute-start(bf16[24,2176]{1,0:T(8,128)(2,1)} %get-tuple-element.110), channel_id=1, source_target_pairs={{0,4},{1,5},{2,6},{3,7},{4,0},{5,1},{6,2},{7,3},{8,12},{9,13},{10,... | collective-permute-start | bytes 313352 | tf_op jit(solution)/shard_map/ppermute | solution.py:55
  105.6 16.2 %collective-permute-start.13 = (bf16[24,2176]{1,0:T(8,128)(2,1)}, bf16[24,2176]{1,0:T(8,128)(2,1)S(1)}, u32[]{:S(2)}, u32[]{:S(2)}) collective-permute-start(bf16[24,2176]{1,0:T(8,128)(2,1)} %get-tuple-element.111), channel_id=1, source_target_pairs={{0,3},{1,4},{2,5},{3,6},{4,7},{5,0},{6,1},{7,2},{8,11},{9,12},{10,... | collective-permute-start | bytes 313352 | tf_op jit(solution)/shard_map/ppermute | solution.py:55
  105.9 15.9 %collective-permute-start.14 = (bf16[24,2176]{1,0:T(8,128)(2,1)}, bf16[24,2176]{1,0:T(8,128)(2,1)S(1)}, u32[]{:S(2)}, u32[]{:S(2)}) collective-permute-start(bf16[24,2176]{1,0:T(8,128)(2,1)} %get-tuple-element.112), channel_id=1, source_target_pairs={{0,2},{1,3},{2,4},{3,5},{4,6},{5,7},{6,0},{7,1},{8,10},{9,11},{10,... | collective-permute-start | bytes 313352 | tf_op jit(solution)/shard_map/ppermute | solution.py:55
  109.0 12.8 %collective-permute-start.15 = (bf16[24,2176]{1,0:T(8,128)(2,1)}, bf16[24,2176]{1,0:T(8,128)(2,1)S(1)}, u32[]{:S(2)}, u32[]{:S(2)}) collective-permute-start(bf16[24,2176]{1,0:T(8,128)(2,1)} %get-tuple-element.113), channel_id=1, source_target_pairs={{0,1},{1,2},{2,3},{3,4},{4,5},{5,6},{6,7},{7,0},{8,9},{9,10},{10,1... | collective-permute-start | bytes 313352 | tf_op jit(solution)/shard_map/ppermute | solution.py:55
  109.0 0.9 copy-start.9
  109.9 0.8 copy-start.22
  110.7 0.8 copy-start.24
  111.4 0.8 copy-start.26
  112.2 0.7 copy-start.28
  112.9 0.7 copy-start.30
  113.6 0.7 copy-start.32
  121.8 0.9 copy-start.12

commit v9 on v8

--- a/solution.py
+++ b/solution.py
@@ -14,7 +14,7 @@
 LANES = 128
 ROWS = 16
 SMALL_VMEM = 16 * 1024 * 1024
-EXPERT_VMEM = 44 * 1024 * 1024
+EXPERT_VMEM = 24 * 1024 * 1024
 NT = (((1,), (1,)), ((), ()))
 TN = (((0,), (0,)), ((), ()))
 

time: 125 us -> 125 us (level)
  no operation moved by 1% of the time
where the time goes in v9:
time: 125 us; the launch traced here: 124 us
  Pallas kernels  47.8 us (38%)
  starting transfers between devices  31.8 us (25%)
  local copies, waits for them, and re-layouts  27.8 us (22%)
  waiting for transfers between devices  16 us (13%)
    pallas_call x2, Pallas kernels, on_device(): call(functools.partial(expert_kernel, sizes, part, held), tuple(result),...  41.4 us
    unnamed x74, local copies, waits for them, and re-layouts  26.6 us
    ppermute x14, starting transfers between devices, exchange(): got[d] = lax.ppermute(blocks[d], 'expert', route)  17 us
    ppermute x14, waiting for transfers between devices, exchange(): got[d] = lax.ppermute(blocks[d], 'expert', route)  9.7 us
    all_to_all x2, starting transfers between devices, exchange(): lax.all_to_all(blocks[0], 'expert', split_axis=0, concat_axis=0, tiled=True)  8.6 us
    ppermute x2, waiting for transfers between devices, from_behind(): return lax.ppermute(block, axis, route)  6.25 us
    ppermute x2, starting transfers between devices, from_behind(): return lax.ppermute(block, axis, route)  6.15 us
  transfers between devices with their start and end apart: 18, of which 5 were waited for; matrix products, arithmetic and copies ran while one was open for 1% of the time, Pallas kernels for 36%

profile of v9, /device:TPU:0, one launch (start us, length us, event | category | flops | bytes accessed | tf_op | source)
XLA Modules:
  0.0 124.3 jit_solution(2072559705378023958)
XLA Ops:
  0.6 4.9 %collective-permute-start = (bf16[64,2048]{1,0:T(8,128)(2,1)}, bf16[64,2048]{1,0:T(8,128)(2,1)S(1)}, u32[]{:S(2)}, u32[]{:S(2)}) collective-permute-start(bf16[64,2048]{1,0:T(8,128)(2,1)} %bitcast.35), channel_id=1, source_target_pairs={{0,8},{8,16},{16,24},{1,9},{9,17},{17,25},{2,10},{10,18},{18,26},{... | collective-permute-start | bytes 786440 | tf_op jit(solution)/shard_map/ppermute | solution.py:45
  5.5 1.3 %collective-permute-start.1 = (bf16[64,2048]{1,0:T(8,128)(2,1)}, bf16[64,2048]{1,0:T(8,128)(2,1)S(1)}, u32[]{:S(2)}, u32[]{:S(2)}) collective-permute-start(bf16[64,2048]{1,0:T(8,128)(2,1)} %bitcast.36), channel_id=1, source_target_pairs={{8,0},{16,8},{24,16},{9,1},{17,9},{25,17},{10,2},{18,10},{26,18},{... | collective-permute-start | bytes 786440 | tf_op jit(solution)/shard_map/ppermute | solution.py:45
  6.8 0.1 pad_add_fusion.place
  6.9 0.9 copy-done.4
  7.8 0.9 copy-done.6
  8.7 0.9 copy-done.7
  9.7 0.7 copy-done.27
  10.4 0.7 copy-done.29
  11.1 0.7 copy-done.34
  11.7 0.8 shard_map.167
  12.6 6.2 %collective-permute-done.1.arrived_b = bf16[64,2048]{1,0:T(8,128)(2,1)S(1)} collective-permute-done((bf16[64,2048]{1,0:T(8,128)(2,1)}, bf16[64,2048]{1,0:T(8,128)(2,1)S(1)}, u32[]{:S(2)}, u32[]{:S(2)}) %collective-permute-start.1) | collective-permute-done | bytes 262176 | tf_op jit(solution)/shard_map/ppermute | solution.py:45
  18.8 1.1 shard_map.169
  19.9 0.1 collective-permute-start.2
  19.9 1.6 %collective-permute-start.3 = (bf16[24,2048]{1,0:T(8,128)(2,1)S(1)}, bf16[24,2048]{1,0:T(8,128)(2,1)S(1)}, u32[]{:S(2)}, u32[]{:S(2)}) collective-permute-start(bf16[24,2048]{1,0:T(8,128)(2,1)S(1)} %get-tuple-element.76), channel_id=1, source_target_pairs={{0,2},{1,3},{2,4},{3,5},{4,6},{5,7},{6,0},{7,1},{8,10},{9,11},{10,... | collective-permute-start | bytes 294920 | tf_op jit(solution)/shard_map/ppermute | solution.py:55
  21.6 2.5 %collective-permute-start.4 = (bf16[24,2048]{1,0:T(8,128)(2,1)S(1)}, bf16[24,2048]{1,0:T(8,128)(2,1)S(1)}, u32[]{:S(2)}, u32[]{:S(2)}) collective-permute-start(bf16[24,2048]{1,0:T(8,128)(2,1)S(1)} %get-tuple-element.77), channel_id=1, source_target_pairs={{0,3},{1,4},{2,5},{3,6},{4,7},{5,0},{6,1},{7,2},{8,11},{9,12},{10,... | collective-permute-start | bytes 294920 | tf_op jit(solution)/shard_map/ppermute | solution.py:55
  24.1 1.2 collective-permute-start.5
  25.3 1.2 collective-permute-start.6
  26.5 1.5 %collective-permute-start.7 = (bf16[24,2048]{1,0:T(8,128)(2,1)S(1)}, bf16[24,2048]{1,0:T(8,128)(2,1)S(1)}, u32[]{:S(2)}, u32[]{:S(2)}) collective-permute-start(bf16[24,2048]{1,0:T(8,128)(2,1)S(1)} %get-tuple-element.80), channel_id=1, source_target_pairs={{0,6},{1,7},{2,0},{3,1},{4,2},{5,3},{6,4},{7,5},{8,14},{9,15},{10,... | collective-permute-start | bytes 294920 | tf_op jit(solution)/shard_map/ppermute | solution.py:55
  28.0 1.5 %collective-permute-start.8 = (bf16[24,2048]{1,0:T(8,128)(2,1)S(1)}, bf16[24,2048]{1,0:T(8,128)(2,1)S(1)}, u32[]{:S(2)}, u32[]{:S(2)}) collective-permute-start(bf16[24,2048]{1,0:T(8,128)(2,1)S(1)} %get-tuple-element.81), channel_id=1, source_target_pairs={{0,7},{1,0},{2,1},{3,2},{4,3},{5,4},{6,5},{7,6},{8,15},{9,8},{10,9... | collective-permute-start | bytes 294920 | tf_op jit(solution)/shard_map/ppermute | solution.py:55
  29.6 1.2 copy.19
  30.8 0.9 copy-done
  31.8 0.9 copy-done.2
  32.7 0.9 copy-done.5
  33.6 0.9 copy-done.10
  34.5 0.7 copy-done.33
  35.2 0.7 copy-done.35
  35.9 0.7 copy-done.36
  36.6 2.5 %shard_map.168 = (bf16[64,2048]{1,0:T(8,128)(2,1)S(1)}, bf16[64,2048]{1,0:T(8,128)(2,1)S(1)}, f32[2,8,64]{2,1,0:T(8,128)S(1)}, bf16[64,192]{1,0:T(8,128)(2,1)S(1...) custom-call(s32[3]{0:T(128)S(1)} %pad_add_fusion.place, ...), custom_call_target="tpu_custom_call" | custom-call | flops 100663296 | bytes 2883584 | tf_op jit(solution)/shard_map/pallas_call | solution.py:422
  39.1 0.7 copy-done.8
  39.7 0.6 copy-done.13
  40.4 0.6 copy-done.19
  41.0 0.6 copy-done.21
  41.6 0.6 copy-done.23
  42.2 0.6 copy-done.25
  42.8 0.6 copy-done.31
  43.5 0.6 copy-done.15
  44.1 0.6 copy-done.17
  44.7 3.5 %all-to-all-start.1 = ((bf16[8,24,2048]{2,1,0:T(8,128)(2,1)}), bf16[8,24,2048]{2,1,0:T(8,128)(2,1)S(1)}, u32[]{:S(2)}, u32[]{:S(2)}) async-start(bf16[8,24,2048]{2,1,0:T(8,128)(2,1)} %bitcast.16), calls=%async_computation.1 | async-start | bytes 1572864 | tf_op jit(solution)/shard_map/all_to_all | solution.py:51
  48.3 0.9 copy-done.16
  49.2 0.9 copy-done.18
  50.1 0.9 copy-done.20
  51.0 20.8 %shard_map.170 = bf16[192,2176]{1,0:T(8,128)(2,1)} custom-call(bf16[256,192]{1,0:T(8,128)(2,1)S(1)} %get-tuple-element.70.order, bf16[192,256]{1,0:T(8,128)(2,1)S(1)} %copy-done.20, bf16[8,32,1024]{2,1,0:T(8,128)(2,1)S(1)} %pad.4.saved_pre, bf16[8,2048,1024]{2,1,0:T(8,128)(2,1)} %up.3, bf16[8,1024,2048]{2,1,0:T(8,128)(2,1)} %down.3, ...), custom_call_target="tpu_custom_call" | custom-call | flops 2147483648 | bytes 33554432 | tf_op jit(solution)/shard_map/pallas_call | solution.py:451
  71.8 5.1 %all-to-all-start = ((bf16[8,24,2176]{2,1,0:T(8,128)(2,1)}), bf16[8,24,2176]{2,1,0:T(8,128)(2,1)S(1)}, u32[]{:S(2)}, u32[]{:S(2)}) async-start(bf16[8,24,2176]{2,1,0:T(8,128)(2,1)} %bitcast.14), calls=%async_computation | async-start | bytes 1671168 | tf_op jit(solution)/shard_map/all_to_all | solution.py:51
  76.8 0.9 copy-done.14
  77.7 20.6 %shard_map.172 = (bf16[24,2176]{1,0:T(8,128)(2,1)S(1)}, bf16[24,2176]{1,0:T(8,128)(2,1)S(1)}, bf16[24,2176]{1,0:T(8,128)(2,1)S(1)}, bf16[24,2176]{1,0:T(8,128)(2...) custom-call(bf16[256,192]{1,0:T(8,128)(2,1)S(1)} %get-tuple-element., ...), custom_call_target="tpu_custom_call" | custom-call | flops 2147483648 | bytes 33554432 | tf_op jit(solution)/shard_map/pallas_call | solution.py:451
  98.4 0.6 copy-done.11
  99.0 3.6 %collective-permute-start.9 = (bf16[24,2176]{1,0:T(8,128)(2,1)S(1)}, bf16[24,2176]{1,0:T(8,128)(2,1)S(1)}, u32[]{:S(2)}, u32[]{:S(2)}) collective-permute-start(bf16[24,2176]{1,0:T(8,128)(2,1)S(1)} %get-tuple-element.107), channel_id=1, source_target_pairs={{0,7},{1,0},{2,1},{3,2},{4,3},{5,4},{6,5},{7,6},{8,15},{9,8},{10,9... | collective-permute-start | bytes 313352 | tf_op jit(solution)/shard_map/ppermute | solution.py:55
  102.6 0.5 collective-permute-start.10
  103.2 2.4 %collective-permute-start.12 = (bf16[24,2176]{1,0:T(8,128)(2,1)}, bf16[24,2176]{1,0:T(8,128)(2,1)S(1)}, u32[]{:S(2)}, u32[]{:S(2)}) collective-permute-start(bf16[24,2176]{1,0:T(8,128)(2,1)} %get-tuple-element.110), channel_id=1, source_target_pairs={{0,4},{1,5},{2,6},{3,7},{4,0},{5,1},{6,2},{7,3},{8,12},{9,13},{10,... | collective-permute-start | bytes 313352 | tf_op jit(solution)/shard_map/ppermute | solution.py:55
  105.6 0.3 collective-permute-done.9.refs_1_
  105.9 0.7 collective-permute-start.14
  106.7 2.3 %collective-permute-done.10.refs_2_ = bf16[24,2176]{1,0:T(8,128)(2,1)S(1)} collective-permute-done((bf16[24,2176]{1,0:T(8,128)(2,1)S(1)}, bf16[24,2176]{1,0:T(8,128)(2,1)S(1)}, u32[]{:S(2)}, u32[]{:S(2)}) %collective-permute-start.10) | collective-permute-done | bytes 104480 | tf_op jit(solution)/shard_map/ppermute | solution.py:55
  109.0 0.9 copy-done.9
  109.9 0.8 copy-done.22
  110.7 0.8 copy-done.24
  111.4 0.8 copy-done.26
  112.2 0.7 copy-done.28
  112.9 0.7 copy-done.30
  113.6 0.7 copy-done.32
  114.3 0.5 shard_map.171
  114.8 6.0 %collective-permute-done.12.refs_4_ = bf16[24,2176]{1,0:T(8,128)(2,1)S(1)} collective-permute-done((bf16[24,2176]{1,0:T(8,128)(2,1)}, bf16[24,2176]{1,0:T(8,128)(2,1)S(1)}, u32[]{:S(2)}, u32[]{:S(2)}) %collective-permute-start.12) | collective-permute-done | bytes 104480 | tf_op jit(solution)/shard_map/ppermute | solution.py:55
  120.8 1.0 collective-permute-done.13.refs_5_
  121.8 0.9 copy-done.12
  122.7 1.5 %shard_map.173 = (bf16[1,64,2048]{2,1,0:T(8,128)(2,1)}, bf16[1,64,2048]{2,1,0:T(8,128)(2,1)}) custom-call(f32[64,2048]{1,0:T(8,128)S(1)} %get-tuple-element.91.early_f, f32[64,2048]{1,0:T(8,128)S(1)} %get-tuple-element.92.early_b, f32[2,8,64]{2,1,0:T(8,128)S(1)} %get-tuple-element.93.early_inner, bf16[64,2048]{1,0:T(8,128)(2,1)S(1)} %get-tuple-element.94.saved, ...), custom_call_target="tpu_custom_call" | custom-call | flops 100663296 | bytes 2883584 | tf_op jit(solution)/shard_map/pallas_call | solution.py:482
  (56 shorter events, 0.2 us)
Async XLA Ops:
  0.6 11.9 %collective-permute-start = (bf16[64,2048]{1,0:T(8,128)(2,1)}, bf16[64,2048]{1,0:T(8,128)(2,1)S(1)}, u32[]{:S(2)}, u32[]{:S(2)}) collective-permute-start(bf16[64,2048]{1,0:T(8,128)(2,1)} %bitcast.35), channel_id=1, source_target_pairs={{0,8},{8,16},{16,24},{1,9},{9,17},{17,25},{2,10},{10,18},{18,26},{... | collective-permute-start | bytes 786440 | tf_op jit(solution)/shard_map/ppermute | solution.py:45
  5.5 13.3 %collective-permute-start.1 = (bf16[64,2048]{1,0:T(8,128)(2,1)}, bf16[64,2048]{1,0:T(8,128)(2,1)S(1)}, u32[]{:S(2)}, u32[]{:S(2)}) collective-permute-start(bf16[64,2048]{1,0:T(8,128)(2,1)} %bitcast.36), channel_id=1, source_target_pairs={{8,0},{16,8},{24,16},{9,1},{17,9},{25,17},{10,2},{18,10},{26,18},{... | collective-permute-start | bytes 786440 | tf_op jit(solution)/shard_map/ppermute | solution.py:45
  6.9 0.9 copy-start.4
  7.8 0.9 copy-start.6
  8.7 0.9 copy-start.7
  9.7 0.7 copy-start.27
  10.4 0.7 copy-start.29
  11.0 0.7 copy-start.34
  19.9 6.7 %collective-permute-start.2 = (bf16[24,2048]{1,0:T(8,128)(2,1)S(1)}, bf16[24,2048]{1,0:T(8,128)(2,1)S(1)}, u32[]{:S(2)}, u32[]{:S(2)}) collective-permute-start(bf16[24,2048]{1,0:T(8,128)(2,1)S(1)} %get-tuple-element.75), channel_id=1, source_target_pairs={{0,1},{1,2},{2,3},{3,4},{4,5},{5,6},{6,7},{7,0},{8,9},{9,10},{10,1... | collective-permute-start | bytes 294920 | tf_op jit(solution)/shard_map/ppermute | solution.py:55
  19.9 8.1 %collective-permute-start.3 = (bf16[24,2048]{1,0:T(8,128)(2,1)S(1)}, bf16[24,2048]{1,0:T(8,128)(2,1)S(1)}, u32[]{:S(2)}, u32[]{:S(2)}) collective-permute-start(bf16[24,2048]{1,0:T(8,128)(2,1)S(1)} %get-tuple-element.76), channel_id=1, source_target_pairs={{0,2},{1,3},{2,4},{3,5},{4,6},{5,7},{6,0},{7,1},{8,10},{9,11},{10,... | collective-permute-start | bytes 294920 | tf_op jit(solution)/shard_map/ppermute | solution.py:55
  21.6 21.9 %collective-permute-start.4 = (bf16[24,2048]{1,0:T(8,128)(2,1)S(1)}, bf16[24,2048]{1,0:T(8,128)(2,1)S(1)}, u32[]{:S(2)}, u32[]{:S(2)}) collective-permute-start(bf16[24,2048]{1,0:T(8,128)(2,1)S(1)} %get-tuple-element.77), channel_id=1, source_target_pairs={{0,3},{1,4},{2,5},{3,6},{4,7},{5,0},{6,1},{7,2},{8,11},{9,12},{10,... | collective-permute-start | bytes 294920 | tf_op jit(solution)/shard_map/ppermute | solution.py:55
  24.1 19.4 %collective-permute-start.5 = (bf16[24,2048]{1,0:T(8,128)(2,1)S(1)}, bf16[24,2048]{1,0:T(8,128)(2,1)S(1)}, u32[]{:S(2)}, u32[]{:S(2)}) collective-permute-start(bf16[24,2048]{1,0:T(8,128)(2,1)S(1)} %get-tuple-element.78), channel_id=1, source_target_pairs={{0,4},{1,5},{2,6},{3,7},{4,0},{5,1},{6,2},{7,3},{8,12},{9,13},{10,... | collective-permute-start | bytes 294920 | tf_op jit(solution)/shard_map/ppermute | solution.py:55
  25.3 18.1 %collective-permute-start.6 = (bf16[24,2048]{1,0:T(8,128)(2,1)S(1)}, bf16[24,2048]{1,0:T(8,128)(2,1)S(1)}, u32[]{:S(2)}, u32[]{:S(2)}) collective-permute-start(bf16[24,2048]{1,0:T(8,128)(2,1)S(1)} %get-tuple-element.79), channel_id=1, source_target_pairs={{0,5},{1,6},{2,7},{3,0},{4,1},{5,2},{6,3},{7,4},{8,13},{9,14},{10,... | collective-permute-start | bytes 294920 | tf_op jit(solution)/shard_map/ppermute | solution.py:55
  26.5 16.9 %collective-permute-start.7 = (bf16[24,2048]{1,0:T(8,128)(2,1)S(1)}, bf16[24,2048]{1,0:T(8,128)(2,1)S(1)}, u32[]{:S(2)}, u32[]{:S(2)}) collective-permute-start(bf16[24,2048]{1,0:T(8,128)(2,1)S(1)} %get-tuple-element.80), channel_id=1, source_target_pairs={{0,6},{1,7},{2,0},{3,1},{4,2},{5,3},{6,4},{7,5},{8,14},{9,15},{10,... | collective-permute-start | bytes 294920 | tf_op jit(solution)/shard_map/ppermute | solution.py:55
  28.0 16.1 %collective-permute-start.8 = (bf16[24,2048]{1,0:T(8,128)(2,1)S(1)}, bf16[24,2048]{1,0:T(8,128)(2,1)S(1)}, u32[]{:S(2)}, u32[]{:S(2)}) collective-permute-start(bf16[24,2048]{1,0:T(8,128)(2,1)S(1)} %get-tuple-element.81), channel_id=1, source_target_pairs={{0,7},{1,0},{2,1},{3,2},{4,3},{5,4},{6,5},{7,6},{8,15},{9,8},{10,9... | collective-permute-start | bytes 294920 | tf_op jit(solution)/shard_map/ppermute | solution.py:55
  30.8 1.0 copy-start
  31.8 0.9 copy-start.2
  32.7 0.9 copy-start.5
  33.6 0.9 copy-start.10
  34.5 0.7 copy-start.33
  35.2 0.7 copy-start.35
  35.9 0.7 copy-start.36
  39.0 0.7 copy-start.8
  39.7 0.6 copy-start.13
  40.4 0.6 copy-start.19
  41.0 0.6 copy-start.21
  41.6 0.6 copy-start.23
  42.2 0.6 copy-start.25
  42.8 0.6 copy-start.31
  43.5 0.6 copy-start.15
  44.1 0.6 copy-start.17
  44.7 27.1 %all-to-all-start.1 = ((bf16[8,24,2048]{2,1,0:T(8,128)(2,1)}), bf16[8,24,2048]{2,1,0:T(8,128)(2,1)S(1)}, u32[]{:S(2)}, u32[]{:S(2)}) async-start(bf16[8,24,2048]{2,1,0:T(8,128)(2,1)} %bitcast.16), calls=%async_computation.1 | async-start | bytes 1572864 | tf_op jit(solution)/shard_map/all_to_all | solution.py:51
  48.3 0.9 copy-start.16
  49.2 0.9 copy-start.18
  50.1 0.9 copy-start.20
  71.8 37.2 %all-to-all-start = ((bf16[8,24,2176]{2,1,0:T(8,128)(2,1)}), bf16[8,24,2176]{2,1,0:T(8,128)(2,1)S(1)}, u32[]{:S(2)}, u32[]{:S(2)}) async-start(bf16[8,24,2176]{2,1,0:T(8,128)(2,1)} %bitcast.14), calls=%async_computation | async-start | bytes 1671168 | tf_op jit(solution)/shard_map/all_to_all | solution.py:51
  76.8 0.9 copy-start.14
  77.7 31.2 %copy-start.1 = (bf16[1,64,2048]{2,1,0:T(8,128)(2,1)S(1)}, bf16[1,64,2048]{2,1,0:T(8,128)(2,1)}, u32[]{:S(2)}) copy-start(bf16[1,64,2048]{2,1,0:T(8,128)(2,1)} %param.21) | copy-start | bytes 786436
  77.7 31.3 %copy-start.3 = (bf16[1,2048,64]{1,2,0:T(8,128)(2,1)S(1)}, bf16[1,2048,64]{1,2,0:T(8,128)(2,1)}, u32[]{:S(2)}) copy-start(bf16[1,2048,64]{1,2,0:T(8,128)(2,1)} %param.25) | copy-start | bytes 786436
  98.4 0.6 copy-start.11
  99.0 6.9 %collective-permute-start.9 = (bf16[24,2176]{1,0:T(8,128)(2,1)S(1)}, bf16[24,2176]{1,0:T(8,128)(2,1)S(1)}, u32[]{:S(2)}, u32[]{:S(2)}) collective-permute-start(bf16[24,2176]{1,0:T(8,128)(2,1)S(1)} %get-tuple-element.107), channel_id=1, source_target_pairs={{0,7},{1,0},{2,1},{3,2},{4,3},{5,4},{6,5},{7,6},{8,15},{9,8},{10,9... | collective-permute-start | bytes 313352 | tf_op jit(solution)/shard_map/ppermute | solution.py:55
  102.6 6.4 %collective-permute-start.10 = (bf16[24,2176]{1,0:T(8,128)(2,1)S(1)}, bf16[24,2176]{1,0:T(8,128)(2,1)S(1)}, u32[]{:S(2)}, u32[]{:S(2)}) collective-permute-start(bf16[24,2176]{1,0:T(8,128)(2,1)S(1)} %get-tuple-element.108), channel_id=1, source_target_pairs={{0,6},{1,7},{2,0},{3,1},{4,2},{5,3},{6,4},{7,5},{8,14},{9,15},{10,... | collective-permute-start | bytes 313352 | tf_op jit(solution)/shard_map/ppermute | solution.py:55
  103.2 11.6 %collective-permute-start.11 = (bf16[24,2176]{1,0:T(8,128)(2,1)}, bf16[24,2176]{1,0:T(8,128)(2,1)S(1)}, u32[]{:S(2)}, u32[]{:S(2)}) collective-permute-start(bf16[24,2176]{1,0:T(8,128)(2,1)} %get-tuple-element.109), channel_id=1, source_target_pairs={{0,5},{1,6},{2,7},{3,0},{4,1},{5,2},{6,3},{7,4},{8,13},{9,14},{10,... | collective-permute-start | bytes 313352 | tf_op jit(solution)/shard_map/ppermute | solution.py:55
  103.2 17.6 %collective-permute-start.12 = (bf16[24,2176]{1,0:T(8,128)(2,1)}, bf16[24,2176]{1,0:T(8,128)(2,1)S(1)}, u32[]{:S(2)}, u32[]{:S(2)}) collective-permute-start(bf16[24,2176]{1,0:T(8,128)(2,1)} %get-tuple-element.110), channel_id=1, source_target_pairs={{0,4},{1,5},{2,6},{3,7},{4,0},{5,1},{6,2},{7,3},{8,12},{9,13},{10,... | collective-permute-start | bytes 313352 | tf_op jit(solution)/shard_map/ppermute | solution.py:55
  105.6 16.2 %collective-permute-start.13 = (bf16[24,2176]{1,0:T(8,128)(2,1)}, bf16[24,2176]{1,0:T(8,128)(2,1)S(1)}, u32[]{:S(2)}, u32[]{:S(2)}) collective-permute-start(bf16[24,2176]{1,0:T(8,128)(2,1)} %get-tuple-element.111), channel_id=1, source_target_pairs={{0,3},{1,4},{2,5},{3,6},{4,7},{5,0},{6,1},{7,2},{8,11},{9,12},{10,... | collective-permute-start | bytes 313352 | tf_op jit(solution)/shard_map/ppermute | solution.py:55
  105.9 15.9 %collective-permute-start.14 = (bf16[24,2176]{1,0:T(8,128)(2,1)}, bf16[24,2176]{1,0:T(8,128)(2,1)S(1)}, u32[]{:S(2)}, u32[]{:S(2)}) collective-permute-start(bf16[24,2176]{1,0:T(8,128)(2,1)} %get-tuple-element.112), channel_id=1, source_target_pairs={{0,2},{1,3},{2,4},{3,5},{4,6},{5,7},{6,0},{7,1},{8,10},{9,11},{10,... | collective-permute-start | bytes 313352 | tf_op jit(solution)/shard_map/ppermute | solution.py:55
  109.0 12.8 %collective-permute-start.15 = (bf16[24,2176]{1,0:T(8,128)(2,1)}, bf16[24,2176]{1,0:T(8,128)(2,1)S(1)}, u32[]{:S(2)}, u32[]{:S(2)}) collective-permute-start(bf16[24,2176]{1,0:T(8,128)(2,1)} %get-tuple-element.113), channel_id=1, source_target_pairs={{0,1},{1,2},{2,3},{3,4},{4,5},{5,6},{6,7},{7,0},{8,9},{9,10},{10,1... | collective-permute-start | bytes 313352 | tf_op jit(solution)/shard_map/ppermute | solution.py:55
  109.0 0.9 copy-start.9
  109.9 0.8 copy-start.22
  110.7 0.8 copy-start.24
  111.4 0.8 copy-start.26
  112.2 0.7 copy-start.28
  112.9 0.7 copy-start.30
  113.6 0.7 copy-start.32
  121.8 0.9 copy-start.12

commit v10 on v9

--- a/solution.py
+++ b/solution.py
@@ -14,7 +14,8 @@
 LANES = 128
 ROWS = 16
 SMALL_VMEM = 16 * 1024 * 1024
-EXPERT_VMEM = 24 * 1024 * 1024
+EXPERT_VMEM = 28 * 1024 * 1024
+LARGE_VMEM = 60 * 1024 * 1024
 NT = (((1,), (1,)), ((), ()))
 TN = (((0,), (0,)), ((), ()))
 
@@ -59,7 +60,9 @@
 def joined(refs):
     if len(refs) == 1:
         return refs[0][...]
-    return jnp.concatenate([ref[...].astype(F32) for ref in refs], axis=0).astype(BF16)
+    blocks = [ref[...].astype(F32) if ref is not None else None for ref in refs]
+    empty = jnp.zeros_like(next(block for block in blocks if block is not None))
+    return jnp.concatenate([empty if b is None else b for b in blocks], axis=0).astype(BF16)
 
 
 def parted(value, refs):
@@ -146,11 +149,11 @@
 
 def mixing_kernel(
     sizes, place, arrived_f, arrived_b, embedded, loss, gain, routes_f, routes_b, columns,
-    lanes, wanted, wanted_lanes, saved, router, tokens, upstream, shares_b, *refs,
+    saved, router, tokens, upstream, shares_b, *refs,
 ):
     experts, capacity = sizes["experts"], sizes["capacity"]
     parts = len(sizes["back"])
-    mixing, orders, sends = refs[: 3 * parts], refs[3 * parts : 5 * parts], refs[5 * parts :]
+    mixing, sends = refs[: 3 * parts], refs[3 * parts :]
     tokens[...], normed, upstream[...] = rows_to_send(
         place, arrived_f, arrived_b, embedded, loss, gain
     )
@@ -172,12 +175,6 @@
             out[...] = jnp.transpose(mixed).astype(BF16)
         for k, table in enumerate(found_b):
             tables_b[k] = table
-        source = (sizes["sources"], -1)
-        have = partners(place[2], lanes[0:1, :], *source, there) * sizes["block_rows"] + lanes[1:2, :]
-        orders[2 * part][...] = (wanted[...] == have).astype(F32).astype(BF16)
-        have = partners(place[2], columns[:, 0:1], *source, back) * sizes["block_rows"]
-        have += columns[:, 1:2]
-        orders[2 * part + 1][...] = (have == wanted_lanes[...]).astype(F32).astype(BF16)
         if part > 0:
             if there != back:
                 keys = keys_of_part(sizes, place[2], columns, part, there)
@@ -188,10 +185,28 @@
             sends = sends[blocks:]
 
 
-def expert_kernel(sizes, part, held, order, back_order, saved_pre, up, down, *refs):
-    blocks = sizes["sources"] if sizes["there"][part] else 1
-    got, out = refs[:blocks], refs[blocks:-5]
-    rows, results, up_held, down_held, sems = refs[-5:]
+def row_order(sizes, me, turned, shape, axis):
+    line = tuple(size if i == axis else 1 for i, size in enumerate(shape))
+    row = lax.broadcasted_iota(jnp.int32, line, axis)
+    block = sum(
+        (row >= k * sizes["block_rows"]).astype(jnp.int32) for k in range(1, sizes["sources"])
+    )
+    within = row - block * sizes["block_rows"]
+    group = sum(
+        (within >= k * sizes["capacity"]).astype(jnp.int32)
+        for k in range(1, sizes["block_rows"] // sizes["capacity"])
+    )
+    source = partners(me, block, sizes["sources"], -1, turned)
+    place = group * (sizes["padded"] - sizes["capacity"]) + source * sizes["capacity"] + within
+    return (place == lax.broadcasted_iota(jnp.int32, shape, 1 - axis)).astype(F32).astype(BF16)
+
+
+def expert_kernel(sizes, part, held, place, saved_all, up, down, *refs):
+    there, back = sizes["there"][part], sizes["back"][part]
+    blocks = sizes["sources"] if there else 1
+    got, out = refs[:blocks], refs[blocks:-7]
+    rows, results, saved_pre, up_held, down_held, saved_sem, sems = refs[-7:]
+    moved = blocks * got[0].shape[0]
     width = rows.shape[1]
     slots, halves = sems.shape[:2]
     half = up.shape[2] // halves
@@ -218,8 +233,17 @@
             for copy in copies(jnp.int32(expert), piece):
                 copy.start()
 
-    rows[...] = dot(order[...], joined(got)).astype(BF16)
+        if expert == 0:
+            saved_copy = pltpu.make_async_copy(
+                saved_all.at[pl.ds(part * held, held)], saved_pre, saved_sem
+            )
+            saved_copy.start()
+
+    order = row_order(sizes, place[2], there, (rows.shape[0], moved), 1)
+    rows[...] = dot(order, joined(got)).astype(BF16)
     results[:, width:] = jnp.zeros((results.shape[0], results.shape[1] - width), BF16)
+
+    saved_copy.wait()
 
     def one_expert(expert, carry):
         slot = lax.rem(expert, slots)
@@ -233,7 +257,7 @@
             pre_act = dot(rows[own_f, :], up_held[slot, :, span])
             hidden_grad = dot(rows[own_b, :], down_held[slot, span, :], NT)
             hidden.append((pre_act / (1.0 + jnp.exp(-pre_act))).astype(BF16))
-            pre = saved_pre[part * held + expert, :, span].astype(F32)
+            pre = saved_pre[expert, :, span].astype(F32)
             gate = 1.0 / (1.0 + jnp.exp(-pre))
             inner += jnp.sum(
                 hidden_grad * (pre * gate).astype(BF16).astype(F32), axis=1, keepdims=True
@@ -254,7 +278,8 @@
         return carry
 
     lax.fori_loop(0, held, one_expert, 0)
-    parted(dot(back_order[...], results[...]), out)
+    order = row_order(sizes, place[2], back, (moved, rows.shape[0]), 0)
+    parted(dot(order, results[...]), out)
 
 
 def add_up(blocks, mixing_f, mixing_b, tables):
@@ -273,11 +298,20 @@
     for given, copied in zip(refs, copies):
         copied[...] = given[...]
     refs = refs[handed : -3 - handed]
+    own = None
+    if sizes["back"][-1]:
+        refs, own = refs[:-4], refs[-4:]
     sum_f, sum_b, sums = tokens[...].astype(F32), None, None
     for turned in sizes["back"][:-1]:
         blocks = sizes["sources"] if turned else 1
         more_f, more_b, more = add_up(refs[3 : 3 + blocks], *refs[:3])
         refs = refs[3 + blocks :]
+        sum_f += more_f
+        sum_b = more_b if sum_b is None else sum_b + more_b
+        sums = more if sums is None else [a + b for a, b in zip(sums, more)]
+    if own is not None:
+        blocks = [own[3]] + [None] * (sizes["sources"] - 1)
+        more_f, more_b, more = add_up(blocks, *own[:3])
         sum_f += more_f
         sum_b = more_b if sum_b is None else sum_b + more_b
         sums = more if sums is None else [a + b for a, b in zip(sums, more)]
@@ -292,14 +326,16 @@
 
 
 def late_kernel(
-    experts, early_f, early_b, early_inner, saved, upstream, gain, router, routes,
+    sizes, early_f, early_b, early_inner, saved, upstream, gain, router, routes,
     mixing_f, mixing_b, tables, shares, *refs,
 ):
     *backs, output, gradient = refs
+    if sizes["back"][-1]:
+        backs = [None] + backs
     more_f, more_b, more = add_up(backs, mixing_f, mixing_b, tables)
     widened = saved[...].astype(F32)
     inv_rms = lax.rsqrt(jnp.mean(widened * widened, axis=-1, keepdims=True) + EPS)
-    hits = expert_hits(routes[...], experts)
+    hits = expert_hits(routes[...], sizes["experts"])
     top = len(hits)
     share = [shares[k][:1, :] for k in range(top)]
     inner = [early_inner[k][:1, :] + more[k] for k in range(top)]
@@ -319,12 +355,11 @@
     gradient[0] = (upstream[...].astype(F32) + grad).astype(BF16)
 
 
-def exchange_order(parts, sources, local, capacity, padded):
+def exchange_columns(parts, sources, local, capacity):
     held = local // parts
     slots = sources * local * capacity
     block_rows = 2 * held * capacity
     columns = np.zeros((sources * block_rows, 2 + parts), np.int32)
-    wanted = np.full((2 * held * padded, 1), -1, np.int32)
     for source in range(sources):
         for batch in range(2):
             for expert in range(held):
@@ -335,8 +370,7 @@
                     for part in range(parts):
                         own = (part * held + expert) * capacity + slot
                         columns[row, 2 + part] = batch * slots + own
-                    wanted[(batch * held + expert) * padded + source * capacity + slot] = row
-    return columns, wanted
+    return columns
 
 
 def on_device(
@@ -371,8 +405,7 @@
     few = sources <= 8
     there = [few and part == 0 for part in range(parts)]
     back = [few and part == parts - 1 for part in range(parts)]
-    columns, wanted = exchange_order(parts, sources, local, capacity, padded)
-    lanes, wanted_lanes = np.ascontiguousarray(columns.T), np.ascontiguousarray(wanted.T)
+    columns = exchange_columns(parts, sources, local, capacity)
     sizes = {
         "experts": experts,
         "capacity": capacity,
@@ -415,10 +448,6 @@
         shape((count, moved), BF16),
         shape((top, moved, count), F32),
     ]
-    order_shapes = [
-        shape((2 * held * padded, moved), BF16),
-        shape((moved, 2 * held * padded), BF16),
-    ]
     tokens, upstream, shares_b, *rest = call(
         functools.partial(mixing_kernel, sizes),
         (
@@ -426,17 +455,17 @@
             row_shape,
             shape((top, 8, count), F32),
             *mixing_shapes * parts,
-            *order_shapes * parts,
             *later,
         ),
         (4 * moved * count * width, 2 * (8 * count + moved) * width),
-        in_specs=[SMEM] + [VMEM] * 13,
+        vmem=LARGE_VMEM,
+        in_specs=[SMEM] + [VMEM] * 10,
     )(
-        *given, routes_f, routes_b, columns, lanes, wanted, wanted_lanes, saved_inputs[0], router_t
+        place, arrived_f, arrived_b, embedded, loss_gradient, norm_gain, routes_f, routes_b, columns,
+        saved_inputs[0], router_t,
     )
     mixing = [rest[3 * part : 3 * part + 3] for part in range(parts)]
-    orders = [rest[3 * parts + 2 * part : 3 * parts + 2 * part + 2] for part in range(parts)]
-    sends = rest[5 * parts :]
+    sends = rest[3 * parts :]
     saved_pre = jnp.transpose(pre_activation[0], (1, 0, 2, 3)).reshape(local, rows, hidden)
     saved_pre = jnp.pad(saved_pre, ((0, 0), (0, padded - rows), (0, 0)))
     backs = []
@@ -453,21 +482,24 @@
             tuple(result),
             (8 * held * padded * width * hidden, 4 * held * width * hidden),
             vmem=EXPERT_VMEM,
-            in_specs=[VMEM] * 3 + [HBM] * 2 + [VMEM] * len(got),
+            in_specs=[SMEM] + [HBM] * 3 + [VMEM] * len(got),
             out_specs=(VMEM,) * len(result),
             scratch_shapes=[
                 pltpu.VMEM((2 * held * padded, width), BF16),
                 pltpu.VMEM((2 * held * padded, width + LANES), BF16),
+                pltpu.VMEM((held, padded, hidden), BF16),
                 pltpu.VMEM((min(2, held), width, hidden), BF16),
                 pltpu.VMEM((min(2, held), hidden, width), BF16),
+                pltpu.SemaphoreType.DMA,
                 pltpu.SemaphoreType.DMA((min(2, held), 2, 2)),
             ],
-        )(*orders[part], saved_pre, up_weight, down_weight, *got)
+        )(place, saved_pre, up_weight, down_weight, *got)
         backs.append(exchange(list(done), -1))
         got = coming if part + 1 < parts else None
     handed = (
         saved_inputs[0], upstream, norm_gain, router_t, routes_b, *mixing[-1], shares_b,
     )
+    own = (*mixing[-1], backs[-1][0]) if back[-1] else ()
     early = call(
         functools.partial(early_kernel, sizes, len(handed)),
         (
@@ -477,13 +509,13 @@
             *[shape(array.shape, array.dtype) for array in handed],
         ),
         (4 * moved * count * width, 2 * (10 * count + moved) * width),
-    )(tokens, *handed, *[ref for part in range(parts - 1) for ref in (*mixing[part], *backs[part])])
+    )(tokens, *handed, *[ref for part in range(parts - 1) for ref in (*mixing[part], *backs[part])], *own)
     return tuple(
         call(
-            functools.partial(late_kernel, experts),
+            functools.partial(late_kernel, sizes),
             (shape((1, count, width), BF16),) * 2,
             (4 * moved * count * width, 2 * (8 * count + moved) * width),
-        )(*early, *backs[-1])
+        )(*early, *(backs[-1][1:] if back[-1] else backs[-1]))
     )
 
 

time: 125 us -> 118 us (0.944)
  local copies, waits for them, and re-layouts: 27.8 us -> 9.27 us
  starting transfers between devices: 31.8 us -> 36.8 us
  waiting for transfers between devices: 16 us -> 20.5 us
  Pallas kernels: 47.8 us -> 50.2 us
    unnamed x74 -> x52, local copies, waits for them, and re-layouts: 26.6 us -> 8.01 us
    all_to_all x2, starting transfers between devices: 8.6 us -> 13.6 us  [exchange(): lax.all_to_all(blocks[0], 'expert', split_axis=0, concat_axis=0, tiled=True)]
    ppermute x14, waiting for transfers between devices: 9.7 us -> 14.2 us  [exchange(): got[d] = lax.ppermute(blocks[d], 'expert', route)]
  transfers between devices with their start and end apart: 18 -> 18, of which waited for: 5 -> 7; matrix products, arithmetic and copies ran while one was open for 1% -> 1% of each run, Pallas kernels for 36% -> 40%
where the time goes in v10:
time: 118 us
  Pallas kernels  50.2 us (43%)
  starting transfers between devices  36.8 us (31%)
  waiting for transfers between devices  20.5 us (17%)
  local copies, waits for them, and re-layouts  9.27 us (8%)
    pallas_call x2, Pallas kernels, on_device(): call(functools.partial(expert_kernel, sizes, part, held), tuple(result),...  42.1 us
    ppermute x14, starting transfers between devices, exchange(): got[d] = lax.ppermute(blocks[d], 'expert', route)  17 us
    ppermute x14, waiting for transfers between devices, exchange(): got[d] = lax.ppermute(blocks[d], 'expert', route)  14.2 us
    all_to_all x2, starting transfers between devices, exchange(): lax.all_to_all(blocks[0], 'expert', split_axis=0, concat_axis=0, tiled=True)  13.6 us
    unnamed x52, local copies, waits for them, and re-layouts  8.01 us
    ppermute x2, waiting for transfers between devices, from_behind(): return lax.ppermute(block, axis, route)  6.24 us
    ppermute x2, starting transfers between devices, from_behind(): return lax.ppermute(block, axis, route)  6.15 us
    pallas_call x1, Pallas kernels, on_device(): call(functools.partial(mixing_kernel, sizes), (row_shape, row_shape, shap...  3.24 us
  transfers between devices with their start and end apart: 18, of which 7 were waited for; matrix products, arithmetic and copies ran while one was open for 1% of the time, Pallas kernels for 40%

profile of v10, /device:TPU:0, one launch (start us, length us, event | category | flops | bytes accessed | tf_op | source)
XLA Modules:
  0.0 117.8 jit_solution(10581108815107767969)
XLA Ops:
  0.6 4.9 %collective-permute-start = (bf16[64,2048]{1,0:T(8,128)(2,1)}, bf16[64,2048]{1,0:T(8,128)(2,1)S(1)}, u32[]{:S(2)}, u32[]{:S(2)}) collective-permute-start(bf16[64,2048]{1,0:T(8,128)(2,1)} %bitcast.36), channel_id=1, source_target_pairs={{0,8},{8,16},{16,24},{1,9},{9,17},{17,25},{2,10},{10,18},{18,26},{... | collective-permute-start | bytes 786440 | tf_op jit(solution)/shard_map/ppermute | solution.py:46
  5.5 1.3 %collective-permute-start.1 = (bf16[64,2048]{1,0:T(8,128)(2,1)}, bf16[64,2048]{1,0:T(8,128)(2,1)S(1)}, u32[]{:S(2)}, u32[]{:S(2)}) collective-permute-start(bf16[64,2048]{1,0:T(8,128)(2,1)} %bitcast.37), channel_id=1, source_target_pairs={{8,0},{16,8},{24,16},{9,1},{17,9},{25,17},{10,2},{18,10},{26,18},{... | collective-permute-start | bytes 786440 | tf_op jit(solution)/shard_map/ppermute | solution.py:46
  6.8 0.1 pad_add_fusion.place
  6.9 1.0 copy-done.2
  7.8 0.9 copy-done.3
  8.8 0.9 copy-done.7
  9.7 0.7 copy-done.15
  10.4 0.7 copy-done.22
  11.1 0.7 copy-done.25
  11.7 0.8 shard_map.141
  12.5 0.0 collective-permute-done.arrived_f
  12.6 0.0 copy-start.4
  12.6 6.2 %collective-permute-done.1.arrived_b = bf16[64,2048]{1,0:T(8,128)(2,1)S(1)} collective-permute-done((bf16[64,2048]{1,0:T(8,128)(2,1)}, bf16[64,2048]{1,0:T(8,128)(2,1)S(1)}, u32[]{:S(2)}, u32[]{:S(2)}) %collective-permute-start.1) | collective-permute-done | bytes 262176 | tf_op jit(solution)/shard_map/ppermute | solution.py:46
  18.8 1.1 shard_map.142
  19.9 0.1 collective-permute-start.2
  19.9 1.6 %collective-permute-start.3 = (bf16[24,2048]{1,0:T(8,128)(2,1)S(1)}, bf16[24,2048]{1,0:T(8,128)(2,1)S(1)}, u32[]{:S(2)}, u32[]{:S(2)}) collective-permute-start(bf16[24,2048]{1,0:T(8,128)(2,1)S(1)} %get-tuple-element.70), channel_id=1, source_target_pairs={{0,2},{1,3},{2,4},{3,5},{4,6},{5,7},{6,0},{7,1},{8,10},{9,11},{10,... | collective-permute-start | bytes 294920 | tf_op jit(solution)/shard_map/ppermute | solution.py:56
  21.6 2.5 %collective-permute-start.4 = (bf16[24,2048]{1,0:T(8,128)(2,1)S(1)}, bf16[24,2048]{1,0:T(8,128)(2,1)S(1)}, u32[]{:S(2)}, u32[]{:S(2)}) collective-permute-start(bf16[24,2048]{1,0:T(8,128)(2,1)S(1)} %get-tuple-element.71), channel_id=1, source_target_pairs={{0,3},{1,4},{2,5},{3,6},{4,7},{5,0},{6,1},{7,2},{8,11},{9,12},{10,... | collective-permute-start | bytes 294920 | tf_op jit(solution)/shard_map/ppermute | solution.py:56
  24.1 1.2 %collective-permute-start.5 = (bf16[24,2048]{1,0:T(8,128)(2,1)S(1)}, bf16[24,2048]{1,0:T(8,128)(2,1)S(1)}, u32[]{:S(2)}, u32[]{:S(2)}) collective-permute-start(bf16[24,2048]{1,0:T(8,128)(2,1)S(1)} %get-tuple-element.72), channel_id=1, source_target_pairs={{0,4},{1,5},{2,6},{3,7},{4,0},{5,1},{6,2},{7,3},{8,12},{9,13},{10,... | collective-permute-start | bytes 294920 | tf_op jit(solution)/shard_map/ppermute | solution.py:56
  25.3 1.2 %collective-permute-start.6 = (bf16[24,2048]{1,0:T(8,128)(2,1)S(1)}, bf16[24,2048]{1,0:T(8,128)(2,1)S(1)}, u32[]{:S(2)}, u32[]{:S(2)}) collective-permute-start(bf16[24,2048]{1,0:T(8,128)(2,1)S(1)} %get-tuple-element.73), channel_id=1, source_target_pairs={{0,5},{1,6},{2,7},{3,0},{4,1},{5,2},{6,3},{7,4},{8,13},{9,14},{10,... | collective-permute-start | bytes 294920 | tf_op jit(solution)/shard_map/ppermute | solution.py:56
  26.5 0.0 collective-permute-done.2.refs_1_
  26.5 1.5 %collective-permute-start.7 = (bf16[24,2048]{1,0:T(8,128)(2,1)S(1)}, bf16[24,2048]{1,0:T(8,128)(2,1)S(1)}, u32[]{:S(2)}, u32[]{:S(2)}) collective-permute-start(bf16[24,2048]{1,0:T(8,128)(2,1)S(1)} %get-tuple-element.74), channel_id=1, source_target_pairs={{0,6},{1,7},{2,0},{3,1},{4,2},{5,3},{6,4},{7,5},{8,14},{9,15},{10,... | collective-permute-start | bytes 294920 | tf_op jit(solution)/shard_map/ppermute | solution.py:56
  28.0 0.0 collective-permute-done.3.refs_2_
  28.0 1.5 %collective-permute-start.8 = (bf16[24,2048]{1,0:T(8,128)(2,1)S(1)}, bf16[24,2048]{1,0:T(8,128)(2,1)S(1)}, u32[]{:S(2)}, u32[]{:S(2)}) collective-permute-start(bf16[24,2048]{1,0:T(8,128)(2,1)S(1)} %get-tuple-element.75), channel_id=1, source_target_pairs={{0,7},{1,0},{2,1},{3,2},{4,3},{5,4},{6,5},{7,6},{8,15},{9,8},{10,9... | collective-permute-start | bytes 294920 | tf_op jit(solution)/shard_map/ppermute | solution.py:56
  29.6 1.2 %copy.16 = bf16[8,24,1024]{2,1,0:T(8,128)(2,1)S(1)} copy(bf16[8,24,1024]{2,0,1:T(8,128)(2,1)} %bitcast.35) | data formatting | bytes 786432 | tf_op jit(solution)/shard_map/reshape | solution.py:469
  30.9 3.2 %shard_map.140 = (bf16[64,2048]{1,0:T(8,128)(2,1)}, bf16[64,2048]{1,0:T(8,128)(2,1)}, f32[2,8,64]{2,1,0:T(8,128)}, bf16[64,192]{1,0:T(8,128)(2,1)}, bf16[64,192]...) custom-call(s32[3]{0:T(128)} %copy-done.19, ...), custom_call_target="tpu_custom_call" | custom-call | flops 100663296 | bytes 2883584 | tf_op jit(solution)/shard_map/pallas_call | solution.py:451
  34.1 1.1 collective-permute-done.4.refs_3_
  35.2 0.2 collective-permute-done.5.refs_4_
  35.4 0.0 collective-permute-done.6.refs_5_
  35.4 0.0 collective-permute-done.7.refs_6_
  35.4 0.0 collective-permute-done.8.refs_7_
  35.4 8.5 %all-to-all-start.1 = ((bf16[8,24,2048]{2,1,0:T(8,128)(2,1)}), bf16[8,24,2048]{2,1,0:T(8,128)(2,1)S(1)}, u32[]{:S(2)}, u32[]{:S(2)}) async-start(bf16[8,24,2048]{2,1,0:T(8,128)(2,1)} %bitcast.34), calls=%async_computation.1 | async-start | bytes 1572864 | tf_op jit(solution)/shard_map/all_to_all | solution.py:52
  44.0 0.6 copy-done.20
  44.6 21.1 %shard_map.143 = bf16[192,2176]{1,0:T(8,128)(2,1)} custom-call(s32[3]{0:T(128)S(1)} %copy-done.20, bf16[8,32,1024]{2,1,0:T(8,128)(2,1)S(1)} %pad.4.saved_all, bf16[8,2048,1024]{2,1,0:T(8,128)(2,1)} %up.3, bf16[8,1024,2048]{2,1,0:T(8,128)(2,1)} %down.3, bf16[24,2048]{1,0:T(8,128)(2,1)S(1)} %get-tuple-element.77.refs_0_, ...), custom_call_target="tpu_custom_call" | custom-call | flops 2147483648 | bytes 33554432 | tf_op jit(solution)/shard_map/pallas_call | solution.py:480
  65.7 0.0 all-to-all-done.1
  65.7 5.1 %all-to-all-start = ((bf16[8,24,2176]{2,1,0:T(8,128)(2,1)}), bf16[8,24,2176]{2,1,0:T(8,128)(2,1)S(1)}, u32[]{:S(2)}, u32[]{:S(2)}) async-start(bf16[8,24,2176]{2,1,0:T(8,128)(2,1)} %bitcast.16), calls=%async_computation | async-start | bytes 1671168 | tf_op jit(solution)/shard_map/all_to_all | solution.py:52
  70.8 0.0 copy-done.21
  70.8 0.0 copy-start
  70.8 0.0 copy-start.1
  70.9 0.0 copy-start.16
  70.9 0.0 copy-start.17
  70.9 0.0 copy-start.18
  70.9 0.0 copy-start.23
  71.0 21.0 %shard_map.144 = (bf16[24,2176]{1,0:T(8,128)(2,1)S(1)}, bf16[24,2176]{1,0:T(8,128)(2,1)S(1)}, bf16[24,2176]{1,0:T(8,128)(2,1)S(1)}, bf16[24,2176]{1,0:T(8,128)(2...) custom-call(s32[3]{0:T(128)S(1)} %copy-done.21, ...), custom_call_target="tpu_custom_call" | custom-call | flops 2147483648 | bytes 33554432 | tf_op jit(solution)/shard_map/pallas_call | solution.py:480
  91.9 0.0 copy-start.13
  92.0 0.7 copy-done.13
  92.6 3.6 %collective-permute-start.9 = (bf16[24,2176]{1,0:T(8,128)(2,1)S(1)}, bf16[24,2176]{1,0:T(8,128)(2,1)S(1)}, u32[]{:S(2)}, u32[]{:S(2)}) collective-permute-start(bf16[24,2176]{1,0:T(8,128)(2,1)S(1)} %get-tuple-element.99), channel_id=1, source_target_pairs={{0,7},{1,0},{2,1},{3,2},{4,3},{5,4},{6,5},{7,6},{8,15},{9,8},{10,9... | collective-permute-start | bytes 313352 | tf_op jit(solution)/shard_map/ppermute | solution.py:56
  96.2 0.6 collective-permute-start.10
  96.7 0.0 collective-permute-start.11
  96.7 2.4 %collective-permute-start.12 = (bf16[24,2176]{1,0:T(8,128)(2,1)}, bf16[24,2176]{1,0:T(8,128)(2,1)S(1)}, u32[]{:S(2)}, u32[]{:S(2)}) collective-permute-start(bf16[24,2176]{1,0:T(8,128)(2,1)} %get-tuple-element.102), channel_id=1, source_target_pairs={{0,4},{1,5},{2,6},{3,7},{4,0},{5,1},{6,2},{7,3},{8,12},{9,13},{10,... | collective-permute-start | bytes 313352 | tf_op jit(solution)/shard_map/ppermute | solution.py:56
  99.2 0.0 collective-permute-start.13
  99.2 0.3 collective-permute-done.9.refs_0_
  99.5 0.7 collective-permute-start.14
  100.2 2.3 %collective-permute-done.10.refs_1_ = bf16[24,2176]{1,0:T(8,128)(2,1)S(1)} collective-permute-done((bf16[24,2176]{1,0:T(8,128)(2,1)S(1)}, bf16[24,2176]{1,0:T(8,128)(2,1)S(1)}, u32[]{:S(2)}, u32[]{:S(2)}) %collective-permute-start.10) | collective-permute-done | bytes 104480 | tf_op jit(solution)/shard_map/ppermute | solution.py:56
  102.5 0.0 collective-permute-start.15
  102.5 0.0 all-to-all-done
  102.6 0.9 copy-done.10
  103.6 0.9 copy-done.14
  104.5 0.6 shard_map.145
  105.1 0.0 collective-permute-done.11.refs_2_
  105.1 9.3 %collective-permute-done.12.refs_3_ = bf16[24,2176]{1,0:T(8,128)(2,1)S(1)} collective-permute-done((bf16[24,2176]{1,0:T(8,128)(2,1)}, bf16[24,2176]{1,0:T(8,128)(2,1)S(1)}, u32[]{:S(2)}, u32[]{:S(2)}) %collective-permute-start.12) | collective-permute-done | bytes 104480 | tf_op jit(solution)/shard_map/ppermute | solution.py:56
  114.4 1.0 collective-permute-done.13.refs_4_
  115.4 0.0 collective-permute-done.14.refs_5_
  115.4 0.0 collective-permute-done.15.refs_6_
  115.4 2.4 %shard_map.146 = (bf16[1,64,2048]{2,1,0:T(8,128)(2,1)}, bf16[1,64,2048]{2,1,0:T(8,128)(2,1)}) custom-call(f32[64,2048]{1,0:T(8,128)S(1)} %get-tuple-element.87.early_f, f32[64,2048]{1,0:T(8,128)S(1)} %get-tuple-element.88.early_b, f32[2,8,64]{2,1,0:T(8,128)S(1)} %get-tuple-element.89.early_inner, bf16[64,2048]{1,0:T(8,128)(2,1)S(1)} %get-tuple-element.90.saved, ...), custom_call_target="tpu_custom_call" | custom-call | flops 100663296 | bytes 2883584 | tf_op jit(solution)/shard_map/pallas_call | solution.py:514
  (34 shorter events, 0.1 us)
Async XLA Ops:
  0.6 11.9 %collective-permute-start = (bf16[64,2048]{1,0:T(8,128)(2,1)}, bf16[64,2048]{1,0:T(8,128)(2,1)S(1)}, u32[]{:S(2)}, u32[]{:S(2)}) collective-permute-start(bf16[64,2048]{1,0:T(8,128)(2,1)} %bitcast.36), channel_id=1, source_target_pairs={{0,8},{8,16},{16,24},{1,9},{9,17},{17,25},{2,10},{10,18},{18,26},{... | collective-permute-start | bytes 786440 | tf_op jit(solution)/shard_map/ppermute | solution.py:46
  5.5 13.3 %collective-permute-start.1 = (bf16[64,2048]{1,0:T(8,128)(2,1)}, bf16[64,2048]{1,0:T(8,128)(2,1)S(1)}, u32[]{:S(2)}, u32[]{:S(2)}) collective-permute-start(bf16[64,2048]{1,0:T(8,128)(2,1)} %bitcast.37), channel_id=1, source_target_pairs={{8,0},{16,8},{24,16},{9,1},{17,9},{25,17},{10,2},{18,10},{26,18},{... | collective-permute-start | bytes 786440 | tf_op jit(solution)/shard_map/ppermute | solution.py:46
  6.9 24.0 %copy-start.19 = (s32[3]{0:T(128)}, s32[3]{0:T(128)S(1)}, u32[]{:S(2)}) copy-start(s32[3]{0:T(128)S(1)} %pad_add_fusion.place) | copy-start | bytes 40
  6.9 1.0 copy-start.2
  7.8 0.9 copy-start.3
  8.8 0.9 copy-start.7
  9.7 0.7 copy-start.15
  10.4 0.7 copy-start.22
  11.1 0.7 copy-start.25
  12.6 18.3 %copy-start.4 = (bf16[64,2048]{1,0:T(8,128)(2,1)}, bf16[64,2048]{1,0:T(8,128)(2,1)S(1)}, u32[]{:S(2)}) copy-start(bf16[64,2048]{1,0:T(8,128)(2,1)S(1)} %collective-permute-done.arrived_f) | copy-start | bytes 786436
  18.8 12.1 %copy-start.5 = (bf16[64,2048]{1,0:T(8,128)(2,1)}, bf16[64,2048]{1,0:T(8,128)(2,1)S(1)}, u32[]{:S(2)}) copy-start(bf16[64,2048]{1,0:T(8,128)(2,1)S(1)} %collective-permute-done.1.arrived_b) | copy-start | bytes 786436
  19.9 6.7 %collective-permute-start.2 = (bf16[24,2048]{1,0:T(8,128)(2,1)S(1)}, bf16[24,2048]{1,0:T(8,128)(2,1)S(1)}, u32[]{:S(2)}, u32[]{:S(2)}) collective-permute-start(bf16[24,2048]{1,0:T(8,128)(2,1)S(1)} %get-tuple-element.69), channel_id=1, source_target_pairs={{0,1},{1,2},{2,3},{3,4},{4,5},{5,6},{6,7},{7,0},{8,9},{9,10},{10,1... | collective-permute-start | bytes 294920 | tf_op jit(solution)/shard_map/ppermute | solution.py:56
  19.9 8.1 %collective-permute-start.3 = (bf16[24,2048]{1,0:T(8,128)(2,1)S(1)}, bf16[24,2048]{1,0:T(8,128)(2,1)S(1)}, u32[]{:S(2)}, u32[]{:S(2)}) collective-permute-start(bf16[24,2048]{1,0:T(8,128)(2,1)S(1)} %get-tuple-element.70), channel_id=1, source_target_pairs={{0,2},{1,3},{2,4},{3,5},{4,6},{5,7},{6,0},{7,1},{8,10},{9,11},{10,... | collective-permute-start | bytes 294920 | tf_op jit(solution)/shard_map/ppermute | solution.py:56
  21.6 13.7 %collective-permute-start.4 = (bf16[24,2048]{1,0:T(8,128)(2,1)S(1)}, bf16[24,2048]{1,0:T(8,128)(2,1)S(1)}, u32[]{:S(2)}, u32[]{:S(2)}) collective-permute-start(bf16[24,2048]{1,0:T(8,128)(2,1)S(1)} %get-tuple-element.71), channel_id=1, source_target_pairs={{0,3},{1,4},{2,5},{3,6},{4,7},{5,0},{6,1},{7,2},{8,11},{9,12},{10,... | collective-permute-start | bytes 294920 | tf_op jit(solution)/shard_map/ppermute | solution.py:56
  24.1 11.3 %collective-permute-start.5 = (bf16[24,2048]{1,0:T(8,128)(2,1)S(1)}, bf16[24,2048]{1,0:T(8,128)(2,1)S(1)}, u32[]{:S(2)}, u32[]{:S(2)}) collective-permute-start(bf16[24,2048]{1,0:T(8,128)(2,1)S(1)} %get-tuple-element.72), channel_id=1, source_target_pairs={{0,4},{1,5},{2,6},{3,7},{4,0},{5,1},{6,2},{7,3},{8,12},{9,13},{10,... | collective-permute-start | bytes 294920 | tf_op jit(solution)/shard_map/ppermute | solution.py:56
  25.3 10.1 %collective-permute-start.6 = (bf16[24,2048]{1,0:T(8,128)(2,1)S(1)}, bf16[24,2048]{1,0:T(8,128)(2,1)S(1)}, u32[]{:S(2)}, u32[]{:S(2)}) collective-permute-start(bf16[24,2048]{1,0:T(8,128)(2,1)S(1)} %get-tuple-element.73), channel_id=1, source_target_pairs={{0,5},{1,6},{2,7},{3,0},{4,1},{5,2},{6,3},{7,4},{8,13},{9,14},{10,... | collective-permute-start | bytes 294920 | tf_op jit(solution)/shard_map/ppermute | solution.py:56
  26.5 8.9 %collective-permute-start.7 = (bf16[24,2048]{1,0:T(8,128)(2,1)S(1)}, bf16[24,2048]{1,0:T(8,128)(2,1)S(1)}, u32[]{:S(2)}, u32[]{:S(2)}) collective-permute-start(bf16[24,2048]{1,0:T(8,128)(2,1)S(1)} %get-tuple-element.74), channel_id=1, source_target_pairs={{0,6},{1,7},{2,0},{3,1},{4,2},{5,3},{6,4},{7,5},{8,14},{9,15},{10,... | collective-permute-start | bytes 294920 | tf_op jit(solution)/shard_map/ppermute | solution.py:56
  28.0 7.4 %collective-permute-start.8 = (bf16[24,2048]{1,0:T(8,128)(2,1)S(1)}, bf16[24,2048]{1,0:T(8,128)(2,1)S(1)}, u32[]{:S(2)}, u32[]{:S(2)}) collective-permute-start(bf16[24,2048]{1,0:T(8,128)(2,1)S(1)} %get-tuple-element.75), channel_id=1, source_target_pairs={{0,7},{1,0},{2,1},{3,2},{4,3},{5,4},{6,5},{7,6},{8,15},{9,8},{10,9... | collective-permute-start | bytes 294920 | tf_op jit(solution)/shard_map/ppermute | solution.py:56
  35.4 30.3 %all-to-all-start.1 = ((bf16[8,24,2048]{2,1,0:T(8,128)(2,1)}), bf16[8,24,2048]{2,1,0:T(8,128)(2,1)S(1)}, u32[]{:S(2)}, u32[]{:S(2)}) async-start(bf16[8,24,2048]{2,1,0:T(8,128)(2,1)} %bitcast.34), calls=%async_computation.1 | async-start | bytes 1572864 | tf_op jit(solution)/shard_map/all_to_all | solution.py:52
  44.0 0.6 copy-start.20
  44.6 26.2 %copy-start.21 = (s32[3]{0:T(128)S(1)}, s32[3]{0:T(128)}, u32[]{:S(2)}) copy-start(s32[3]{0:T(128)} %copy-done.19) | copy-start | bytes 40
  65.7 36.8 %all-to-all-start = ((bf16[8,24,2176]{2,1,0:T(8,128)(2,1)}), bf16[8,24,2176]{2,1,0:T(8,128)(2,1)S(1)}, u32[]{:S(2)}, u32[]{:S(2)}) async-start(bf16[8,24,2176]{2,1,0:T(8,128)(2,1)} %bitcast.16), calls=%async_computation | async-start | bytes 1671168 | tf_op jit(solution)/shard_map/all_to_all | solution.py:52
  70.8 31.7 %copy-start = (bf16[1,64,2048]{2,1,0:T(8,128)(2,1)S(1)}, bf16[1,64,2048]{2,1,0:T(8,128)(2,1)}, u32[]{:S(2)}) copy-start(bf16[1,64,2048]{2,1,0:T(8,128)(2,1)} %param.18) | copy-start | bytes 786436
  70.8 31.7 %copy-start.1 = (bf16[1,2048,64]{1,2,0:T(8,128)(2,1)S(1)}, bf16[1,2048,64]{1,2,0:T(8,128)(2,1)}, u32[]{:S(2)}) copy-start(bf16[1,2048,64]{1,2,0:T(8,128)(2,1)} %param.22) | copy-start | bytes 786436
  70.9 31.7 %copy-start.6 = (f32[2,192,64]{2,1,0:T(8,128)S(1)}, f32[2,192,64]{2,1,0:T(8,128)}, u32[]{:S(2)}) copy-start(f32[2,192,64]{2,1,0:T(8,128)} %get-tuple-element.58.refs_7_.refs_15_) | copy-start | bytes 294916
  70.9 31.7 %copy-start.8 = (bf16[64,2048]{1,0:T(8,128)(2,1)S(1)}, bf16[64,2048]{1,0:T(8,128)(2,1)}, u32[]{:S(2)}) copy-start(bf16[64,2048]{1,0:T(8,128)(2,1)} %get-tuple-element.54.tokens) | copy-start | bytes 786436
  70.9 31.7 %copy-start.9 = (bf16[64,2048]{1,0:T(8,128)(2,1)S(1)}, bf16[64,2048]{1,0:T(8,128)(2,1)}, u32[]{:S(2)}) copy-start(bf16[64,2048]{1,0:T(8,128)(2,1)} %get-tuple-element.55.refs_1_) | copy-start | bytes 786436
  70.9 31.7 %copy-start.11 = (bf16[64,192]{1,0:T(8,128)(2,1)S(1)}, bf16[64,192]{1,0:T(8,128)(2,1)}, u32[]{:S(2)}) copy-start(bf16[64,192]{1,0:T(8,128)(2,1)} %get-tuple-element.56.refs_5_.refs_13_) | copy-start | bytes 73732
  70.9 31.7 %copy-start.12 = (bf16[64,192]{1,0:T(8,128)(2,1)S(1)}, bf16[64,192]{1,0:T(8,128)(2,1)}, u32[]{:S(2)}) copy-start(bf16[64,192]{1,0:T(8,128)(2,1)} %get-tuple-element.57.refs_6_.refs_14_) | copy-start | bytes 73732
  70.9 31.7 %copy-start.16 = (bf16[1,2048]{1,0:T(2,128)(2,1)S(1)}, bf16[1,2048]{1,0:T(2,128)(2,1)}, u32[]{:S(2)}) copy-start(bf16[1,2048]{1,0:T(2,128)(2,1)} %refs_2_.1) | copy-start | bytes 12292
  70.9 31.7 %copy-start.17 = (bf16[64,192]{1,0:T(8,128)(2,1)S(1)}, bf16[64,192]{1,0:T(8,128)(2,1)}, u32[]{:S(2)}) copy-start(bf16[64,192]{1,0:T(8,128)(2,1)} %get-tuple-element.60.refs_9_) | copy-start | bytes 73732
  70.9 31.7 %copy-start.18 = (bf16[64,192]{1,0:T(8,128)(2,1)S(1)}, bf16[64,192]{1,0:T(8,128)(2,1)}, u32[]{:S(2)}) copy-start(bf16[64,192]{1,0:T(8,128)(2,1)} %get-tuple-element.61.refs_10_) | copy-start | bytes 73732
  70.9 31.7 %copy-start.23 = (s32[1,64,2]{1,2,0:T(2,128)S(1)}, s32[1,64,2]{1,2,0:T(2,128)}, u32[]{:S(2)}) copy-start(s32[1,64,2]{1,2,0:T(2,128)} %param.19) | copy-start | bytes 1540
  70.9 31.7 %copy-start.24 = (f32[2,8,64]{2,1,0:T(8,128)S(1)}, f32[2,8,64]{2,1,0:T(8,128)}, u32[]{:S(2)}) copy-start(f32[2,8,64]{2,1,0:T(8,128)} %get-tuple-element.59.refs_8_) | copy-start | bytes 12292
  91.9 0.7 copy-start.13
  92.6 6.9 %collective-permute-start.9 = (bf16[24,2176]{1,0:T(8,128)(2,1)S(1)}, bf16[24,2176]{1,0:T(8,128)(2,1)S(1)}, u32[]{:S(2)}, u32[]{:S(2)}) collective-permute-start(bf16[24,2176]{1,0:T(8,128)(2,1)S(1)} %get-tuple-element.99), channel_id=1, source_target_pairs={{0,7},{1,0},{2,1},{3,2},{4,3},{5,4},{6,5},{7,6},{8,15},{9,8},{10,9... | collective-permute-start | bytes 313352 | tf_op jit(solution)/shard_map/ppermute | solution.py:56
  96.2 6.3 %collective-permute-start.10 = (bf16[24,2176]{1,0:T(8,128)(2,1)S(1)}, bf16[24,2176]{1,0:T(8,128)(2,1)S(1)}, u32[]{:S(2)}, u32[]{:S(2)}) collective-permute-start(bf16[24,2176]{1,0:T(8,128)(2,1)S(1)} %get-tuple-element.100), channel_id=1, source_target_pairs={{0,6},{1,7},{2,0},{3,1},{4,2},{5,3},{6,4},{7,5},{8,14},{9,15},{10,... | collective-permute-start | bytes 313352 | tf_op jit(solution)/shard_map/ppermute | solution.py:56
  96.7 8.3 %collective-permute-start.11 = (bf16[24,2176]{1,0:T(8,128)(2,1)}, bf16[24,2176]{1,0:T(8,128)(2,1)S(1)}, u32[]{:S(2)}, u32[]{:S(2)}) collective-permute-start(bf16[24,2176]{1,0:T(8,128)(2,1)} %get-tuple-element.101), channel_id=1, source_target_pairs={{0,5},{1,6},{2,7},{3,0},{4,1},{5,2},{6,3},{7,4},{8,13},{9,14},{10,... | collective-permute-start | bytes 313352 | tf_op jit(solution)/shard_map/ppermute | solution.py:56
  96.7 17.6 %collective-permute-start.12 = (bf16[24,2176]{1,0:T(8,128)(2,1)}, bf16[24,2176]{1,0:T(8,128)(2,1)S(1)}, u32[]{:S(2)}, u32[]{:S(2)}) collective-permute-start(bf16[24,2176]{1,0:T(8,128)(2,1)} %get-tuple-element.102), channel_id=1, source_target_pairs={{0,4},{1,5},{2,6},{3,7},{4,0},{5,1},{6,2},{7,3},{8,12},{9,13},{10,... | collective-permute-start | bytes 313352 | tf_op jit(solution)/shard_map/ppermute | solution.py:56
  99.2 16.2 %collective-permute-start.13 = (bf16[24,2176]{1,0:T(8,128)(2,1)}, bf16[24,2176]{1,0:T(8,128)(2,1)S(1)}, u32[]{:S(2)}, u32[]{:S(2)}) collective-permute-start(bf16[24,2176]{1,0:T(8,128)(2,1)} %get-tuple-element.103), channel_id=1, source_target_pairs={{0,3},{1,4},{2,5},{3,6},{4,7},{5,0},{6,1},{7,2},{8,11},{9,12},{10,... | collective-permute-start | bytes 313352 | tf_op jit(solution)/shard_map/ppermute | solution.py:56
  99.5 15.9 %collective-permute-start.14 = (bf16[24,2176]{1,0:T(8,128)(2,1)}, bf16[24,2176]{1,0:T(8,128)(2,1)S(1)}, u32[]{:S(2)}, u32[]{:S(2)}) collective-permute-start(bf16[24,2176]{1,0:T(8,128)(2,1)} %get-tuple-element.104), channel_id=1, source_target_pairs={{0,2},{1,3},{2,4},{3,5},{4,6},{5,7},{6,0},{7,1},{8,10},{9,11},{10,... | collective-permute-start | bytes 313352 | tf_op jit(solution)/shard_map/ppermute | solution.py:56
  102.5 12.9 %collective-permute-start.15 = (bf16[24,2176]{1,0:T(8,128)(2,1)}, bf16[24,2176]{1,0:T(8,128)(2,1)}, u32[]{:S(2)}, u32[]{:S(2)}) collective-permute-start(bf16[24,2176]{1,0:T(8,128)(2,1)} %get-tuple-element.105), channel_id=1, source_target_pairs={{0,1},{1,2},{2,3},{3,4},{4,5},{5,6},{6,7},{7,0},{8,9},{9,10},{10,1... | collective-permute-start | bytes 313352 | tf_op jit(solution)/shard_map/ppermute | solution.py:56
  102.6 0.9 copy-start.10
  103.6 0.9 copy-start.14

commit v11 on v10

--- a/solution.py
+++ b/solution.py
@@ -472,7 +472,12 @@
     got = exchange(send, 1)
     for part in range(parts):
         if part + 1 < parts:
-            sends, saved_pre, got = lax.optimization_barrier((sends, saved_pre, got))
+            near = got[1 : len(got) // 2] if there[part] else got
+            sends, saved_pre, near = lax.optimization_barrier((sends, saved_pre, near))
+            if there[part]:
+                got[1 : len(got) // 2] = near
+            else:
+                got = near
             blocks = len(blocks_of(there[part + 1], width))
             coming = exchange(sends[:blocks], 1)
             sends = sends[blocks:]

time: 118 us -> 137 us (1.16)
  waiting for transfers between devices: 20.5 us -> 41.5 us
  starting transfers between devices: 36.8 us -> 34.7 us
    ppermute x14, waiting for transfers between devices: 14.2 us -> 35.2 us  [exchange(): got[d] = lax.ppermute(blocks[d], 'expert', route)]
    all_to_all x2, starting transfers between devices: 13.6 us -> 10.3 us  [exchange(): lax.all_to_all(blocks[0], 'expert', split_axis=0, concat_axis=0, tiled=True)]
  transfers between devices with their start and end apart: 18 -> 18, of which waited for: 7 -> 7; matrix products, arithmetic and copies ran while one was open for 1% -> 1% of each run, Pallas kernels for 40% -> 34%
where the time goes in v11:
time: 137 us
  Pallas kernels  50.2 us (37%)
  waiting for transfers between devices  41.5 us (30%)
  starting transfers between devices  34.7 us (25%)
  local copies, waits for them, and re-layouts  9.26 us (7%)
    pallas_call x2, Pallas kernels, on_device(): call(functools.partial(expert_kernel, sizes, part, held), tuple(result),...  42.1 us
    ppermute x14, waiting for transfers between devices, exchange(): got[d] = lax.ppermute(blocks[d], 'expert', route)  35.2 us
    ppermute x14, starting transfers between devices, exchange(): got[d] = lax.ppermute(blocks[d], 'expert', route)  18.2 us
    all_to_all x2, starting transfers between devices, exchange(): lax.all_to_all(blocks[0], 'expert', split_axis=0, concat_axis=0, tiled=True)  10.3 us
    unnamed x52, local copies, waits for them, and re-layouts  8 us
    ppermute x2, waiting for transfers between devices, from_behind(): return lax.ppermute(block, axis, route)  6.24 us
    ppermute x2, starting transfers between devices, from_behind(): return lax.ppermute(block, axis, route)  6.15 us
    pallas_call x1, Pallas kernels, on_device(): call(functools.partial(mixing_kernel, sizes), (row_shape, row_shape, shap...  3.24 us
  transfers between devices with their start and end apart: 18, of which 7 were waited for; matrix products, arithmetic and copies ran while one was open for 1% of the time, Pallas kernels for 34%

profile of v11, /device:TPU:0, one launch (start us, length us, event | category | flops | bytes accessed | tf_op | source)
XLA Modules:
  0.0 136.7 jit_solution(5210633036018498945)
XLA Ops:
  0.6 4.9 %collective-permute-start = (bf16[64,2048]{1,0:T(8,128)(2,1)}, bf16[64,2048]{1,0:T(8,128)(2,1)S(1)}, u32[]{:S(2)}, u32[]{:S(2)}) collective-permute-start(bf16[64,2048]{1,0:T(8,128)(2,1)} %bitcast.36), channel_id=1, source_target_pairs={{0,8},{8,16},{16,24},{1,9},{9,17},{17,25},{2,10},{10,18},{18,26},{... | collective-permute-start | bytes 786440 | tf_op jit(solution)/shard_map/ppermute | solution.py:46
  5.5 1.3 collective-permute-start.1
  6.8 0.1 pad_add_fusion.place
  6.9 1.0 copy-done.2
  7.8 0.9 copy-done.3
  8.8 0.9 copy-done.7
  9.7 0.7 copy-done.15
  10.4 0.7 copy-done.22
  11.1 0.7 copy-done.25
  11.7 0.8 shard_map.141
  12.5 0.0 collective-permute-done.arrived_f
  12.6 0.0 copy-start.4
  12.6 6.2 %collective-permute-done.1.arrived_b = bf16[64,2048]{1,0:T(8,128)(2,1)S(1)} collective-permute-done((bf16[64,2048]{1,0:T(8,128)(2,1)}, bf16[64,2048]{1,0:T(8,128)(2,1)S(1)}, u32[]{:S(2)}, u32[]{:S(2)}) %collective-permute-start.1) | collective-permute-done | bytes 262176 | tf_op jit(solution)/shard_map/ppermute | solution.py:46
  18.8 1.1 shard_map.142
  19.9 0.1 collective-permute-start.2
  19.9 1.6 %collective-permute-start.3 = (bf16[24,2048]{1,0:T(8,128)(2,1)S(1)}, bf16[24,2048]{1,0:T(8,128)(2,1)S(1)}, u32[]{:S(2)}, u32[]{:S(2)}) collective-permute-start(bf16[24,2048]{1,0:T(8,128)(2,1)S(1)} %get-tuple-element.64), channel_id=1, source_target_pairs={{0,2},{1,3},{2,4},{3,5},{4,6},{5,7},{6,0},{7,1},{8,10},{9,11},{10,... | collective-permute-start | bytes 294920 | tf_op jit(solution)/shard_map/ppermute | solution.py:56
  21.6 2.5 %collective-permute-start.4 = (bf16[24,2048]{1,0:T(8,128)(2,1)S(1)}, bf16[24,2048]{1,0:T(8,128)(2,1)S(1)}, u32[]{:S(2)}, u32[]{:S(2)}) collective-permute-start(bf16[24,2048]{1,0:T(8,128)(2,1)S(1)} %get-tuple-element.65), channel_id=1, source_target_pairs={{0,3},{1,4},{2,5},{3,6},{4,7},{5,0},{6,1},{7,2},{8,11},{9,12},{10,... | collective-permute-start | bytes 294920 | tf_op jit(solution)/shard_map/ppermute | solution.py:56
  24.1 1.2 copy.16
  25.4 0.0 copy-done.19
  25.4 0.0 copy-done.4
  25.4 0.0 copy-done.5
  25.4 3.2 %shard_map.140 = (bf16[64,2048]{1,0:T(8,128)(2,1)}, bf16[64,2048]{1,0:T(8,128)(2,1)}, f32[2,8,64]{2,1,0:T(8,128)}, bf16[64,192]{1,0:T(8,128)(2,1)}, bf16[64,192]...) custom-call(s32[3]{0:T(128)} %copy-done.19, ...), custom_call_target="tpu_custom_call" | custom-call | flops 100663296 | bytes 2883584 | tf_op jit(solution)/shard_map/pallas_call | solution.py:451
  28.6 0.0 collective-permute-done.2.refs_1_
  28.6 0.0 collective-permute-done.3.refs_2_
  28.6 2.4 %collective-permute-done.4.refs_3_ = bf16[24,2048]{1,0:T(8,128)(2,1)S(1)} collective-permute-done((bf16[24,2048]{1,0:T(8,128)(2,1)S(1)}, bf16[24,2048]{1,0:T(8,128)(2,1)S(1)}, u32[]{:S(2)}, u32[]{:S(2)}) %collective-permute-start.4) | collective-permute-done | bytes 98336 | tf_op jit(solution)/shard_map/ppermute | solution.py:56
  31.0 3.5 %all-to-all-start.1 = ((bf16[8,24,2048]{2,1,0:T(8,128)(2,1)}), bf16[8,24,2048]{2,1,0:T(8,128)(2,1)S(1)}, u32[]{:S(2)}, u32[]{:S(2)}) async-start(bf16[8,24,2048]{2,1,0:T(8,128)(2,1)} %bitcast.34), calls=%async_computation.1 | async-start | bytes 1572864 | tf_op jit(solution)/shard_map/all_to_all | solution.py:52
  34.6 2.8 %collective-permute-start.5 = (bf16[24,2048]{1,0:T(8,128)(2,1)S(1)}, bf16[24,2048]{1,0:T(8,128)(2,1)S(1)}, u32[]{:S(2)}, u32[]{:S(2)}) collective-permute-start(bf16[24,2048]{1,0:T(8,128)(2,1)S(1)} %get-tuple-element.71), channel_id=1, source_target_pairs={{0,4},{1,5},{2,6},{3,7},{4,0},{5,1},{6,2},{7,3},{8,12},{9,13},{10,... | collective-permute-start | bytes 294920 | tf_op jit(solution)/shard_map/ppermute | solution.py:56
  37.4 0.0 collective-permute-start.6
  37.4 3.3 %collective-permute-start.7 = (bf16[24,2048]{1,0:T(8,128)(2,1)S(1)}, bf16[24,2048]{1,0:T(8,128)(2,1)S(1)}, u32[]{:S(2)}, u32[]{:S(2)}) collective-permute-start(bf16[24,2048]{1,0:T(8,128)(2,1)S(1)} %get-tuple-element.73), channel_id=1, source_target_pairs={{0,6},{1,7},{2,0},{3,1},{4,2},{5,3},{6,4},{7,5},{8,14},{9,15},{10,... | collective-permute-start | bytes 294920 | tf_op jit(solution)/shard_map/ppermute | solution.py:56
  40.7 0.5 collective-permute-start.8
  41.3 20.0 %collective-permute-done.5.refs_4_ = bf16[24,2048]{1,0:T(8,128)(2,1)S(1)} collective-permute-done((bf16[24,2048]{1,0:T(8,128)(2,1)S(1)}, bf16[24,2048]{1,0:T(8,128)(2,1)S(1)}, u32[]{:S(2)}, u32[]{:S(2)}) %collective-permute-start.5) | collective-permute-done | bytes 98336 | tf_op jit(solution)/shard_map/ppermute | solution.py:56
  61.2 0.0 collective-permute-done.6.refs_5_
  61.2 0.0 collective-permute-done.7.refs_6_
  61.2 0.0 collective-permute-done.8.refs_7_
  61.2 0.6 copy-done.20
  61.9 21.1 %shard_map.143 = bf16[192,2176]{1,0:T(8,128)(2,1)} custom-call(s32[3]{0:T(128)S(1)} %copy-done.20, bf16[8,32,1024]{2,1,0:T(8,128)(2,1)S(1)} %pad.4.saved_all, bf16[8,2048,1024]{2,1,0:T(8,128)(2,1)} %up.3, bf16[8,1024,2048]{2,1,0:T(8,128)(2,1)} %down.3, bf16[24,2048]{1,0:T(8,128)(2,1)S(1)} %get-tuple-element.67.refs_0_, ...), custom_call_target="tpu_custom_call" | custom-call | flops 2147483648 | bytes 33554432 | tf_op jit(solution)/shard_map/pallas_call | solution.py:485
  83.0 0.0 all-to-all-done.1
  83.0 6.8 %all-to-all-start = ((bf16[8,24,2176]{2,1,0:T(8,128)(2,1)}), bf16[8,24,2176]{2,1,0:T(8,128)(2,1)S(1)}, u32[]{:S(2)}, u32[]{:S(2)}) async-start(bf16[8,24,2176]{2,1,0:T(8,128)(2,1)} %bitcast.16), calls=%async_computation | async-start | bytes 1671168 | tf_op jit(solution)/shard_map/all_to_all | solution.py:52
  89.7 0.0 copy-start
  89.7 0.0 copy-start.1
  89.8 0.0 copy-start.6
  89.8 0.0 copy-start.16
  89.8 0.0 copy-start.23
  89.9 21.0 %shard_map.144 = (bf16[24,2176]{1,0:T(8,128)(2,1)S(1)}, bf16[24,2176]{1,0:T(8,128)(2,1)S(1)}, bf16[24,2176]{1,0:T(8,128)(2,1)S(1)}, bf16[24,2176]{1,0:T(8,128)(2...) custom-call(s32[3]{0:T(128)S(1)} %copy-done.21, ...), custom_call_target="tpu_custom_call" | custom-call | flops 2147483648 | bytes 33554432 | tf_op jit(solution)/shard_map/pallas_call | solution.py:485
  110.9 0.7 copy-done.13
  111.5 3.6 %collective-permute-start.9 = (bf16[24,2176]{1,0:T(8,128)(2,1)S(1)}, bf16[24,2176]{1,0:T(8,128)(2,1)S(1)}, u32[]{:S(2)}, u32[]{:S(2)}) collective-permute-start(bf16[24,2176]{1,0:T(8,128)(2,1)S(1)} %get-tuple-element.89), channel_id=1, source_target_pairs={{0,7},{1,0},{2,1},{3,2},{4,3},{5,4},{6,5},{7,6},{8,15},{9,8},{10,9... | collective-permute-start | bytes 313352 | tf_op jit(solution)/shard_map/ppermute | solution.py:56
  115.1 0.6 collective-permute-start.10
  115.6 0.0 collective-permute-start.11
  115.6 2.4 %collective-permute-start.12 = (bf16[24,2176]{1,0:T(8,128)(2,1)}, bf16[24,2176]{1,0:T(8,128)(2,1)S(1)}, u32[]{:S(2)}, u32[]{:S(2)}) collective-permute-start(bf16[24,2176]{1,0:T(8,128)(2,1)} %get-tuple-element.92), channel_id=1, source_target_pairs={{0,4},{1,5},{2,6},{3,7},{4,0},{5,1},{6,2},{7,3},{8,12},{9,13},{10,... | collective-permute-start | bytes 313352 | tf_op jit(solution)/shard_map/ppermute | solution.py:56
  118.1 0.0 collective-permute-start.13
  118.1 0.3 collective-permute-done.9.refs_0_
  118.4 0.7 collective-permute-start.14
  119.1 2.3 %collective-permute-done.10.refs_1_ = bf16[24,2176]{1,0:T(8,128)(2,1)S(1)} collective-permute-done((bf16[24,2176]{1,0:T(8,128)(2,1)S(1)}, bf16[24,2176]{1,0:T(8,128)(2,1)S(1)}, u32[]{:S(2)}, u32[]{:S(2)}) %collective-permute-start.10) | collective-permute-done | bytes 104480 | tf_op jit(solution)/shard_map/ppermute | solution.py:56
  121.4 0.0 collective-permute-start.15
  121.4 0.0 all-to-all-done
  121.6 0.9 copy-done.10
  122.5 0.9 copy-done.14
  123.4 0.6 shard_map.145
  124.0 0.0 collective-permute-done.11.refs_2_
  124.0 9.3 %collective-permute-done.12.refs_3_ = bf16[24,2176]{1,0:T(8,128)(2,1)S(1)} collective-permute-done((bf16[24,2176]{1,0:T(8,128)(2,1)}, bf16[24,2176]{1,0:T(8,128)(2,1)S(1)}, u32[]{:S(2)}, u32[]{:S(2)}) %collective-permute-start.12) | collective-permute-done | bytes 104480 | tf_op jit(solution)/shard_map/ppermute | solution.py:56
  133.3 1.0 collective-permute-done.13.refs_4_
  134.3 0.0 collective-permute-done.14.refs_5_
  134.3 0.0 collective-permute-done.15.refs_6_
  134.3 2.4 %shard_map.146 = (bf16[1,64,2048]{2,1,0:T(8,128)(2,1)}, bf16[1,64,2048]{2,1,0:T(8,128)(2,1)}) custom-call(f32[64,2048]{1,0:T(8,128)S(1)} %get-tuple-element.77.early_f, f32[64,2048]{1,0:T(8,128)S(1)} %get-tuple-element.78.early_b, f32[2,8,64]{2,1,0:T(8,128)S(1)} %get-tuple-element.79.early_inner, bf16[64,2048]{1,0:T(8,128)(2,1)S(1)} %get-tuple-element.80.saved, ...), custom_call_target="tpu_custom_call" | custom-call | flops 100663296 | bytes 2883584 | tf_op jit(solution)/shard_map/pallas_call | solution.py:519
  (34 shorter events, 0.1 us)
Async XLA Ops:
  0.6 11.9 %collective-permute-start = (bf16[64,2048]{1,0:T(8,128)(2,1)}, bf16[64,2048]{1,0:T(8,128)(2,1)S(1)}, u32[]{:S(2)}, u32[]{:S(2)}) collective-permute-start(bf16[64,2048]{1,0:T(8,128)(2,1)} %bitcast.36), channel_id=1, source_target_pairs={{0,8},{8,16},{16,24},{1,9},{9,17},{17,25},{2,10},{10,18},{18,26},{... | collective-permute-start | bytes 786440 | tf_op jit(solution)/shard_map/ppermute | solution.py:46
  5.5 13.3 %collective-permute-start.1 = (bf16[64,2048]{1,0:T(8,128)(2,1)}, bf16[64,2048]{1,0:T(8,128)(2,1)S(1)}, u32[]{:S(2)}, u32[]{:S(2)}) collective-permute-start(bf16[64,2048]{1,0:T(8,128)(2,1)} %bitcast.37), channel_id=1, source_target_pairs={{8,0},{16,8},{24,16},{9,1},{17,9},{25,17},{10,2},{18,10},{26,18},{... | collective-permute-start | bytes 786440 | tf_op jit(solution)/shard_map/ppermute | solution.py:46
  6.9 18.5 %copy-start.19 = (s32[3]{0:T(128)}, s32[3]{0:T(128)S(1)}, u32[]{:S(2)}) copy-start(s32[3]{0:T(128)S(1)} %pad_add_fusion.place) | copy-start | bytes 40
  6.9 1.0 copy-start.2
  7.8 0.9 copy-start.3
  8.8 0.9 copy-start.7
  9.7 0.7 copy-start.15
  10.4 0.7 copy-start.22
  11.1 0.7 copy-start.25
  12.6 12.8 %copy-start.4 = (bf16[64,2048]{1,0:T(8,128)(2,1)}, bf16[64,2048]{1,0:T(8,128)(2,1)S(1)}, u32[]{:S(2)}) copy-start(bf16[64,2048]{1,0:T(8,128)(2,1)S(1)} %collective-permute-done.arrived_f) | copy-start | bytes 786436
  18.8 6.6 %copy-start.5 = (bf16[64,2048]{1,0:T(8,128)(2,1)}, bf16[64,2048]{1,0:T(8,128)(2,1)S(1)}, u32[]{:S(2)}) copy-start(bf16[64,2048]{1,0:T(8,128)(2,1)S(1)} %collective-permute-done.1.arrived_b) | copy-start | bytes 786436
  19.9 8.8 %collective-permute-start.2 = (bf16[24,2048]{1,0:T(8,128)(2,1)S(1)}, bf16[24,2048]{1,0:T(8,128)(2,1)S(1)}, u32[]{:S(2)}, u32[]{:S(2)}) collective-permute-start(bf16[24,2048]{1,0:T(8,128)(2,1)S(1)} %get-tuple-element.63), channel_id=1, source_target_pairs={{0,1},{1,2},{2,3},{3,4},{4,5},{5,6},{6,7},{7,0},{8,9},{9,10},{10,1... | collective-permute-start | bytes 294920 | tf_op jit(solution)/shard_map/ppermute | solution.py:56
  19.9 8.7 %collective-permute-start.3 = (bf16[24,2048]{1,0:T(8,128)(2,1)S(1)}, bf16[24,2048]{1,0:T(8,128)(2,1)S(1)}, u32[]{:S(2)}, u32[]{:S(2)}) collective-permute-start(bf16[24,2048]{1,0:T(8,128)(2,1)S(1)} %get-tuple-element.64), channel_id=1, source_target_pairs={{0,2},{1,3},{2,4},{3,5},{4,6},{5,7},{6,0},{7,1},{8,10},{9,11},{10,... | collective-permute-start | bytes 294920 | tf_op jit(solution)/shard_map/ppermute | solution.py:56
  21.6 9.5 %collective-permute-start.4 = (bf16[24,2048]{1,0:T(8,128)(2,1)S(1)}, bf16[24,2048]{1,0:T(8,128)(2,1)S(1)}, u32[]{:S(2)}, u32[]{:S(2)}) collective-permute-start(bf16[24,2048]{1,0:T(8,128)(2,1)S(1)} %get-tuple-element.65), channel_id=1, source_target_pairs={{0,3},{1,4},{2,5},{3,6},{4,7},{5,0},{6,1},{7,2},{8,11},{9,12},{10,... | collective-permute-start | bytes 294920 | tf_op jit(solution)/shard_map/ppermute | solution.py:56
  31.0 51.9 %all-to-all-start.1 = ((bf16[8,24,2048]{2,1,0:T(8,128)(2,1)}), bf16[8,24,2048]{2,1,0:T(8,128)(2,1)S(1)}, u32[]{:S(2)}, u32[]{:S(2)}) async-start(bf16[8,24,2048]{2,1,0:T(8,128)(2,1)} %bitcast.34), calls=%async_computation.1 | async-start | bytes 1572864 | tf_op jit(solution)/shard_map/all_to_all | solution.py:52
  34.6 26.6 %collective-permute-start.5 = (bf16[24,2048]{1,0:T(8,128)(2,1)S(1)}, bf16[24,2048]{1,0:T(8,128)(2,1)S(1)}, u32[]{:S(2)}, u32[]{:S(2)}) collective-permute-start(bf16[24,2048]{1,0:T(8,128)(2,1)S(1)} %get-tuple-element.71), channel_id=1, source_target_pairs={{0,4},{1,5},{2,6},{3,7},{4,0},{5,1},{6,2},{7,3},{8,12},{9,13},{10,... | collective-permute-start | bytes 294920 | tf_op jit(solution)/shard_map/ppermute | solution.py:56
  37.4 23.8 %collective-permute-start.6 = (bf16[24,2048]{1,0:T(8,128)(2,1)S(1)}, bf16[24,2048]{1,0:T(8,128)(2,1)S(1)}, u32[]{:S(2)}, u32[]{:S(2)}) collective-permute-start(bf16[24,2048]{1,0:T(8,128)(2,1)S(1)} %get-tuple-element.72), channel_id=1, source_target_pairs={{0,5},{1,6},{2,7},{3,0},{4,1},{5,2},{6,3},{7,4},{8,13},{9,14},{10,... | collective-permute-start | bytes 294920 | tf_op jit(solution)/shard_map/ppermute | solution.py:56
  37.4 23.8 %collective-permute-start.7 = (bf16[24,2048]{1,0:T(8,128)(2,1)S(1)}, bf16[24,2048]{1,0:T(8,128)(2,1)S(1)}, u32[]{:S(2)}, u32[]{:S(2)}) collective-permute-start(bf16[24,2048]{1,0:T(8,128)(2,1)S(1)} %get-tuple-element.73), channel_id=1, source_target_pairs={{0,6},{1,7},{2,0},{3,1},{4,2},{5,3},{6,4},{7,5},{8,14},{9,15},{10,... | collective-permute-start | bytes 294920 | tf_op jit(solution)/shard_map/ppermute | solution.py:56
  40.7 20.5 %collective-permute-start.8 = (bf16[24,2048]{1,0:T(8,128)(2,1)S(1)}, bf16[24,2048]{1,0:T(8,128)(2,1)S(1)}, u32[]{:S(2)}, u32[]{:S(2)}) collective-permute-start(bf16[24,2048]{1,0:T(8,128)(2,1)S(1)} %get-tuple-element.74), channel_id=1, source_target_pairs={{0,7},{1,0},{2,1},{3,2},{4,3},{5,4},{6,5},{7,6},{8,15},{9,8},{10,9... | collective-permute-start | bytes 294920 | tf_op jit(solution)/shard_map/ppermute | solution.py:56
  61.2 0.6 copy-start.20
  61.8 27.9 %copy-start.21 = (s32[3]{0:T(128)S(1)}, s32[3]{0:T(128)}, u32[]{:S(2)}) copy-start(s32[3]{0:T(128)} %copy-done.19) | copy-start | bytes 40
  83.0 38.5 %all-to-all-start = ((bf16[8,24,2176]{2,1,0:T(8,128)(2,1)}), bf16[8,24,2176]{2,1,0:T(8,128)(2,1)S(1)}, u32[]{:S(2)}, u32[]{:S(2)}) async-start(bf16[8,24,2176]{2,1,0:T(8,128)(2,1)} %bitcast.16), calls=%async_computation | async-start | bytes 1671168 | tf_op jit(solution)/shard_map/all_to_all | solution.py:52
  89.7 31.7 %copy-start = (bf16[1,64,2048]{2,1,0:T(8,128)(2,1)S(1)}, bf16[1,64,2048]{2,1,0:T(8,128)(2,1)}, u32[]{:S(2)}) copy-start(bf16[1,64,2048]{2,1,0:T(8,128)(2,1)} %param.18) | copy-start | bytes 786436
  89.7 31.7 %copy-start.1 = (bf16[1,2048,64]{1,2,0:T(8,128)(2,1)S(1)}, bf16[1,2048,64]{1,2,0:T(8,128)(2,1)}, u32[]{:S(2)}) copy-start(bf16[1,2048,64]{1,2,0:T(8,128)(2,1)} %param.22) | copy-start | bytes 786436
  89.8 31.7 %copy-start.6 = (f32[2,192,64]{2,1,0:T(8,128)S(1)}, f32[2,192,64]{2,1,0:T(8,128)}, u32[]{:S(2)}) copy-start(f32[2,192,64]{2,1,0:T(8,128)} %get-tuple-element.53.refs_7_.refs_15_) | copy-start | bytes 294916
  89.8 31.7 %copy-start.8 = (bf16[64,2048]{1,0:T(8,128)(2,1)S(1)}, bf16[64,2048]{1,0:T(8,128)(2,1)}, u32[]{:S(2)}) copy-start(bf16[64,2048]{1,0:T(8,128)(2,1)} %get-tuple-element.49.tokens) | copy-start | bytes 786436
  89.8 31.7 %copy-start.9 = (bf16[64,2048]{1,0:T(8,128)(2,1)S(1)}, bf16[64,2048]{1,0:T(8,128)(2,1)}, u32[]{:S(2)}) copy-start(bf16[64,2048]{1,0:T(8,128)(2,1)} %get-tuple-element.50.refs_1_) | copy-start | bytes 786436
  89.8 31.7 %copy-start.11 = (bf16[64,192]{1,0:T(8,128)(2,1)S(1)}, bf16[64,192]{1,0:T(8,128)(2,1)}, u32[]{:S(2)}) copy-start(bf16[64,192]{1,0:T(8,128)(2,1)} %get-tuple-element.51.refs_5_.refs_13_) | copy-start | bytes 73732
  89.8 31.7 %copy-start.12 = (bf16[64,192]{1,0:T(8,128)(2,1)S(1)}, bf16[64,192]{1,0:T(8,128)(2,1)}, u32[]{:S(2)}) copy-start(bf16[64,192]{1,0:T(8,128)(2,1)} %get-tuple-element.52.refs_6_.refs_14_) | copy-start | bytes 73732
  89.8 31.7 %copy-start.16 = (bf16[1,2048]{1,0:T(2,128)(2,1)S(1)}, bf16[1,2048]{1,0:T(2,128)(2,1)}, u32[]{:S(2)}) copy-start(bf16[1,2048]{1,0:T(2,128)(2,1)} %refs_2_.1) | copy-start | bytes 12292
  89.8 31.7 %copy-start.17 = (bf16[64,192]{1,0:T(8,128)(2,1)S(1)}, bf16[64,192]{1,0:T(8,128)(2,1)}, u32[]{:S(2)}) copy-start(bf16[64,192]{1,0:T(8,128)(2,1)} %get-tuple-element.55.refs_9_) | copy-start | bytes 73732
  89.8 31.7 %copy-start.18 = (bf16[64,192]{1,0:T(8,128)(2,1)S(1)}, bf16[64,192]{1,0:T(8,128)(2,1)}, u32[]{:S(2)}) copy-start(bf16[64,192]{1,0:T(8,128)(2,1)} %get-tuple-element.56.refs_10_) | copy-start | bytes 73732
  89.8 31.7 %copy-start.23 = (s32[1,64,2]{1,2,0:T(2,128)S(1)}, s32[1,64,2]{1,2,0:T(2,128)}, u32[]{:S(2)}) copy-start(s32[1,64,2]{1,2,0:T(2,128)} %param.19) | copy-start | bytes 1540
  89.9 31.7 %copy-start.24 = (f32[2,8,64]{2,1,0:T(8,128)S(1)}, f32[2,8,64]{2,1,0:T(8,128)}, u32[]{:S(2)}) copy-start(f32[2,8,64]{2,1,0:T(8,128)} %get-tuple-element.54.refs_8_) | copy-start | bytes 12292
  110.8 0.7 copy-start.13
  111.5 6.9 %collective-permute-start.9 = (bf16[24,2176]{1,0:T(8,128)(2,1)S(1)}, bf16[24,2176]{1,0:T(8,128)(2,1)S(1)}, u32[]{:S(2)}, u32[]{:S(2)}) collective-permute-start(bf16[24,2176]{1,0:T(8,128)(2,1)S(1)} %get-tuple-element.89), channel_id=1, source_target_pairs={{0,7},{1,0},{2,1},{3,2},{4,3},{5,4},{6,5},{7,6},{8,15},{9,8},{10,9... | collective-permute-start | bytes 313352 | tf_op jit(solution)/shard_map/ppermute | solution.py:56
  115.1 6.4 %collective-permute-start.10 = (bf16[24,2176]{1,0:T(8,128)(2,1)S(1)}, bf16[24,2176]{1,0:T(8,128)(2,1)S(1)}, u32[]{:S(2)}, u32[]{:S(2)}) collective-permute-start(bf16[24,2176]{1,0:T(8,128)(2,1)S(1)} %get-tuple-element.90), channel_id=1, source_target_pairs={{0,6},{1,7},{2,0},{3,1},{4,2},{5,3},{6,4},{7,5},{8,14},{9,15},{10,... | collective-permute-start | bytes 313352 | tf_op jit(solution)/shard_map/ppermute | solution.py:56
  115.6 8.3 %collective-permute-start.11 = (bf16[24,2176]{1,0:T(8,128)(2,1)}, bf16[24,2176]{1,0:T(8,128)(2,1)S(1)}, u32[]{:S(2)}, u32[]{:S(2)}) collective-permute-start(bf16[24,2176]{1,0:T(8,128)(2,1)} %get-tuple-element.91), channel_id=1, source_target_pairs={{0,5},{1,6},{2,7},{3,0},{4,1},{5,2},{6,3},{7,4},{8,13},{9,14},{10,... | collective-permute-start | bytes 313352 | tf_op jit(solution)/shard_map/ppermute | solution.py:56
  115.6 17.6 %collective-permute-start.12 = (bf16[24,2176]{1,0:T(8,128)(2,1)}, bf16[24,2176]{1,0:T(8,128)(2,1)S(1)}, u32[]{:S(2)}, u32[]{:S(2)}) collective-permute-start(bf16[24,2176]{1,0:T(8,128)(2,1)} %get-tuple-element.92), channel_id=1, source_target_pairs={{0,4},{1,5},{2,6},{3,7},{4,0},{5,1},{6,2},{7,3},{8,12},{9,13},{10,... | collective-permute-start | bytes 313352 | tf_op jit(solution)/shard_map/ppermute | solution.py:56
  118.1 16.2 %collective-permute-start.13 = (bf16[24,2176]{1,0:T(8,128)(2,1)}, bf16[24,2176]{1,0:T(8,128)(2,1)S(1)}, u32[]{:S(2)}, u32[]{:S(2)}) collective-permute-start(bf16[24,2176]{1,0:T(8,128)(2,1)} %get-tuple-element.93), channel_id=1, source_target_pairs={{0,3},{1,4},{2,5},{3,6},{4,7},{5,0},{6,1},{7,2},{8,11},{9,12},{10,... | collective-permute-start | bytes 313352 | tf_op jit(solution)/shard_map/ppermute | solution.py:56
  118.4 15.9 %collective-permute-start.14 = (bf16[24,2176]{1,0:T(8,128)(2,1)}, bf16[24,2176]{1,0:T(8,128)(2,1)S(1)}, u32[]{:S(2)}, u32[]{:S(2)}) collective-permute-start(bf16[24,2176]{1,0:T(8,128)(2,1)} %get-tuple-element.94), channel_id=1, source_target_pairs={{0,2},{1,3},{2,4},{3,5},{4,6},{5,7},{6,0},{7,1},{8,10},{9,11},{10,... | collective-permute-start | bytes 313352 | tf_op jit(solution)/shard_map/ppermute | solution.py:56
  121.4 12.9 %collective-permute-start.15 = (bf16[24,2176]{1,0:T(8,128)(2,1)}, bf16[24,2176]{1,0:T(8,128)(2,1)}, u32[]{:S(2)}, u32[]{:S(2)}) collective-permute-start(bf16[24,2176]{1,0:T(8,128)(2,1)} %get-tuple-element.95), channel_id=1, source_target_pairs={{0,1},{1,2},{2,3},{3,4},{4,5},{5,6},{6,7},{7,0},{8,9},{9,10},{10,1... | collective-permute-start | bytes 313352 | tf_op jit(solution)/shard_map/ppermute | solution.py:56
  121.5 0.9 copy-start.10
  122.5 0.9 copy-start.14

commit v12 on v10

--- a/solution.py
+++ b/solution.py
@@ -35,7 +35,6 @@
     )
 
 
-SMEM = pl.BlockSpec(memory_space=pltpu.SMEM)
 VMEM = pl.BlockSpec(memory_space=pltpu.VMEM)
 HBM = pl.BlockSpec(memory_space=pl.ANY)
 
@@ -71,10 +70,10 @@
         ref[...] = value[d * share : (d + 1) * share].astype(BF16)
 
 
-def partners(me, distance, sources, direction, turned):
+def partners(distance, sources, direction, turned):
     if not turned:
         return distance
-    device = me + direction * distance
+    device = lax.axis_index("expert") + direction * distance
     return jnp.where(device < 0, device + sources, jnp.where(device >= sources, device - sources, device))
 
 
@@ -115,25 +114,27 @@
     return [exponent / total for exponent in exponents]
 
 
-def keys_of_part(sizes, me, columns, part, turned):
-    device = partners(me, columns[:, 0:1], sizes["sources"], 1, turned)
+def keys_of_part(sizes, columns, part, turned):
+    device = partners(columns[:, 0:1], sizes["sources"], 1, turned)
     return columns[:, 2 + part : 3 + part] + device * sizes["share"]
 
 
-def rows_to_send(place, arrived_f, arrived_b, embedded, loss, gain):
-    tokens = jnp.where(place[0] == 0, embedded[...], arrived_f[...])
-    upstream = jnp.where(place[0] == place[1], loss[...], arrived_b[...])
+def rows_to_send(arrived_f, arrived_b, embedded, loss, gain):
+    section = lax.axis_index("section")
+    last = lax.axis_size("section") - 1
+    tokens = jnp.where(section == 0, embedded[...], arrived_f[...])
+    upstream = jnp.where(section == last, loss[...], arrived_b[...])
     return tokens, normalise(tokens, gain[...])[2], upstream
 
 
 def table_kernel(
-    sizes, place, embedded, loss, gain, routes_f, routes_b, columns,
+    sizes, embedded, loss, gain, routes_f, routes_b, columns,
     table, embedded_out, loss_out, gain_out,
 ):
     experts, capacity = sizes["experts"], sizes["capacity"]
     targets_f, _ = slot_targets(routes_f[...], experts, capacity)
     targets_b, _ = slot_targets(routes_b[...], experts, capacity)
-    keys = keys_of_part(sizes, place[2], columns, 0, sizes["there"][0])
+    keys = keys_of_part(sizes, columns, 0, sizes["there"][0])
     table_f = sum(tables_of(targets_f, keys))
     table_b = sum(tables_of([t + experts * capacity for t in targets_b], keys))
     table[...] = jnp.concatenate([table_f, table_b], axis=1).astype(BF16)
@@ -142,20 +143,20 @@
     gain_out[...] = gain[...]
 
 
-def first_send_kernel(place, arrived_f, arrived_b, embedded, loss, gain, table, *send):
-    _, normed, upstream = rows_to_send(place, arrived_f, arrived_b, embedded, loss, gain)
+def first_send_kernel(arrived_f, arrived_b, embedded, loss, gain, table, *send):
+    _, normed, upstream = rows_to_send(arrived_f, arrived_b, embedded, loss, gain)
     parted(dot(table[...], jnp.concatenate([normed, upstream], axis=0)), send)
 
 
 def mixing_kernel(
-    sizes, place, arrived_f, arrived_b, embedded, loss, gain, routes_f, routes_b, columns,
+    sizes, arrived_f, arrived_b, embedded, loss, gain, routes_f, routes_b, columns,
     saved, router, tokens, upstream, shares_b, *refs,
 ):
     experts, capacity = sizes["experts"], sizes["capacity"]
     parts = len(sizes["back"])
     mixing, sends = refs[: 3 * parts], refs[3 * parts :]
     tokens[...], normed, upstream[...] = rows_to_send(
-        place, arrived_f, arrived_b, embedded, loss, gain
+        arrived_f, arrived_b, embedded, loss, gain
     )
     data = jnp.concatenate([normed, upstream[...]], axis=0)
     targets_f, hits = slot_targets(routes_f[...], experts, capacity)
@@ -168,16 +169,16 @@
     for part in range(parts):
         there, back = sizes["there"][part], sizes["back"][part]
         mixing_f, mixing_b, tables_b = mixing[3 * part : 3 * part + 3]
-        keys = keys_of_part(sizes, place[2], columns, part, back)
+        keys = keys_of_part(sizes, columns, part, back)
         found_f, found_b = tables_of(targets_f, keys), tables_of(targets_b, keys)
         for out, found, shares in ((mixing_f, found_f, shares_f), (mixing_b, found_b, own_shares)):
             mixed = sum(t * s.astype(BF16).astype(F32) for t, s in zip(found, shares))
             out[...] = jnp.transpose(mixed).astype(BF16)
         for k, table in enumerate(found_b):
-            tables_b[k] = table
+            tables_b[k] = table.astype(BF16)
         if part > 0:
             if there != back:
-                keys = keys_of_part(sizes, place[2], columns, part, there)
+                keys = keys_of_part(sizes, columns, part, there)
                 found_f, found_b = tables_of(targets_f, keys), tables_of(targets_b, keys)
             blocks = sizes["sources"] if there else 1
             table = jnp.concatenate([sum(found_f), sum(found_b)], axis=1).astype(BF16)
@@ -185,7 +186,7 @@
             sends = sends[blocks:]
 
 
-def row_order(sizes, me, turned, shape, axis):
+def row_order(sizes, turned, shape, axis):
     line = tuple(size if i == axis else 1 for i, size in enumerate(shape))
     row = lax.broadcasted_iota(jnp.int32, line, axis)
     block = sum(
@@ -196,12 +197,12 @@
         (within >= k * sizes["capacity"]).astype(jnp.int32)
         for k in range(1, sizes["block_rows"] // sizes["capacity"])
     )
-    source = partners(me, block, sizes["sources"], -1, turned)
+    source = partners(block, sizes["sources"], -1, turned)
     place = group * (sizes["padded"] - sizes["capacity"]) + source * sizes["capacity"] + within
     return (place == lax.broadcasted_iota(jnp.int32, shape, 1 - axis)).astype(F32).astype(BF16)
 
 
-def expert_kernel(sizes, part, held, place, saved_all, up, down, *refs):
+def expert_kernel(sizes, part, held, saved_all, up, down, *refs):
     there, back = sizes["there"][part], sizes["back"][part]
     blocks = sizes["sources"] if there else 1
     got, out = refs[:blocks], refs[blocks:-7]
@@ -239,7 +240,7 @@
             )
             saved_copy.start()
 
-    order = row_order(sizes, place[2], there, (rows.shape[0], moved), 1)
+    order = row_order(sizes, there, (rows.shape[0], moved), 1)
     rows[...] = dot(order, joined(got)).astype(BF16)
     results[:, width:] = jnp.zeros((results.shape[0], results.shape[1] - width), BF16)
 
@@ -278,7 +279,7 @@
         return carry
 
     lax.fori_loop(0, held, one_expert, 0)
-    order = row_order(sizes, place[2], back, (moved, rows.shape[0]), 0)
+    order = row_order(sizes, back, (moved, rows.shape[0]), 0)
     parted(dot(order, results[...]), out)
 
 
@@ -289,7 +290,7 @@
     return (
         dot(mixing_f[...], back[:, :width]),
         dot(mixing_b[...], back[:, :width]),
-        [jnp.sum(tables[k] * sums, axis=0, keepdims=True) for k in range(tables.shape[0])],
+        [jnp.sum(tables[k].astype(F32) * sums, axis=0, keepdims=True) for k in range(tables.shape[0])],
     )
 
 
@@ -387,8 +388,6 @@
     up_weight,
     down_weight,
 ):
-    section = lax.axis_index("section")
-    last = lax.axis_size("section") - 1
     sources = lax.axis_size("expert")
     experts = router.shape[2]
     capacity = pre_activation.shape[3]
@@ -416,8 +415,6 @@
         "padded": padded,
         "block_rows": moved // sources,
     }
-    place = jnp.stack([section, jnp.full_like(section, last), lax.axis_index("expert")])
-    place = place.astype(jnp.int32)
 
     def blocks_of(turned, columns):
         blocks = sources if turned else 1
@@ -434,19 +431,19 @@
         functools.partial(table_kernel, sizes),
         (shape((moved, 2 * count), BF16), row_shape, row_shape, shape((1, width), BF16)),
         (4 * moved * count, 4 * (2 * count + moved) * width),
-        in_specs=[SMEM] + [VMEM] * 6,
-    )(place, embedded, loss_gradient, norm_gain, routes_f, routes_b, columns)
-    given = (place, arrived_f, arrived_b, embedded_held, loss_held, gain_held)
+        in_specs=[VMEM] * 6,
+    )(embedded, loss_gradient, norm_gain, routes_f, routes_b, columns)
+    given = (arrived_f, arrived_b, embedded_held, loss_held, gain_held)
     send = call(
         first_send_kernel,
         tuple(blocks_of(there[0], width)),
         (4 * moved * count * width, 2 * (4 * count + moved) * width),
-        in_specs=[SMEM] + [VMEM] * 6,
+        in_specs=[VMEM] * 6,
     )(*given, table)
     mixing_shapes = [
         shape((count, moved), BF16),
         shape((count, moved), BF16),
-        shape((top, moved, count), F32),
+        shape((top, moved, count), BF16),
     ]
     tokens, upstream, shares_b, *rest = call(
         functools.partial(mixing_kernel, sizes),
@@ -459,9 +456,9 @@
         ),
         (4 * moved * count * width, 2 * (8 * count + moved) * width),
         vmem=LARGE_VMEM,
-        in_specs=[SMEM] + [VMEM] * 10,
+        in_specs=[VMEM] * 10,
     )(
-        place, arrived_f, arrived_b, embedded, loss_gradient, norm_gain, routes_f, routes_b, columns,
+        arrived_f, arrived_b, embedded, loss_gradient, norm_gain, routes_f, routes_b, columns,
         saved_inputs[0], router_t,
     )
     mixing = [rest[3 * part : 3 * part + 3] for part in range(parts)]
@@ -482,7 +479,7 @@
             tuple(result),
             (8 * held * padded * width * hidden, 4 * held * width * hidden),
             vmem=EXPERT_VMEM,
-            in_specs=[SMEM] + [HBM] * 3 + [VMEM] * len(got),
+            in_specs=[HBM] * 3 + [VMEM] * len(got),
             out_specs=(VMEM,) * len(result),
             scratch_shapes=[
                 pltpu.VMEM((2 * held * padded, width), BF16),
@@ -493,7 +490,7 @@
                 pltpu.SemaphoreType.DMA,
                 pltpu.SemaphoreType.DMA((min(2, held), 2, 2)),
             ],
-        )(place, saved_pre, up_weight, down_weight, *got)
+        )(saved_pre, up_weight, down_weight, *got)
         backs.append(exchange(list(done), -1))
         got = coming if part + 1 < parts else None
     handed = (

time: 118 us -> 116 us (0.983)
  local copies, waits for them, and re-layouts: 9.27 us -> 7.05 us
  Pallas kernels: 50.2 us -> 48.1 us
  waiting for transfers between devices: 20.5 us -> 22.5 us
    unnamed x52 -> x42, local copies, waits for them, and re-layouts: 8.01 us -> 5.79 us
  transfers between devices with their start and end apart: 18 -> 18, of which waited for: 7 -> 8; matrix products, arithmetic and copies ran while one was open for 1% -> 1% of each run, Pallas kernels for 40% -> 39%
where the time goes in v12:
time: 116 us; the launch traced here: 115 us
  Pallas kernels  48.1 us (41%)
  starting transfers between devices  36.4 us (31%)
  waiting for transfers between devices  22.5 us (19%)
  local copies, waits for them, and re-layouts  7.05 us (6%)
    pallas_call x2, Pallas kernels, on_device(): call(functools.partial(expert_kernel, sizes, part, held), tuple(result),...  41.1 us
    ppermute x14, starting transfers between devices, exchange(): got[d] = lax.ppermute(blocks[d], 'expert', route)  17 us
    ppermute x14, waiting for transfers between devices, exchange(): got[d] = lax.ppermute(blocks[d], 'expert', route)  15.2 us
    all_to_all x2, starting transfers between devices, exchange(): lax.all_to_all(blocks[0], 'expert', split_axis=0, concat_axis=0, tiled=True)  13.2 us
    ppermute x2, waiting for transfers between devices, from_behind(): return lax.ppermute(block, axis, route)  6.87 us
    ppermute x2, starting transfers between devices, from_behind(): return lax.ppermute(block, axis, route)  6.15 us
    unnamed x42, local copies, waits for them, and re-layouts  5.79 us
    pallas_call x1, Pallas kernels, on_device(): call(functools.partial(mixing_kernel, sizes), (row_shape, row_shape, shap...  3.21 us
  transfers between devices with their start and end apart: 18, of which 8 were waited for; matrix products, arithmetic and copies ran while one was open for 1% of the time, Pallas kernels for 39%

profile of v12, /device:TPU:0, one launch (start us, length us, event | category | flops | bytes accessed | tf_op | source)
XLA Modules:
  0.0 115.0 jit_solution(5323105295580153532)
XLA Ops:
  0.6 4.9 %collective-permute-start = (bf16[64,2048]{1,0:T(8,128)(2,1)}, bf16[64,2048]{1,0:T(8,128)(2,1)S(1)}, u32[]{:S(2)}, u32[]{:S(2)}) collective-permute-start(bf16[64,2048]{1,0:T(8,128)(2,1)} %bitcast.34), channel_id=1, source_target_pairs={{0,8},{8,16},{16,24},{1,9},{9,17},{17,25},{2,10},{10,18},{18,26},{... | collective-permute-start | bytes 786440 | tf_op jit(solution)/shard_map/ppermute | solution.py:45
  5.5 1.3 %collective-permute-start.1 = (bf16[64,2048]{1,0:T(8,128)(2,1)}, bf16[64,2048]{1,0:T(8,128)(2,1)S(1)}, u32[]{:S(2)}, u32[]{:S(2)}) collective-permute-start(bf16[64,2048]{1,0:T(8,128)(2,1)} %bitcast.35), channel_id=1, source_target_pairs={{8,0},{16,8},{24,16},{9,1},{17,9},{25,17},{10,2},{18,10},{26,18},{... | collective-permute-start | bytes 786440 | tf_op jit(solution)/shard_map/ppermute | solution.py:45
  6.8 0.0 copy-start
  6.8 0.9 copy-done
  7.8 0.9 copy-done.1
  8.7 0.9 copy-done.6
  9.6 0.7 copy-done.13
  10.3 0.7 copy-done.17
  11.0 0.7 copy-done.20
  11.6 0.3 shard_map.141
  11.9 0.0 collective-permute-done.arrived_f
  11.9 0.0 copy-start.2
  11.9 6.9 %collective-permute-done.1.arrived_b = bf16[64,2048]{1,0:T(8,128)(2,1)S(1)} collective-permute-done((bf16[64,2048]{1,0:T(8,128)(2,1)}, bf16[64,2048]{1,0:T(8,128)(2,1)S(1)}, u32[]{:S(2)}, u32[]{:S(2)}) %collective-permute-start.1) | collective-permute-done | bytes 262176 | tf_op jit(solution)/shard_map/ppermute | solution.py:45
  18.8 0.5 shard_map.142
  19.3 0.1 collective-permute-start.2
  19.4 1.6 %collective-permute-start.3 = (bf16[24,2048]{1,0:T(8,128)(2,1)S(1)}, bf16[24,2048]{1,0:T(8,128)(2,1)S(1)}, u32[]{:S(2)}, u32[]{:S(2)}) collective-permute-start(bf16[24,2048]{1,0:T(8,128)(2,1)S(1)} %get-tuple-element.70), channel_id=1, source_target_pairs={{0,2},{1,3},{2,4},{3,5},{4,6},{5,7},{6,0},{7,1},{8,10},{9,11},{10,... | collective-permute-start | bytes 294920 | tf_op jit(solution)/shard_map/ppermute | solution.py:55
  21.0 2.5 %collective-permute-start.4 = (bf16[24,2048]{1,0:T(8,128)(2,1)S(1)}, bf16[24,2048]{1,0:T(8,128)(2,1)S(1)}, u32[]{:S(2)}, u32[]{:S(2)}) collective-permute-start(bf16[24,2048]{1,0:T(8,128)(2,1)S(1)} %get-tuple-element.71), channel_id=1, source_target_pairs={{0,3},{1,4},{2,5},{3,6},{4,7},{5,0},{6,1},{7,2},{8,11},{9,12},{10,... | collective-permute-start | bytes 294920 | tf_op jit(solution)/shard_map/ppermute | solution.py:55
  23.5 1.2 %collective-permute-start.5 = (bf16[24,2048]{1,0:T(8,128)(2,1)S(1)}, bf16[24,2048]{1,0:T(8,128)(2,1)S(1)}, u32[]{:S(2)}, u32[]{:S(2)}) collective-permute-start(bf16[24,2048]{1,0:T(8,128)(2,1)S(1)} %get-tuple-element.72), channel_id=1, source_target_pairs={{0,4},{1,5},{2,6},{3,7},{4,0},{5,1},{6,2},{7,3},{8,12},{9,13},{10,... | collective-permute-start | bytes 294920 | tf_op jit(solution)/shard_map/ppermute | solution.py:55
  24.8 1.2 %collective-permute-start.6 = (bf16[24,2048]{1,0:T(8,128)(2,1)S(1)}, bf16[24,2048]{1,0:T(8,128)(2,1)S(1)}, u32[]{:S(2)}, u32[]{:S(2)}) collective-permute-start(bf16[24,2048]{1,0:T(8,128)(2,1)S(1)} %get-tuple-element.73), channel_id=1, source_target_pairs={{0,5},{1,6},{2,7},{3,0},{4,1},{5,2},{6,3},{7,4},{8,13},{9,14},{10,... | collective-permute-start | bytes 294920 | tf_op jit(solution)/shard_map/ppermute | solution.py:55
  26.0 0.0 collective-permute-done.2.refs_1_
  26.0 1.5 %collective-permute-start.7 = (bf16[24,2048]{1,0:T(8,128)(2,1)S(1)}, bf16[24,2048]{1,0:T(8,128)(2,1)S(1)}, u32[]{:S(2)}, u32[]{:S(2)}) collective-permute-start(bf16[24,2048]{1,0:T(8,128)(2,1)S(1)} %get-tuple-element.74), channel_id=1, source_target_pairs={{0,6},{1,7},{2,0},{3,1},{4,2},{5,3},{6,4},{7,5},{8,14},{9,15},{10,... | collective-permute-start | bytes 294920 | tf_op jit(solution)/shard_map/ppermute | solution.py:55
  27.5 0.0 collective-permute-done.3.refs_2_
  27.5 1.5 %collective-permute-start.8 = (bf16[24,2048]{1,0:T(8,128)(2,1)S(1)}, bf16[24,2048]{1,0:T(8,128)(2,1)S(1)}, u32[]{:S(2)}, u32[]{:S(2)}) collective-permute-start(bf16[24,2048]{1,0:T(8,128)(2,1)S(1)} %get-tuple-element.75), channel_id=1, source_target_pairs={{0,7},{1,0},{2,1},{3,2},{4,3},{5,4},{6,5},{7,6},{8,15},{9,8},{10,9... | collective-permute-start | bytes 294920 | tf_op jit(solution)/shard_map/ppermute | solution.py:55
  29.0 1.2 %copy.16 = bf16[8,24,1024]{2,1,0:T(8,128)(2,1)S(1)} copy(bf16[8,24,1024]{2,0,1:T(8,128)(2,1)} %bitcast.33) | data formatting | bytes 786432 | tf_op jit(solution)/shard_map/reshape | solution.py:466
  30.3 0.0 copy-done.2
  30.3 0.0 copy-done.3
  30.3 3.2 %shard_map.140 = (bf16[64,2048]{1,0:T(8,128)(2,1)}, bf16[64,2048]{1,0:T(8,128)(2,1)}, f32[2,8,64]{2,1,0:T(8,128)}, bf16[64,192]{1,0:T(8,128)(2,1)}, bf16[64,192]...) custom-call(bf16[64,2048]{1,0:T(8,128)(2,1)} %copy-done.2, ...), custom_call_target="tpu_custom_call" | custom-call | flops 100663296 | bytes 2883584 | tf_op jit(solution)/shard_map/pallas_call | solution.py:448
  33.5 1.2 %collective-permute-done.4.refs_3_ = bf16[24,2048]{1,0:T(8,128)(2,1)S(1)} collective-permute-done((bf16[24,2048]{1,0:T(8,128)(2,1)S(1)}, bf16[24,2048]{1,0:T(8,128)(2,1)S(1)}, u32[]{:S(2)}, u32[]{:S(2)}) %collective-permute-start.4) | collective-permute-done | bytes 98336 | tf_op jit(solution)/shard_map/ppermute | solution.py:55
  34.7 0.2 collective-permute-done.5.refs_4_
  34.9 0.0 collective-permute-done.6.refs_5_
  34.9 0.0 collective-permute-done.7.refs_6_
  34.9 0.0 collective-permute-done.8.refs_7_
  34.9 8.5 %all-to-all-start.1 = ((bf16[8,24,2048]{2,1,0:T(8,128)(2,1)}), bf16[8,24,2048]{2,1,0:T(8,128)(2,1)S(1)}, u32[]{:S(2)}, u32[]{:S(2)}) async-start(bf16[8,24,2048]{2,1,0:T(8,128)(2,1)} %bitcast.32), calls=%async_computation.1 | async-start | bytes 1572864 | tf_op jit(solution)/shard_map/all_to_all | solution.py:51
  43.4 20.6 %shard_map.143 = bf16[192,2176]{1,0:T(8,128)(2,1)} custom-call(bf16[8,32,1024]{2,1,0:T(8,128)(2,1)S(1)} %pad.4.saved_all, bf16[8,2048,1024]{2,1,0:T(8,128)(2,1)} %up.3, bf16[8,1024,2048]{2,1,0:T(8,128)(2,1)} %down.3, bf16[24,2048]{1,0:T(8,128)(2,1)S(1)} %get-tuple-element.77.refs_0_, bf16[24,2048]{1,0:T(8,128)(2,1)S(1)} %collective-permute-done.2.refs_1_, ...), custom_call_target="tpu_custom_call" | custom-call | flops 2147483648 | bytes 33554432 | tf_op jit(solution)/shard_map/pallas_call | solution.py:477
  64.0 0.4 all-to-all-done.1
  64.4 4.7 %all-to-all-start = ((bf16[8,24,2176]{2,1,0:T(8,128)(2,1)}), bf16[8,24,2176]{2,1,0:T(8,128)(2,1)S(1)}, u32[]{:S(2)}, u32[]{:S(2)}) async-start(bf16[8,24,2176]{2,1,0:T(8,128)(2,1)} %bitcast.14), calls=%async_computation | async-start | bytes 1671168 | tf_op jit(solution)/shard_map/all_to_all | solution.py:51
  69.1 0.0 copy-start.5
  69.1 0.0 copy-start.7
  69.1 0.0 copy-start.8
  69.1 0.0 copy-start.9
  69.2 0.0 copy-start.10
  69.2 0.0 copy-start.11
  69.2 0.0 copy-start.14
  69.2 0.0 copy-start.18
  69.2 20.5 %shard_map.144 = (bf16[24,2176]{1,0:T(8,128)(2,1)S(1)}, bf16[24,2176]{1,0:T(8,128)(2,1)S(1)}, bf16[24,2176]{1,0:T(8,128)(2,1)S(1)}, bf16[24,2176]{1,0:T(8,128)(2...) custom-call(bf16[8,32,1024]{2,1,0:T(8,128)(2,1)S(1)} %pad.4.saved_al, ...), custom_call_target="tpu_custom_call" | custom-call | flops 2147483648 | bytes 33554432 | tf_op jit(solution)/shard_map/pallas_call | solution.py:477
  89.7 3.6 %collective-permute-start.9 = (bf16[24,2176]{1,0:T(8,128)(2,1)S(1)}, bf16[24,2176]{1,0:T(8,128)(2,1)S(1)}, u32[]{:S(2)}, u32[]{:S(2)}) collective-permute-start(bf16[24,2176]{1,0:T(8,128)(2,1)S(1)} %get-tuple-element.99), channel_id=1, source_target_pairs={{0,7},{1,0},{2,1},{3,2},{4,3},{5,4},{6,5},{7,6},{8,15},{9,8},{10,9... | collective-permute-start | bytes 313352 | tf_op jit(solution)/shard_map/ppermute | solution.py:55
  93.3 0.6 collective-permute-start.10
  93.9 0.0 collective-permute-start.11
  93.9 2.4 %collective-permute-start.12 = (bf16[24,2176]{1,0:T(8,128)(2,1)}, bf16[24,2176]{1,0:T(8,128)(2,1)S(1)}, u32[]{:S(2)}, u32[]{:S(2)}) collective-permute-start(bf16[24,2176]{1,0:T(8,128)(2,1)} %get-tuple-element.102), channel_id=1, source_target_pairs={{0,4},{1,5},{2,6},{3,7},{4,0},{5,1},{6,2},{7,3},{8,12},{9,13},{10,... | collective-permute-start | bytes 313352 | tf_op jit(solution)/shard_map/ppermute | solution.py:55
  96.3 0.0 collective-permute-start.13
  96.3 0.3 collective-permute-done.9.refs_0_
  96.7 0.7 collective-permute-start.14
  97.4 2.3 %collective-permute-done.10.refs_1_ = bf16[24,2176]{1,0:T(8,128)(2,1)S(1)} collective-permute-done((bf16[24,2176]{1,0:T(8,128)(2,1)S(1)}, bf16[24,2176]{1,0:T(8,128)(2,1)S(1)}, u32[]{:S(2)}, u32[]{:S(2)}) %collective-permute-start.10) | collective-permute-done | bytes 104480 | tf_op jit(solution)/shard_map/ppermute | solution.py:55
  99.7 0.0 collective-permute-start.15
  99.7 0.0 all-to-all-done
  99.7 0.0 copy-done.4
  99.8 0.9 copy-done.12
  100.7 0.6 shard_map.145
  101.3 0.0 collective-permute-done.11.refs_2_
  101.3 10.2 %collective-permute-done.12.refs_3_ = bf16[24,2176]{1,0:T(8,128)(2,1)S(1)} collective-permute-done((bf16[24,2176]{1,0:T(8,128)(2,1)}, bf16[24,2176]{1,0:T(8,128)(2,1)S(1)}, u32[]{:S(2)}, u32[]{:S(2)}) %collective-permute-start.12) | collective-permute-done | bytes 104480 | tf_op jit(solution)/shard_map/ppermute | solution.py:55
  111.5 1.0 collective-permute-done.13.refs_4_
  112.6 0.0 collective-permute-done.14.refs_5_
  112.6 0.0 collective-permute-done.15.refs_6_
  112.6 2.4 %shard_map.146 = (bf16[1,64,2048]{2,1,0:T(8,128)(2,1)}, bf16[1,64,2048]{2,1,0:T(8,128)(2,1)}) custom-call(f32[64,2048]{1,0:T(8,128)S(1)} %get-tuple-element.87.early_f, f32[64,2048]{1,0:T(8,128)S(1)} %get-tuple-element.88.early_b, f32[2,8,64]{2,1,0:T(8,128)S(1)} %get-tuple-element.89.early_inner, bf16[64,2048]{1,0:T(8,128)(2,1)S(1)} %get-tuple-element.90.saved, ...), custom_call_target="tpu_custom_call" | custom-call | flops 100663296 | bytes 2883584 | tf_op jit(solution)/shard_map/pallas_call | solution.py:511
  (23 shorter events, 0.1 us)
Async XLA Ops:
  0.6 11.3 %collective-permute-start = (bf16[64,2048]{1,0:T(8,128)(2,1)}, bf16[64,2048]{1,0:T(8,128)(2,1)S(1)}, u32[]{:S(2)}, u32[]{:S(2)}) collective-permute-start(bf16[64,2048]{1,0:T(8,128)(2,1)} %bitcast.34), channel_id=1, source_target_pairs={{0,8},{8,16},{16,24},{1,9},{9,17},{17,25},{2,10},{10,18},{18,26},{... | collective-permute-start | bytes 786440 | tf_op jit(solution)/shard_map/ppermute | solution.py:45
  5.5 13.3 %collective-permute-start.1 = (bf16[64,2048]{1,0:T(8,128)(2,1)}, bf16[64,2048]{1,0:T(8,128)(2,1)S(1)}, u32[]{:S(2)}, u32[]{:S(2)}) collective-permute-start(bf16[64,2048]{1,0:T(8,128)(2,1)} %bitcast.35), channel_id=1, source_target_pairs={{8,0},{16,8},{24,16},{9,1},{17,9},{25,17},{10,2},{18,10},{26,18},{... | collective-permute-start | bytes 786440 | tf_op jit(solution)/shard_map/ppermute | solution.py:45
  6.8 1.0 copy-start
  7.7 0.9 copy-start.1
  8.7 0.9 copy-start.6
  9.6 0.7 copy-start.13
  10.3 0.7 copy-start.17
  11.0 0.7 copy-start.20
  11.9 18.4 %copy-start.2 = (bf16[64,2048]{1,0:T(8,128)(2,1)}, bf16[64,2048]{1,0:T(8,128)(2,1)S(1)}, u32[]{:S(2)}) copy-start(bf16[64,2048]{1,0:T(8,128)(2,1)S(1)} %collective-permute-done.arrived_f) | copy-start | bytes 786436
  18.8 11.5 %copy-start.3 = (bf16[64,2048]{1,0:T(8,128)(2,1)}, bf16[64,2048]{1,0:T(8,128)(2,1)S(1)}, u32[]{:S(2)}) copy-start(bf16[64,2048]{1,0:T(8,128)(2,1)S(1)} %collective-permute-done.1.arrived_b) | copy-start | bytes 786436
  19.3 6.7 %collective-permute-start.2 = (bf16[24,2048]{1,0:T(8,128)(2,1)S(1)}, bf16[24,2048]{1,0:T(8,128)(2,1)S(1)}, u32[]{:S(2)}, u32[]{:S(2)}) collective-permute-start(bf16[24,2048]{1,0:T(8,128)(2,1)S(1)} %get-tuple-element.69), channel_id=1, source_target_pairs={{0,1},{1,2},{2,3},{3,4},{4,5},{5,6},{6,7},{7,0},{8,9},{9,10},{10,1... | collective-permute-start | bytes 294920 | tf_op jit(solution)/shard_map/ppermute | solution.py:55
  19.4 8.1 %collective-permute-start.3 = (bf16[24,2048]{1,0:T(8,128)(2,1)S(1)}, bf16[24,2048]{1,0:T(8,128)(2,1)S(1)}, u32[]{:S(2)}, u32[]{:S(2)}) collective-permute-start(bf16[24,2048]{1,0:T(8,128)(2,1)S(1)} %get-tuple-element.70), channel_id=1, source_target_pairs={{0,2},{1,3},{2,4},{3,5},{4,6},{5,7},{6,0},{7,1},{8,10},{9,11},{10,... | collective-permute-start | bytes 294920 | tf_op jit(solution)/shard_map/ppermute | solution.py:55
  21.0 13.7 %collective-permute-start.4 = (bf16[24,2048]{1,0:T(8,128)(2,1)S(1)}, bf16[24,2048]{1,0:T(8,128)(2,1)S(1)}, u32[]{:S(2)}, u32[]{:S(2)}) collective-permute-start(bf16[24,2048]{1,0:T(8,128)(2,1)S(1)} %get-tuple-element.71), channel_id=1, source_target_pairs={{0,3},{1,4},{2,5},{3,6},{4,7},{5,0},{6,1},{7,2},{8,11},{9,12},{10,... | collective-permute-start | bytes 294920 | tf_op jit(solution)/shard_map/ppermute | solution.py:55
  23.5 11.3 %collective-permute-start.5 = (bf16[24,2048]{1,0:T(8,128)(2,1)S(1)}, bf16[24,2048]{1,0:T(8,128)(2,1)S(1)}, u32[]{:S(2)}, u32[]{:S(2)}) collective-permute-start(bf16[24,2048]{1,0:T(8,128)(2,1)S(1)} %get-tuple-element.72), channel_id=1, source_target_pairs={{0,4},{1,5},{2,6},{3,7},{4,0},{5,1},{6,2},{7,3},{8,12},{9,13},{10,... | collective-permute-start | bytes 294920 | tf_op jit(solution)/shard_map/ppermute | solution.py:55
  24.8 10.1 %collective-permute-start.6 = (bf16[24,2048]{1,0:T(8,128)(2,1)S(1)}, bf16[24,2048]{1,0:T(8,128)(2,1)S(1)}, u32[]{:S(2)}, u32[]{:S(2)}) collective-permute-start(bf16[24,2048]{1,0:T(8,128)(2,1)S(1)} %get-tuple-element.73), channel_id=1, source_target_pairs={{0,5},{1,6},{2,7},{3,0},{4,1},{5,2},{6,3},{7,4},{8,13},{9,14},{10,... | collective-permute-start | bytes 294920 | tf_op jit(solution)/shard_map/ppermute | solution.py:55
  26.0 8.9 %collective-permute-start.7 = (bf16[24,2048]{1,0:T(8,128)(2,1)S(1)}, bf16[24,2048]{1,0:T(8,128)(2,1)S(1)}, u32[]{:S(2)}, u32[]{:S(2)}) collective-permute-start(bf16[24,2048]{1,0:T(8,128)(2,1)S(1)} %get-tuple-element.74), channel_id=1, source_target_pairs={{0,6},{1,7},{2,0},{3,1},{4,2},{5,3},{6,4},{7,5},{8,14},{9,15},{10,... | collective-permute-start | bytes 294920 | tf_op jit(solution)/shard_map/ppermute | solution.py:55
  27.5 7.4 %collective-permute-start.8 = (bf16[24,2048]{1,0:T(8,128)(2,1)S(1)}, bf16[24,2048]{1,0:T(8,128)(2,1)S(1)}, u32[]{:S(2)}, u32[]{:S(2)}) collective-permute-start(bf16[24,2048]{1,0:T(8,128)(2,1)S(1)} %get-tuple-element.75), channel_id=1, source_target_pairs={{0,7},{1,0},{2,1},{3,2},{4,3},{5,4},{6,5},{7,6},{8,15},{9,8},{10,9... | collective-permute-start | bytes 294920 | tf_op jit(solution)/shard_map/ppermute | solution.py:55
  34.9 29.5 %all-to-all-start.1 = ((bf16[8,24,2048]{2,1,0:T(8,128)(2,1)}), bf16[8,24,2048]{2,1,0:T(8,128)(2,1)S(1)}, u32[]{:S(2)}, u32[]{:S(2)}) async-start(bf16[8,24,2048]{2,1,0:T(8,128)(2,1)} %bitcast.32), calls=%async_computation.1 | async-start | bytes 1572864 | tf_op jit(solution)/shard_map/all_to_all | solution.py:51
  64.4 35.3 %all-to-all-start = ((bf16[8,24,2176]{2,1,0:T(8,128)(2,1)}), bf16[8,24,2176]{2,1,0:T(8,128)(2,1)S(1)}, u32[]{:S(2)}, u32[]{:S(2)}) async-start(bf16[8,24,2176]{2,1,0:T(8,128)(2,1)} %bitcast.14), calls=%async_computation | async-start | bytes 1671168 | tf_op jit(solution)/shard_map/all_to_all | solution.py:51
  69.1 30.6 %copy-start.4 = (bf16[1,64,2048]{2,1,0:T(8,128)(2,1)S(1)}, bf16[1,64,2048]{2,1,0:T(8,128)(2,1)}, u32[]{:S(2)}) copy-start(bf16[1,64,2048]{2,1,0:T(8,128)(2,1)} %param.18) | copy-start | bytes 786436
  69.1 30.6 %copy-start.5 = (bf16[1,2048,64]{1,2,0:T(8,128)(2,1)S(1)}, bf16[1,2048,64]{1,2,0:T(8,128)(2,1)}, u32[]{:S(2)}) copy-start(bf16[1,2048,64]{1,2,0:T(8,128)(2,1)} %param.22) | copy-start | bytes 786436
  69.1 30.6 %copy-start.7 = (bf16[2,192,64]{2,1,0:T(8,128)(2,1)S(1)}, bf16[2,192,64]{2,1,0:T(8,128)(2,1)}, u32[]{:S(2)}) copy-start(bf16[2,192,64]{2,1,0:T(8,128)(2,1)} %get-tuple-element.58.refs_7_.refs_15_) | copy-start | bytes 147460
  69.1 30.6 %copy-start.8 = (bf16[64,2048]{1,0:T(8,128)(2,1)S(1)}, bf16[64,2048]{1,0:T(8,128)(2,1)}, u32[]{:S(2)}) copy-start(bf16[64,2048]{1,0:T(8,128)(2,1)} %get-tuple-element.54.tokens) | copy-start | bytes 786436
  69.1 30.6 %copy-start.9 = (bf16[64,2048]{1,0:T(8,128)(2,1)S(1)}, bf16[64,2048]{1,0:T(8,128)(2,1)}, u32[]{:S(2)}) copy-start(bf16[64,2048]{1,0:T(8,128)(2,1)} %get-tuple-element.55.refs_1_) | copy-start | bytes 786436
  69.2 30.6 %copy-start.10 = (bf16[64,192]{1,0:T(8,128)(2,1)S(1)}, bf16[64,192]{1,0:T(8,128)(2,1)}, u32[]{:S(2)}) copy-start(bf16[64,192]{1,0:T(8,128)(2,1)} %get-tuple-element.56.refs_5_.refs_13_) | copy-start | bytes 73732
  69.2 30.6 %copy-start.11 = (bf16[64,192]{1,0:T(8,128)(2,1)S(1)}, bf16[64,192]{1,0:T(8,128)(2,1)}, u32[]{:S(2)}) copy-start(bf16[64,192]{1,0:T(8,128)(2,1)} %get-tuple-element.57.refs_6_.refs_14_) | copy-start | bytes 73732
  69.2 30.6 %copy-start.14 = (bf16[1,2048]{1,0:T(2,128)(2,1)S(1)}, bf16[1,2048]{1,0:T(2,128)(2,1)}, u32[]{:S(2)}) copy-start(bf16[1,2048]{1,0:T(2,128)(2,1)} %refs_2_.1) | copy-start | bytes 12292
  69.2 30.6 %copy-start.15 = (bf16[64,192]{1,0:T(8,128)(2,1)S(1)}, bf16[64,192]{1,0:T(8,128)(2,1)}, u32[]{:S(2)}) copy-start(bf16[64,192]{1,0:T(8,128)(2,1)} %get-tuple-element.60.refs_9_) | copy-start | bytes 73732
  69.2 30.6 %copy-start.16 = (bf16[64,192]{1,0:T(8,128)(2,1)S(1)}, bf16[64,192]{1,0:T(8,128)(2,1)}, u32[]{:S(2)}) copy-start(bf16[64,192]{1,0:T(8,128)(2,1)} %get-tuple-element.61.refs_10_) | copy-start | bytes 73732
  69.2 30.6 %copy-start.18 = (s32[1,64,2]{1,2,0:T(2,128)S(1)}, s32[1,64,2]{1,2,0:T(2,128)}, u32[]{:S(2)}) copy-start(s32[1,64,2]{1,2,0:T(2,128)} %param.19) | copy-start | bytes 1540
  69.2 30.6 %copy-start.19 = (f32[2,8,64]{2,1,0:T(8,128)S(1)}, f32[2,8,64]{2,1,0:T(8,128)}, u32[]{:S(2)}) copy-start(f32[2,8,64]{2,1,0:T(8,128)} %get-tuple-element.59.refs_8_) | copy-start | bytes 12292
  89.7 6.9 %collective-permute-start.9 = (bf16[24,2176]{1,0:T(8,128)(2,1)S(1)}, bf16[24,2176]{1,0:T(8,128)(2,1)S(1)}, u32[]{:S(2)}, u32[]{:S(2)}) collective-permute-start(bf16[24,2176]{1,0:T(8,128)(2,1)S(1)} %get-tuple-element.99), channel_id=1, source_target_pairs={{0,7},{1,0},{2,1},{3,2},{4,3},{5,4},{6,5},{7,6},{8,15},{9,8},{10,9... | collective-permute-start | bytes 313352 | tf_op jit(solution)/shard_map/ppermute | solution.py:55
  93.3 6.4 %collective-permute-start.10 = (bf16[24,2176]{1,0:T(8,128)(2,1)S(1)}, bf16[24,2176]{1,0:T(8,128)(2,1)S(1)}, u32[]{:S(2)}, u32[]{:S(2)}) collective-permute-start(bf16[24,2176]{1,0:T(8,128)(2,1)S(1)} %get-tuple-element.100), channel_id=1, source_target_pairs={{0,6},{1,7},{2,0},{3,1},{4,2},{5,3},{6,4},{7,5},{8,14},{9,15},{10,... | collective-permute-start | bytes 313352 | tf_op jit(solution)/shard_map/ppermute | solution.py:55
  93.9 7.4 %collective-permute-start.11 = (bf16[24,2176]{1,0:T(8,128)(2,1)}, bf16[24,2176]{1,0:T(8,128)(2,1)S(1)}, u32[]{:S(2)}, u32[]{:S(2)}) collective-permute-start(bf16[24,2176]{1,0:T(8,128)(2,1)} %get-tuple-element.101), channel_id=1, source_target_pairs={{0,5},{1,6},{2,7},{3,0},{4,1},{5,2},{6,3},{7,4},{8,13},{9,14},{10,... | collective-permute-start | bytes 313352 | tf_op jit(solution)/shard_map/ppermute | solution.py:55
  93.9 17.6 %collective-permute-start.12 = (bf16[24,2176]{1,0:T(8,128)(2,1)}, bf16[24,2176]{1,0:T(8,128)(2,1)S(1)}, u32[]{:S(2)}, u32[]{:S(2)}) collective-permute-start(bf16[24,2176]{1,0:T(8,128)(2,1)} %get-tuple-element.102), channel_id=1, source_target_pairs={{0,4},{1,5},{2,6},{3,7},{4,0},{5,1},{6,2},{7,3},{8,12},{9,13},{10,... | collective-permute-start | bytes 313352 | tf_op jit(solution)/shard_map/ppermute | solution.py:55
  96.3 16.2 %collective-permute-start.13 = (bf16[24,2176]{1,0:T(8,128)(2,1)}, bf16[24,2176]{1,0:T(8,128)(2,1)S(1)}, u32[]{:S(2)}, u32[]{:S(2)}) collective-permute-start(bf16[24,2176]{1,0:T(8,128)(2,1)} %get-tuple-element.103), channel_id=1, source_target_pairs={{0,3},{1,4},{2,5},{3,6},{4,7},{5,0},{6,1},{7,2},{8,11},{9,12},{10,... | collective-permute-start | bytes 313352 | tf_op jit(solution)/shard_map/ppermute | solution.py:55
  96.7 15.9 %collective-permute-start.14 = (bf16[24,2176]{1,0:T(8,128)(2,1)}, bf16[24,2176]{1,0:T(8,128)(2,1)S(1)}, u32[]{:S(2)}, u32[]{:S(2)}) collective-permute-start(bf16[24,2176]{1,0:T(8,128)(2,1)} %get-tuple-element.104), channel_id=1, source_target_pairs={{0,2},{1,3},{2,4},{3,5},{4,6},{5,7},{6,0},{7,1},{8,10},{9,11},{10,... | collective-permute-start | bytes 313352 | tf_op jit(solution)/shard_map/ppermute | solution.py:55
  99.7 12.9 %collective-permute-start.15 = (bf16[24,2176]{1,0:T(8,128)(2,1)}, bf16[24,2176]{1,0:T(8,128)(2,1)}, u32[]{:S(2)}, u32[]{:S(2)}) collective-permute-start(bf16[24,2176]{1,0:T(8,128)(2,1)} %get-tuple-element.105), channel_id=1, source_target_pairs={{0,1},{1,2},{2,3},{3,4},{4,5},{5,6},{6,7},{7,0},{8,9},{9,10},{10,1... | collective-permute-start | bytes 313352 | tf_op jit(solution)/shard_map/ppermute | solution.py:55
  99.8 0.9 copy-start.12

commit v13 on v12

--- a/solution.py
+++ b/solution.py
@@ -45,12 +45,23 @@
     return lax.ppermute(block, axis, route)
 
 
+def far_first(size):
+    return sorted(range(size), key=lambda d: (abs(2 * d - size), d)) if size > 1 else [0]
+
+
+def by_block(refs):
+    ordered = [None] * len(refs)
+    for ref, d in zip(refs, far_first(len(refs))):
+        ordered[d] = ref
+    return ordered
+
+
 def exchange(blocks, direction):
     size = lax.axis_size("expert")
     if len(blocks) == 1:
         return [lax.all_to_all(blocks[0], "expert", split_axis=0, concat_axis=0, tiled=True)]
     got = list(blocks)
-    for d in sorted(range(1, size), key=lambda d: abs(2 * d - size)):
+    for d in far_first(size)[:-1]:
         route = [(i, (i + direction * d) % size) for i in range(size)]
         got[d] = lax.ppermute(blocks[d], "expert", route)
     return got
@@ -205,7 +216,7 @@
 def expert_kernel(sizes, part, held, saved_all, up, down, *refs):
     there, back = sizes["there"][part], sizes["back"][part]
     blocks = sizes["sources"] if there else 1
-    got, out = refs[:blocks], refs[blocks:-7]
+    got, out = by_block(refs[:blocks]), refs[blocks:-7]
     rows, results, saved_pre, up_held, down_held, saved_sem, sems = refs[-7:]
     moved = blocks * got[0].shape[0]
     width = rows.shape[1]
@@ -327,12 +338,12 @@
 
 
 def late_kernel(
-    sizes, early_f, early_b, early_inner, saved, upstream, gain, router, routes,
-    mixing_f, mixing_b, tables, shares, *refs,
+    sizes, early_f, early_b, early_inner, saved, upstream, gain, router, routes, shares,
+    mixing_f, mixing_b, tables, *refs,
 ):
     *backs, output, gradient = refs
     if sizes["back"][-1]:
-        backs = [None] + backs
+        backs = by_block(backs + [None])
     more_f, more_b, more = add_up(backs, mixing_f, mixing_b, tables)
     widened = saved[...].astype(F32)
     inv_rms = lax.rsqrt(jnp.mean(widened * widened, axis=-1, keepdims=True) + EPS)
@@ -469,7 +480,9 @@
     got = exchange(send, 1)
     for part in range(parts):
         if part + 1 < parts:
+            got = [got[d] for d in far_first(len(got))]
             sends, saved_pre, got = lax.optimization_barrier((sends, saved_pre, got))
+            got = by_block(got)
             blocks = len(blocks_of(there[part + 1], width))
             coming = exchange(sends[:blocks], 1)
             sends = sends[blocks:]
@@ -490,11 +503,11 @@
                 pltpu.SemaphoreType.DMA,
                 pltpu.SemaphoreType.DMA((min(2, held), 2, 2)),
             ],
-        )(saved_pre, up_weight, down_weight, *got)
+        )(saved_pre, up_weight, down_weight, *[got[d] for d in far_first(len(got))])
         backs.append(exchange(list(done), -1))
         got = coming if part + 1 < parts else None
     handed = (
-        saved_inputs[0], upstream, norm_gain, router_t, routes_b, *mixing[-1], shares_b,
+        saved_inputs[0], upstream, norm_gain, router_t, routes_b, shares_b,
     )
     own = (*mixing[-1], backs[-1][0]) if back[-1] else ()
     early = call(
@@ -512,7 +525,11 @@
             functools.partial(late_kernel, sizes),
             (shape((1, count, width), BF16),) * 2,
             (4 * moved * count * width, 2 * (8 * count + moved) * width),
-        )(*early, *(backs[-1][1:] if back[-1] else backs[-1]))
+        )(
+            *early,
+            *mixing[-1],
+            *[backs[-1][d] for d in far_first(len(backs[-1])) if d > 0 or not back[-1]],
+        )
     )
 
 

time: 116 us -> 116 us (level)
  starting transfers between devices: 36.4 us -> 39 us
  waiting for transfers between devices: 22.5 us -> 20.8 us
    ppermute x14, starting transfers between devices: 17 us -> 22.5 us  [exchange(): got[d] = lax.ppermute(blocks[d], 'expert', route)]
    all_to_all x2, starting transfers between devices: 13.2 us -> 10.3 us  [exchange(): lax.all_to_all(blocks[0], 'expert', split_axis=0, concat_axis=0, tiled=True)]
    ppermute x14, waiting for transfers between devices: 15.2 us -> 13.6 us  [exchange(): got[d] = lax.ppermute(blocks[d], 'expert', route)]
  transfers between devices with their start and end apart: 18 -> 18, of which waited for: 8 -> 7; matrix products, arithmetic and copies ran while one was open for 1% -> 1% of each run, Pallas kernels for 39% -> 39%
where the time goes in v13:
time: 116 us
  Pallas kernels  48 us (41%)
  starting transfers between devices  39 us (34%)
  waiting for transfers between devices  20.8 us (18%)
  local copies, waits for them, and re-layouts  7.05 us (6%)
    pallas_call x2, Pallas kernels, on_device(): call(functools.partial(expert_kernel, sizes, part, held), tuple(result),...  41.1 us
    ppermute x14, starting transfers between devices, exchange(): got[d] = lax.ppermute(blocks[d], 'expert', route)  22.5 us
    ppermute x14, waiting for transfers between devices, exchange(): got[d] = lax.ppermute(blocks[d], 'expert', route)  13.6 us
    all_to_all x2, starting transfers between devices, exchange(): lax.all_to_all(blocks[0], 'expert', split_axis=0, concat_axis=0, tiled=True)  10.3 us
    ppermute x2, waiting for transfers between devices, from_behind(): return lax.ppermute(block, axis, route)  6.87 us
    ppermute x2, starting transfers between devices, from_behind(): return lax.ppermute(block, axis, route)  6.15 us
    unnamed x42, local copies, waits for them, and re-layouts  5.79 us
    pallas_call x1, Pallas kernels, on_device(): call(functools.partial(mixing_kernel, sizes), (row_shape, row_shape, shap...  3.21 us
  transfers between devices with their start and end apart: 18, of which 7 were waited for; matrix products, arithmetic and copies ran while one was open for 1% of the time, Pallas kernels for 39%

profile of v13, /device:TPU:0, one launch (start us, length us, event | category | flops | bytes accessed | tf_op | source)
XLA Modules:
  0.0 115.9 jit_solution(12259696506458516385)
XLA Ops:
  0.6 4.9 %collective-permute-start = (bf16[64,2048]{1,0:T(8,128)(2,1)}, bf16[64,2048]{1,0:T(8,128)(2,1)S(1)}, u32[]{:S(2)}, u32[]{:S(2)}) collective-permute-start(bf16[64,2048]{1,0:T(8,128)(2,1)} %bitcast.34), channel_id=1, source_target_pairs={{0,8},{8,16},{16,24},{1,9},{9,17},{17,25},{2,10},{10,18},{18,26},{... | collective-permute-start | bytes 786440 | tf_op jit(solution)/shard_map/ppermute | solution.py:45
  5.5 1.3 %collective-permute-start.1 = (bf16[64,2048]{1,0:T(8,128)(2,1)}, bf16[64,2048]{1,0:T(8,128)(2,1)S(1)}, u32[]{:S(2)}, u32[]{:S(2)}) collective-permute-start(bf16[64,2048]{1,0:T(8,128)(2,1)} %bitcast.35), channel_id=1, source_target_pairs={{8,0},{16,8},{24,16},{9,1},{17,9},{25,17},{10,2},{18,10},{26,18},{... | collective-permute-start | bytes 786440 | tf_op jit(solution)/shard_map/ppermute | solution.py:45
  6.8 0.0 copy-start.2
  6.8 0.9 copy-done.2
  7.8 0.9 copy-done.3
  8.7 0.9 copy-done.7
  9.6 0.7 copy-done.13
  10.3 0.7 copy-done.17
  11.0 0.7 copy-done.20
  11.6 0.3 shard_map.141
  11.9 0.0 collective-permute-done.arrived_f
  11.9 0.0 copy-start.4
  11.9 6.9 %collective-permute-done.1.arrived_b = bf16[64,2048]{1,0:T(8,128)(2,1)S(1)} collective-permute-done((bf16[64,2048]{1,0:T(8,128)(2,1)}, bf16[64,2048]{1,0:T(8,128)(2,1)S(1)}, u32[]{:S(2)}, u32[]{:S(2)}) %collective-permute-start.1) | collective-permute-done | bytes 262176 | tf_op jit(solution)/shard_map/ppermute | solution.py:45
  18.8 0.5 shard_map.142
  19.3 2.7 %collective-permute-start.2 = (bf16[24,2048]{1,0:T(8,128)(2,1)S(1)}, bf16[24,2048]{1,0:T(8,128)(2,1)S(1)}, u32[]{:S(2)}, u32[]{:S(2)}) collective-permute-start(bf16[24,2048]{1,0:T(8,128)(2,1)S(1)} %get-tuple-element.62), channel_id=1, source_target_pairs={{0,4},{1,5},{2,6},{3,7},{4,0},{5,1},{6,2},{7,3},{8,12},{9,13},{10,... | collective-permute-start | bytes 294920 | tf_op jit(solution)/shard_map/ppermute | solution.py:66
  22.0 0.0 collective-permute-start.3
  22.0 2.6 %collective-permute-start.4 = (bf16[24,2048]{1,0:T(8,128)(2,1)S(1)}, bf16[24,2048]{1,0:T(8,128)(2,1)S(1)}, u32[]{:S(2)}, u32[]{:S(2)}) collective-permute-start(bf16[24,2048]{1,0:T(8,128)(2,1)S(1)} %get-tuple-element.64), channel_id=1, source_target_pairs={{0,5},{1,6},{2,7},{3,0},{4,1},{5,2},{6,3},{7,4},{8,13},{9,14},{10,... | collective-permute-start | bytes 294920 | tf_op jit(solution)/shard_map/ppermute | solution.py:66
  24.6 1.6 %collective-permute-start.5 = (bf16[24,2048]{1,0:T(8,128)(2,1)S(1)}, bf16[24,2048]{1,0:T(8,128)(2,1)S(1)}, u32[]{:S(2)}, u32[]{:S(2)}) collective-permute-start(bf16[24,2048]{1,0:T(8,128)(2,1)S(1)} %get-tuple-element.65), channel_id=1, source_target_pairs={{0,2},{1,3},{2,4},{3,5},{4,6},{5,7},{6,0},{7,1},{8,10},{9,11},{10,... | collective-permute-start | bytes 294920 | tf_op jit(solution)/shard_map/ppermute | solution.py:66
  26.2 2.2 %collective-permute-start.6 = (bf16[24,2048]{1,0:T(8,128)(2,1)S(1)}, bf16[24,2048]{1,0:T(8,128)(2,1)S(1)}, u32[]{:S(2)}, u32[]{:S(2)}) collective-permute-start(bf16[24,2048]{1,0:T(8,128)(2,1)S(1)} %get-tuple-element.66), channel_id=1, source_target_pairs={{0,6},{1,7},{2,0},{3,1},{4,2},{5,3},{6,4},{7,5},{8,14},{9,15},{10,... | collective-permute-start | bytes 294920 | tf_op jit(solution)/shard_map/ppermute | solution.py:66
  28.4 0.4 collective-permute-done.2.refs_0_
  28.9 0.0 collective-permute-start.7
  28.9 4.7 %collective-permute-done.3.refs_1_ = bf16[24,2048]{1,0:T(8,128)(2,1)S(1)} collective-permute-done((bf16[24,2048]{1,0:T(8,128)(2,1)S(1)}, bf16[24,2048]{1,0:T(8,128)(2,1)S(1)}, u32[]{:S(2)}, u32[]{:S(2)}) %collective-permute-start.3) | collective-permute-done | bytes 98336 | tf_op jit(solution)/shard_map/ppermute | solution.py:66
  33.5 0.0 collective-permute-start.8
  33.5 1.2 %copy.16 = bf16[8,24,1024]{2,1,0:T(8,128)(2,1)S(1)} copy(bf16[8,24,1024]{2,0,1:T(8,128)(2,1)} %bitcast.33) | data formatting | bytes 786432 | tf_op jit(solution)/shard_map/reshape | solution.py:477
  34.8 0.0 copy-done.4
  34.8 0.0 copy-done.5
  34.8 3.2 %shard_map.140 = (bf16[64,2048]{1,0:T(8,128)(2,1)}, bf16[64,2048]{1,0:T(8,128)(2,1)}, f32[2,8,64]{2,1,0:T(8,128)}, bf16[64,192]{1,0:T(8,128)(2,1)}, bf16[64,192]...) custom-call(bf16[64,2048]{1,0:T(8,128)(2,1)} %copy-done.4, ...), custom_call_target="tpu_custom_call" | custom-call | flops 100663296 | bytes 2883584 | tf_op jit(solution)/shard_map/pallas_call | solution.py:459
  38.0 0.0 collective-permute-done.4.refs_2_
  38.0 0.0 collective-permute-done.5.refs_3_
  38.0 0.0 collective-permute-done.6.refs_4_
  38.1 0.0 collective-permute-done.7.refs_5_
  38.1 0.0 collective-permute-done.8.refs_6_
  38.1 5.6 %all-to-all-start.1 = ((bf16[8,24,2048]{2,1,0:T(8,128)(2,1)}), bf16[8,24,2048]{2,1,0:T(8,128)(2,1)S(1)}, u32[]{:S(2)}, u32[]{:S(2)}) async-start(bf16[8,24,2048]{2,1,0:T(8,128)(2,1)} %bitcast.32), calls=%async_computation.1 | async-start | bytes 1572864 | tf_op jit(solution)/shard_map/all_to_all | solution.py:62
  43.7 20.6 %shard_map.143 = bf16[192,2176]{1,0:T(8,128)(2,1)} custom-call(bf16[8,32,1024]{2,1,0:T(8,128)(2,1)S(1)} %pad.4.saved_all, bf16[8,2048,1024]{2,1,0:T(8,128)(2,1)} %up.3, bf16[8,1024,2048]{2,1,0:T(8,128)(2,1)} %down.3, bf16[24,2048]{1,0:T(8,128)(2,1)S(1)} %collective-permute-done.2.refs_0_, bf16[24,2048]{1,0:T(8,128)(2,1)S(1)} %collective-permute-done.3.refs_1_, ...), custom_call_target="tpu_custom_call" | custom-call | flops 2147483648 | bytes 33554432 | tf_op jit(solution)/shard_map/pallas_call | solution.py:490
  64.2 0.4 all-to-all-done.1
  64.6 4.7 %all-to-all-start = ((bf16[8,24,2176]{2,1,0:T(8,128)(2,1)}), bf16[8,24,2176]{2,1,0:T(8,128)(2,1)S(1)}, u32[]{:S(2)}, u32[]{:S(2)}) async-start(bf16[8,24,2176]{2,1,0:T(8,128)(2,1)} %bitcast.14), calls=%async_computation | async-start | bytes 1671168 | tf_op jit(solution)/shard_map/all_to_all | solution.py:62
  69.4 0.0 copy-start.1
  69.4 0.0 copy-start.6
  69.4 0.0 copy-start.8
  69.4 0.0 copy-start.9
  69.4 0.0 copy-start.10
  69.4 0.0 copy-start.11
  69.4 0.0 copy-start.14
  69.4 0.0 copy-start.15
  69.5 0.0 copy-start.18
  69.5 20.5 %shard_map.144 = (bf16[24,2176]{1,0:T(8,128)(2,1)S(1)}, bf16[24,2176]{1,0:T(8,128)(2,1)}, bf16[24,2176]{1,0:T(8,128)(2,1)}, bf16[24,2176]{1,0:T(8,128)(2,1)S(1)}...) custom-call(bf16[8,32,1024]{2,1,0:T(8,128)(2,1)S(1)} %pad.4.saved_al, ...), custom_call_target="tpu_custom_call" | custom-call | flops 2147483648 | bytes 33554432 | tf_op jit(solution)/shard_map/pallas_call | solution.py:490
  90.0 3.0 %collective-permute-start.9 = (bf16[24,2176]{1,0:T(8,128)(2,1)S(1)}, bf16[24,2176]{1,0:T(8,128)(2,1)S(1)}, u32[]{:S(2)}, u32[]{:S(2)}) collective-permute-start(bf16[24,2176]{1,0:T(8,128)(2,1)S(1)} %get-tuple-element.93), channel_id=1, source_target_pairs={{0,4},{1,5},{2,6},{3,7},{4,0},{5,1},{6,2},{7,3},{8,12},{9,13},{10,... | collective-permute-start | bytes 313352 | tf_op jit(solution)/shard_map/ppermute | solution.py:66
  92.9 0.0 collective-permute-start.10
  93.0 1.7 %collective-permute-start.11 = (bf16[24,2176]{1,0:T(8,128)(2,1)}, bf16[24,2176]{1,0:T(8,128)(2,1)S(1)}, u32[]{:S(2)}, u32[]{:S(2)}) collective-permute-start(bf16[24,2176]{1,0:T(8,128)(2,1)} %get-tuple-element.95), channel_id=1, source_target_pairs={{0,3},{1,4},{2,5},{3,6},{4,7},{5,0},{6,1},{7,2},{8,11},{9,12},{10,... | collective-permute-start | bytes 313352 | tf_op jit(solution)/shard_map/ppermute | solution.py:66
  94.7 3.3 %collective-permute-start.12 = (bf16[24,2176]{1,0:T(8,128)(2,1)}, bf16[24,2176]{1,0:T(8,128)(2,1)S(1)}, u32[]{:S(2)}, u32[]{:S(2)}) collective-permute-start(bf16[24,2176]{1,0:T(8,128)(2,1)} %get-tuple-element.96), channel_id=1, source_target_pairs={{0,6},{1,7},{2,0},{3,1},{4,2},{5,3},{6,4},{7,5},{8,14},{9,15},{10,... | collective-permute-start | bytes 313352 | tf_op jit(solution)/shard_map/ppermute | solution.py:66
  98.0 0.0 collective-permute-start.13
  98.0 3.9 %collective-permute-done.9.refs_0_ = bf16[24,2176]{1,0:T(8,128)(2,1)S(1)} collective-permute-done((bf16[24,2176]{1,0:T(8,128)(2,1)S(1)}, bf16[24,2176]{1,0:T(8,128)(2,1)S(1)}, u32[]{:S(2)}, u32[]{:S(2)}) %collective-permute-start.9) | collective-permute-done | bytes 104480 | tf_op jit(solution)/shard_map/ppermute | solution.py:66
  101.8 5.4 %collective-permute-start.14 = (bf16[24,2176]{1,0:T(8,128)(2,1)}, bf16[24,2176]{1,0:T(8,128)(2,1)S(1)}, u32[]{:S(2)}, u32[]{:S(2)}) collective-permute-start(bf16[24,2176]{1,0:T(8,128)(2,1)} %get-tuple-element.98), channel_id=1, source_target_pairs={{0,7},{1,0},{2,1},{3,2},{4,3},{5,4},{6,5},{7,6},{8,15},{9,8},{10,9... | collective-permute-start | bytes 313352 | tf_op jit(solution)/shard_map/ppermute | solution.py:66
  107.3 0.0 collective-permute-done.10.refs_1_
  107.3 0.0 collective-permute-start.15
  107.3 0.0 all-to-all-done
  107.4 0.9 copy-done.12
  108.3 0.6 shard_map.145
  108.9 0.0 collective-permute-done.11.refs_2_
  108.9 0.0 collective-permute-done.12.refs_3_
  108.9 0.0 collective-permute-done.13.refs_4_
  108.9 1.3 %collective-permute-done.14.refs_5_ = bf16[24,2176]{1,0:T(8,128)(2,1)S(1)} collective-permute-done((bf16[24,2176]{1,0:T(8,128)(2,1)}, bf16[24,2176]{1,0:T(8,128)(2,1)S(1)}, u32[]{:S(2)}, u32[]{:S(2)}) %collective-permute-start.14) | collective-permute-done | bytes 104480 | tf_op jit(solution)/shard_map/ppermute | solution.py:66
  110.2 3.3 %collective-permute-done.15.refs_6_ = bf16[24,2176]{1,0:T(8,128)(2,1)} collective-permute-done((bf16[24,2176]{1,0:T(8,128)(2,1)}, bf16[24,2176]{1,0:T(8,128)(2,1)}, u32[]{:S(2)}, u32[]{:S(2)}) %collective-permute-start.15) | collective-permute-done | bytes 104480 | tf_op jit(solution)/shard_map/ppermute | solution.py:66
  113.5 2.4 %shard_map.146 = (bf16[1,64,2048]{2,1,0:T(8,128)(2,1)}, bf16[1,64,2048]{2,1,0:T(8,128)(2,1)}) custom-call(f32[64,2048]{1,0:T(8,128)S(1)} %get-tuple-element.84.early_f, f32[64,2048]{1,0:T(8,128)S(1)} %get-tuple-element.85.early_b, f32[2,8,64]{2,1,0:T(8,128)S(1)} %get-tuple-element.86.early_inner, bf16[64,2048]{1,0:T(8,128)(2,1)S(1)} %get-tuple-element.87.saved, ...), custom_call_target="tpu_custom_call" | custom-call | flops 100663296 | bytes 2883584 | tf_op jit(solution)/shard_map/pallas_call | solution.py:524
  (23 shorter events, 0.1 us)
Async XLA Ops:
  0.6 11.3 %collective-permute-start = (bf16[64,2048]{1,0:T(8,128)(2,1)}, bf16[64,2048]{1,0:T(8,128)(2,1)S(1)}, u32[]{:S(2)}, u32[]{:S(2)}) collective-permute-start(bf16[64,2048]{1,0:T(8,128)(2,1)} %bitcast.34), channel_id=1, source_target_pairs={{0,8},{8,16},{16,24},{1,9},{9,17},{17,25},{2,10},{10,18},{18,26},{... | collective-permute-start | bytes 786440 | tf_op jit(solution)/shard_map/ppermute | solution.py:45
  5.5 13.3 %collective-permute-start.1 = (bf16[64,2048]{1,0:T(8,128)(2,1)}, bf16[64,2048]{1,0:T(8,128)(2,1)S(1)}, u32[]{:S(2)}, u32[]{:S(2)}) collective-permute-start(bf16[64,2048]{1,0:T(8,128)(2,1)} %bitcast.35), channel_id=1, source_target_pairs={{8,0},{16,8},{24,16},{9,1},{17,9},{25,17},{10,2},{18,10},{26,18},{... | collective-permute-start | bytes 786440 | tf_op jit(solution)/shard_map/ppermute | solution.py:45
  6.8 1.0 copy-start.2
  7.7 0.9 copy-start.3
  8.7 0.9 copy-start.7
  9.6 0.7 copy-start.13
  10.3 0.7 copy-start.17
  11.0 0.7 copy-start.20
  11.9 22.9 %copy-start.4 = (bf16[64,2048]{1,0:T(8,128)(2,1)}, bf16[64,2048]{1,0:T(8,128)(2,1)S(1)}, u32[]{:S(2)}) copy-start(bf16[64,2048]{1,0:T(8,128)(2,1)S(1)} %collective-permute-done.arrived_f) | copy-start | bytes 786436
  18.8 16.0 %copy-start.5 = (bf16[64,2048]{1,0:T(8,128)(2,1)}, bf16[64,2048]{1,0:T(8,128)(2,1)S(1)}, u32[]{:S(2)}) copy-start(bf16[64,2048]{1,0:T(8,128)(2,1)S(1)} %collective-permute-done.1.arrived_b) | copy-start | bytes 786436
  19.3 9.5 %collective-permute-start.2 = (bf16[24,2048]{1,0:T(8,128)(2,1)S(1)}, bf16[24,2048]{1,0:T(8,128)(2,1)S(1)}, u32[]{:S(2)}, u32[]{:S(2)}) collective-permute-start(bf16[24,2048]{1,0:T(8,128)(2,1)S(1)} %get-tuple-element.62), channel_id=1, source_target_pairs={{0,4},{1,5},{2,6},{3,7},{4,0},{5,1},{6,2},{7,3},{8,12},{9,13},{10,... | collective-permute-start | bytes 294920 | tf_op jit(solution)/shard_map/ppermute | solution.py:66
  22.0 11.6 %collective-permute-start.3 = (bf16[24,2048]{1,0:T(8,128)(2,1)S(1)}, bf16[24,2048]{1,0:T(8,128)(2,1)S(1)}, u32[]{:S(2)}, u32[]{:S(2)}) collective-permute-start(bf16[24,2048]{1,0:T(8,128)(2,1)S(1)} %get-tuple-element.63), channel_id=1, source_target_pairs={{0,3},{1,4},{2,5},{3,6},{4,7},{5,0},{6,1},{7,2},{8,11},{9,12},{10,... | collective-permute-start | bytes 294920 | tf_op jit(solution)/shard_map/ppermute | solution.py:66
  22.0 16.1 %collective-permute-start.4 = (bf16[24,2048]{1,0:T(8,128)(2,1)S(1)}, bf16[24,2048]{1,0:T(8,128)(2,1)S(1)}, u32[]{:S(2)}, u32[]{:S(2)}) collective-permute-start(bf16[24,2048]{1,0:T(8,128)(2,1)S(1)} %get-tuple-element.64), channel_id=1, source_target_pairs={{0,5},{1,6},{2,7},{3,0},{4,1},{5,2},{6,3},{7,4},{8,13},{9,14},{10,... | collective-permute-start | bytes 294920 | tf_op jit(solution)/shard_map/ppermute | solution.py:66
  24.6 13.4 %collective-permute-start.5 = (bf16[24,2048]{1,0:T(8,128)(2,1)S(1)}, bf16[24,2048]{1,0:T(8,128)(2,1)S(1)}, u32[]{:S(2)}, u32[]{:S(2)}) collective-permute-start(bf16[24,2048]{1,0:T(8,128)(2,1)S(1)} %get-tuple-element.65), channel_id=1, source_target_pairs={{0,2},{1,3},{2,4},{3,5},{4,6},{5,7},{6,0},{7,1},{8,10},{9,11},{10,... | collective-permute-start | bytes 294920 | tf_op jit(solution)/shard_map/ppermute | solution.py:66
  26.2 11.8 %collective-permute-start.6 = (bf16[24,2048]{1,0:T(8,128)(2,1)S(1)}, bf16[24,2048]{1,0:T(8,128)(2,1)S(1)}, u32[]{:S(2)}, u32[]{:S(2)}) collective-permute-start(bf16[24,2048]{1,0:T(8,128)(2,1)S(1)} %get-tuple-element.66), channel_id=1, source_target_pairs={{0,6},{1,7},{2,0},{3,1},{4,2},{5,3},{6,4},{7,5},{8,14},{9,15},{10,... | collective-permute-start | bytes 294920 | tf_op jit(solution)/shard_map/ppermute | solution.py:66
  28.9 9.2 %collective-permute-start.7 = (bf16[24,2048]{1,0:T(8,128)(2,1)S(1)}, bf16[24,2048]{1,0:T(8,128)(2,1)S(1)}, u32[]{:S(2)}, u32[]{:S(2)}) collective-permute-start(bf16[24,2048]{1,0:T(8,128)(2,1)S(1)} %get-tuple-element.67), channel_id=1, source_target_pairs={{0,1},{1,2},{2,3},{3,4},{4,5},{5,6},{6,7},{7,0},{8,9},{9,10},{10,1... | collective-permute-start | bytes 294920 | tf_op jit(solution)/shard_map/ppermute | solution.py:66
  33.5 4.5 %collective-permute-start.8 = (bf16[24,2048]{1,0:T(8,128)(2,1)S(1)}, bf16[24,2048]{1,0:T(8,128)(2,1)S(1)}, u32[]{:S(2)}, u32[]{:S(2)}) collective-permute-start(bf16[24,2048]{1,0:T(8,128)(2,1)S(1)} %get-tuple-element.68), channel_id=1, source_target_pairs={{0,7},{1,0},{2,1},{3,2},{4,3},{5,4},{6,5},{7,6},{8,15},{9,8},{10,9... | collective-permute-start | bytes 294920 | tf_op jit(solution)/shard_map/ppermute | solution.py:66
  38.1 26.6 %all-to-all-start.1 = ((bf16[8,24,2048]{2,1,0:T(8,128)(2,1)}), bf16[8,24,2048]{2,1,0:T(8,128)(2,1)S(1)}, u32[]{:S(2)}, u32[]{:S(2)}) async-start(bf16[8,24,2048]{2,1,0:T(8,128)(2,1)} %bitcast.32), calls=%async_computation.1 | async-start | bytes 1572864 | tf_op jit(solution)/shard_map/all_to_all | solution.py:62
  64.6 42.6 %all-to-all-start = ((bf16[8,24,2176]{2,1,0:T(8,128)(2,1)}), bf16[8,24,2176]{2,1,0:T(8,128)(2,1)S(1)}, u32[]{:S(2)}, u32[]{:S(2)}) async-start(bf16[8,24,2176]{2,1,0:T(8,128)(2,1)} %bitcast.14), calls=%async_computation | async-start | bytes 1671168 | tf_op jit(solution)/shard_map/all_to_all | solution.py:62
  69.4 37.9 %copy-start = (bf16[1,64,2048]{2,1,0:T(8,128)(2,1)S(1)}, bf16[1,64,2048]{2,1,0:T(8,128)(2,1)}, u32[]{:S(2)}) copy-start(bf16[1,64,2048]{2,1,0:T(8,128)(2,1)} %param.18) | copy-start | bytes 786436
  69.4 37.9 %copy-start.1 = (bf16[1,2048,64]{1,2,0:T(8,128)(2,1)S(1)}, bf16[1,2048,64]{1,2,0:T(8,128)(2,1)}, u32[]{:S(2)}) copy-start(bf16[1,2048,64]{1,2,0:T(8,128)(2,1)} %param.22) | copy-start | bytes 786436
  69.4 37.9 %copy-start.6 = (bf16[2,192,64]{2,1,0:T(8,128)(2,1)S(1)}, bf16[2,192,64]{2,1,0:T(8,128)(2,1)}, u32[]{:S(2)}) copy-start(bf16[2,192,64]{2,1,0:T(8,128)(2,1)} %get-tuple-element.81.refs_12_.tables) | copy-start | bytes 147460
  69.4 37.9 %copy-start.8 = (bf16[64,2048]{1,0:T(8,128)(2,1)S(1)}, bf16[64,2048]{1,0:T(8,128)(2,1)}, u32[]{:S(2)}) copy-start(bf16[64,2048]{1,0:T(8,128)(2,1)} %get-tuple-element.51.tokens) | copy-start | bytes 786436
  69.4 37.9 %copy-start.9 = (bf16[64,2048]{1,0:T(8,128)(2,1)S(1)}, bf16[64,2048]{1,0:T(8,128)(2,1)}, u32[]{:S(2)}) copy-start(bf16[64,2048]{1,0:T(8,128)(2,1)} %get-tuple-element.52.refs_1_) | copy-start | bytes 786436
  69.4 37.9 %copy-start.10 = (bf16[64,192]{1,0:T(8,128)(2,1)S(1)}, bf16[64,192]{1,0:T(8,128)(2,1)}, u32[]{:S(2)}) copy-start(bf16[64,192]{1,0:T(8,128)(2,1)} %get-tuple-element.79.refs_10_.mixing_f) | copy-start | bytes 73732
  69.4 37.9 %copy-start.11 = (bf16[64,192]{1,0:T(8,128)(2,1)S(1)}, bf16[64,192]{1,0:T(8,128)(2,1)}, u32[]{:S(2)}) copy-start(bf16[64,192]{1,0:T(8,128)(2,1)} %get-tuple-element.80.refs_11_.mixing_b) | copy-start | bytes 73732
  69.4 37.9 %copy-start.14 = (bf16[1,2048]{1,0:T(2,128)(2,1)S(1)}, bf16[1,2048]{1,0:T(2,128)(2,1)}, u32[]{:S(2)}) copy-start(bf16[1,2048]{1,0:T(2,128)(2,1)} %refs_2_.1) | copy-start | bytes 12292
  69.4 37.9 %copy-start.15 = (bf16[64,192]{1,0:T(8,128)(2,1)S(1)}, bf16[64,192]{1,0:T(8,128)(2,1)}, u32[]{:S(2)}) copy-start(bf16[64,192]{1,0:T(8,128)(2,1)} %get-tuple-element.54.refs_6_) | copy-start | bytes 73732
  69.4 37.9 %copy-start.16 = (bf16[64,192]{1,0:T(8,128)(2,1)S(1)}, bf16[64,192]{1,0:T(8,128)(2,1)}, u32[]{:S(2)}) copy-start(bf16[64,192]{1,0:T(8,128)(2,1)} %get-tuple-element.55.refs_7_) | copy-start | bytes 73732
  69.5 37.9 %copy-start.18 = (s32[1,64,2]{1,2,0:T(2,128)S(1)}, s32[1,64,2]{1,2,0:T(2,128)}, u32[]{:S(2)}) copy-start(s32[1,64,2]{1,2,0:T(2,128)} %param.19) | copy-start | bytes 1540
  69.5 37.9 %copy-start.19 = (f32[2,8,64]{2,1,0:T(8,128)S(1)}, f32[2,8,64]{2,1,0:T(8,128)}, u32[]{:S(2)}) copy-start(f32[2,8,64]{2,1,0:T(8,128)} %get-tuple-element.53.refs_5_) | copy-start | bytes 12292
  90.0 11.9 %collective-permute-start.9 = (bf16[24,2176]{1,0:T(8,128)(2,1)S(1)}, bf16[24,2176]{1,0:T(8,128)(2,1)S(1)}, u32[]{:S(2)}, u32[]{:S(2)}) collective-permute-start(bf16[24,2176]{1,0:T(8,128)(2,1)S(1)} %get-tuple-element.93), channel_id=1, source_target_pairs={{0,4},{1,5},{2,6},{3,7},{4,0},{5,1},{6,2},{7,3},{8,12},{9,13},{10,... | collective-permute-start | bytes 313352 | tf_op jit(solution)/shard_map/ppermute | solution.py:66
  92.9 14.3 %collective-permute-start.10 = (bf16[24,2176]{1,0:T(8,128)(2,1)S(1)}, bf16[24,2176]{1,0:T(8,128)(2,1)S(1)}, u32[]{:S(2)}, u32[]{:S(2)}) collective-permute-start(bf16[24,2176]{1,0:T(8,128)(2,1)S(1)} %get-tuple-element.94), channel_id=1, source_target_pairs={{0,5},{1,6},{2,7},{3,0},{4,1},{5,2},{6,3},{7,4},{8,13},{9,14},{10,... | collective-permute-start | bytes 313352 | tf_op jit(solution)/shard_map/ppermute | solution.py:66
  93.0 15.9 %collective-permute-start.11 = (bf16[24,2176]{1,0:T(8,128)(2,1)}, bf16[24,2176]{1,0:T(8,128)(2,1)S(1)}, u32[]{:S(2)}, u32[]{:S(2)}) collective-permute-start(bf16[24,2176]{1,0:T(8,128)(2,1)} %get-tuple-element.95), channel_id=1, source_target_pairs={{0,3},{1,4},{2,5},{3,6},{4,7},{5,0},{6,1},{7,2},{8,11},{9,12},{10,... | collective-permute-start | bytes 313352 | tf_op jit(solution)/shard_map/ppermute | solution.py:66
  94.7 14.2 %collective-permute-start.12 = (bf16[24,2176]{1,0:T(8,128)(2,1)}, bf16[24,2176]{1,0:T(8,128)(2,1)S(1)}, u32[]{:S(2)}, u32[]{:S(2)}) collective-permute-start(bf16[24,2176]{1,0:T(8,128)(2,1)} %get-tuple-element.96), channel_id=1, source_target_pairs={{0,6},{1,7},{2,0},{3,1},{4,2},{5,3},{6,4},{7,5},{8,14},{9,15},{10,... | collective-permute-start | bytes 313352 | tf_op jit(solution)/shard_map/ppermute | solution.py:66
  98.0 10.9 %collective-permute-start.13 = (bf16[24,2176]{1,0:T(8,128)(2,1)}, bf16[24,2176]{1,0:T(8,128)(2,1)S(1)}, u32[]{:S(2)}, u32[]{:S(2)}) collective-permute-start(bf16[24,2176]{1,0:T(8,128)(2,1)} %get-tuple-element.97), channel_id=1, source_target_pairs={{0,2},{1,3},{2,4},{3,5},{4,6},{5,7},{6,0},{7,1},{8,10},{9,11},{10,... | collective-permute-start | bytes 313352 | tf_op jit(solution)/shard_map/ppermute | solution.py:66
  101.8 8.3 %collective-permute-start.14 = (bf16[24,2176]{1,0:T(8,128)(2,1)}, bf16[24,2176]{1,0:T(8,128)(2,1)S(1)}, u32[]{:S(2)}, u32[]{:S(2)}) collective-permute-start(bf16[24,2176]{1,0:T(8,128)(2,1)} %get-tuple-element.98), channel_id=1, source_target_pairs={{0,7},{1,0},{2,1},{3,2},{4,3},{5,4},{6,5},{7,6},{8,15},{9,8},{10,9... | collective-permute-start | bytes 313352 | tf_op jit(solution)/shard_map/ppermute | solution.py:66
  107.3 6.2 %collective-permute-start.15 = (bf16[24,2176]{1,0:T(8,128)(2,1)}, bf16[24,2176]{1,0:T(8,128)(2,1)}, u32[]{:S(2)}, u32[]{:S(2)}) collective-permute-start(bf16[24,2176]{1,0:T(8,128)(2,1)} %get-tuple-element.99), channel_id=1, source_target_pairs={{0,1},{1,2},{2,3},{3,4},{4,5},{5,6},{6,7},{7,0},{8,9},{9,10},{10,1... | collective-permute-start | bytes 313352 | tf_op jit(solution)/shard_map/ppermute | solution.py:66
  107.4 0.9 copy-start.12

commit v14 on v13

--- a/solution.py
+++ b/solution.py
@@ -46,7 +46,9 @@
 
 
 def far_first(size):
-    return sorted(range(size), key=lambda d: (abs(2 * d - size), d)) if size > 1 else [0]
+    if size == 1:
+        return [0]
+    return [1, *range(max(2, size // 2), size), *range(2, size // 2), 0]
 
 
 def by_block(refs):
@@ -56,14 +58,13 @@
     return ordered
 
 
-def exchange(blocks, direction):
+def exchange(blocks):
     size = lax.axis_size("expert")
     if len(blocks) == 1:
         return [lax.all_to_all(blocks[0], "expert", split_axis=0, concat_axis=0, tiled=True)]
     got = list(blocks)
     for d in far_first(size)[:-1]:
-        route = [(i, (i + direction * d) % size) for i in range(size)]
-        got[d] = lax.ppermute(blocks[d], "expert", route)
+        got[d] = lax.ppermute(blocks[d], "expert", [(i, i ^ d) for i in range(size)])
     return got
 
 
@@ -81,11 +82,8 @@
         ref[...] = value[d * share : (d + 1) * share].astype(BF16)
 
 
-def partners(distance, sources, direction, turned):
-    if not turned:
-        return distance
-    device = lax.axis_index("expert") + direction * distance
-    return jnp.where(device < 0, device + sources, jnp.where(device >= sources, device - sources, device))
+def partners(block, swapped):
+    return lax.bitwise_xor(block, jnp.full_like(block, lax.axis_index("expert"))) if swapped else block
 
 
 def expert_hits(routes, experts):
@@ -125,8 +123,8 @@
     return [exponent / total for exponent in exponents]
 
 
-def keys_of_part(sizes, columns, part, turned):
-    device = partners(columns[:, 0:1], sizes["sources"], 1, turned)
+def keys_of_part(sizes, columns, part, swapped):
+    device = partners(columns[:, 0:1], swapped)
     return columns[:, 2 + part : 3 + part] + device * sizes["share"]
 
 
@@ -197,7 +195,7 @@
             sends = sends[blocks:]
 
 
-def row_order(sizes, turned, shape, axis):
+def row_order(sizes, swapped, shape, axis):
     line = tuple(size if i == axis else 1 for i, size in enumerate(shape))
     row = lax.broadcasted_iota(jnp.int32, line, axis)
     block = sum(
@@ -208,7 +206,7 @@
         (within >= k * sizes["capacity"]).astype(jnp.int32)
         for k in range(1, sizes["block_rows"] // sizes["capacity"])
     )
-    source = partners(block, sizes["sources"], -1, turned)
+    source = partners(block, swapped)
     place = group * (sizes["padded"] - sizes["capacity"]) + source * sizes["capacity"] + within
     return (place == lax.broadcasted_iota(jnp.int32, shape, 1 - axis)).astype(F32).astype(BF16)
 
@@ -314,8 +312,8 @@
     if sizes["back"][-1]:
         refs, own = refs[:-4], refs[-4:]
     sum_f, sum_b, sums = tokens[...].astype(F32), None, None
-    for turned in sizes["back"][:-1]:
-        blocks = sizes["sources"] if turned else 1
+    for swapped in sizes["back"][:-1]:
+        blocks = sizes["sources"] if swapped else 1
         more_f, more_b, more = add_up(refs[3 : 3 + blocks], *refs[:3])
         refs = refs[3 + blocks :]
         sum_f += more_f
@@ -412,7 +410,7 @@
     parts = 2 if local % 2 == 0 else 1
     held = local // parts
     moved = 2 * slots // parts
-    few = sources <= 8
+    few = sources in (2, 4, 8)
     there = [few and part == 0 for part in range(parts)]
     back = [few and part == parts - 1 for part in range(parts)]
     columns = exchange_columns(parts, sources, local, capacity)
@@ -427,11 +425,11 @@
         "block_rows": moved // sources,
     }
 
-    def blocks_of(turned, columns):
-        blocks = sources if turned else 1
+    def blocks_of(swapped, columns):
+        blocks = sources if swapped else 1
         return [shape((moved // blocks, columns), BF16)] * blocks
 
-    later = [block for turned in there[1:] for block in blocks_of(turned, width)]
+    later = [block for swapped in there[1:] for block in blocks_of(swapped, width)]
 
     router_t = router[0].T
     routes_f, routes_b = forward_routes[0].T, backward_routes[0].T
@@ -477,14 +475,14 @@
     saved_pre = jnp.transpose(pre_activation[0], (1, 0, 2, 3)).reshape(local, rows, hidden)
     saved_pre = jnp.pad(saved_pre, ((0, 0), (0, padded - rows), (0, 0)))
     backs = []
-    got = exchange(send, 1)
+    got = exchange(send)
     for part in range(parts):
         if part + 1 < parts:
             got = [got[d] for d in far_first(len(got))]
             sends, saved_pre, got = lax.optimization_barrier((sends, saved_pre, got))
             got = by_block(got)
             blocks = len(blocks_of(there[part + 1], width))
-            coming = exchange(sends[:blocks], 1)
+            coming = exchange(sends[:blocks])
             sends = sends[blocks:]
         result = blocks_of(back[part], width + LANES)
         done = call(
@@ -504,7 +502,7 @@
                 pltpu.SemaphoreType.DMA((min(2, held), 2, 2)),
             ],
         )(saved_pre, up_weight, down_weight, *[got[d] for d in far_first(len(got))])
-        backs.append(exchange(list(done), -1))
+        backs.append(exchange(list(done)))
         got = coming if part + 1 < parts else None
     handed = (
         saved_inputs[0], upstream, norm_gain, router_t, routes_b, shares_b,

time: 116 us -> 116 us (level)
  starting transfers between devices: 39 us -> 29.4 us
  waiting for transfers between devices: 20.8 us -> 30.1 us
    ppermute x14, starting transfers between devices: 22.5 us -> 13.2 us  [exchange(): lax.ppermute(blocks[d], 'expert', [(i, i ^ d) for i in range(size)])]
    ppermute x14, waiting for transfers between devices: 13.6 us -> 22.8 us  [exchange(): lax.ppermute(blocks[d], 'expert', [(i, i ^ d) for i in range(size)])]
where the time goes in v14:
time: 116 us
  Pallas kernels  48 us (41%)
  waiting for transfers between devices  30.1 us (26%)
  starting transfers between devices  29.4 us (25%)
  local copies, waits for them, and re-layouts  7.05 us (6%)
    pallas_call x2, Pallas kernels, on_device(): call(functools.partial(expert_kernel, sizes, part, held), tuple(result),...  41.1 us
    ppermute x14, waiting for transfers between devices, exchange(): lax.ppermute(blocks[d], 'expert', [(i, i ^ d) for i in range(size)])  22.8 us
    ppermute x14, starting transfers between devices, exchange(): lax.ppermute(blocks[d], 'expert', [(i, i ^ d) for i in range(size)])  13.2 us
    all_to_all x2, starting transfers between devices, exchange(): lax.all_to_all(blocks[0], 'expert', split_axis=0, concat_axis=0, tiled=True)  10.1 us
    ppermute x2, waiting for transfers between devices, from_behind(): return lax.ppermute(block, axis, route)  6.87 us
    ppermute x2, starting transfers between devices, from_behind(): return lax.ppermute(block, axis, route)  6.15 us
    unnamed x42, local copies, waits for them, and re-layouts  5.79 us
    pallas_call x1, Pallas kernels, on_device(): call(functools.partial(mixing_kernel, sizes), (row_shape, row_shape, shap...  3.21 us
  transfers between devices with their start and end apart: 18, of which 7 were waited for; matrix products, arithmetic and copies ran while one was open for 1% of the time, Pallas kernels for 39%

profile of v14, /device:TPU:0, one launch (start us, length us, event | category | flops | bytes accessed | tf_op | source)
XLA Modules:
  0.0 115.6 jit_solution(5516261864501226927)
XLA Ops:
  0.6 4.9 %collective-permute-start = (bf16[64,2048]{1,0:T(8,128)(2,1)}, bf16[64,2048]{1,0:T(8,128)(2,1)S(1)}, u32[]{:S(2)}, u32[]{:S(2)}) collective-permute-start(bf16[64,2048]{1,0:T(8,128)(2,1)} %bitcast.34), channel_id=1, source_target_pairs={{0,8},{8,16},{16,24},{1,9},{9,17},{17,25},{2,10},{10,18},{18,26},{... | collective-permute-start | bytes 786440 | tf_op jit(solution)/shard_map/ppermute | solution.py:45
  5.5 1.3 %collective-permute-start.1 = (bf16[64,2048]{1,0:T(8,128)(2,1)}, bf16[64,2048]{1,0:T(8,128)(2,1)S(1)}, u32[]{:S(2)}, u32[]{:S(2)}) collective-permute-start(bf16[64,2048]{1,0:T(8,128)(2,1)} %bitcast.35), channel_id=1, source_target_pairs={{8,0},{16,8},{24,16},{9,1},{17,9},{25,17},{10,2},{18,10},{26,18},{... | collective-permute-start | bytes 786440 | tf_op jit(solution)/shard_map/ppermute | solution.py:45
  6.8 0.0 copy-start.2
  6.8 0.9 copy-done.2
  7.8 0.9 copy-done.3
  8.7 0.9 copy-done.7
  9.6 0.7 copy-done.13
  10.3 0.7 copy-done.17
  11.0 0.7 copy-done.20
  11.6 0.3 shard_map.141
  11.9 0.0 collective-permute-done.arrived_f
  11.9 0.0 copy-start.4
  11.9 6.9 %collective-permute-done.1.arrived_b = bf16[64,2048]{1,0:T(8,128)(2,1)S(1)} collective-permute-done((bf16[64,2048]{1,0:T(8,128)(2,1)}, bf16[64,2048]{1,0:T(8,128)(2,1)S(1)}, u32[]{:S(2)}, u32[]{:S(2)}) %collective-permute-start.1) | collective-permute-done | bytes 262176 | tf_op jit(solution)/shard_map/ppermute | solution.py:45
  18.8 0.5 shard_map.142
  19.3 0.1 collective-permute-start.2
  19.4 2.7 %collective-permute-start.3 = (bf16[24,2048]{1,0:T(8,128)(2,1)S(1)}, bf16[24,2048]{1,0:T(8,128)(2,1)S(1)}, u32[]{:S(2)}, u32[]{:S(2)}) collective-permute-start(bf16[24,2048]{1,0:T(8,128)(2,1)S(1)} %get-tuple-element.63), channel_id=1, source_target_pairs={{0,4},{1,5},{2,6},{3,7},{4,0},{5,1},{6,2},{7,3},{8,12},{9,13},{10,... | collective-permute-start | bytes 294920 | tf_op jit(solution)/shard_map/ppermute | solution.py:67
  22.0 0.1 collective-permute-start.4
  22.2 3.6 %collective-permute-start.5 = (bf16[24,2048]{1,0:T(8,128)(2,1)S(1)}, bf16[24,2048]{1,0:T(8,128)(2,1)S(1)}, u32[]{:S(2)}, u32[]{:S(2)}) collective-permute-start(bf16[24,2048]{1,0:T(8,128)(2,1)S(1)} %get-tuple-element.65), channel_id=1, source_target_pairs={{0,6},{1,7},{2,4},{3,5},{4,2},{5,3},{6,0},{7,1},{8,14},{9,15},{10,... | collective-permute-start | bytes 294920 | tf_op jit(solution)/shard_map/ppermute | solution.py:67
  25.8 0.0 collective-permute-start.6
  25.8 0.0 collective-permute-done.2.refs_0_
  25.8 0.0 collective-permute-start.7
  25.8 8.7 %collective-permute-done.3.refs_1_ = bf16[24,2048]{1,0:T(8,128)(2,1)S(1)} collective-permute-done((bf16[24,2048]{1,0:T(8,128)(2,1)S(1)}, bf16[24,2048]{1,0:T(8,128)(2,1)S(1)}, u32[]{:S(2)}, u32[]{:S(2)}) %collective-permute-start.3) | collective-permute-done | bytes 98336 | tf_op jit(solution)/shard_map/ppermute | solution.py:67
  34.5 0.0 collective-permute-start.8
  34.5 1.2 %copy.16 = bf16[8,24,1024]{2,1,0:T(8,128)(2,1)S(1)} copy(bf16[8,24,1024]{2,0,1:T(8,128)(2,1)} %bitcast.33) | data formatting | bytes 786432 | tf_op jit(solution)/shard_map/reshape | solution.py:475
  35.8 0.0 copy-done.4
  35.8 0.0 copy-done.5
  35.8 3.2 %shard_map.140 = (bf16[64,2048]{1,0:T(8,128)(2,1)}, bf16[64,2048]{1,0:T(8,128)(2,1)}, f32[2,8,64]{2,1,0:T(8,128)}, bf16[64,192]{1,0:T(8,128)(2,1)}, bf16[64,192]...) custom-call(bf16[64,2048]{1,0:T(8,128)(2,1)} %copy-done.4, ...), custom_call_target="tpu_custom_call" | custom-call | flops 100663296 | bytes 2883584 | tf_op jit(solution)/shard_map/pallas_call | solution.py:457
  39.0 0.0 collective-permute-done.4.refs_2_
  39.0 0.0 collective-permute-done.5.refs_3_
  39.0 0.0 collective-permute-done.6.refs_4_
  39.0 0.0 collective-permute-done.7.refs_5_
  39.0 0.6 collective-permute-done.8.refs_6_
  39.6 5.3 %all-to-all-start.1 = ((bf16[8,24,2048]{2,1,0:T(8,128)(2,1)}), bf16[8,24,2048]{2,1,0:T(8,128)(2,1)S(1)}, u32[]{:S(2)}, u32[]{:S(2)}) async-start(bf16[8,24,2048]{2,1,0:T(8,128)(2,1)} %bitcast.32), calls=%async_computation.1 | async-start | bytes 1572864 | tf_op jit(solution)/shard_map/all_to_all | solution.py:64
  45.0 20.6 %shard_map.143 = bf16[192,2176]{1,0:T(8,128)(2,1)} custom-call(bf16[8,32,1024]{2,1,0:T(8,128)(2,1)S(1)} %pad.4.saved_all, bf16[8,2048,1024]{2,1,0:T(8,128)(2,1)} %up.3, bf16[8,1024,2048]{2,1,0:T(8,128)(2,1)} %down.3, bf16[24,2048]{1,0:T(8,128)(2,1)S(1)} %collective-permute-done.2.refs_0_, bf16[24,2048]{1,0:T(8,128)(2,1)S(1)} %collective-permute-done.3.refs_1_, ...), custom_call_target="tpu_custom_call" | custom-call | flops 2147483648 | bytes 33554432 | tf_op jit(solution)/shard_map/pallas_call | solution.py:488
  65.5 0.4 all-to-all-done.1
  65.9 4.7 %all-to-all-start = ((bf16[8,24,2176]{2,1,0:T(8,128)(2,1)}), bf16[8,24,2176]{2,1,0:T(8,128)(2,1)S(1)}, u32[]{:S(2)}, u32[]{:S(2)}) async-start(bf16[8,24,2176]{2,1,0:T(8,128)(2,1)} %bitcast.14), calls=%async_computation | async-start | bytes 1671168 | tf_op jit(solution)/shard_map/all_to_all | solution.py:64
  70.7 0.0 copy-start.1
  70.7 0.0 copy-start.6
  70.7 0.0 copy-start.8
  70.7 0.0 copy-start.9
  70.7 0.0 copy-start.10
  70.7 0.0 copy-start.11
  70.7 0.0 copy-start.14
  70.7 0.0 copy-start.15
  70.8 0.0 copy-start.18
  70.8 20.5 %shard_map.144 = (bf16[24,2176]{1,0:T(8,128)(2,1)S(1)}, bf16[24,2176]{1,0:T(8,128)(2,1)S(1)}, bf16[24,2176]{1,0:T(8,128)(2,1)}, bf16[24,2176]{1,0:T(8,128)(2,1)}...) custom-call(bf16[8,32,1024]{2,1,0:T(8,128)(2,1)S(1)} %pad.4.saved_al, ...), custom_call_target="tpu_custom_call" | custom-call | flops 2147483648 | bytes 33554432 | tf_op jit(solution)/shard_map/pallas_call | solution.py:488
  91.3 0.6 collective-permute-start.9
  91.9 2.6 %collective-permute-start.10 = (bf16[24,2176]{1,0:T(8,128)(2,1)S(1)}, bf16[24,2176]{1,0:T(8,128)(2,1)S(1)}, u32[]{:S(2)}, u32[]{:S(2)}) collective-permute-start(bf16[24,2176]{1,0:T(8,128)(2,1)S(1)} %get-tuple-element.94), channel_id=1, source_target_pairs={{0,4},{1,5},{2,6},{3,7},{4,0},{5,1},{6,2},{7,3},{8,12},{9,13},{10,... | collective-permute-start | bytes 313352 | tf_op jit(solution)/shard_map/ppermute | solution.py:67
  94.4 0.0 collective-permute-start.11
  94.4 3.5 %collective-permute-start.12 = (bf16[24,2176]{1,0:T(8,128)(2,1)}, bf16[24,2176]{1,0:T(8,128)(2,1)S(1)}, u32[]{:S(2)}, u32[]{:S(2)}) collective-permute-start(bf16[24,2176]{1,0:T(8,128)(2,1)} %get-tuple-element.96), channel_id=1, source_target_pairs={{0,6},{1,7},{2,4},{3,5},{4,2},{5,3},{6,0},{7,1},{8,14},{9,15},{10,... | collective-permute-start | bytes 313352 | tf_op jit(solution)/shard_map/ppermute | solution.py:67
  97.9 0.1 collective-permute-start.13
  98.0 0.0 collective-permute-done.9.refs_0_
  98.0 0.0 collective-permute-start.14
  98.0 9.5 %collective-permute-done.10.refs_1_ = bf16[24,2176]{1,0:T(8,128)(2,1)S(1)} collective-permute-done((bf16[24,2176]{1,0:T(8,128)(2,1)S(1)}, bf16[24,2176]{1,0:T(8,128)(2,1)S(1)}, u32[]{:S(2)}, u32[]{:S(2)}) %collective-permute-start.10) | collective-permute-done | bytes 104480 | tf_op jit(solution)/shard_map/ppermute | solution.py:67
  107.6 0.0 collective-permute-start.15
  107.6 0.0 all-to-all-done
  107.7 0.9 copy-done.12
  108.6 0.6 shard_map.145
  109.2 0.0 collective-permute-done.11.refs_2_
  109.2 0.0 collective-permute-done.12.refs_3_
  109.2 0.0 collective-permute-done.13.refs_4_
  109.2 1.6 %collective-permute-done.14.refs_5_ = bf16[24,2176]{1,0:T(8,128)(2,1)S(1)} collective-permute-done((bf16[24,2176]{1,0:T(8,128)(2,1)}, bf16[24,2176]{1,0:T(8,128)(2,1)S(1)}, u32[]{:S(2)}, u32[]{:S(2)}) %collective-permute-start.14) | collective-permute-done | bytes 104480 | tf_op jit(solution)/shard_map/ppermute | solution.py:67
  110.8 2.3 %collective-permute-done.15.refs_6_ = bf16[24,2176]{1,0:T(8,128)(2,1)} collective-permute-done((bf16[24,2176]{1,0:T(8,128)(2,1)}, bf16[24,2176]{1,0:T(8,128)(2,1)}, u32[]{:S(2)}, u32[]{:S(2)}) %collective-permute-start.15) | collective-permute-done | bytes 104480 | tf_op jit(solution)/shard_map/ppermute | solution.py:67
  113.2 2.4 %shard_map.146 = (bf16[1,64,2048]{2,1,0:T(8,128)(2,1)}, bf16[1,64,2048]{2,1,0:T(8,128)(2,1)}) custom-call(f32[64,2048]{1,0:T(8,128)S(1)} %get-tuple-element.84.early_f, f32[64,2048]{1,0:T(8,128)S(1)} %get-tuple-element.85.early_b, f32[2,8,64]{2,1,0:T(8,128)S(1)} %get-tuple-element.86.early_inner, bf16[64,2048]{1,0:T(8,128)(2,1)S(1)} %get-tuple-element.87.saved, ...), custom_call_target="tpu_custom_call" | custom-call | flops 100663296 | bytes 2883584 | tf_op jit(solution)/shard_map/pallas_call | solution.py:522
  (23 shorter events, 0.1 us)
Async XLA Ops:
  0.6 11.3 %collective-permute-start = (bf16[64,2048]{1,0:T(8,128)(2,1)}, bf16[64,2048]{1,0:T(8,128)(2,1)S(1)}, u32[]{:S(2)}, u32[]{:S(2)}) collective-permute-start(bf16[64,2048]{1,0:T(8,128)(2,1)} %bitcast.34), channel_id=1, source_target_pairs={{0,8},{8,16},{16,24},{1,9},{9,17},{17,25},{2,10},{10,18},{18,26},{... | collective-permute-start | bytes 786440 | tf_op jit(solution)/shard_map/ppermute | solution.py:45
  5.5 13.3 %collective-permute-start.1 = (bf16[64,2048]{1,0:T(8,128)(2,1)}, bf16[64,2048]{1,0:T(8,128)(2,1)S(1)}, u32[]{:S(2)}, u32[]{:S(2)}) collective-permute-start(bf16[64,2048]{1,0:T(8,128)(2,1)} %bitcast.35), channel_id=1, source_target_pairs={{8,0},{16,8},{24,16},{9,1},{17,9},{25,17},{10,2},{18,10},{26,18},{... | collective-permute-start | bytes 786440 | tf_op jit(solution)/shard_map/ppermute | solution.py:45
  6.8 1.0 copy-start.2
  7.7 0.9 copy-start.3
  8.7 0.9 copy-start.7
  9.6 0.7 copy-start.13
  10.3 0.7 copy-start.17
  11.0 0.7 copy-start.20
  11.9 23.8 %copy-start.4 = (bf16[64,2048]{1,0:T(8,128)(2,1)}, bf16[64,2048]{1,0:T(8,128)(2,1)S(1)}, u32[]{:S(2)}) copy-start(bf16[64,2048]{1,0:T(8,128)(2,1)S(1)} %collective-permute-done.arrived_f) | copy-start | bytes 786436
  18.8 17.0 %copy-start.5 = (bf16[64,2048]{1,0:T(8,128)(2,1)}, bf16[64,2048]{1,0:T(8,128)(2,1)S(1)}, u32[]{:S(2)}) copy-start(bf16[64,2048]{1,0:T(8,128)(2,1)S(1)} %collective-permute-done.1.arrived_b) | copy-start | bytes 786436
  19.3 6.5 %collective-permute-start.2 = (bf16[24,2048]{1,0:T(8,128)(2,1)S(1)}, bf16[24,2048]{1,0:T(8,128)(2,1)S(1)}, u32[]{:S(2)}, u32[]{:S(2)}) collective-permute-start(bf16[24,2048]{1,0:T(8,128)(2,1)S(1)} %get-tuple-element.62), channel_id=1, source_target_pairs={{0,1},{1,0},{2,3},{3,2},{4,5},{5,4},{6,7},{7,6},{8,9},{9,8},{10,11... | collective-permute-start | bytes 294920 | tf_op jit(solution)/shard_map/ppermute | solution.py:67
  19.4 15.1 %collective-permute-start.3 = (bf16[24,2048]{1,0:T(8,128)(2,1)S(1)}, bf16[24,2048]{1,0:T(8,128)(2,1)S(1)}, u32[]{:S(2)}, u32[]{:S(2)}) collective-permute-start(bf16[24,2048]{1,0:T(8,128)(2,1)S(1)} %get-tuple-element.63), channel_id=1, source_target_pairs={{0,4},{1,5},{2,6},{3,7},{4,0},{5,1},{6,2},{7,3},{8,12},{9,13},{10,... | collective-permute-start | bytes 294920 | tf_op jit(solution)/shard_map/ppermute | solution.py:67
  22.0 16.9 %collective-permute-start.4 = (bf16[24,2048]{1,0:T(8,128)(2,1)S(1)}, bf16[24,2048]{1,0:T(8,128)(2,1)S(1)}, u32[]{:S(2)}, u32[]{:S(2)}) collective-permute-start(bf16[24,2048]{1,0:T(8,128)(2,1)S(1)} %get-tuple-element.64), channel_id=1, source_target_pairs={{0,5},{1,4},{2,7},{3,6},{4,1},{5,0},{6,3},{7,2},{8,13},{9,12},{10,... | collective-permute-start | bytes 294920 | tf_op jit(solution)/shard_map/ppermute | solution.py:67
  22.2 16.8 %collective-permute-start.5 = (bf16[24,2048]{1,0:T(8,128)(2,1)S(1)}, bf16[24,2048]{1,0:T(8,128)(2,1)S(1)}, u32[]{:S(2)}, u32[]{:S(2)}) collective-permute-start(bf16[24,2048]{1,0:T(8,128)(2,1)S(1)} %get-tuple-element.65), channel_id=1, source_target_pairs={{0,6},{1,7},{2,4},{3,5},{4,2},{5,3},{6,0},{7,1},{8,14},{9,15},{10,... | collective-permute-start | bytes 294920 | tf_op jit(solution)/shard_map/ppermute | solution.py:67
  25.8 13.2 %collective-permute-start.6 = (bf16[24,2048]{1,0:T(8,128)(2,1)S(1)}, bf16[24,2048]{1,0:T(8,128)(2,1)S(1)}, u32[]{:S(2)}, u32[]{:S(2)}) collective-permute-start(bf16[24,2048]{1,0:T(8,128)(2,1)S(1)} %get-tuple-element.66), channel_id=1, source_target_pairs={{0,7},{1,6},{2,5},{3,4},{4,3},{5,2},{6,1},{7,0},{8,15},{9,14},{10,... | collective-permute-start | bytes 294920 | tf_op jit(solution)/shard_map/ppermute | solution.py:67
  25.8 13.2 %collective-permute-start.7 = (bf16[24,2048]{1,0:T(8,128)(2,1)S(1)}, bf16[24,2048]{1,0:T(8,128)(2,1)S(1)}, u32[]{:S(2)}, u32[]{:S(2)}) collective-permute-start(bf16[24,2048]{1,0:T(8,128)(2,1)S(1)} %get-tuple-element.67), channel_id=1, source_target_pairs={{0,2},{1,3},{2,0},{3,1},{4,6},{5,7},{6,4},{7,5},{8,10},{9,11},{10,... | collective-permute-start | bytes 294920 | tf_op jit(solution)/shard_map/ppermute | solution.py:67
  34.5 5.2 %collective-permute-start.8 = (bf16[24,2048]{1,0:T(8,128)(2,1)S(1)}, bf16[24,2048]{1,0:T(8,128)(2,1)S(1)}, u32[]{:S(2)}, u32[]{:S(2)}) collective-permute-start(bf16[24,2048]{1,0:T(8,128)(2,1)S(1)} %get-tuple-element.68), channel_id=1, source_target_pairs={{0,3},{1,2},{2,1},{3,0},{4,7},{5,6},{6,5},{7,4},{8,11},{9,10},{10,... | collective-permute-start | bytes 294920 | tf_op jit(solution)/shard_map/ppermute | solution.py:67
  39.6 26.3 %all-to-all-start.1 = ((bf16[8,24,2048]{2,1,0:T(8,128)(2,1)}), bf16[8,24,2048]{2,1,0:T(8,128)(2,1)S(1)}, u32[]{:S(2)}, u32[]{:S(2)}) async-start(bf16[8,24,2048]{2,1,0:T(8,128)(2,1)} %bitcast.32), calls=%async_computation.1 | async-start | bytes 1572864 | tf_op jit(solution)/shard_map/all_to_all | solution.py:64
  65.9 41.6 %all-to-all-start = ((bf16[8,24,2176]{2,1,0:T(8,128)(2,1)}), bf16[8,24,2176]{2,1,0:T(8,128)(2,1)S(1)}, u32[]{:S(2)}, u32[]{:S(2)}) async-start(bf16[8,24,2176]{2,1,0:T(8,128)(2,1)} %bitcast.14), calls=%async_computation | async-start | bytes 1671168 | tf_op jit(solution)/shard_map/all_to_all | solution.py:64
  70.7 36.9 %copy-start = (bf16[1,64,2048]{2,1,0:T(8,128)(2,1)S(1)}, bf16[1,64,2048]{2,1,0:T(8,128)(2,1)}, u32[]{:S(2)}) copy-start(bf16[1,64,2048]{2,1,0:T(8,128)(2,1)} %param.18) | copy-start | bytes 786436
  70.7 36.9 %copy-start.1 = (bf16[1,2048,64]{1,2,0:T(8,128)(2,1)S(1)}, bf16[1,2048,64]{1,2,0:T(8,128)(2,1)}, u32[]{:S(2)}) copy-start(bf16[1,2048,64]{1,2,0:T(8,128)(2,1)} %param.22) | copy-start | bytes 786436
  70.7 36.9 %copy-start.6 = (bf16[2,192,64]{2,1,0:T(8,128)(2,1)S(1)}, bf16[2,192,64]{2,1,0:T(8,128)(2,1)}, u32[]{:S(2)}) copy-start(bf16[2,192,64]{2,1,0:T(8,128)(2,1)} %get-tuple-element.81.refs_12_.tables) | copy-start | bytes 147460
  70.7 36.9 %copy-start.8 = (bf16[64,2048]{1,0:T(8,128)(2,1)S(1)}, bf16[64,2048]{1,0:T(8,128)(2,1)}, u32[]{:S(2)}) copy-start(bf16[64,2048]{1,0:T(8,128)(2,1)} %get-tuple-element.51.tokens) | copy-start | bytes 786436
  70.7 36.9 %copy-start.9 = (bf16[64,2048]{1,0:T(8,128)(2,1)S(1)}, bf16[64,2048]{1,0:T(8,128)(2,1)}, u32[]{:S(2)}) copy-start(bf16[64,2048]{1,0:T(8,128)(2,1)} %get-tuple-element.52.refs_1_) | copy-start | bytes 786436
  70.7 36.9 %copy-start.10 = (bf16[64,192]{1,0:T(8,128)(2,1)S(1)}, bf16[64,192]{1,0:T(8,128)(2,1)}, u32[]{:S(2)}) copy-start(bf16[64,192]{1,0:T(8,128)(2,1)} %get-tuple-element.79.refs_10_.mixing_f) | copy-start | bytes 73732
  70.7 36.9 %copy-start.11 = (bf16[64,192]{1,0:T(8,128)(2,1)S(1)}, bf16[64,192]{1,0:T(8,128)(2,1)}, u32[]{:S(2)}) copy-start(bf16[64,192]{1,0:T(8,128)(2,1)} %get-tuple-element.80.refs_11_.mixing_b) | copy-start | bytes 73732
  70.7 36.9 %copy-start.14 = (bf16[1,2048]{1,0:T(2,128)(2,1)S(1)}, bf16[1,2048]{1,0:T(2,128)(2,1)}, u32[]{:S(2)}) copy-start(bf16[1,2048]{1,0:T(2,128)(2,1)} %refs_2_.1) | copy-start | bytes 12292
  70.7 36.9 %copy-start.15 = (bf16[64,192]{1,0:T(8,128)(2,1)S(1)}, bf16[64,192]{1,0:T(8,128)(2,1)}, u32[]{:S(2)}) copy-start(bf16[64,192]{1,0:T(8,128)(2,1)} %get-tuple-element.54.refs_6_) | copy-start | bytes 73732
  70.8 36.9 %copy-start.16 = (bf16[64,192]{1,0:T(8,128)(2,1)S(1)}, bf16[64,192]{1,0:T(8,128)(2,1)}, u32[]{:S(2)}) copy-start(bf16[64,192]{1,0:T(8,128)(2,1)} %get-tuple-element.55.refs_7_) | copy-start | bytes 73732
  70.8 36.9 %copy-start.18 = (s32[1,64,2]{1,2,0:T(2,128)S(1)}, s32[1,64,2]{1,2,0:T(2,128)}, u32[]{:S(2)}) copy-start(s32[1,64,2]{1,2,0:T(2,128)} %param.19) | copy-start | bytes 1540
  70.8 36.9 %copy-start.19 = (f32[2,8,64]{2,1,0:T(8,128)S(1)}, f32[2,8,64]{2,1,0:T(8,128)}, u32[]{:S(2)}) copy-start(f32[2,8,64]{2,1,0:T(8,128)} %get-tuple-element.53.refs_5_) | copy-start | bytes 12292
  91.3 6.8 %collective-permute-start.9 = (bf16[24,2176]{1,0:T(8,128)(2,1)S(1)}, bf16[24,2176]{1,0:T(8,128)(2,1)S(1)}, u32[]{:S(2)}, u32[]{:S(2)}) collective-permute-start(bf16[24,2176]{1,0:T(8,128)(2,1)S(1)} %get-tuple-element.93), channel_id=1, source_target_pairs={{0,1},{1,0},{2,3},{3,2},{4,5},{5,4},{6,7},{7,6},{8,9},{9,8},{10,11... | collective-permute-start | bytes 313352 | tf_op jit(solution)/shard_map/ppermute | solution.py:67
  91.9 15.7 %collective-permute-start.10 = (bf16[24,2176]{1,0:T(8,128)(2,1)S(1)}, bf16[24,2176]{1,0:T(8,128)(2,1)S(1)}, u32[]{:S(2)}, u32[]{:S(2)}) collective-permute-start(bf16[24,2176]{1,0:T(8,128)(2,1)S(1)} %get-tuple-element.94), channel_id=1, source_target_pairs={{0,4},{1,5},{2,6},{3,7},{4,0},{5,1},{6,2},{7,3},{8,12},{9,13},{10,... | collective-permute-start | bytes 313352 | tf_op jit(solution)/shard_map/ppermute | solution.py:67
  94.4 14.7 %collective-permute-start.11 = (bf16[24,2176]{1,0:T(8,128)(2,1)}, bf16[24,2176]{1,0:T(8,128)(2,1)S(1)}, u32[]{:S(2)}, u32[]{:S(2)}) collective-permute-start(bf16[24,2176]{1,0:T(8,128)(2,1)} %get-tuple-element.95), channel_id=1, source_target_pairs={{0,5},{1,4},{2,7},{3,6},{4,1},{5,0},{6,3},{7,2},{8,13},{9,12},{10,... | collective-permute-start | bytes 313352 | tf_op jit(solution)/shard_map/ppermute | solution.py:67
  94.4 14.7 %collective-permute-start.12 = (bf16[24,2176]{1,0:T(8,128)(2,1)}, bf16[24,2176]{1,0:T(8,128)(2,1)S(1)}, u32[]{:S(2)}, u32[]{:S(2)}) collective-permute-start(bf16[24,2176]{1,0:T(8,128)(2,1)} %get-tuple-element.96), channel_id=1, source_target_pairs={{0,6},{1,7},{2,4},{3,5},{4,2},{5,3},{6,0},{7,1},{8,14},{9,15},{10,... | collective-permute-start | bytes 313352 | tf_op jit(solution)/shard_map/ppermute | solution.py:67
  97.9 11.3 %collective-permute-start.13 = (bf16[24,2176]{1,0:T(8,128)(2,1)}, bf16[24,2176]{1,0:T(8,128)(2,1)S(1)}, u32[]{:S(2)}, u32[]{:S(2)}) collective-permute-start(bf16[24,2176]{1,0:T(8,128)(2,1)} %get-tuple-element.97), channel_id=1, source_target_pairs={{0,7},{1,6},{2,5},{3,4},{4,3},{5,2},{6,1},{7,0},{8,15},{9,14},{10,... | collective-permute-start | bytes 313352 | tf_op jit(solution)/shard_map/ppermute | solution.py:67
  98.0 12.8 %collective-permute-start.14 = (bf16[24,2176]{1,0:T(8,128)(2,1)}, bf16[24,2176]{1,0:T(8,128)(2,1)S(1)}, u32[]{:S(2)}, u32[]{:S(2)}) collective-permute-start(bf16[24,2176]{1,0:T(8,128)(2,1)} %get-tuple-element.98), channel_id=1, source_target_pairs={{0,2},{1,3},{2,0},{3,1},{4,6},{5,7},{6,4},{7,5},{8,10},{9,11},{10,... | collective-permute-start | bytes 313352 | tf_op jit(solution)/shard_map/ppermute | solution.py:67
  107.6 5.6 %collective-permute-start.15 = (bf16[24,2176]{1,0:T(8,128)(2,1)}, bf16[24,2176]{1,0:T(8,128)(2,1)}, u32[]{:S(2)}, u32[]{:S(2)}) collective-permute-start(bf16[24,2176]{1,0:T(8,128)(2,1)} %get-tuple-element.99), channel_id=1, source_target_pairs={{0,3},{1,2},{2,1},{3,0},{4,7},{5,6},{6,5},{7,4},{8,11},{9,10},{10,... | collective-permute-start | bytes 313352 | tf_op jit(solution)/shard_map/ppermute | solution.py:67
  107.7 0.9 copy-start.12

commit v15 on v14

--- a/solution.py
+++ b/solution.py
@@ -45,15 +45,15 @@
     return lax.ppermute(block, axis, route)
 
 
-def far_first(size):
-    if size == 1:
-        return [0]
-    return [1, *range(max(2, size // 2), size), *range(2, size // 2), 0]
+def start_order(size):
+    near = [d for d in (1, 2) if d < max(2, size // 2)] if size > 1 else []
+    far = [d for d in range(max(2, size // 2), size)]
+    return near + far + [d for d in range(3, size // 2)] + [0]
 
 
 def by_block(refs):
     ordered = [None] * len(refs)
-    for ref, d in zip(refs, far_first(len(refs))):
+    for ref, d in zip(refs, start_order(len(refs))):
         ordered[d] = ref
     return ordered
 
@@ -63,7 +63,7 @@
     if len(blocks) == 1:
         return [lax.all_to_all(blocks[0], "expert", split_axis=0, concat_axis=0, tiled=True)]
     got = list(blocks)
-    for d in far_first(size)[:-1]:
+    for d in start_order(size)[:-1]:
         got[d] = lax.ppermute(blocks[d], "expert", [(i, i ^ d) for i in range(size)])
     return got
 
@@ -478,7 +478,7 @@
     got = exchange(send)
     for part in range(parts):
         if part + 1 < parts:
-            got = [got[d] for d in far_first(len(got))]
+            got = [got[d] for d in start_order(len(got))]
             sends, saved_pre, got = lax.optimization_barrier((sends, saved_pre, got))
             got = by_block(got)
             blocks = len(blocks_of(there[part + 1], width))
@@ -501,7 +501,7 @@
                 pltpu.SemaphoreType.DMA,
                 pltpu.SemaphoreType.DMA((min(2, held), 2, 2)),
             ],
-        )(saved_pre, up_weight, down_weight, *[got[d] for d in far_first(len(got))])
+        )(saved_pre, up_weight, down_weight, *[got[d] for d in start_order(len(got))])
         backs.append(exchange(list(done)))
         got = coming if part + 1 < parts else None
     handed = (
@@ -526,7 +526,7 @@
         )(
             *early,
             *mixing[-1],
-            *[backs[-1][d] for d in far_first(len(backs[-1])) if d > 0 or not back[-1]],
+            *[backs[-1][d] for d in start_order(len(backs[-1])) if d > 0 or not back[-1]],
         )
     )
 

time: 116 us -> 115 us (level)
  waiting for transfers between devices: 30.1 us -> 24.7 us
  starting transfers between devices: 29.4 us -> 32.7 us
    ppermute x14, waiting for transfers between devices: 22.8 us -> 17.4 us  [exchange(): lax.ppermute(blocks[d], 'expert', [(i, i ^ d) for i in range(size)])]
    ppermute x14, starting transfers between devices: 13.2 us -> 16.3 us  [exchange(): lax.ppermute(blocks[d], 'expert', [(i, i ^ d) for i in range(size)])]
  transfers between devices with their start and end apart: 18 -> 18, of which waited for: 7 -> 8; matrix products, arithmetic and copies ran while one was open for 1% -> 1% of each run, Pallas kernels for 39% -> 40%
where the time goes in v15:
time: 115 us; the launch traced here: 113 us
  Pallas kernels  48.1 us (42%)
  starting transfers between devices  32.7 us (28%)
  waiting for transfers between devices  24.7 us (21%)
  local copies, waits for them, and re-layouts  7.05 us (6%)
    pallas_call x2, Pallas kernels, on_device(): call(functools.partial(expert_kernel, sizes, part, held), tuple(result),...  41.1 us
    ppermute x14, waiting for transfers between devices, exchange(): lax.ppermute(blocks[d], 'expert', [(i, i ^ d) for i in range(size)])  17.4 us
    ppermute x14, starting transfers between devices, exchange(): lax.ppermute(blocks[d], 'expert', [(i, i ^ d) for i in range(size)])  16.3 us
    all_to_all x2, starting transfers between devices, exchange(): lax.all_to_all(blocks[0], 'expert', split_axis=0, concat_axis=0, tiled=True)  10.3 us
    ppermute x2, waiting for transfers between devices, from_behind(): return lax.ppermute(block, axis, route)  6.87 us
    ppermute x2, starting transfers between devices, from_behind(): return lax.ppermute(block, axis, route)  6.15 us
    unnamed x42, local copies, waits for them, and re-layouts  5.79 us
    pallas_call x1, Pallas kernels, on_device(): call(functools.partial(mixing_kernel, sizes), (row_shape, row_shape, shap...  3.23 us
  transfers between devices with their start and end apart: 18, of which 8 were waited for; matrix products, arithmetic and copies ran while one was open for 1% of the time, Pallas kernels for 40%

profile of v15, /device:TPU:0, one launch (start us, length us, event | category | flops | bytes accessed | tf_op | source)
XLA Modules:
  0.0 113.5 jit_solution(12997792026461396363)
XLA Ops:
  0.6 4.9 %collective-permute-start = (bf16[64,2048]{1,0:T(8,128)(2,1)}, bf16[64,2048]{1,0:T(8,128)(2,1)S(1)}, u32[]{:S(2)}, u32[]{:S(2)}) collective-permute-start(bf16[64,2048]{1,0:T(8,128)(2,1)} %bitcast.34), channel_id=1, source_target_pairs={{0,8},{8,16},{16,24},{1,9},{9,17},{17,25},{2,10},{10,18},{18,26},{... | collective-permute-start | bytes 786440 | tf_op jit(solution)/shard_map/ppermute | solution.py:45
  5.5 1.3 %collective-permute-start.1 = (bf16[64,2048]{1,0:T(8,128)(2,1)}, bf16[64,2048]{1,0:T(8,128)(2,1)S(1)}, u32[]{:S(2)}, u32[]{:S(2)}) collective-permute-start(bf16[64,2048]{1,0:T(8,128)(2,1)} %bitcast.35), channel_id=1, source_target_pairs={{8,0},{16,8},{24,16},{9,1},{17,9},{25,17},{10,2},{18,10},{26,18},{... | collective-permute-start | bytes 786440 | tf_op jit(solution)/shard_map/ppermute | solution.py:45
  6.8 0.0 copy-start.2
  6.8 0.9 copy-done.2
  7.8 0.9 copy-done.3
  8.7 0.9 copy-done.7
  9.6 0.7 copy-done.13
  10.3 0.7 copy-done.17
  11.0 0.7 copy-done.20
  11.6 0.3 shard_map.141
  11.9 0.0 collective-permute-done.arrived_f
  11.9 0.0 copy-start.4
  11.9 6.9 %collective-permute-done.1.arrived_b = bf16[64,2048]{1,0:T(8,128)(2,1)S(1)} collective-permute-done((bf16[64,2048]{1,0:T(8,128)(2,1)}, bf16[64,2048]{1,0:T(8,128)(2,1)S(1)}, u32[]{:S(2)}, u32[]{:S(2)}) %collective-permute-start.1) | collective-permute-done | bytes 262176 | tf_op jit(solution)/shard_map/ppermute | solution.py:45
  18.8 0.5 shard_map.142
  19.3 0.1 collective-permute-start.2
  19.4 1.6 %collective-permute-start.3 = (bf16[24,2048]{1,0:T(8,128)(2,1)S(1)}, bf16[24,2048]{1,0:T(8,128)(2,1)S(1)}, u32[]{:S(2)}, u32[]{:S(2)}) collective-permute-start(bf16[24,2048]{1,0:T(8,128)(2,1)S(1)} %get-tuple-element.63), channel_id=1, source_target_pairs={{0,2},{1,3},{2,0},{3,1},{4,6},{5,7},{6,4},{7,5},{8,10},{9,11},{10,... | collective-permute-start | bytes 294920 | tf_op jit(solution)/shard_map/ppermute | solution.py:67
  21.0 2.6 %collective-permute-start.4 = (bf16[24,2048]{1,0:T(8,128)(2,1)S(1)}, bf16[24,2048]{1,0:T(8,128)(2,1)S(1)}, u32[]{:S(2)}, u32[]{:S(2)}) collective-permute-start(bf16[24,2048]{1,0:T(8,128)(2,1)S(1)} %get-tuple-element.64), channel_id=1, source_target_pairs={{0,4},{1,5},{2,6},{3,7},{4,0},{5,1},{6,2},{7,3},{8,12},{9,13},{10,... | collective-permute-start | bytes 294920 | tf_op jit(solution)/shard_map/ppermute | solution.py:67
  23.6 0.0 collective-permute-start.5
  23.6 2.3 %collective-permute-start.6 = (bf16[24,2048]{1,0:T(8,128)(2,1)S(1)}, bf16[24,2048]{1,0:T(8,128)(2,1)S(1)}, u32[]{:S(2)}, u32[]{:S(2)}) collective-permute-start(bf16[24,2048]{1,0:T(8,128)(2,1)S(1)} %get-tuple-element.66), channel_id=1, source_target_pairs={{0,6},{1,7},{2,4},{3,5},{4,2},{5,3},{6,0},{7,1},{8,14},{9,15},{10,... | collective-permute-start | bytes 294920 | tf_op jit(solution)/shard_map/ppermute | solution.py:67
  25.9 0.0 collective-permute-done.2.refs_0_
  25.9 1.3 %collective-permute-start.7 = (bf16[24,2048]{1,0:T(8,128)(2,1)S(1)}, bf16[24,2048]{1,0:T(8,128)(2,1)S(1)}, u32[]{:S(2)}, u32[]{:S(2)}) collective-permute-start(bf16[24,2048]{1,0:T(8,128)(2,1)S(1)} %get-tuple-element.67), channel_id=1, source_target_pairs={{0,7},{1,6},{2,5},{3,4},{4,3},{5,2},{6,1},{7,0},{8,15},{9,14},{10,... | collective-permute-start | bytes 294920 | tf_op jit(solution)/shard_map/ppermute | solution.py:67
  27.2 0.0 collective-permute-done.3.refs_1_
  27.2 0.0 collective-permute-start.8
  27.2 1.2 %copy.16 = bf16[8,24,1024]{2,1,0:T(8,128)(2,1)S(1)} copy(bf16[8,24,1024]{2,0,1:T(8,128)(2,1)} %bitcast.33) | data formatting | bytes 786432 | tf_op jit(solution)/shard_map/reshape | solution.py:475
  28.5 0.0 copy-done.4
  28.5 0.0 copy-done.5
  28.5 3.2 %shard_map.140 = (bf16[64,2048]{1,0:T(8,128)(2,1)}, bf16[64,2048]{1,0:T(8,128)(2,1)}, f32[2,8,64]{2,1,0:T(8,128)}, bf16[64,192]{1,0:T(8,128)(2,1)}, bf16[64,192]...) custom-call(bf16[64,2048]{1,0:T(8,128)(2,1)} %copy-done.4, ...), custom_call_target="tpu_custom_call" | custom-call | flops 100663296 | bytes 2883584 | tf_op jit(solution)/shard_map/pallas_call | solution.py:457
  31.8 3.3 %collective-permute-done.4.refs_2_ = bf16[24,2048]{1,0:T(8,128)(2,1)S(1)} collective-permute-done((bf16[24,2048]{1,0:T(8,128)(2,1)S(1)}, bf16[24,2048]{1,0:T(8,128)(2,1)S(1)}, u32[]{:S(2)}, u32[]{:S(2)}) %collective-permute-start.4) | collective-permute-done | bytes 98336 | tf_op jit(solution)/shard_map/ppermute | solution.py:67
  35.0 2.4 %collective-permute-done.5.refs_3_ = bf16[24,2048]{1,0:T(8,128)(2,1)S(1)} collective-permute-done((bf16[24,2048]{1,0:T(8,128)(2,1)S(1)}, bf16[24,2048]{1,0:T(8,128)(2,1)S(1)}, u32[]{:S(2)}, u32[]{:S(2)}) %collective-permute-start.5) | collective-permute-done | bytes 98336 | tf_op jit(solution)/shard_map/ppermute | solution.py:67
  37.4 0.0 collective-permute-done.6.refs_4_
  37.4 0.0 collective-permute-done.7.refs_5_
  37.4 1.0 collective-permute-done.8.refs_6_
  38.4 5.5 %all-to-all-start.1 = ((bf16[8,24,2048]{2,1,0:T(8,128)(2,1)}), bf16[8,24,2048]{2,1,0:T(8,128)(2,1)S(1)}, u32[]{:S(2)}, u32[]{:S(2)}) async-start(bf16[8,24,2048]{2,1,0:T(8,128)(2,1)} %bitcast.32), calls=%async_computation.1 | async-start | bytes 1572864 | tf_op jit(solution)/shard_map/all_to_all | solution.py:64
  43.9 20.6 %shard_map.143 = bf16[192,2176]{1,0:T(8,128)(2,1)} custom-call(bf16[8,32,1024]{2,1,0:T(8,128)(2,1)S(1)} %pad.4.saved_all, bf16[8,2048,1024]{2,1,0:T(8,128)(2,1)} %up.3, bf16[8,1024,2048]{2,1,0:T(8,128)(2,1)} %down.3, bf16[24,2048]{1,0:T(8,128)(2,1)S(1)} %collective-permute-done.2.refs_0_, bf16[24,2048]{1,0:T(8,128)(2,1)S(1)} %collective-permute-done.3.refs_1_, ...), custom_call_target="tpu_custom_call" | custom-call | flops 2147483648 | bytes 33554432 | tf_op jit(solution)/shard_map/pallas_call | solution.py:488
  64.5 0.4 all-to-all-done.1
  64.9 4.7 %all-to-all-start = ((bf16[8,24,2176]{2,1,0:T(8,128)(2,1)}), bf16[8,24,2176]{2,1,0:T(8,128)(2,1)S(1)}, u32[]{:S(2)}, u32[]{:S(2)}) async-start(bf16[8,24,2176]{2,1,0:T(8,128)(2,1)} %bitcast.14), calls=%async_computation | async-start | bytes 1671168 | tf_op jit(solution)/shard_map/all_to_all | solution.py:64
  69.6 0.0 copy-start.1
  69.6 0.0 copy-start.6
  69.7 0.0 copy-start.8
  69.7 0.0 copy-start.9
  69.7 0.0 copy-start.10
  69.7 0.0 copy-start.11
  69.7 0.0 copy-start.14
  69.7 0.0 copy-start.18
  69.7 0.0 copy-start.19
  69.7 20.5 %shard_map.144 = (bf16[24,2176]{1,0:T(8,128)(2,1)S(1)}, bf16[24,2176]{1,0:T(8,128)(2,1)S(1)}, bf16[24,2176]{1,0:T(8,128)(2,1)S(1)}, bf16[24,2176]{1,0:T(8,128)(2...) custom-call(bf16[8,32,1024]{2,1,0:T(8,128)(2,1)S(1)} %pad.4.saved_al, ...), custom_call_target="tpu_custom_call" | custom-call | flops 2147483648 | bytes 33554432 | tf_op jit(solution)/shard_map/pallas_call | solution.py:488
  90.2 0.6 collective-permute-start.9
  90.8 1.7 %collective-permute-start.10 = (bf16[24,2176]{1,0:T(8,128)(2,1)S(1)}, bf16[24,2176]{1,0:T(8,128)(2,1)S(1)}, u32[]{:S(2)}, u32[]{:S(2)}) collective-permute-start(bf16[24,2176]{1,0:T(8,128)(2,1)S(1)} %get-tuple-element.94), channel_id=1, source_target_pairs={{0,2},{1,3},{2,0},{3,1},{4,6},{5,7},{6,4},{7,5},{8,10},{9,11},{10,... | collective-permute-start | bytes 313352 | tf_op jit(solution)/shard_map/ppermute | solution.py:67
  92.5 2.4 %collective-permute-start.11 = (bf16[24,2176]{1,0:T(8,128)(2,1)}, bf16[24,2176]{1,0:T(8,128)(2,1)S(1)}, u32[]{:S(2)}, u32[]{:S(2)}) collective-permute-start(bf16[24,2176]{1,0:T(8,128)(2,1)} %get-tuple-element.95), channel_id=1, source_target_pairs={{0,4},{1,5},{2,6},{3,7},{4,0},{5,1},{6,2},{7,3},{8,12},{9,13},{10,... | collective-permute-start | bytes 313352 | tf_op jit(solution)/shard_map/ppermute | solution.py:67
  94.8 0.0 collective-permute-start.12
  94.8 2.3 %collective-permute-start.13 = (bf16[24,2176]{1,0:T(8,128)(2,1)}, bf16[24,2176]{1,0:T(8,128)(2,1)S(1)}, u32[]{:S(2)}, u32[]{:S(2)}) collective-permute-start(bf16[24,2176]{1,0:T(8,128)(2,1)} %get-tuple-element.97), channel_id=1, source_target_pairs={{0,6},{1,7},{2,4},{3,5},{4,2},{5,3},{6,0},{7,1},{8,14},{9,15},{10,... | collective-permute-start | bytes 313352 | tf_op jit(solution)/shard_map/ppermute | solution.py:67
  97.2 0.0 collective-permute-done.9.refs_0_
  97.2 1.5 %collective-permute-start.14 = (bf16[24,2176]{1,0:T(8,128)(2,1)}, bf16[24,2176]{1,0:T(8,128)(2,1)S(1)}, u32[]{:S(2)}, u32[]{:S(2)}) collective-permute-start(bf16[24,2176]{1,0:T(8,128)(2,1)} %get-tuple-element.98), channel_id=1, source_target_pairs={{0,7},{1,6},{2,5},{3,4},{4,3},{5,2},{6,1},{7,0},{8,15},{9,14},{10,... | collective-permute-start | bytes 313352 | tf_op jit(solution)/shard_map/ppermute | solution.py:67
  98.7 0.0 collective-permute-done.10.refs_1_
  98.7 0.0 collective-permute-start.15
  98.7 0.0 all-to-all-done
  98.8 0.9 copy-done.12
  99.7 0.6 shard_map.145
  100.3 7.6 %collective-permute-done.11.refs_2_ = bf16[24,2176]{1,0:T(8,128)(2,1)S(1)} collective-permute-done((bf16[24,2176]{1,0:T(8,128)(2,1)}, bf16[24,2176]{1,0:T(8,128)(2,1)S(1)}, u32[]{:S(2)}, u32[]{:S(2)}) %collective-permute-start.11) | collective-permute-done | bytes 104480 | tf_op jit(solution)/shard_map/ppermute | solution.py:67
  107.9 1.6 %collective-permute-done.12.refs_3_ = bf16[24,2176]{1,0:T(8,128)(2,1)S(1)} collective-permute-done((bf16[24,2176]{1,0:T(8,128)(2,1)}, bf16[24,2176]{1,0:T(8,128)(2,1)S(1)}, u32[]{:S(2)}, u32[]{:S(2)}) %collective-permute-start.12) | collective-permute-done | bytes 104480 | tf_op jit(solution)/shard_map/ppermute | solution.py:67
  109.4 0.0 collective-permute-done.13.refs_4_
  109.4 0.0 collective-permute-done.14.refs_5_
  109.5 1.6 %collective-permute-done.15.refs_6_ = bf16[24,2176]{1,0:T(8,128)(2,1)} collective-permute-done((bf16[24,2176]{1,0:T(8,128)(2,1)}, bf16[24,2176]{1,0:T(8,128)(2,1)}, u32[]{:S(2)}, u32[]{:S(2)}) %collective-permute-start.15) | collective-permute-done | bytes 104480 | tf_op jit(solution)/shard_map/ppermute | solution.py:67
  111.1 2.4 %shard_map.146 = (bf16[1,64,2048]{2,1,0:T(8,128)(2,1)}, bf16[1,64,2048]{2,1,0:T(8,128)(2,1)}) custom-call(f32[64,2048]{1,0:T(8,128)S(1)} %get-tuple-element.84.early_f, f32[64,2048]{1,0:T(8,128)S(1)} %get-tuple-element.85.early_b, f32[2,8,64]{2,1,0:T(8,128)S(1)} %get-tuple-element.86.early_inner, bf16[64,2048]{1,0:T(8,128)(2,1)S(1)} %get-tuple-element.87.saved, ...), custom_call_target="tpu_custom_call" | custom-call | flops 100663296 | bytes 2883584 | tf_op jit(solution)/shard_map/pallas_call | solution.py:522
  (23 shorter events, 0.1 us)
Async XLA Ops:
  0.6 11.3 %collective-permute-start = (bf16[64,2048]{1,0:T(8,128)(2,1)}, bf16[64,2048]{1,0:T(8,128)(2,1)S(1)}, u32[]{:S(2)}, u32[]{:S(2)}) collective-permute-start(bf16[64,2048]{1,0:T(8,128)(2,1)} %bitcast.34), channel_id=1, source_target_pairs={{0,8},{8,16},{16,24},{1,9},{9,17},{17,25},{2,10},{10,18},{18,26},{... | collective-permute-start | bytes 786440 | tf_op jit(solution)/shard_map/ppermute | solution.py:45
  5.5 13.3 %collective-permute-start.1 = (bf16[64,2048]{1,0:T(8,128)(2,1)}, bf16[64,2048]{1,0:T(8,128)(2,1)S(1)}, u32[]{:S(2)}, u32[]{:S(2)}) collective-permute-start(bf16[64,2048]{1,0:T(8,128)(2,1)} %bitcast.35), channel_id=1, source_target_pairs={{8,0},{16,8},{24,16},{9,1},{17,9},{25,17},{10,2},{18,10},{26,18},{... | collective-permute-start | bytes 786440 | tf_op jit(solution)/shard_map/ppermute | solution.py:45
  6.8 1.0 copy-start.2
  7.7 0.9 copy-start.3
  8.7 0.9 copy-start.7
  9.6 0.7 copy-start.13
  10.3 0.7 copy-start.17
  11.0 0.7 copy-start.20
  11.9 16.6 %copy-start.4 = (bf16[64,2048]{1,0:T(8,128)(2,1)}, bf16[64,2048]{1,0:T(8,128)(2,1)S(1)}, u32[]{:S(2)}) copy-start(bf16[64,2048]{1,0:T(8,128)(2,1)S(1)} %collective-permute-done.arrived_f) | copy-start | bytes 786436
  18.8 9.7 %copy-start.5 = (bf16[64,2048]{1,0:T(8,128)(2,1)}, bf16[64,2048]{1,0:T(8,128)(2,1)S(1)}, u32[]{:S(2)}) copy-start(bf16[64,2048]{1,0:T(8,128)(2,1)S(1)} %collective-permute-done.1.arrived_b) | copy-start | bytes 786436
  19.3 6.6 %collective-permute-start.2 = (bf16[24,2048]{1,0:T(8,128)(2,1)S(1)}, bf16[24,2048]{1,0:T(8,128)(2,1)S(1)}, u32[]{:S(2)}, u32[]{:S(2)}) collective-permute-start(bf16[24,2048]{1,0:T(8,128)(2,1)S(1)} %get-tuple-element.62), channel_id=1, source_target_pairs={{0,1},{1,0},{2,3},{3,2},{4,5},{5,4},{6,7},{7,6},{8,9},{9,8},{10,11... | collective-permute-start | bytes 294920 | tf_op jit(solution)/shard_map/ppermute | solution.py:67
  19.4 7.8 %collective-permute-start.3 = (bf16[24,2048]{1,0:T(8,128)(2,1)S(1)}, bf16[24,2048]{1,0:T(8,128)(2,1)S(1)}, u32[]{:S(2)}, u32[]{:S(2)}) collective-permute-start(bf16[24,2048]{1,0:T(8,128)(2,1)S(1)} %get-tuple-element.63), channel_id=1, source_target_pairs={{0,2},{1,3},{2,0},{3,1},{4,6},{5,7},{6,4},{7,5},{8,10},{9,11},{10,... | collective-permute-start | bytes 294920 | tf_op jit(solution)/shard_map/ppermute | solution.py:67
  21.0 14.0 %collective-permute-start.4 = (bf16[24,2048]{1,0:T(8,128)(2,1)S(1)}, bf16[24,2048]{1,0:T(8,128)(2,1)S(1)}, u32[]{:S(2)}, u32[]{:S(2)}) collective-permute-start(bf16[24,2048]{1,0:T(8,128)(2,1)S(1)} %get-tuple-element.64), channel_id=1, source_target_pairs={{0,4},{1,5},{2,6},{3,7},{4,0},{5,1},{6,2},{7,3},{8,12},{9,13},{10,... | collective-permute-start | bytes 294920 | tf_op jit(solution)/shard_map/ppermute | solution.py:67
  23.6 13.8 %collective-permute-start.5 = (bf16[24,2048]{1,0:T(8,128)(2,1)S(1)}, bf16[24,2048]{1,0:T(8,128)(2,1)S(1)}, u32[]{:S(2)}, u32[]{:S(2)}) collective-permute-start(bf16[24,2048]{1,0:T(8,128)(2,1)S(1)} %get-tuple-element.65), channel_id=1, source_target_pairs={{0,5},{1,4},{2,7},{3,6},{4,1},{5,0},{6,3},{7,2},{8,13},{9,12},{10,... | collective-permute-start | bytes 294920 | tf_op jit(solution)/shard_map/ppermute | solution.py:67
  23.6 13.8 %collective-permute-start.6 = (bf16[24,2048]{1,0:T(8,128)(2,1)S(1)}, bf16[24,2048]{1,0:T(8,128)(2,1)S(1)}, u32[]{:S(2)}, u32[]{:S(2)}) collective-permute-start(bf16[24,2048]{1,0:T(8,128)(2,1)S(1)} %get-tuple-element.66), channel_id=1, source_target_pairs={{0,6},{1,7},{2,4},{3,5},{4,2},{5,3},{6,0},{7,1},{8,14},{9,15},{10,... | collective-permute-start | bytes 294920 | tf_op jit(solution)/shard_map/ppermute | solution.py:67
  25.9 11.5 %collective-permute-start.7 = (bf16[24,2048]{1,0:T(8,128)(2,1)S(1)}, bf16[24,2048]{1,0:T(8,128)(2,1)S(1)}, u32[]{:S(2)}, u32[]{:S(2)}) collective-permute-start(bf16[24,2048]{1,0:T(8,128)(2,1)S(1)} %get-tuple-element.67), channel_id=1, source_target_pairs={{0,7},{1,6},{2,5},{3,4},{4,3},{5,2},{6,1},{7,0},{8,15},{9,14},{10,... | collective-permute-start | bytes 294920 | tf_op jit(solution)/shard_map/ppermute | solution.py:67
  27.2 11.2 %collective-permute-start.8 = (bf16[24,2048]{1,0:T(8,128)(2,1)S(1)}, bf16[24,2048]{1,0:T(8,128)(2,1)S(1)}, u32[]{:S(2)}, u32[]{:S(2)}) collective-permute-start(bf16[24,2048]{1,0:T(8,128)(2,1)S(1)} %get-tuple-element.68), channel_id=1, source_target_pairs={{0,3},{1,2},{2,1},{3,0},{4,7},{5,6},{6,5},{7,4},{8,11},{9,10},{10,... | collective-permute-start | bytes 294920 | tf_op jit(solution)/shard_map/ppermute | solution.py:67
  38.4 26.5 %all-to-all-start.1 = ((bf16[8,24,2048]{2,1,0:T(8,128)(2,1)}), bf16[8,24,2048]{2,1,0:T(8,128)(2,1)S(1)}, u32[]{:S(2)}, u32[]{:S(2)}) async-start(bf16[8,24,2048]{2,1,0:T(8,128)(2,1)} %bitcast.32), calls=%async_computation.1 | async-start | bytes 1572864 | tf_op jit(solution)/shard_map/all_to_all | solution.py:64
  64.9 33.8 %all-to-all-start = ((bf16[8,24,2176]{2,1,0:T(8,128)(2,1)}), bf16[8,24,2176]{2,1,0:T(8,128)(2,1)S(1)}, u32[]{:S(2)}, u32[]{:S(2)}) async-start(bf16[8,24,2176]{2,1,0:T(8,128)(2,1)} %bitcast.14), calls=%async_computation | async-start | bytes 1671168 | tf_op jit(solution)/shard_map/all_to_all | solution.py:64
  69.6 29.0 %copy-start = (bf16[1,64,2048]{2,1,0:T(8,128)(2,1)S(1)}, bf16[1,64,2048]{2,1,0:T(8,128)(2,1)}, u32[]{:S(2)}) copy-start(bf16[1,64,2048]{2,1,0:T(8,128)(2,1)} %param.18) | copy-start | bytes 786436
  69.6 29.1 %copy-start.1 = (bf16[1,2048,64]{1,2,0:T(8,128)(2,1)S(1)}, bf16[1,2048,64]{1,2,0:T(8,128)(2,1)}, u32[]{:S(2)}) copy-start(bf16[1,2048,64]{1,2,0:T(8,128)(2,1)} %param.22) | copy-start | bytes 786436
  69.6 29.1 %copy-start.6 = (bf16[2,192,64]{2,1,0:T(8,128)(2,1)S(1)}, bf16[2,192,64]{2,1,0:T(8,128)(2,1)}, u32[]{:S(2)}) copy-start(bf16[2,192,64]{2,1,0:T(8,128)(2,1)} %get-tuple-element.81.refs_12_.tables) | copy-start | bytes 147460
  69.7 29.1 %copy-start.8 = (bf16[64,2048]{1,0:T(8,128)(2,1)S(1)}, bf16[64,2048]{1,0:T(8,128)(2,1)}, u32[]{:S(2)}) copy-start(bf16[64,2048]{1,0:T(8,128)(2,1)} %get-tuple-element.51.tokens) | copy-start | bytes 786436
  69.7 29.1 %copy-start.9 = (bf16[64,2048]{1,0:T(8,128)(2,1)S(1)}, bf16[64,2048]{1,0:T(8,128)(2,1)}, u32[]{:S(2)}) copy-start(bf16[64,2048]{1,0:T(8,128)(2,1)} %get-tuple-element.52.refs_1_) | copy-start | bytes 786436
  69.7 29.1 %copy-start.10 = (bf16[64,192]{1,0:T(8,128)(2,1)S(1)}, bf16[64,192]{1,0:T(8,128)(2,1)}, u32[]{:S(2)}) copy-start(bf16[64,192]{1,0:T(8,128)(2,1)} %get-tuple-element.79.refs_10_.mixing_f) | copy-start | bytes 73732
  69.7 29.1 %copy-start.11 = (bf16[64,192]{1,0:T(8,128)(2,1)S(1)}, bf16[64,192]{1,0:T(8,128)(2,1)}, u32[]{:S(2)}) copy-start(bf16[64,192]{1,0:T(8,128)(2,1)} %get-tuple-element.80.refs_11_.mixing_b) | copy-start | bytes 73732
  69.7 29.1 %copy-start.14 = (bf16[1,2048]{1,0:T(2,128)(2,1)S(1)}, bf16[1,2048]{1,0:T(2,128)(2,1)}, u32[]{:S(2)}) copy-start(bf16[1,2048]{1,0:T(2,128)(2,1)} %refs_2_.1) | copy-start | bytes 12292
  69.7 29.0 %copy-start.15 = (bf16[64,192]{1,0:T(8,128)(2,1)S(1)}, bf16[64,192]{1,0:T(8,128)(2,1)}, u32[]{:S(2)}) copy-start(bf16[64,192]{1,0:T(8,128)(2,1)} %get-tuple-element.54.refs_6_) | copy-start | bytes 73732
  69.7 29.0 %copy-start.16 = (bf16[64,192]{1,0:T(8,128)(2,1)S(1)}, bf16[64,192]{1,0:T(8,128)(2,1)}, u32[]{:S(2)}) copy-start(bf16[64,192]{1,0:T(8,128)(2,1)} %get-tuple-element.55.refs_7_) | copy-start | bytes 73732
  69.7 29.0 %copy-start.18 = (s32[1,64,2]{1,2,0:T(2,128)S(1)}, s32[1,64,2]{1,2,0:T(2,128)}, u32[]{:S(2)}) copy-start(s32[1,64,2]{1,2,0:T(2,128)} %param.19) | copy-start | bytes 1540
  69.7 29.0 %copy-start.19 = (f32[2,8,64]{2,1,0:T(8,128)S(1)}, f32[2,8,64]{2,1,0:T(8,128)}, u32[]{:S(2)}) copy-start(f32[2,8,64]{2,1,0:T(8,128)} %get-tuple-element.53.refs_5_) | copy-start | bytes 12292
  90.2 6.9 %collective-permute-start.9 = (bf16[24,2176]{1,0:T(8,128)(2,1)S(1)}, bf16[24,2176]{1,0:T(8,128)(2,1)S(1)}, u32[]{:S(2)}, u32[]{:S(2)}) collective-permute-start(bf16[24,2176]{1,0:T(8,128)(2,1)S(1)} %get-tuple-element.93), channel_id=1, source_target_pairs={{0,1},{1,0},{2,3},{3,2},{4,5},{5,4},{6,7},{7,6},{8,9},{9,8},{10,11... | collective-permute-start | bytes 313352 | tf_op jit(solution)/shard_map/ppermute | solution.py:67
  90.8 7.9 %collective-permute-start.10 = (bf16[24,2176]{1,0:T(8,128)(2,1)S(1)}, bf16[24,2176]{1,0:T(8,128)(2,1)S(1)}, u32[]{:S(2)}, u32[]{:S(2)}) collective-permute-start(bf16[24,2176]{1,0:T(8,128)(2,1)S(1)} %get-tuple-element.94), channel_id=1, source_target_pairs={{0,2},{1,3},{2,0},{3,1},{4,6},{5,7},{6,4},{7,5},{8,10},{9,11},{10,... | collective-permute-start | bytes 313352 | tf_op jit(solution)/shard_map/ppermute | solution.py:67
  92.5 15.4 %collective-permute-start.11 = (bf16[24,2176]{1,0:T(8,128)(2,1)}, bf16[24,2176]{1,0:T(8,128)(2,1)S(1)}, u32[]{:S(2)}, u32[]{:S(2)}) collective-permute-start(bf16[24,2176]{1,0:T(8,128)(2,1)} %get-tuple-element.95), channel_id=1, source_target_pairs={{0,4},{1,5},{2,6},{3,7},{4,0},{5,1},{6,2},{7,3},{8,12},{9,13},{10,... | collective-permute-start | bytes 313352 | tf_op jit(solution)/shard_map/ppermute | solution.py:67
  94.8 14.6 %collective-permute-start.12 = (bf16[24,2176]{1,0:T(8,128)(2,1)}, bf16[24,2176]{1,0:T(8,128)(2,1)S(1)}, u32[]{:S(2)}, u32[]{:S(2)}) collective-permute-start(bf16[24,2176]{1,0:T(8,128)(2,1)} %get-tuple-element.96), channel_id=1, source_target_pairs={{0,5},{1,4},{2,7},{3,6},{4,1},{5,0},{6,3},{7,2},{8,13},{9,12},{10,... | collective-permute-start | bytes 313352 | tf_op jit(solution)/shard_map/ppermute | solution.py:67
  94.8 14.6 %collective-permute-start.13 = (bf16[24,2176]{1,0:T(8,128)(2,1)}, bf16[24,2176]{1,0:T(8,128)(2,1)S(1)}, u32[]{:S(2)}, u32[]{:S(2)}) collective-permute-start(bf16[24,2176]{1,0:T(8,128)(2,1)} %get-tuple-element.97), channel_id=1, source_target_pairs={{0,6},{1,7},{2,4},{3,5},{4,2},{5,3},{6,0},{7,1},{8,14},{9,15},{10,... | collective-permute-start | bytes 313352 | tf_op jit(solution)/shard_map/ppermute | solution.py:67
  97.2 12.3 %collective-permute-start.14 = (bf16[24,2176]{1,0:T(8,128)(2,1)}, bf16[24,2176]{1,0:T(8,128)(2,1)S(1)}, u32[]{:S(2)}, u32[]{:S(2)}) collective-permute-start(bf16[24,2176]{1,0:T(8,128)(2,1)} %get-tuple-element.98), channel_id=1, source_target_pairs={{0,7},{1,6},{2,5},{3,4},{4,3},{5,2},{6,1},{7,0},{8,15},{9,14},{10,... | collective-permute-start | bytes 313352 | tf_op jit(solution)/shard_map/ppermute | solution.py:67
  98.7 12.4 %collective-permute-start.15 = (bf16[24,2176]{1,0:T(8,128)(2,1)}, bf16[24,2176]{1,0:T(8,128)(2,1)}, u32[]{:S(2)}, u32[]{:S(2)}) collective-permute-start(bf16[24,2176]{1,0:T(8,128)(2,1)} %get-tuple-element.99), channel_id=1, source_target_pairs={{0,3},{1,2},{2,1},{3,0},{4,7},{5,6},{6,5},{7,4},{8,11},{9,10},{10,... | collective-permute-start | bytes 313352 | tf_op jit(solution)/shard_map/ppermute | solution.py:67
  98.8 0.9 copy-start.12

commit v16 on v15

--- a/solution.py
+++ b/solution.py
@@ -336,7 +336,7 @@
 
 
 def late_kernel(
-    sizes, early_f, early_b, early_inner, saved, upstream, gain, router, routes, shares,
+    sizes, early_f, early_b, early_inner, upstream, gain, routes, shares, saved, router,
     mixing_f, mixing_b, tables, *refs,
 ):
     *backs, output, gradient = refs
@@ -505,7 +505,7 @@
         backs.append(exchange(list(done)))
         got = coming if part + 1 < parts else None
     handed = (
-        saved_inputs[0], upstream, norm_gain, router_t, routes_b, shares_b,
+        upstream, norm_gain, routes_b, shares_b,
     )
     own = (*mixing[-1], backs[-1][0]) if back[-1] else ()
     early = call(
@@ -525,6 +525,8 @@
             (4 * moved * count * width, 2 * (8 * count + moved) * width),
         )(
             *early,
+            saved_inputs[0],
+            router_t,
             *mixing[-1],
             *[backs[-1][d] for d in start_order(len(backs[-1])) if d > 0 or not back[-1]],
         )

time: 115 us -> 115 us (level)
  no operation moved by 1% of the time
where the time goes in v16:
time: 115 us; the launch traced here: 114 us
  Pallas kernels  48 us (42%)
  starting transfers between devices  32.7 us (28%)
  waiting for transfers between devices  24.8 us (22%)
  local copies, waits for them, and re-layouts  7.05 us (6%)
    pallas_call x2, Pallas kernels, on_device(): call(functools.partial(expert_kernel, sizes, part, held), tuple(result),...  41.1 us
    ppermute x14, waiting for transfers between devices, exchange(): lax.ppermute(blocks[d], 'expert', [(i, i ^ d) for i in range(size)])  17.5 us
    ppermute x14, starting transfers between devices, exchange(): lax.ppermute(blocks[d], 'expert', [(i, i ^ d) for i in range(size)])  16.3 us
    all_to_all x2, starting transfers between devices, exchange(): lax.all_to_all(blocks[0], 'expert', split_axis=0, concat_axis=0, tiled=True)  10.3 us
    ppermute x2, waiting for transfers between devices, from_behind(): return lax.ppermute(block, axis, route)  6.87 us
    ppermute x2, starting transfers between devices, from_behind(): return lax.ppermute(block, axis, route)  6.15 us
    unnamed x42, local copies, waits for them, and re-layouts  5.79 us
    pallas_call x1, Pallas kernels, on_device(): call(functools.partial(mixing_kernel, sizes), (row_shape, row_shape, shap...  3.23 us
  transfers between devices with their start and end apart: 18, of which 8 were waited for; matrix products, arithmetic and copies ran while one was open for 1% of the time, Pallas kernels for 40%

profile of v16, /device:TPU:0, one launch (start us, length us, event | category | flops | bytes accessed | tf_op | source)
XLA Modules:
  0.0 113.5 jit_solution(9237778499481331965)
XLA Ops:
  0.6 4.9 %collective-permute-start = (bf16[64,2048]{1,0:T(8,128)(2,1)}, bf16[64,2048]{1,0:T(8,128)(2,1)S(1)}, u32[]{:S(2)}, u32[]{:S(2)}) collective-permute-start(bf16[64,2048]{1,0:T(8,128)(2,1)} %bitcast.34), channel_id=1, source_target_pairs={{0,8},{8,16},{16,24},{1,9},{9,17},{17,25},{2,10},{10,18},{18,26},{... | collective-permute-start | bytes 786440 | tf_op jit(solution)/shard_map/ppermute | solution.py:45
  5.5 1.3 %collective-permute-start.1 = (bf16[64,2048]{1,0:T(8,128)(2,1)}, bf16[64,2048]{1,0:T(8,128)(2,1)S(1)}, u32[]{:S(2)}, u32[]{:S(2)}) collective-permute-start(bf16[64,2048]{1,0:T(8,128)(2,1)} %bitcast.35), channel_id=1, source_target_pairs={{8,0},{16,8},{24,16},{9,1},{17,9},{25,17},{10,2},{18,10},{26,18},{... | collective-permute-start | bytes 786440 | tf_op jit(solution)/shard_map/ppermute | solution.py:45
  6.8 0.0 copy-start.2
  6.8 0.9 copy-done.2
  7.8 0.9 copy-done.3
  8.7 0.9 copy-done.7
  9.6 0.7 copy-done.13
  10.3 0.7 copy-done.17
  11.0 0.7 copy-done.20
  11.6 0.3 shard_map.141
  11.9 0.0 collective-permute-done.arrived_f
  11.9 0.0 copy-start.4
  11.9 6.9 %collective-permute-done.1.arrived_b = bf16[64,2048]{1,0:T(8,128)(2,1)S(1)} collective-permute-done((bf16[64,2048]{1,0:T(8,128)(2,1)}, bf16[64,2048]{1,0:T(8,128)(2,1)S(1)}, u32[]{:S(2)}, u32[]{:S(2)}) %collective-permute-start.1) | collective-permute-done | bytes 262176 | tf_op jit(solution)/shard_map/ppermute | solution.py:45
  18.8 0.5 shard_map.142
  19.3 0.1 collective-permute-start.2
  19.4 1.6 %collective-permute-start.3 = (bf16[24,2048]{1,0:T(8,128)(2,1)S(1)}, bf16[24,2048]{1,0:T(8,128)(2,1)S(1)}, u32[]{:S(2)}, u32[]{:S(2)}) collective-permute-start(bf16[24,2048]{1,0:T(8,128)(2,1)S(1)} %get-tuple-element.61), channel_id=1, source_target_pairs={{0,2},{1,3},{2,0},{3,1},{4,6},{5,7},{6,4},{7,5},{8,10},{9,11},{10,... | collective-permute-start | bytes 294920 | tf_op jit(solution)/shard_map/ppermute | solution.py:67
  21.0 2.6 %collective-permute-start.4 = (bf16[24,2048]{1,0:T(8,128)(2,1)S(1)}, bf16[24,2048]{1,0:T(8,128)(2,1)S(1)}, u32[]{:S(2)}, u32[]{:S(2)}) collective-permute-start(bf16[24,2048]{1,0:T(8,128)(2,1)S(1)} %get-tuple-element.62), channel_id=1, source_target_pairs={{0,4},{1,5},{2,6},{3,7},{4,0},{5,1},{6,2},{7,3},{8,12},{9,13},{10,... | collective-permute-start | bytes 294920 | tf_op jit(solution)/shard_map/ppermute | solution.py:67
  23.6 0.0 collective-permute-start.5
  23.6 2.3 %collective-permute-start.6 = (bf16[24,2048]{1,0:T(8,128)(2,1)S(1)}, bf16[24,2048]{1,0:T(8,128)(2,1)S(1)}, u32[]{:S(2)}, u32[]{:S(2)}) collective-permute-start(bf16[24,2048]{1,0:T(8,128)(2,1)S(1)} %get-tuple-element.64), channel_id=1, source_target_pairs={{0,6},{1,7},{2,4},{3,5},{4,2},{5,3},{6,0},{7,1},{8,14},{9,15},{10,... | collective-permute-start | bytes 294920 | tf_op jit(solution)/shard_map/ppermute | solution.py:67
  25.9 0.0 collective-permute-done.2.refs_0_
  25.9 1.3 %collective-permute-start.7 = (bf16[24,2048]{1,0:T(8,128)(2,1)S(1)}, bf16[24,2048]{1,0:T(8,128)(2,1)S(1)}, u32[]{:S(2)}, u32[]{:S(2)}) collective-permute-start(bf16[24,2048]{1,0:T(8,128)(2,1)S(1)} %get-tuple-element.65), channel_id=1, source_target_pairs={{0,7},{1,6},{2,5},{3,4},{4,3},{5,2},{6,1},{7,0},{8,15},{9,14},{10,... | collective-permute-start | bytes 294920 | tf_op jit(solution)/shard_map/ppermute | solution.py:67
  27.2 0.0 collective-permute-done.3.refs_1_
  27.2 0.0 collective-permute-start.8
  27.2 1.2 %copy.16 = bf16[8,24,1024]{2,1,0:T(8,128)(2,1)S(1)} copy(bf16[8,24,1024]{2,0,1:T(8,128)(2,1)} %bitcast.33) | data formatting | bytes 786432 | tf_op jit(solution)/shard_map/reshape | solution.py:475
  28.5 0.0 copy-done.4
  28.5 0.0 copy-done.5
  28.5 3.2 %shard_map.140 = (bf16[64,2048]{1,0:T(8,128)(2,1)}, bf16[64,2048]{1,0:T(8,128)(2,1)}, f32[2,8,64]{2,1,0:T(8,128)}, bf16[64,192]{1,0:T(8,128)(2,1)}, bf16[64,192]...) custom-call(bf16[64,2048]{1,0:T(8,128)(2,1)} %copy-done.4, ...), custom_call_target="tpu_custom_call" | custom-call | flops 100663296 | bytes 2883584 | tf_op jit(solution)/shard_map/pallas_call | solution.py:457
  31.8 3.3 %collective-permute-done.4.refs_2_ = bf16[24,2048]{1,0:T(8,128)(2,1)S(1)} collective-permute-done((bf16[24,2048]{1,0:T(8,128)(2,1)S(1)}, bf16[24,2048]{1,0:T(8,128)(2,1)S(1)}, u32[]{:S(2)}, u32[]{:S(2)}) %collective-permute-start.4) | collective-permute-done | bytes 98336 | tf_op jit(solution)/shard_map/ppermute | solution.py:67
  35.0 2.4 %collective-permute-done.5.refs_3_ = bf16[24,2048]{1,0:T(8,128)(2,1)S(1)} collective-permute-done((bf16[24,2048]{1,0:T(8,128)(2,1)S(1)}, bf16[24,2048]{1,0:T(8,128)(2,1)S(1)}, u32[]{:S(2)}, u32[]{:S(2)}) %collective-permute-start.5) | collective-permute-done | bytes 98336 | tf_op jit(solution)/shard_map/ppermute | solution.py:67
  37.4 0.0 collective-permute-done.6.refs_4_
  37.4 0.0 collective-permute-done.7.refs_5_
  37.4 1.0 collective-permute-done.8.refs_6_
  38.4 5.5 %all-to-all-start.1 = ((bf16[8,24,2048]{2,1,0:T(8,128)(2,1)}), bf16[8,24,2048]{2,1,0:T(8,128)(2,1)S(1)}, u32[]{:S(2)}, u32[]{:S(2)}) async-start(bf16[8,24,2048]{2,1,0:T(8,128)(2,1)} %bitcast.32), calls=%async_computation.1 | async-start | bytes 1572864 | tf_op jit(solution)/shard_map/all_to_all | solution.py:64
  43.9 20.6 %shard_map.143 = bf16[192,2176]{1,0:T(8,128)(2,1)} custom-call(bf16[8,32,1024]{2,1,0:T(8,128)(2,1)S(1)} %pad.4.saved_all, bf16[8,2048,1024]{2,1,0:T(8,128)(2,1)} %up.3, bf16[8,1024,2048]{2,1,0:T(8,128)(2,1)} %down.3, bf16[24,2048]{1,0:T(8,128)(2,1)S(1)} %collective-permute-done.2.refs_0_, bf16[24,2048]{1,0:T(8,128)(2,1)S(1)} %collective-permute-done.3.refs_1_, ...), custom_call_target="tpu_custom_call" | custom-call | flops 2147483648 | bytes 33554432 | tf_op jit(solution)/shard_map/pallas_call | solution.py:488
  64.5 0.4 all-to-all-done.1
  64.9 4.7 %all-to-all-start = ((bf16[8,24,2176]{2,1,0:T(8,128)(2,1)}), bf16[8,24,2176]{2,1,0:T(8,128)(2,1)S(1)}, u32[]{:S(2)}, u32[]{:S(2)}) async-start(bf16[8,24,2176]{2,1,0:T(8,128)(2,1)} %bitcast.14), calls=%async_computation | async-start | bytes 1671168 | tf_op jit(solution)/shard_map/all_to_all | solution.py:64
  69.6 0.0 copy-start.8
  69.6 0.0 copy-start.9
  69.7 0.0 copy-start.10
  69.7 0.0 copy-start.11
  69.7 0.0 copy-start.14
  69.7 0.0 copy-start.15
  69.7 0.0 copy-start.18
  69.7 0.0 copy-start
  69.7 0.0 copy-start.1
  69.7 20.5 %shard_map.144 = (bf16[24,2176]{1,0:T(8,128)(2,1)S(1)}, bf16[24,2176]{1,0:T(8,128)(2,1)S(1)}, bf16[24,2176]{1,0:T(8,128)(2,1)S(1)}, bf16[24,2176]{1,0:T(8,128)(2...) custom-call(bf16[8,32,1024]{2,1,0:T(8,128)(2,1)S(1)} %pad.4.saved_al, ...), custom_call_target="tpu_custom_call" | custom-call | flops 2147483648 | bytes 33554432 | tf_op jit(solution)/shard_map/pallas_call | solution.py:488
  90.3 0.5 collective-permute-start.9
  90.8 1.7 %collective-permute-start.10 = (bf16[24,2176]{1,0:T(8,128)(2,1)S(1)}, bf16[24,2176]{1,0:T(8,128)(2,1)S(1)}, u32[]{:S(2)}, u32[]{:S(2)}) collective-permute-start(bf16[24,2176]{1,0:T(8,128)(2,1)S(1)} %get-tuple-element.90), channel_id=1, source_target_pairs={{0,2},{1,3},{2,0},{3,1},{4,6},{5,7},{6,4},{7,5},{8,10},{9,11},{10,... | collective-permute-start | bytes 313352 | tf_op jit(solution)/shard_map/ppermute | solution.py:67
  92.5 2.4 %collective-permute-start.11 = (bf16[24,2176]{1,0:T(8,128)(2,1)}, bf16[24,2176]{1,0:T(8,128)(2,1)S(1)}, u32[]{:S(2)}, u32[]{:S(2)}) collective-permute-start(bf16[24,2176]{1,0:T(8,128)(2,1)} %get-tuple-element.91), channel_id=1, source_target_pairs={{0,4},{1,5},{2,6},{3,7},{4,0},{5,1},{6,2},{7,3},{8,12},{9,13},{10,... | collective-permute-start | bytes 313352 | tf_op jit(solution)/shard_map/ppermute | solution.py:67
  94.8 0.0 collective-permute-start.12
  94.8 2.3 %collective-permute-start.13 = (bf16[24,2176]{1,0:T(8,128)(2,1)}, bf16[24,2176]{1,0:T(8,128)(2,1)S(1)}, u32[]{:S(2)}, u32[]{:S(2)}) collective-permute-start(bf16[24,2176]{1,0:T(8,128)(2,1)} %get-tuple-element.93), channel_id=1, source_target_pairs={{0,6},{1,7},{2,4},{3,5},{4,2},{5,3},{6,0},{7,1},{8,14},{9,15},{10,... | collective-permute-start | bytes 313352 | tf_op jit(solution)/shard_map/ppermute | solution.py:67
  97.2 0.0 collective-permute-done.9.refs_0_
  97.2 1.5 %collective-permute-start.14 = (bf16[24,2176]{1,0:T(8,128)(2,1)}, bf16[24,2176]{1,0:T(8,128)(2,1)S(1)}, u32[]{:S(2)}, u32[]{:S(2)}) collective-permute-start(bf16[24,2176]{1,0:T(8,128)(2,1)} %get-tuple-element.94), channel_id=1, source_target_pairs={{0,7},{1,6},{2,5},{3,4},{4,3},{5,2},{6,1},{7,0},{8,15},{9,14},{10,... | collective-permute-start | bytes 313352 | tf_op jit(solution)/shard_map/ppermute | solution.py:67
  98.7 0.0 collective-permute-done.10.refs_1_
  98.7 0.0 collective-permute-start.15
  98.7 0.0 all-to-all-done
  98.8 0.9 copy-done.12
  99.7 0.6 shard_map.145
  100.2 7.6 %collective-permute-done.11.refs_2_ = bf16[24,2176]{1,0:T(8,128)(2,1)S(1)} collective-permute-done((bf16[24,2176]{1,0:T(8,128)(2,1)}, bf16[24,2176]{1,0:T(8,128)(2,1)S(1)}, u32[]{:S(2)}, u32[]{:S(2)}) %collective-permute-start.11) | collective-permute-done | bytes 104480 | tf_op jit(solution)/shard_map/ppermute | solution.py:67
  107.9 1.6 %collective-permute-done.12.refs_3_ = bf16[24,2176]{1,0:T(8,128)(2,1)S(1)} collective-permute-done((bf16[24,2176]{1,0:T(8,128)(2,1)}, bf16[24,2176]{1,0:T(8,128)(2,1)S(1)}, u32[]{:S(2)}, u32[]{:S(2)}) %collective-permute-start.12) | collective-permute-done | bytes 104480 | tf_op jit(solution)/shard_map/ppermute | solution.py:67
  109.5 0.0 collective-permute-done.13.refs_4_
  109.5 0.0 collective-permute-done.14.refs_5_
  109.5 1.6 %collective-permute-done.15.refs_6_ = bf16[24,2176]{1,0:T(8,128)(2,1)} collective-permute-done((bf16[24,2176]{1,0:T(8,128)(2,1)}, bf16[24,2176]{1,0:T(8,128)(2,1)}, u32[]{:S(2)}, u32[]{:S(2)}) %collective-permute-start.15) | collective-permute-done | bytes 104480 | tf_op jit(solution)/shard_map/ppermute | solution.py:67
  111.1 2.4 %shard_map.146 = (bf16[1,64,2048]{2,1,0:T(8,128)(2,1)}, bf16[1,64,2048]{2,1,0:T(8,128)(2,1)}) custom-call(f32[64,2048]{1,0:T(8,128)S(1)} %get-tuple-element.82.early_f, f32[64,2048]{1,0:T(8,128)S(1)} %get-tuple-element.83.early_b, f32[2,8,64]{2,1,0:T(8,128)S(1)} %get-tuple-element.84.early_inner, bf16[64,2048]{1,0:T(8,128)(2,1)S(1)} %get-tuple-element.85.upstream, ...), custom_call_target="tpu_custom_call" | custom-call | flops 100663296 | bytes 2883584 | tf_op jit(solution)/shard_map/pallas_call | solution.py:522
  (23 shorter events, 0.1 us)
Async XLA Ops:
  0.6 11.3 %collective-permute-start = (bf16[64,2048]{1,0:T(8,128)(2,1)}, bf16[64,2048]{1,0:T(8,128)(2,1)S(1)}, u32[]{:S(2)}, u32[]{:S(2)}) collective-permute-start(bf16[64,2048]{1,0:T(8,128)(2,1)} %bitcast.34), channel_id=1, source_target_pairs={{0,8},{8,16},{16,24},{1,9},{9,17},{17,25},{2,10},{10,18},{18,26},{... | collective-permute-start | bytes 786440 | tf_op jit(solution)/shard_map/ppermute | solution.py:45
  5.5 13.3 %collective-permute-start.1 = (bf16[64,2048]{1,0:T(8,128)(2,1)}, bf16[64,2048]{1,0:T(8,128)(2,1)S(1)}, u32[]{:S(2)}, u32[]{:S(2)}) collective-permute-start(bf16[64,2048]{1,0:T(8,128)(2,1)} %bitcast.35), channel_id=1, source_target_pairs={{8,0},{16,8},{24,16},{9,1},{17,9},{25,17},{10,2},{18,10},{26,18},{... | collective-permute-start | bytes 786440 | tf_op jit(solution)/shard_map/ppermute | solution.py:45
  6.8 1.0 copy-start.2
  7.7 0.9 copy-start.3
  8.7 0.9 copy-start.7
  9.6 0.7 copy-start.13
  10.3 0.7 copy-start.17
  11.0 0.7 copy-start.20
  11.9 16.6 %copy-start.4 = (bf16[64,2048]{1,0:T(8,128)(2,1)}, bf16[64,2048]{1,0:T(8,128)(2,1)S(1)}, u32[]{:S(2)}) copy-start(bf16[64,2048]{1,0:T(8,128)(2,1)S(1)} %collective-permute-done.arrived_f) | copy-start | bytes 786436
  18.8 9.7 %copy-start.5 = (bf16[64,2048]{1,0:T(8,128)(2,1)}, bf16[64,2048]{1,0:T(8,128)(2,1)S(1)}, u32[]{:S(2)}) copy-start(bf16[64,2048]{1,0:T(8,128)(2,1)S(1)} %collective-permute-done.1.arrived_b) | copy-start | bytes 786436
  19.3 6.6 %collective-permute-start.2 = (bf16[24,2048]{1,0:T(8,128)(2,1)S(1)}, bf16[24,2048]{1,0:T(8,128)(2,1)S(1)}, u32[]{:S(2)}, u32[]{:S(2)}) collective-permute-start(bf16[24,2048]{1,0:T(8,128)(2,1)S(1)} %get-tuple-element.60), channel_id=1, source_target_pairs={{0,1},{1,0},{2,3},{3,2},{4,5},{5,4},{6,7},{7,6},{8,9},{9,8},{10,11... | collective-permute-start | bytes 294920 | tf_op jit(solution)/shard_map/ppermute | solution.py:67
  19.4 7.8 %collective-permute-start.3 = (bf16[24,2048]{1,0:T(8,128)(2,1)S(1)}, bf16[24,2048]{1,0:T(8,128)(2,1)S(1)}, u32[]{:S(2)}, u32[]{:S(2)}) collective-permute-start(bf16[24,2048]{1,0:T(8,128)(2,1)S(1)} %get-tuple-element.61), channel_id=1, source_target_pairs={{0,2},{1,3},{2,0},{3,1},{4,6},{5,7},{6,4},{7,5},{8,10},{9,11},{10,... | collective-permute-start | bytes 294920 | tf_op jit(solution)/shard_map/ppermute | solution.py:67
  21.0 14.0 %collective-permute-start.4 = (bf16[24,2048]{1,0:T(8,128)(2,1)S(1)}, bf16[24,2048]{1,0:T(8,128)(2,1)S(1)}, u32[]{:S(2)}, u32[]{:S(2)}) collective-permute-start(bf16[24,2048]{1,0:T(8,128)(2,1)S(1)} %get-tuple-element.62), channel_id=1, source_target_pairs={{0,4},{1,5},{2,6},{3,7},{4,0},{5,1},{6,2},{7,3},{8,12},{9,13},{10,... | collective-permute-start | bytes 294920 | tf_op jit(solution)/shard_map/ppermute | solution.py:67
  23.6 13.8 %collective-permute-start.5 = (bf16[24,2048]{1,0:T(8,128)(2,1)S(1)}, bf16[24,2048]{1,0:T(8,128)(2,1)S(1)}, u32[]{:S(2)}, u32[]{:S(2)}) collective-permute-start(bf16[24,2048]{1,0:T(8,128)(2,1)S(1)} %get-tuple-element.63), channel_id=1, source_target_pairs={{0,5},{1,4},{2,7},{3,6},{4,1},{5,0},{6,3},{7,2},{8,13},{9,12},{10,... | collective-permute-start | bytes 294920 | tf_op jit(solution)/shard_map/ppermute | solution.py:67
  23.6 13.8 %collective-permute-start.6 = (bf16[24,2048]{1,0:T(8,128)(2,1)S(1)}, bf16[24,2048]{1,0:T(8,128)(2,1)S(1)}, u32[]{:S(2)}, u32[]{:S(2)}) collective-permute-start(bf16[24,2048]{1,0:T(8,128)(2,1)S(1)} %get-tuple-element.64), channel_id=1, source_target_pairs={{0,6},{1,7},{2,4},{3,5},{4,2},{5,3},{6,0},{7,1},{8,14},{9,15},{10,... | collective-permute-start | bytes 294920 | tf_op jit(solution)/shard_map/ppermute | solution.py:67
  25.9 11.5 %collective-permute-start.7 = (bf16[24,2048]{1,0:T(8,128)(2,1)S(1)}, bf16[24,2048]{1,0:T(8,128)(2,1)S(1)}, u32[]{:S(2)}, u32[]{:S(2)}) collective-permute-start(bf16[24,2048]{1,0:T(8,128)(2,1)S(1)} %get-tuple-element.65), channel_id=1, source_target_pairs={{0,7},{1,6},{2,5},{3,4},{4,3},{5,2},{6,1},{7,0},{8,15},{9,14},{10,... | collective-permute-start | bytes 294920 | tf_op jit(solution)/shard_map/ppermute | solution.py:67
  27.2 11.2 %collective-permute-start.8 = (bf16[24,2048]{1,0:T(8,128)(2,1)S(1)}, bf16[24,2048]{1,0:T(8,128)(2,1)S(1)}, u32[]{:S(2)}, u32[]{:S(2)}) collective-permute-start(bf16[24,2048]{1,0:T(8,128)(2,1)S(1)} %get-tuple-element.66), channel_id=1, source_target_pairs={{0,3},{1,2},{2,1},{3,0},{4,7},{5,6},{6,5},{7,4},{8,11},{9,10},{10,... | collective-permute-start | bytes 294920 | tf_op jit(solution)/shard_map/ppermute | solution.py:67
  38.4 26.5 %all-to-all-start.1 = ((bf16[8,24,2048]{2,1,0:T(8,128)(2,1)}), bf16[8,24,2048]{2,1,0:T(8,128)(2,1)S(1)}, u32[]{:S(2)}, u32[]{:S(2)}) async-start(bf16[8,24,2048]{2,1,0:T(8,128)(2,1)} %bitcast.32), calls=%async_computation.1 | async-start | bytes 1572864 | tf_op jit(solution)/shard_map/all_to_all | solution.py:64
  64.9 33.8 %all-to-all-start = ((bf16[8,24,2176]{2,1,0:T(8,128)(2,1)}), bf16[8,24,2176]{2,1,0:T(8,128)(2,1)S(1)}, u32[]{:S(2)}, u32[]{:S(2)}) async-start(bf16[8,24,2176]{2,1,0:T(8,128)(2,1)} %bitcast.14), calls=%async_computation | async-start | bytes 1671168 | tf_op jit(solution)/shard_map/all_to_all | solution.py:64
  69.6 29.1 %copy-start.6 = (bf16[2,192,64]{2,1,0:T(8,128)(2,1)S(1)}, bf16[2,192,64]{2,1,0:T(8,128)(2,1)}, u32[]{:S(2)}) copy-start(bf16[2,192,64]{2,1,0:T(8,128)(2,1)} %get-tuple-element.79.refs_10_.tables) | copy-start | bytes 147460
  69.6 29.1 %copy-start.8 = (bf16[64,2048]{1,0:T(8,128)(2,1)S(1)}, bf16[64,2048]{1,0:T(8,128)(2,1)}, u32[]{:S(2)}) copy-start(bf16[64,2048]{1,0:T(8,128)(2,1)} %get-tuple-element.49.tokens) | copy-start | bytes 786436
  69.6 29.1 %copy-start.9 = (bf16[64,2048]{1,0:T(8,128)(2,1)S(1)}, bf16[64,2048]{1,0:T(8,128)(2,1)}, u32[]{:S(2)}) copy-start(bf16[64,2048]{1,0:T(8,128)(2,1)} %get-tuple-element.50.refs_0_) | copy-start | bytes 786436
  69.7 29.1 %copy-start.10 = (bf16[64,192]{1,0:T(8,128)(2,1)S(1)}, bf16[64,192]{1,0:T(8,128)(2,1)}, u32[]{:S(2)}) copy-start(bf16[64,192]{1,0:T(8,128)(2,1)} %get-tuple-element.77.refs_8_.mixing_f) | copy-start | bytes 73732
  69.7 29.1 %copy-start.11 = (bf16[64,192]{1,0:T(8,128)(2,1)S(1)}, bf16[64,192]{1,0:T(8,128)(2,1)}, u32[]{:S(2)}) copy-start(bf16[64,192]{1,0:T(8,128)(2,1)} %get-tuple-element.78.refs_9_.mixing_b) | copy-start | bytes 73732
  69.7 29.1 %copy-start.14 = (bf16[1,2048]{1,0:T(2,128)(2,1)S(1)}, bf16[1,2048]{1,0:T(2,128)(2,1)}, u32[]{:S(2)}) copy-start(bf16[1,2048]{1,0:T(2,128)(2,1)} %refs_1_.1) | copy-start | bytes 12292
  69.7 29.1 %copy-start.15 = (bf16[64,192]{1,0:T(8,128)(2,1)S(1)}, bf16[64,192]{1,0:T(8,128)(2,1)}, u32[]{:S(2)}) copy-start(bf16[64,192]{1,0:T(8,128)(2,1)} %get-tuple-element.52.refs_4_) | copy-start | bytes 73732
  69.7 29.1 %copy-start.16 = (bf16[64,192]{1,0:T(8,128)(2,1)S(1)}, bf16[64,192]{1,0:T(8,128)(2,1)}, u32[]{:S(2)}) copy-start(bf16[64,192]{1,0:T(8,128)(2,1)} %get-tuple-element.53.refs_5_) | copy-start | bytes 73732
  69.7 29.1 %copy-start.18 = (s32[1,64,2]{1,2,0:T(2,128)S(1)}, s32[1,64,2]{1,2,0:T(2,128)}, u32[]{:S(2)}) copy-start(s32[1,64,2]{1,2,0:T(2,128)} %param.19) | copy-start | bytes 1540
  69.7 29.1 %copy-start.19 = (f32[2,8,64]{2,1,0:T(8,128)S(1)}, f32[2,8,64]{2,1,0:T(8,128)}, u32[]{:S(2)}) copy-start(f32[2,8,64]{2,1,0:T(8,128)} %get-tuple-element.51.refs_3_) | copy-start | bytes 12292
  69.7 41.4 %copy-start = (bf16[1,64,2048]{2,1,0:T(8,128)(2,1)S(1)}, bf16[1,64,2048]{2,1,0:T(8,128)(2,1)}, u32[]{:S(2)}) copy-start(bf16[1,64,2048]{2,1,0:T(8,128)(2,1)} %param.18) | copy-start | bytes 786436
  69.7 41.4 %copy-start.1 = (bf16[1,2048,64]{1,2,0:T(8,128)(2,1)S(1)}, bf16[1,2048,64]{1,2,0:T(8,128)(2,1)}, u32[]{:S(2)}) copy-start(bf16[1,2048,64]{1,2,0:T(8,128)(2,1)} %param.22) | copy-start | bytes 786436
  90.3 6.9 %collective-permute-start.9 = (bf16[24,2176]{1,0:T(8,128)(2,1)S(1)}, bf16[24,2176]{1,0:T(8,128)(2,1)S(1)}, u32[]{:S(2)}, u32[]{:S(2)}) collective-permute-start(bf16[24,2176]{1,0:T(8,128)(2,1)S(1)} %get-tuple-element.89), channel_id=1, source_target_pairs={{0,1},{1,0},{2,3},{3,2},{4,5},{5,4},{6,7},{7,6},{8,9},{9,8},{10,11... | collective-permute-start | bytes 313352 | tf_op jit(solution)/shard_map/ppermute | solution.py:67
  90.8 7.9 %collective-permute-start.10 = (bf16[24,2176]{1,0:T(8,128)(2,1)S(1)}, bf16[24,2176]{1,0:T(8,128)(2,1)S(1)}, u32[]{:S(2)}, u32[]{:S(2)}) collective-permute-start(bf16[24,2176]{1,0:T(8,128)(2,1)S(1)} %get-tuple-element.90), channel_id=1, source_target_pairs={{0,2},{1,3},{2,0},{3,1},{4,6},{5,7},{6,4},{7,5},{8,10},{9,11},{10,... | collective-permute-start | bytes 313352 | tf_op jit(solution)/shard_map/ppermute | solution.py:67
  92.5 15.4 %collective-permute-start.11 = (bf16[24,2176]{1,0:T(8,128)(2,1)}, bf16[24,2176]{1,0:T(8,128)(2,1)S(1)}, u32[]{:S(2)}, u32[]{:S(2)}) collective-permute-start(bf16[24,2176]{1,0:T(8,128)(2,1)} %get-tuple-element.91), channel_id=1, source_target_pairs={{0,4},{1,5},{2,6},{3,7},{4,0},{5,1},{6,2},{7,3},{8,12},{9,13},{10,... | collective-permute-start | bytes 313352 | tf_op jit(solution)/shard_map/ppermute | solution.py:67
  94.8 14.6 %collective-permute-start.12 = (bf16[24,2176]{1,0:T(8,128)(2,1)}, bf16[24,2176]{1,0:T(8,128)(2,1)S(1)}, u32[]{:S(2)}, u32[]{:S(2)}) collective-permute-start(bf16[24,2176]{1,0:T(8,128)(2,1)} %get-tuple-element.92), channel_id=1, source_target_pairs={{0,5},{1,4},{2,7},{3,6},{4,1},{5,0},{6,3},{7,2},{8,13},{9,12},{10,... | collective-permute-start | bytes 313352 | tf_op jit(solution)/shard_map/ppermute | solution.py:67
  94.8 14.6 %collective-permute-start.13 = (bf16[24,2176]{1,0:T(8,128)(2,1)}, bf16[24,2176]{1,0:T(8,128)(2,1)S(1)}, u32[]{:S(2)}, u32[]{:S(2)}) collective-permute-start(bf16[24,2176]{1,0:T(8,128)(2,1)} %get-tuple-element.93), channel_id=1, source_target_pairs={{0,6},{1,7},{2,4},{3,5},{4,2},{5,3},{6,0},{7,1},{8,14},{9,15},{10,... | collective-permute-start | bytes 313352 | tf_op jit(solution)/shard_map/ppermute | solution.py:67
  97.2 12.3 %collective-permute-start.14 = (bf16[24,2176]{1,0:T(8,128)(2,1)}, bf16[24,2176]{1,0:T(8,128)(2,1)S(1)}, u32[]{:S(2)}, u32[]{:S(2)}) collective-permute-start(bf16[24,2176]{1,0:T(8,128)(2,1)} %get-tuple-element.94), channel_id=1, source_target_pairs={{0,7},{1,6},{2,5},{3,4},{4,3},{5,2},{6,1},{7,0},{8,15},{9,14},{10,... | collective-permute-start | bytes 313352 | tf_op jit(solution)/shard_map/ppermute | solution.py:67
  98.7 12.4 %collective-permute-start.15 = (bf16[24,2176]{1,0:T(8,128)(2,1)}, bf16[24,2176]{1,0:T(8,128)(2,1)}, u32[]{:S(2)}, u32[]{:S(2)}) collective-permute-start(bf16[24,2176]{1,0:T(8,128)(2,1)} %get-tuple-element.95), channel_id=1, source_target_pairs={{0,3},{1,2},{2,1},{3,0},{4,7},{5,6},{6,5},{7,4},{8,11},{9,10},{10,... | collective-permute-start | bytes 313352 | tf_op jit(solution)/shard_map/ppermute | solution.py:67
  98.8 0.9 copy-start.12
